TPU v7x, 32 devices: a whole 2x2x4 slice. The times are simulated.
32 devices in a mesh: groups: 2 (over y), wide: 16 (over z, x, core).
Axes of the slice: x: 2, y: 2, z: 4, core: 2. Of those that a mesh axis runs over, the one named last changes fastest.
Arguments:
- tokens: bfloat16 [4096, 16384], P(('groups', 'wide')), parts along dimension 0, may hold values from -36 to 36, as said below
- norm_gain: float32 [16384], replicated, may hold values from 0.5 to 1.5
- gate_weight: bfloat16 [16384, 256], P('wide'), may hold values from -0.046875 to 0.046875
- up_weight: bfloat16 [16384, 256], P('wide'), may hold values from -0.046875 to 0.046875
- down_weight: bfloat16 [256, 16384], P(None, 'wide'), may hold values from -0.375 to 0.375
- owner_rows: int32 [16], replicated, may hold values from 0 to 15, each once
- seg_counts: int32 [32], P(('groups', 'wide')), parts along dimension 0, may hold values from 1 to 112, as said below
Outputs:
- mlp_out: bfloat16 [4096, 16384], P(('groups', 'wide')), parts along dimension 0
There are 2 independent parts, one for each index of `groups`. A program takes and returns all parts, laid end to end along the dimension named above; an argument that names none is the same for every part. Nothing has to cross between parts.
Inputs may be any that keep to these rules, and one draw needn't show every extreme that they name: `tokens`: activations of mixed scale. `owner_rows`: each index of wide stores exactly one block. `seg_counts`: some document has all 112 segment tokens live.
All inputs are finite; a program needn't handle non-finite values.
Results may differ from a plain program's by a relative error of at most 0.0065.
Values may be sent and summed in bfloat16 or wider, within the bound.
No kernel may reach another device: no remote copies, remote signals or barrier semaphores. Data moves between devices by JAX's collectives and lax.ppermute only.
A program may use at most 128 MiB of HBM per device.

v0:
```python
import jax
import jax.numpy as jnp
from jax import lax
from jax.sharding import PartitionSpec as P

MEM = 16


def shards(tokens, norm_gain, gate_weight, up_weight, down_weight, owner_rows, seg_counts):
    row_count = tokens.shape[0]
    model_width = tokens.shape[1]
    owners = lax.axis_size("wide")
    block_rows = model_width // owners
    indices = jnp.arange(owners, dtype=jnp.int32)
    holder = jnp.sum(
        indices[:, None] * (owner_rows[:, None] == indices[None, :]).astype(jnp.int32), axis=0
    )
    features = tokens.astype(jnp.float32)
    mean_square = jnp.mean(features * features, axis=1, keepdims=True)
    normed = (features * lax.rsqrt(mean_square + 1e-05) * norm_gain[None, :]).astype(jnp.bfloat16)
    stored = normed.reshape(row_count, owners, block_rows)[:, holder, :].reshape(
        row_count, model_width
    )

    def partial_product(portion):
        return jnp.dot(stored, portion, preferred_element_type=jnp.float32)

    gate_sum = partial_product(lax.all_gather(gate_weight, "wide", axis=0, tiled=True))
    up_sum = partial_product(lax.all_gather(up_weight, "wide", axis=0, tiled=True))
    hidden = (jax.nn.silu(gate_sum) * up_sum).astype(jnp.bfloat16)
    stored_out = jnp.dot(
        hidden,
        lax.all_gather(down_weight, "wide", axis=1, tiled=True),
        preferred_element_type=jnp.float32,
    ).astype(jnp.bfloat16)
    product = stored_out.reshape(row_count, owners, block_rows)[:, owner_rows, :].reshape(
        row_count, model_width
    )
    live_mask = (jnp.arange(row_count, dtype=jnp.int32) < MEM + seg_counts[0]).astype(jnp.bfloat16)
    return product * live_mask[:, None]


def solution(mesh):
    placed = (
        P(("groups", "wide"), None),
        P(),
        P("wide", None),
        P("wide", None),
        P(None, "wide"),
        P(),
        P(("groups", "wide")),
    )
    return jax.shard_map(
        shards, mesh=mesh, in_specs=placed, out_specs=P(("groups", "wide"), None), check_vma=False
    )
```

profile of v0, /device:TPU:0, one launch (start us, length us, event | category | flops | bytes accessed | tf_op | source)
XLA Modules:
  0.0 284.3 jit_solution(15611034805441645362)
XLA Ops:
  6.5 0.7 all-gather.4.cloned.1.call-update
  7.3 0.0 all-gather.6.cloned.1.call-start
  7.3 0.7 all-gather.6.cloned.1.call-update
  8.0 0.0 all-gather.8.cloned.1.call-start
  8.1 0.7 all-gather.8.cloned.1.call-update
  8.8 6.4 %copy.15 = bf16[128,16384]{0,1:T(8,128)(2,1)} copy(bf16[128,16384]{1,0:T(8,128)(2,1)} %param.7) | data formatting | bytes 8388608 | tf_op args[0]
  15.1 3.9 %fusion = f32[128]{0:T(128)S(1)} fusion(bf16[128,16384]{0,1:T(8,128)(2,1)} %copy.15), kind=kLoop, calls=%fused_computation.5 | loop fusion | flops 6291328 | bytes 4194816 | tf_op jit(solution)/shard_map/reduce_sum | solution.py:19
  19.1 7.8 %fusion.2 = bf16[128,16384]{0,1:T(8,128)(2,1)} fusion(bf16[128,16384]{0,1:T(8,128)(2,1)S(1)} %copy-done, f32[16384]{0:T(1024)S(1)} %copy-done.1, f32[128]{0:T(128)S(1)} %add_rsqrt_fusion), kind=kLoop, calls=%fused_computation.7 | loop fusion | flops 8388608 | bytes 8454656 | tf_op jit(solution)/shard_map/convert_element_type | solution.py:20
  26.9 6.4 %copy.16 = bf16[128,16,1024]{2,0,1:T(8,128)(2,1)} copy(bf16[128,16,1024]{0,2,1:T(8,128)(2,1)} %bitcast.23) | data formatting | bytes 8388608 | tf_op jit(solution)/shard_map/reshape | solution.py:21
  33.2 0.1 select_reduce_fusion
  33.4 5.0 %gather_fusion = bf16[16,128,1024]{2,1,0:T(8,128)(2,1)} fusion(bf16[128,16,1024]{2,0,1:T(8,128)(2,1)} %copy.16, s32[1024]{0:T(1024)S(1)} %pad_clamp_fusion.1), kind=kCustom, calls=%fused_computation | custom fusion | bytes 8388672 | tf_op jit(solution)/shard_map/gather | solution.py:21
  38.4 6.4 %copy.17 = bf16[128,16,1024]{0,2,1:T(8,128)(2,1)} copy(bf16[128,16,1024]{2,0,1:T(8,128)(2,1)} %bitcast.24) | data formatting | bytes 8388608 | tf_op jit(solution)/shard_map/gather | solution.py:21
  45.4 0.5 compare_convert_fusion
  45.9 0.6 pad_clamp_fusion
  46.5 40.6 %all-gather.4.cloned.1.call-done = bf16[16384,256]{1,0:T(8,128)(2,1)} async-done(((bf16[1024,256]{1,0:T(8,128)(2,1)}), bf16[16384,256]{1,0:T(8,128)(2,1)}) %all-gather.4.cloned.1.call-update) | async-done | bytes 8388624 | tf_op jit(solution)/shard_map/all_gather | solution.py:28
  87.1 6.2 %fusion.12 = f32[128,256]{1,0:T(8,128)S(1)} fusion(bf16[128,16384]{0,1:T(8,128)(2,1)} %bitcast.20, bf16[16384,256]{1,0:T(8,128)(2,1)} %all-gather.4.cloned.1.call-done), kind=kOutput, calls=%fused_computation.28 | convolution fusion | flops 1073741824 | bytes 12713984 | tf_op jit(solution)/shard_map/dot_general | solution.py:26
  93.3 69.2 %all-gather.6.cloned.1.call-done = bf16[16384,256]{1,0:T(8,128)(2,1)} async-done(((bf16[1024,256]{1,0:T(8,128)(2,1)}), bf16[16384,256]{1,0:T(8,128)(2,1)}) %all-gather.6.cloned.1.call-update) | async-done | bytes 8388624 | tf_op jit(solution)/shard_map/all_gather | solution.py:29
  162.5 75.4 %all-gather.8.cloned.1.call-done = bf16[256,16384]{1,0:T(8,128)(2,1)} async-done(((bf16[256,1024]{1,0:T(8,128)(2,1)}), bf16[256,16384]{1,0:T(8,128)(2,1)}) %all-gather.8.cloned.1.call-update) | async-done | bytes 8388624 | tf_op jit(solution)/shard_map/all_gather | solution.py:33
  237.9 13.6 %convolution_convert_fusion = bf16[128,16384]{1,0:T(8,128)(2,1)} fusion(bf16[256,16384]{1,0:T(8,128)(2,1)} %all-gather.8.cloned.1.call-done, bf16[128,16384]{0,1:T(8,128)(2,1)} %bitcast.21, bf16[16384,256]{1,0:T(8,128)(2,1)} %all-gather.6.cloned.1.call-done, f32[128,256]{1,0:T(8,128)S(1)} %fusion.12), kind=kOutput, calls=%fused_computation.2 | convolution fusion | flops 2149777408 | bytes 25296896 | tf_op jit(solution)/shard_map/dot_general | solution.py:31
  251.5 4.8 %copy.23 = bf16[16,16,8,1024]{3,2,0,1:T(8,128)(2,1)} copy(bf16[16,16,8,1024]{3,2,1,0:T(8,128)(2,1)} %bitcast.22) | data formatting | bytes 8388608 | tf_op jit(solution)/shard_map/reshape | solution.py:36
  256.2 5.1 %gather_fusion.1 = bf16[16,128,1024]{2,1,0:T(8,128)(2,1)} fusion(bf16[128,16,1024]{2,0,1:T(8,128)(2,1)} %bitcast.25, s32[1024]{0:T(1024)} %pad_clamp_fusion), kind=kCustom, calls=%fused_computation.1 | custom fusion | bytes 8388672 | tf_op jit(solution)/shard_map/gather | solution.py:36
  261.4 6.4 %copy.19 = bf16[128,16,1024]{0,2,1:T(8,128)(2,1)} copy(bf16[128,16,1024]{2,0,1:T(8,128)(2,1)} %bitcast.26) | data formatting | bytes 8388608 | tf_op jit(solution)/shard_map/gather | solution.py:36
  267.7 3.7 %bitcast_multiply_fusion = bf16[128,16384]{0,1:T(8,128)(2,1)} fusion(bf16[128,16,1024]{0,2,1:T(8,128)(2,1)} %copy.19, bf16[128]{0:T(256)(128)(2,1)S(1)} %copy-done.2), kind=kLoop, calls=%fused_computation.9 | loop fusion | flops 2097152 | bytes 8388864 | tf_op jit(solution)/shard_map/mul | solution.py:40
  271.5 6.4 %copy.20 = bf16[128,16384]{1,0:T(8,128)(2,1)} copy(bf16[128,16384]{0,1:T(8,128)(2,1)} %bitcast_multiply_fusion) | data formatting | bytes 8388608 | tf_op jit(solution)/shard_map/mul | solution.py:40
  (13 shorter events, 0.0 us)
Async XLA Ops:
  6.5 80.6 %all-gather.4.cloned.1.call-start = ((), (), s32[]{:S(2)}) async-start(), calls=%async_computation | async-start | bytes 8912896 | tf_op jit(solution)/shard_map/all_gather | solution.py:28
  7.3 155.2 %all-gather.6.cloned.1.call-start = ((), (), s32[]{:S(2)}) async-start(), calls=%async_computation.1 | async-start | bytes 8912896 | tf_op jit(solution)/shard_map/all_gather | solution.py:29
  8.0 229.9 %all-gather.8.cloned.1.call-start = ((), (), s32[]{:S(2)}) async-start(), calls=%async_computation.2 | async-start | bytes 8912896 | tf_op jit(solution)/shard_map/all_gather | solution.py:33
  8.7 10.3 %copy-start.1 = (f32[16384]{0:T(1024)S(1)}, f32[16384]{0:T(1024)}, u32[]{:S(2)}) copy-start(f32[16384]{0:T(1024)} %param.8) | copy-start | bytes 196612
  15.1 3.9 %copy-start = (bf16[128,16384]{0,1:T(8,128)(2,1)S(1)}, bf16[128,16384]{0,1:T(8,128)(2,1)}, u32[]{:S(2)}) copy-start(bf16[128,16384]{0,1:T(8,128)(2,1)} %copy.15) | copy-start | bytes 12582916
  26.9 6.4 %copy-start.3 = (s32[16]{0:T(128)S(1)}, s32[16]{0:T(128)}, u32[]{:S(2)}) copy-start(s32[16]{0:T(128)} %param.12) | copy-start | bytes 196
  261.4 6.4 %copy-start.2 = (bf16[128]{0:T(256)(128)(2,1)S(1)}, bf16[128]{0:T(256)(128)(2,1)}, u32[]{:S(2)}) copy-start(bf16[128]{0:T(256)(128)(2,1)} %compare_convert_fusion) | copy-start | bytes 772
Sparse Core Ops, SparseCore 0:
  9.5 77.5 all-gather.3
  89.3 73.1 all-gather.5
  164.7 73.1 all-gather.7
where the time goes:
time: 285 us; the launch traced here: 284 us
  waiting for transfers between devices  187 us (66%)
  local copies, waits for them, and re-layouts  46.8 us (16%)
  matrix products  19.8 us (7%)
  other arithmetic  16.6 us (6%)
  between operations  13.8 us (5%)
    all_gather x1, waiting for transfers between devices, shards(): lax.all_gather(down_weight, 'wide', axis=1, tiled=True)  75.4 us
    all_gather x1, waiting for transfers between devices, shards(): lax.all_gather(up_weight, 'wide', axis=0, tiled=True)  69.2 us
    all_gather x1, waiting for transfers between devices, shards(): lax.all_gather(gate_weight, 'wide', axis=0, tiled=True)  40.6 us
    dot_general x1, matrix products, shards(): jnp.dot(hidden, lax.all_gather(down_weight, 'wide', axis=1, tiled=True),...  13.6 us
    gather x2, local copies, waits for them, and re-layouts, shards(): stored_out.reshape(row_count, owners, block_rows)[:, owner_rows, :]  11.5 us
    gather x2, local copies, waits for them, and re-layouts, shards(): normed.reshape(row_count, owners, block_rows)[:, holder, :]  11.4 us
    convert_element_type x1, other arithmetic, shards(): (features * lax.rsqrt(mean_square + 1e-05) * norm_gain[None, :]).astype(j...  7.78 us
    unnamed x9, local copies, waits for them, and re-layouts  6.41 us
  transfers between devices with their start and end apart: 3, of which 3 were waited for; matrix products, arithmetic and copies ran while one was open for 15% of the time, Pallas kernels for 0%

commit v1 on v0

v1 whole, which is shorter than its diff:
```python
import functools

import jax
import jax.numpy as jnp
from jax import lax
from jax.experimental import pallas as pl
from jax.experimental.pallas import tpu as pltpu
from jax.sharding import PartitionSpec as P

MEM = 16
ALL = ("groups", "wide")
F32, BF16 = jnp.float32, jnp.bfloat16
VMEM = pl.BlockSpec(memory_space=pltpu.VMEM)
SMEM = pl.BlockSpec(memory_space=pltpu.SMEM)


def gathered(tokens, norm_gain, gate_weight, up_weight, down_weight, owner_rows, seg_counts):
    row_count, model_width = tokens.shape
    owners = lax.axis_size("wide")
    block_rows = model_width // owners
    indices = jnp.arange(owners, dtype=jnp.int32)
    holder = jnp.sum(
        indices[:, None] * (owner_rows[:, None] == indices[None, :]).astype(jnp.int32), axis=0
    )
    features = tokens.astype(F32)
    mean_square = jnp.mean(features * features, axis=1, keepdims=True)
    normed = (features * lax.rsqrt(mean_square + 1e-05) * norm_gain[None, :]).astype(BF16)
    stored = normed.reshape(row_count, owners, block_rows)[:, holder, :].reshape(
        row_count, model_width
    )

    def partial_product(portion):
        return jnp.dot(stored, portion, preferred_element_type=F32)

    gate_sum = partial_product(lax.all_gather(gate_weight, "wide", axis=0, tiled=True))
    up_sum = partial_product(lax.all_gather(up_weight, "wide", axis=0, tiled=True))
    hidden = (jax.nn.silu(gate_sum) * up_sum).astype(BF16)
    stored_out = jnp.dot(
        hidden,
        lax.all_gather(down_weight, "wide", axis=1, tiled=True),
        preferred_element_type=F32,
    ).astype(BF16)
    product = stored_out.reshape(row_count, owners, block_rows)[:, owner_rows, :].reshape(
        row_count, model_width
    )
    live_mask = (jnp.arange(row_count, dtype=jnp.int32) < MEM + seg_counts[0]).astype(BF16)
    return product * live_mask[:, None]


def norm_kernel(places_ref, tokens_ref, gain_ref, *rest):
    *outs, scale_ref = rest
    i = pl.program_id(0)
    per_quarter = pl.num_programs(0) // len(outs)
    width = outs[0].shape[2]

    @pl.when(i == 0)
    def _():
        total = jnp.zeros((tokens_ref.shape[0], 128), F32)
        for start in range(0, tokens_ref.shape[1], 128):
            part = tokens_ref[:, start : start + 128].astype(F32)
            total += part * part
        mean = jnp.sum(total, axis=1, keepdims=True) / tokens_ref.shape[1]
        scale_ref[...] = jnp.broadcast_to(lax.rsqrt(mean + 1e-05), scale_ref.shape)

    columns = pl.ds(pl.multiple_of(places_ref[i] * width, width), width)
    normed = tokens_ref[:, columns].astype(F32) * scale_ref[:, :1] * gain_ref[:, columns]
    for q, out in enumerate(outs):

        @pl.when(i // per_quarter == q)
        def _(out=out):
            out[0] = normed.astype(BF16)


def normed_quarters(tokens, gain, places, quarters):
    rows, model_width = tokens.shape
    blocks = places.shape[0]
    per_quarter = blocks // quarters
    width = model_width // blocks

    def out_spec(q):
        return pl.BlockSpec(
            (1, rows, width),
            lambda i, places: (jnp.clip(i - q * per_quarter, 0, per_quarter - 1), 0, 0),
        )

    return pl.pallas_call(
        norm_kernel,
        grid_spec=pltpu.PrefetchScalarGridSpec(
            num_scalar_prefetch=1,
            grid=(blocks,),
            in_specs=[
                pl.BlockSpec((rows, model_width), lambda i, places: (0, 0)),
                pl.BlockSpec((1, model_width), lambda i, places: (0, 0)),
            ],
            out_specs=[out_spec(q) for q in range(quarters)],
            scratch_shapes=[pltpu.VMEM((rows, 128), F32)],
        ),
        out_shape=[jax.ShapeDtypeStruct((per_quarter, rows, width), BF16)] * quarters,
        compiler_params=pltpu.CompilerParams(vmem_limit_bytes=20 << 20),
        cost_estimate=pl.CostEstimate(
            flops=6 * rows * model_width, bytes_accessed=4 * rows * model_width, transcendentals=0
        ),
        name="norm_quarters",
    )(places, tokens, gain.reshape(1, model_width))


def partial_kernel(count, types, where_ref, *refs):
    inputs, rest = refs[:count], refs[count:]
    outs = rest[-len(types) :]
    weights = rest[: -len(types)]
    half = len(weights) // 2
    hid = weights[0].shape[1]
    swap = where_ref[half]
    for rows, out, kind in zip(inputs, outs, types):
        sums = []
        for side in range(2):
            total = jnp.zeros((rows.shape[1], hid), F32)
            for j in range(half):
                total += jnp.dot(
                    rows[where_ref[j]], weights[side * half + j][...], preferred_element_type=F32
                )
            sums.append(total)
        mine, other = sums
        first = swap == 0
        out[:, :hid] = jnp.where(first, mine, other).astype(kind)
        out[:, hid:] = jnp.where(first, other, mine).astype(kind)


def partial_sums(where, inputs, weights, types):
    rows, hid = inputs[0].shape[1], weights[0].shape[1]
    depth = weights[0].shape[0] * len(weights) // 2
    return pl.pallas_call(
        functools.partial(partial_kernel, len(inputs), types),
        in_specs=[SMEM] + [VMEM] * (len(inputs) + len(weights)),
        out_specs=[VMEM] * len(inputs),
        out_shape=[jax.ShapeDtypeStruct((rows, 2 * hid), kind) for kind in types],
        compiler_params=pltpu.CompilerParams(vmem_limit_bytes=20 << 20),
        cost_estimate=pl.CostEstimate(
            flops=4 * len(inputs) * rows * depth * hid,
            bytes_accessed=2 * depth * (len(inputs) * rows + 2 * hid),
            transcendentals=0,
        ),
        name="partial_sums",
    )(where, *inputs, *weights)


def down_kernel(shapes, at_ref, live_ref, own, *refs):
    partials, weights, out = refs[:3], refs[3:-1], refs[-1]
    hid = own.shape[1] // 2
    total = own[...]
    for part in partials:
        total += part[...].astype(F32)
    gate, up = total[:, :hid], total[:, hid:]
    hidden = (gate / (1.0 + jnp.exp(-gate)) * up).astype(BF16)
    rows = lax.broadcasted_iota(jnp.int32, (out.shape[0], 1), 0)
    live = (rows < MEM + live_ref[0]).astype(F32)
    piece = 0
    for ref, stacked in zip(weights, shapes):
        for k in range(stacked):
            block = ref[k]
            width = block.shape[1]
            product = jnp.dot(hidden, block, preferred_element_type=F32).astype(BF16)
            columns = pl.ds(pl.multiple_of(at_ref[piece], 128), width)
            out[:, columns] = (product.astype(F32) * live).astype(BF16)
            piece += 1


def down_product(at, seg_counts, own, partials, weights, model_width):
    rows = own.shape[0]
    shapes = tuple(w.shape[0] for w in weights)
    hid = own.shape[1] // 2
    return pl.pallas_call(
        functools.partial(down_kernel, shapes),
        in_specs=[SMEM, SMEM] + [VMEM] * (1 + len(partials) + len(weights)),
        out_specs=VMEM,
        out_shape=jax.ShapeDtypeStruct((rows, model_width), BF16),
        compiler_params=pltpu.CompilerParams(vmem_limit_bytes=24 << 20),
        cost_estimate=pl.CostEstimate(
            flops=2 * rows * hid * model_width,
            bytes_accessed=2 * model_width * (rows + hid),
            transcendentals=rows * hid,
        ),
        name="down_product",
    )(at, seg_counts, own, *partials, *weights)


def split(groups, owners, tokens, norm_gain, gate_weight, up_weight, down_weight, owner_rows, seg_counts):
    model_width = tokens.shape[1]
    block = model_width // owners
    half = block // 2
    group, here = lax.axis_index("groups"), lax.axis_index("wide")
    core, across, near, far, other = (0, 1), (0, 2), (0, 4), (0, 8), (1, 0)
    both = (0, 3)

    def swap(value, way):
        pairs = [
            (g * owners + w, (g ^ way[0]) * owners + (w ^ way[1]))
            for g in range(groups)
            for w in range(owners)
        ]
        return lax.ppermute(value, ALL, pairs)

    first = group == 0
    indices = jnp.arange(owners, dtype=jnp.int32)
    holder = jnp.sum(
        indices[:, None] * (owner_rows[:, None] == indices[None, :]).astype(jnp.int32), axis=0
    )

    halves = (down_weight[:, :half], down_weight[:, half:])
    mine = jnp.where(first, halves[0], halves[1])
    rest = jnp.where(first, halves[1], halves[0])
    mine_x = swap(mine, across)
    rest_x = swap(mine_x, other)

    a0 = jnp.where(first, gate_weight, up_weight)
    b0 = jnp.where(first, up_weight, gate_weight)
    a1 = swap(a0, near)
    a2 = swap(a0, far)
    a3 = swap(a2, near)
    b1, b2, b3 = (swap(a, other) for a in (a1, a2, a3))

    turns = (3, 2, 1, 0)
    slots = jnp.concatenate(
        [(jnp.arange(owners // 4, dtype=jnp.int32) * 4 + ((here & 3) ^ turn)) for turn in turns]
    )
    t3, t2, t1, t0 = normed_quarters(tokens, norm_gain, holder[slots], 4)
    t3 = swap(t3, both)
    t2 = swap(t2, across)
    t1 = swap(t1, core)

    d0 = jnp.stack([mine, mine_x])
    d1 = swap(d0, near)
    d2 = swap(d0, far)
    d3 = swap(d2, near)
    e1, e2, e3 = (swap(d, other) for d in (d1, d2, d3))
    e0 = jnp.stack([rest, rest_x])

    z = here >> 2
    where = jnp.stack([z, z ^ 1, z ^ 2, z ^ 3, group]).astype(jnp.int32)
    weights = (a0, a1, a2, a3, b0, b1, b2, b3)
    p0, p1 = partial_sums(where, (t0, t1), weights, (F32, F32))
    p2, p3 = partial_sums(where, (t2, t3), weights, (BF16, BF16))
    p1 = swap(p1, core)
    p2 = swap(p2, across)
    p3 = swap(p3, both)

    downs = [d0, e0, d1, e1, d2, e2, d3, e3]
    downs = downs + [swap(d, core) for d in downs]
    at = []
    for turn in (0, 1):
        for hop in range(4):
            for plane in (group, 1 - group):
                for x in (0, 2):
                    at.append(holder[here ^ (4 * hop + x + turn)] * block + plane * half)
    return down_product(jnp.stack(at).astype(jnp.int32), seg_counts, p0, (p1, p2, p3), downs, model_width)


def solution(mesh):
    placed = (
        P(("groups", "wide"), None),
        P(),
        P("wide", None),
        P("wide", None),
        P(None, "wide"),
        P(),
        P(("groups", "wide")),
    )
    groups, owners = mesh.shape["groups"], mesh.shape["wide"]
    plan = functools.partial(split, groups, owners) if (groups, owners) == (2, 16) else gathered
    return jax.shard_map(
        plan, mesh=mesh, in_specs=placed, out_specs=P(("groups", "wide"), None), check_vma=False
    )
```

time: 285 us -> 157 us (0.55)
  the two profiles are of different devices: /device:TPU:0 before, /device:TPU:17 now
where the time goes in v1:
time: 157 us; the launch traced here: 156 us
  waiting for transfers between devices  71.3 us (45%)
  starting transfers between devices  33.3 us (21%)
  local copies, waits for them, and re-layouts  21.7 us (14%)
  Pallas kernels  14.7 us (9%)
  between operations  10.8 us (7%)
  other arithmetic  4.37 us (3%)
    ppermute x28, waiting for transfers between devices, swap(): return lax.ppermute(value, ALL, pairs)  71.3 us
    ppermute x28, starting transfers between devices, swap(): return lax.ppermute(value, ALL, pairs)  33.3 us
    unnamed x52, local copies, waits for them, and re-layouts  20.1 us
    pallas_call x1, Pallas kernels, down_product(): pl.pallas_call(functools.partial(down_kernel, shapes), in_specs=[SMEM, SM...  6.11 us
    pallas_call x2, Pallas kernels, partial_sums(): pl.pallas_call(functools.partial(partial_kernel, len(inputs), types), in_...  4.44 us
    pallas_call x1, Pallas kernels, normed_quarters(): pl.pallas_call(norm_kernel, grid_spec=pltpu.PrefetchScalarGridSpec(num_sc...  4.19 us
  transfers between devices with their start and end apart: 28, of which 10 were waited for; matrix products, arithmetic and copies ran while one was open for 3% of the time, Pallas kernels for 6%

profile of v1, /device:TPU:17, one launch (start us, length us, event | category | flops | bytes accessed | tf_op | source)
XLA Modules:
  0.0 156.2 jit_solution(14811936773018887733)
XLA Ops:
  1.4 1.4 collective-permute-start.1
  5.2 5.3 %collective-permute-done.12 = bf16[256,512]{1,0:T(8,128)(2,1)S(1)} collective-permute-done((bf16[256,512]{1,0:T(8,128)(2,1)S(1)}, bf16[256,512]{1,0:T(8,128)(2,1)S(1)}, u32[]{:S(2)}, u32[]{:S(2)}) %collective-permute-start.12) | collective-permute-done | bytes 262176 | tf_op jit(solution)/shard_map/ppermute | solution.py:201
  13.1 2.2 %copy-done = bf16[128,16384]{1,0:T(8,128)(2,1)S(1)} copy-done((bf16[128,16384]{1,0:T(8,128)(2,1)S(1)}, bf16[128,16384]{1,0:T(8,128)(2,1)}, u32[]{:S(2)}) %copy-start) | copy-done | bytes 4194328
  16.1 4.2 %norm_quarters.1 = (bf16[4,128,1024]{2,1,0:T(8,128)(2,1)S(1)}, bf16[4,128,1024]{2,1,0:T(8,128)(2,1)S(1)}, bf16[4,128,1024]{2,1,0:T(8,128)(2,1)S(1)}, bf16[4,128,1024]{2,1,0:T(8,128)(2,1)S(1)}) custom-call(s32[16]{0:T(128)S(1)} %gather_fusion, bf16[128,16384]{1,0:T(8,128)(2,1)S(1)} %copy-done, f32[1,16384]{1,0:T(1,128)S(1)} %bitcast.69), custom_call_target="tpu_custom_call" | custom-call | flops 12582912 | bytes 8388608 | tf_op jit(solution)/shard_map/norm_quarters/pallas_call | solution.py:86
  21.7 2.3 %collective-permute-start.16 = (bf16[2,256,512]{2,1,0:T(8,128)(2,1)S(1)}, bf16[2,256,512]{2,1,0:T(8,128)(2,1)}, u32[]{:S(2)}, u32[]{:S(2)}) collective-permute-start(bf16[2,256,512]{2,1,0:T(8,128)(2,1)S(1)} %pad_maximum_fusion.refs_3_), channel_id=1, source_target_pairs={{0,8},{1,9},{2,10},{3,11},{4,12},{5,13},{6,14},{7,15},{8,0},{9,1},... | collective-permute-start | bytes 1572872 | tf_op jit(solution)/shard_map/ppermute | solution.py:201
  24.0 3.2 %collective-permute-start.9 = (bf16[4,128,1024]{2,1,0:T(8,128)(2,1)S(1)}, bf16[4,128,1024]{2,1,0:T(8,128)(2,1)S(1)}, u32[]{:S(2)}, u32[]{:S(2)}) collective-permute-start(bf16[4,128,1024]{2,1,0:T(8,128)(2,1)S(1)} %get-tuple-element.18), channel_id=1, source_target_pairs={{0,3},{1,2},{2,1},{3,0},{4,7},{5,6},{6,5},{7,4},{8,11},{9,10},{10,... | collective-permute-start | bytes 3145736 | tf_op jit(solution)/shard_map/ppermute | solution.py:201
  27.1 4.2 %collective-permute-start.14 = (bf16[2,256,512]{2,1,0:T(8,128)(2,1)S(1)}, bf16[2,256,512]{2,1,0:T(8,128)(2,1)}, u32[]{:S(2)}, u32[]{:S(2)}) collective-permute-start(bf16[2,256,512]{2,1,0:T(8,128)(2,1)S(1)} %pad_maximum_fusion.refs_3_), channel_id=1, source_target_pairs={{0,4},{1,5},{2,6},{3,7},{4,0},{5,1},{6,2},{7,3},{8,12},{9,13},{10,... | collective-permute-start | bytes 1572872 | tf_op jit(solution)/shard_map/ppermute | solution.py:201
  32.2 13.7 %collective-permute-done.16.refs_7_ = bf16[2,256,512]{2,1,0:T(8,128)(2,1)} collective-permute-done((bf16[2,256,512]{2,1,0:T(8,128)(2,1)S(1)}, bf16[2,256,512]{2,1,0:T(8,128)(2,1)}, u32[]{:S(2)}, u32[]{:S(2)}) %collective-permute-start.16) | collective-permute-done | bytes 524320 | tf_op jit(solution)/shard_map/ppermute | solution.py:201
  45.9 1.5 collective-permute-start
  47.4 6.6 %collective-permute-done.14.refs_5_ = bf16[2,256,512]{2,1,0:T(8,128)(2,1)} collective-permute-done((bf16[2,256,512]{2,1,0:T(8,128)(2,1)S(1)}, bf16[2,256,512]{2,1,0:T(8,128)(2,1)}, u32[]{:S(2)}, u32[]{:S(2)}) %collective-permute-start.14) | collective-permute-done | bytes 524320 | tf_op jit(solution)/shard_map/ppermute | solution.py:201
  54.0 2.3 %collective-permute-start.3 = (bf16[1024,256]{1,0:T(8,128)(2,1)S(1)}, bf16[1024,256]{1,0:T(8,128)(2,1)S(1)}, u32[]{:S(2)}, u32[]{:S(2)}) collective-permute-start(bf16[1024,256]{1,0:T(8,128)(2,1)S(1)} %collective-permute-done.2.refs_4_), channel_id=1, source_target_pairs={{0,4},{1,5},{2,6},{3,7},{4,0},{5,1},{6,2},{7,3},{8,12},{9,13},{10,... | collective-permute-start | bytes 1572872 | tf_op jit(solution)/shard_map/ppermute | solution.py:201
  59.7 8.4 %collective-permute-done.9.refs_1_ = bf16[4,128,1024]{2,1,0:T(8,128)(2,1)S(1)} collective-permute-done((bf16[4,128,1024]{2,1,0:T(8,128)(2,1)S(1)}, bf16[4,128,1024]{2,1,0:T(8,128)(2,1)S(1)}, u32[]{:S(2)}, u32[]{:S(2)}) %collective-permute-start.9) | collective-permute-done | bytes 1048608 | tf_op jit(solution)/shard_map/ppermute | solution.py:201
  70.8 10.1 %collective-permute-done.4.refs_7_ = bf16[1024,256]{1,0:T(8,128)(2,1)S(1)} collective-permute-done((bf16[1024,256]{1,0:T(8,128)(2,1)S(1)}, bf16[1024,256]{1,0:T(8,128)(2,1)S(1)}, u32[]{:S(2)}, u32[]{:S(2)}) %collective-permute-start.4) | collective-permute-done | bytes 524320 | tf_op jit(solution)/shard_map/ppermute | solution.py:201
  85.0 3.7 %collective-permute-start.24 = (bf16[2,256,512]{2,1,0:T(8,128)(2,1)}, bf16[2,256,512]{2,1,0:T(8,128)(2,1)}, u32[]{:S(2)}, u32[]{:S(2)}) collective-permute-start(bf16[2,256,512]{2,1,0:T(8,128)(2,1)} %collective-permute-done.16.refs_7_), channel_id=1, source_target_pairs={{0,1},{1,0},{2,3},{3,2},{4,5},{5,4},{6,7},{7,6},{8,9},{9,8},{10,11... | collective-permute-start | bytes 1572872 | tf_op jit(solution)/shard_map/ppermute | solution.py:201
  88.7 3.3 %collective-permute-done.6.refs_9_ = bf16[1024,256]{1,0:T(8,128)(2,1)S(1)} collective-permute-done((bf16[1024,256]{1,0:T(8,128)(2,1)S(1)}, bf16[1024,256]{1,0:T(8,128)(2,1)S(1)}, u32[]{:S(2)}, u32[]{:S(2)}) %collective-permute-start.6) | collective-permute-done | bytes 524320 | tf_op jit(solution)/shard_map/ppermute | solution.py:201
  98.8 1.9 %partial_sums.3 = (bf16[128,512]{1,0:T(8,128)(2,1)S(1)}, bf16[128,512]{1,0:T(8,128)(2,1)S(1)}) custom-call(s32[5]{0:T(128)S(1)} %stack.173.where_ref, bf16[4,128,1024]{2,1,0:T(8,128)(2,1)S(1)} %copy-done.16, bf16[4,128,1024]{2,1,0:T(8,128)(2,1)S(1)} %copy-done.18, bf16[1024,256]{1,0:T(8,128)(2,1)S(1)} %get-tuple-element.22.refs_2_, ...), custom_call_target="tpu_custom_call" | custom-call | flops 1073741824 | bytes 6291456 | tf_op jit(solution)/shard_map/partial_sums/pallas_call | solution.py:132
  100.6 2.8 %collective-permute-done.17.refs_8_ = bf16[2,256,512]{2,1,0:T(8,128)(2,1)} collective-permute-done((bf16[2,256,512]{2,1,0:T(8,128)(2,1)}, bf16[2,256,512]{2,1,0:T(8,128)(2,1)}, u32[]{:S(2)}, u32[]{:S(2)}) %collective-permute-start.17) | collective-permute-done | bytes 524320 | tf_op jit(solution)/shard_map/ppermute | solution.py:201
  103.5 11.2 %collective-permute-done.15.refs_6_ = bf16[2,256,512]{2,1,0:T(8,128)(2,1)} collective-permute-done((bf16[2,256,512]{2,1,0:T(8,128)(2,1)}, bf16[2,256,512]{2,1,0:T(8,128)(2,1)}, u32[]{:S(2)}, u32[]{:S(2)}) %collective-permute-start.15) | collective-permute-done | bytes 524320 | tf_op jit(solution)/shard_map/ppermute | solution.py:201
  114.6 3.2 %collective-permute-start.26 = (bf16[2,256,512]{2,1,0:T(8,128)(2,1)}, bf16[2,256,512]{2,1,0:T(8,128)(2,1)}, u32[]{:S(2)}, u32[]{:S(2)}) collective-permute-start(bf16[2,256,512]{2,1,0:T(8,128)(2,1)} %collective-permute-done.18.refs_9_), channel_id=1, source_target_pairs={{0,1},{1,0},{2,3},{3,2},{4,5},{5,4},{6,7},{7,6},{8,9},{9,8},{10,11... | collective-permute-start | bytes 1572872 | tf_op jit(solution)/shard_map/ppermute | solution.py:201
  118.4 7.5 %collective-permute-done.19.refs_10_ = bf16[2,256,512]{2,1,0:T(8,128)(2,1)} collective-permute-done((bf16[2,256,512]{2,1,0:T(8,128)(2,1)}, bf16[2,256,512]{2,1,0:T(8,128)(2,1)}, u32[]{:S(2)}, u32[]{:S(2)}) %collective-permute-start.19) | collective-permute-done | bytes 524320 | tf_op jit(solution)/shard_map/ppermute | solution.py:201
  125.9 1.8 %collective-permute-start.27 = (bf16[2,256,512]{2,1,0:T(8,128)(2,1)}, bf16[2,256,512]{2,1,0:T(8,128)(2,1)}, u32[]{:S(2)}, u32[]{:S(2)}) collective-permute-start(bf16[2,256,512]{2,1,0:T(8,128)(2,1)} %collective-permute-done.19.refs_10_), channel_id=1, source_target_pairs={{0,1},{1,0},{2,3},{3,2},{4,5},{5,4},{6,7},{7,6},{8,9},{9,8},{10,11... | collective-permute-start | bytes 1572872 | tf_op jit(solution)/shard_map/ppermute | solution.py:201
  127.8 2.6 %partial_sums.2 = (f32[128,512]{1,0:T(8,128)S(1)}, f32[128,512]{1,0:T(8,128)}) custom-call(s32[5]{0:T(128)S(1)} %stack.173.where_ref, bf16[4,128,1024]{2,1,0:T(8,128)(2,1)S(1)} %copy-done.12, bf16[4,128,1024]{2,1,0:T(8,128)(2,1)S(1)} %copy-done.14, bf16[1024,256]{1,0:T(8,128)(2,1)S(1)} %get-tuple-element.22.refs_2_, ...), custom_call_target="tpu_custom_call" | custom-call | flops 1073741824 | bytes 6291456 | tf_op jit(solution)/shard_map/partial_sums/pallas_call | solution.py:132
  130.3 2.5 %collective-permute-done.11.refs_2_ = bf16[128,512]{1,0:T(8,128)(2,1)S(1)} collective-permute-done((bf16[128,512]{1,0:T(8,128)(2,1)S(1)}, bf16[128,512]{1,0:T(8,128)(2,1)S(1)}, u32[]{:S(2)}, u32[]{:S(2)}) %collective-permute-start.11) | collective-permute-done | bytes 131104 | tf_op jit(solution)/shard_map/ppermute | solution.py:201
  150.1 6.1 %down_product.1 = bf16[128,16384]{1,0:T(8,128)(2,1)} custom-call(s32[32]{0:T(128)S(1)} %stack.167.at_ref, s32[1]{0:T(128)S(6)} %copy.8.live_ref, f32[128,512]{1,0:T(8,128)S(1)} %get-tuple-element.15.own, f32[128,512]{1,0:T(8,128)S(1)} %collective-permute-done.7.refs_0_, bf16[128,512]{1,0:T(8,128)(2,1)S(1)} %collective-permute-done.10.refs_1_, ...), custom_call_target="tpu_custom_call" | custom-call | flops 1073741824 | bytes 12582912 | tf_op jit(solution)/shard_map/down_product/pallas_call | solution.py:172
  (101 shorter events, 33.6 us)
Async XLA Ops:
  1.3 22.7 %collective-permute-start.2 = (bf16[1024,256]{1,0:T(8,128)(2,1)S(1)}, bf16[1024,256]{1,0:T(8,128)(2,1)S(1)}, u32[]{:S(2)}, u32[]{:S(2)}) collective-permute-start(bf16[1024,256]{1,0:T(8,128)(2,1)S(1)} %get-tuple-element.22.refs_2_), channel_id=1, source_target_pairs={{0,8},{1,9},{2,10},{3,11},{4,12},{5,13},{6,14},{7,15},{8,0},{9,1},... | collective-permute-start | bytes 1572872 | tf_op jit(solution)/shard_map/ppermute | solution.py:201
  1.4 25.8 %collective-permute-start.1 = (bf16[1024,256]{1,0:T(8,128)(2,1)S(1)}, bf16[1024,256]{1,0:T(8,128)(2,1)S(1)}, u32[]{:S(2)}, u32[]{:S(2)}) collective-permute-start(bf16[1024,256]{1,0:T(8,128)(2,1)S(1)} %get-tuple-element.22.refs_2_), channel_id=1, source_target_pairs={{0,4},{1,5},{2,6},{3,7},{4,0},{5,1},{6,2},{7,3},{8,12},{9,13},{10,... | collective-permute-start | bytes 1572872 | tf_op jit(solution)/shard_map/ppermute | solution.py:201
  10.4 20.9 %collective-permute-start.13 = (bf16[256,512]{1,0:T(8,128)(2,1)S(1)}, bf16[256,512]{1,0:T(8,128)(2,1)}, u32[]{:S(2)}, u32[]{:S(2)}) collective-permute-start(bf16[256,512]{1,0:T(8,128)(2,1)S(1)} %collective-permute-done.12), channel_id=1, source_target_pairs={{0,16},{1,17},{2,18},{3,19},{4,20},{5,21},{6,22},{7,23},{8,24},{9,... | collective-permute-start | bytes 786440 | tf_op jit(solution)/shard_map/ppermute | solution.py:201
  20.3 38.0 %collective-permute-start.8 = (bf16[4,128,1024]{2,1,0:T(8,128)(2,1)S(1)}, bf16[4,128,1024]{2,1,0:T(8,128)(2,1)S(1)}, u32[]{:S(2)}, u32[]{:S(2)}) collective-permute-start(bf16[4,128,1024]{2,1,0:T(8,128)(2,1)S(1)} %get-tuple-element.17), channel_id=1, source_target_pairs={{0,2},{1,3},{2,0},{3,1},{4,6},{5,7},{6,4},{7,5},{8,10},{9,11},{10,... | collective-permute-start | bytes 3145736 | tf_op jit(solution)/shard_map/ppermute | solution.py:201
  21.7 24.2 %collective-permute-start.16 = (bf16[2,256,512]{2,1,0:T(8,128)(2,1)S(1)}, bf16[2,256,512]{2,1,0:T(8,128)(2,1)}, u32[]{:S(2)}, u32[]{:S(2)}) collective-permute-start(bf16[2,256,512]{2,1,0:T(8,128)(2,1)S(1)} %pad_maximum_fusion.refs_3_), channel_id=1, source_target_pairs={{0,8},{1,9},{2,10},{3,11},{4,12},{5,13},{6,14},{7,15},{8,0},{9,1},... | collective-permute-start | bytes 1572872 | tf_op jit(solution)/shard_map/ppermute | solution.py:201
  24.0 44.1 %collective-permute-start.9 = (bf16[4,128,1024]{2,1,0:T(8,128)(2,1)S(1)}, bf16[4,128,1024]{2,1,0:T(8,128)(2,1)S(1)}, u32[]{:S(2)}, u32[]{:S(2)}) collective-permute-start(bf16[4,128,1024]{2,1,0:T(8,128)(2,1)S(1)} %get-tuple-element.18), channel_id=1, source_target_pairs={{0,3},{1,2},{2,1},{3,0},{4,7},{5,6},{6,5},{7,4},{8,11},{9,10},{10,... | collective-permute-start | bytes 3145736 | tf_op jit(solution)/shard_map/ppermute | solution.py:201
  27.1 26.8 %collective-permute-start.14 = (bf16[2,256,512]{2,1,0:T(8,128)(2,1)S(1)}, bf16[2,256,512]{2,1,0:T(8,128)(2,1)}, u32[]{:S(2)}, u32[]{:S(2)}) collective-permute-start(bf16[2,256,512]{2,1,0:T(8,128)(2,1)S(1)} %pad_maximum_fusion.refs_3_), channel_id=1, source_target_pairs={{0,4},{1,5},{2,6},{3,7},{4,0},{5,1},{6,2},{7,3},{8,12},{9,13},{10,... | collective-permute-start | bytes 1572872 | tf_op jit(solution)/shard_map/ppermute | solution.py:201
  31.4 24.9 %collective-permute-start.20 = (bf16[2,256,512]{2,1,0:T(8,128)(2,1)S(1)}, bf16[2,256,512]{2,1,0:T(8,128)(2,1)S(1)}, u32[]{:S(2)}, u32[]{:S(2)}) collective-permute-start(bf16[2,256,512]{2,1,0:T(8,128)(2,1)S(1)} %pad_maximum_fusion.refs_3_), channel_id=1, source_target_pairs={{0,1},{1,0},{2,3},{3,2},{4,5},{5,4},{6,7},{7,6},{8,9},{9,8},{10,11... | collective-permute-start | bytes 1572872 | tf_op jit(solution)/shard_map/ppermute | solution.py:201
  45.9 37.1 %collective-permute-start = (bf16[4,128,1024]{2,1,0:T(8,128)(2,1)S(1)}, bf16[4,128,1024]{2,1,0:T(8,128)(2,1)S(1)}, u32[]{:S(2)}, u32[]{:S(2)}) collective-permute-start(bf16[4,128,1024]{2,1,0:T(8,128)(2,1)S(1)} %get-tuple-element.14), channel_id=1, source_target_pairs={{0,1},{1,0},{2,3},{3,2},{4,5},{5,4},{6,7},{7,6},{8,9},{9,8},{10,11... | collective-permute-start | bytes 3145736 | tf_op jit(solution)/shard_map/ppermute | solution.py:201
  54.0 15.9 %collective-permute-start.3 = (bf16[1024,256]{1,0:T(8,128)(2,1)S(1)}, bf16[1024,256]{1,0:T(8,128)(2,1)S(1)}, u32[]{:S(2)}, u32[]{:S(2)}) collective-permute-start(bf16[1024,256]{1,0:T(8,128)(2,1)S(1)} %collective-permute-done.2.refs_4_), channel_id=1, source_target_pairs={{0,4},{1,5},{2,6},{3,7},{4,0},{5,1},{6,2},{7,3},{8,12},{9,13},{10,... | collective-permute-start | bytes 1572872 | tf_op jit(solution)/shard_map/ppermute | solution.py:201
  58.3 22.6 %collective-permute-start.4 = (bf16[1024,256]{1,0:T(8,128)(2,1)S(1)}, bf16[1024,256]{1,0:T(8,128)(2,1)S(1)}, u32[]{:S(2)}, u32[]{:S(2)}) collective-permute-start(bf16[1024,256]{1,0:T(8,128)(2,1)S(1)} %collective-permute-done.1.refs_3_), channel_id=1, source_target_pairs={{0,16},{1,17},{2,18},{3,19},{4,20},{5,21},{6,22},{7,23},{8,24},{9,... | collective-permute-start | bytes 1572872 | tf_op jit(solution)/shard_map/ppermute | solution.py:201
  69.0 15.2 %collective-permute-start.21 = (bf16[2,256,512]{2,1,0:T(8,128)(2,1)S(1)}, bf16[2,256,512]{2,1,0:T(8,128)(2,1)S(1)}, u32[]{:S(2)}, u32[]{:S(2)}) collective-permute-start(bf16[2,256,512]{2,1,0:T(8,128)(2,1)S(1)} %pad_maximum_fusion.1.refs_4_), channel_id=1, source_target_pairs={{0,1},{1,0},{2,3},{3,2},{4,5},{5,4},{6,7},{7,6},{8,9},{9,8},{10,11... | collective-permute-start | bytes 1572872 | tf_op jit(solution)/shard_map/ppermute | solution.py:201
  69.8 18.9 %collective-permute-start.18 = (bf16[2,256,512]{2,1,0:T(8,128)(2,1)}, bf16[2,256,512]{2,1,0:T(8,128)(2,1)}, u32[]{:S(2)}, u32[]{:S(2)}) collective-permute-start(bf16[2,256,512]{2,1,0:T(8,128)(2,1)} %collective-permute-done.16.refs_7_), channel_id=1, source_target_pairs={{0,4},{1,5},{2,6},{3,7},{4,0},{5,1},{6,2},{7,3},{8,12},{9,13},{10,... | collective-permute-start | bytes 1572872 | tf_op jit(solution)/shard_map/ppermute | solution.py:201
  70.0 22.1 %collective-permute-start.6 = (bf16[1024,256]{1,0:T(8,128)(2,1)S(1)}, bf16[1024,256]{1,0:T(8,128)(2,1)S(1)}, u32[]{:S(2)}, u32[]{:S(2)}) collective-permute-start(bf16[1024,256]{1,0:T(8,128)(2,1)S(1)} %collective-permute-done.3.refs_5_), channel_id=1, source_target_pairs={{0,16},{1,17},{2,18},{3,19},{4,20},{5,21},{6,22},{7,23},{8,24},{9,... | collective-permute-start | bytes 1572872 | tf_op jit(solution)/shard_map/ppermute | solution.py:201
  81.8 21.7 %collective-permute-start.17 = (bf16[2,256,512]{2,1,0:T(8,128)(2,1)}, bf16[2,256,512]{2,1,0:T(8,128)(2,1)}, u32[]{:S(2)}, u32[]{:S(2)}) collective-permute-start(bf16[2,256,512]{2,1,0:T(8,128)(2,1)} %collective-permute-done.16.refs_7_), channel_id=1, source_target_pairs={{0,16},{1,17},{2,18},{3,19},{4,20},{5,21},{6,22},{7,23},{8,24},{9,... | collective-permute-start | bytes 1572872 | tf_op jit(solution)/shard_map/ppermute | solution.py:201
  84.0 30.6 %collective-permute-start.15 = (bf16[2,256,512]{2,1,0:T(8,128)(2,1)}, bf16[2,256,512]{2,1,0:T(8,128)(2,1)}, u32[]{:S(2)}, u32[]{:S(2)}) collective-permute-start(bf16[2,256,512]{2,1,0:T(8,128)(2,1)} %collective-permute-done.14.refs_5_), channel_id=1, source_target_pairs={{0,16},{1,17},{2,18},{3,19},{4,20},{5,21},{6,22},{7,23},{8,24},{9,... | collective-permute-start | bytes 1572872 | tf_op jit(solution)/shard_map/ppermute | solution.py:201
  85.0 32.8 %collective-permute-start.24 = (bf16[2,256,512]{2,1,0:T(8,128)(2,1)}, bf16[2,256,512]{2,1,0:T(8,128)(2,1)}, u32[]{:S(2)}, u32[]{:S(2)}) collective-permute-start(bf16[2,256,512]{2,1,0:T(8,128)(2,1)} %collective-permute-done.16.refs_7_), channel_id=1, source_target_pairs={{0,1},{1,0},{2,3},{3,2},{4,5},{5,4},{6,7},{7,6},{8,9},{9,8},{10,11... | collective-permute-start | bytes 1572872 | tf_op jit(solution)/shard_map/ppermute | solution.py:201
  88.7 29.1 %collective-permute-start.22 = (bf16[2,256,512]{2,1,0:T(8,128)(2,1)}, bf16[2,256,512]{2,1,0:T(8,128)(2,1)}, u32[]{:S(2)}, u32[]{:S(2)}) collective-permute-start(bf16[2,256,512]{2,1,0:T(8,128)(2,1)} %collective-permute-done.14.refs_5_), channel_id=1, source_target_pairs={{0,1},{1,0},{2,3},{3,2},{4,5},{5,4},{6,7},{7,6},{8,9},{9,8},{10,11... | collective-permute-start | bytes 1572872 | tf_op jit(solution)/shard_map/ppermute | solution.py:201
  92.9 33.0 %collective-permute-start.19 = (bf16[2,256,512]{2,1,0:T(8,128)(2,1)}, bf16[2,256,512]{2,1,0:T(8,128)(2,1)}, u32[]{:S(2)}, u32[]{:S(2)}) collective-permute-start(bf16[2,256,512]{2,1,0:T(8,128)(2,1)} %collective-permute-done.18.refs_9_), channel_id=1, source_target_pairs={{0,16},{1,17},{2,18},{3,19},{4,20},{5,21},{6,22},{7,23},{8,24},{9,... | collective-permute-start | bytes 1572872 | tf_op jit(solution)/shard_map/ppermute | solution.py:201
  103.4 24.3 %collective-permute-start.10 = (bf16[128,512]{1,0:T(8,128)(2,1)S(1)}, bf16[128,512]{1,0:T(8,128)(2,1)S(1)}, u32[]{:S(2)}, u32[]{:S(2)}) collective-permute-start(bf16[128,512]{1,0:T(8,128)(2,1)S(1)} %get-tuple-element.19), channel_id=1, source_target_pairs={{0,2},{1,3},{2,0},{3,1},{4,6},{5,7},{6,4},{7,5},{8,10},{9,11},{10,... | collective-permute-start | bytes 393224 | tf_op jit(solution)/shard_map/ppermute | solution.py:201
  114.6 30.3 %collective-permute-start.26 = (bf16[2,256,512]{2,1,0:T(8,128)(2,1)}, bf16[2,256,512]{2,1,0:T(8,128)(2,1)}, u32[]{:S(2)}, u32[]{:S(2)}) collective-permute-start(bf16[2,256,512]{2,1,0:T(8,128)(2,1)} %collective-permute-done.18.refs_9_), channel_id=1, source_target_pairs={{0,1},{1,0},{2,3},{3,2},{4,5},{5,4},{6,7},{7,6},{8,9},{9,8},{10,11... | collective-permute-start | bytes 1572872 | tf_op jit(solution)/shard_map/ppermute | solution.py:201
  117.9 27.1 %collective-permute-start.25 = (bf16[2,256,512]{2,1,0:T(8,128)(2,1)}, bf16[2,256,512]{2,1,0:T(8,128)(2,1)}, u32[]{:S(2)}, u32[]{:S(2)}) collective-permute-start(bf16[2,256,512]{2,1,0:T(8,128)(2,1)} %collective-permute-done.17.refs_8_), channel_id=1, source_target_pairs={{0,1},{1,0},{2,3},{3,2},{4,5},{5,4},{6,7},{7,6},{8,9},{9,8},{10,11... | collective-permute-start | bytes 1572872 | tf_op jit(solution)/shard_map/ppermute | solution.py:201
  117.9 27.1 %collective-permute-start.23 = (bf16[2,256,512]{2,1,0:T(8,128)(2,1)}, bf16[2,256,512]{2,1,0:T(8,128)(2,1)}, u32[]{:S(2)}, u32[]{:S(2)}) collective-permute-start(bf16[2,256,512]{2,1,0:T(8,128)(2,1)} %collective-permute-done.15.refs_6_), channel_id=1, source_target_pairs={{0,1},{1,0},{2,3},{3,2},{4,5},{5,4},{6,7},{7,6},{8,9},{9,8},{10,11... | collective-permute-start | bytes 1572872 | tf_op jit(solution)/shard_map/ppermute | solution.py:201
  125.9 19.1 %collective-permute-start.27 = (bf16[2,256,512]{2,1,0:T(8,128)(2,1)}, bf16[2,256,512]{2,1,0:T(8,128)(2,1)}, u32[]{:S(2)}, u32[]{:S(2)}) collective-permute-start(bf16[2,256,512]{2,1,0:T(8,128)(2,1)} %collective-permute-done.19.refs_10_), channel_id=1, source_target_pairs={{0,1},{1,0},{2,3},{3,2},{4,5},{5,4},{6,7},{7,6},{8,9},{9,8},{10,11... | collective-permute-start | bytes 1572872 | tf_op jit(solution)/shard_map/ppermute | solution.py:201
  (30 other events, 277.8 us)

commit v2 on v1

v2 whole, which is shorter than its diff:
```python
import functools

import jax
import jax.numpy as jnp
from jax import lax
from jax.experimental import pallas as pl
from jax.experimental.pallas import tpu as pltpu
from jax.sharding import PartitionSpec as P

MEM = 16
FULL = 60 << 20
ALL = ("groups", "wide")
F32, BF16 = jnp.float32, jnp.bfloat16
VMEM = pl.BlockSpec(memory_space=pltpu.VMEM)
SMEM = pl.BlockSpec(memory_space=pltpu.SMEM)
HBM = pl.BlockSpec(memory_space=pltpu.HBM)


def gathered(tokens, norm_gain, gate_weight, up_weight, down_weight, owner_rows, seg_counts):
    row_count, model_width = tokens.shape
    owners = lax.axis_size("wide")
    block_rows = model_width // owners
    indices = jnp.arange(owners, dtype=jnp.int32)
    holder = jnp.sum(
        indices[:, None] * (owner_rows[:, None] == indices[None, :]).astype(jnp.int32), axis=0
    )
    features = tokens.astype(F32)
    mean_square = jnp.mean(features * features, axis=1, keepdims=True)
    normed = (features * lax.rsqrt(mean_square + 1e-05) * norm_gain[None, :]).astype(BF16)
    stored = normed.reshape(row_count, owners, block_rows)[:, holder, :].reshape(
        row_count, model_width
    )

    def partial_product(portion):
        return jnp.dot(stored, portion, preferred_element_type=F32)

    gate_sum = partial_product(lax.all_gather(gate_weight, "wide", axis=0, tiled=True))
    up_sum = partial_product(lax.all_gather(up_weight, "wide", axis=0, tiled=True))
    hidden = (jax.nn.silu(gate_sum) * up_sum).astype(BF16)
    stored_out = jnp.dot(
        hidden,
        lax.all_gather(down_weight, "wide", axis=1, tiled=True),
        preferred_element_type=F32,
    ).astype(BF16)
    product = stored_out.reshape(row_count, owners, block_rows)[:, owner_rows, :].reshape(
        row_count, model_width
    )
    live_mask = (jnp.arange(row_count, dtype=jnp.int32) < MEM + seg_counts[0]).astype(BF16)
    return product * live_mask[:, None]


def norm_kernel(firsts, places_ref, tokens_ref, gain_ref, *rest):
    *outs, scale_ref = rest
    i = pl.program_id(0)
    width = outs[0].shape[2]

    @pl.when(i == 0)
    def _():
        total = jnp.zeros((tokens_ref.shape[0], 128), F32)
        for start in range(0, tokens_ref.shape[1], 128):
            part = tokens_ref[:, start : start + 128].astype(F32)
            total += part * part
        mean = jnp.sum(total, axis=1, keepdims=True) / tokens_ref.shape[1]
        scale_ref[...] = jnp.broadcast_to(lax.rsqrt(mean + 1e-05), scale_ref.shape)

    columns = pl.ds(pl.multiple_of(places_ref[i] * width, width), width)
    normed = tokens_ref[:, columns].astype(F32) * scale_ref[:, :1] * gain_ref[:, columns]
    for q, out in enumerate(outs):

        @pl.when((i >= firsts[q]) & (i < firsts[q + 1]))
        def _(out=out):
            out[0] = normed.astype(BF16)


def normed_blocks(tokens, gain, places, counts):
    rows, model_width = tokens.shape
    blocks = places.shape[0]
    width = model_width // blocks
    firsts = tuple(sum(counts[:q]) for q in range(len(counts) + 1))

    def out_spec(q):
        return pl.BlockSpec(
            (1, rows, width),
            lambda i, places: (jnp.clip(i - firsts[q], 0, counts[q] - 1), 0, 0),
        )

    return pl.pallas_call(
        functools.partial(norm_kernel, firsts),
        grid_spec=pltpu.PrefetchScalarGridSpec(
            num_scalar_prefetch=1,
            grid=(blocks,),
            in_specs=[
                pl.BlockSpec((rows, model_width), lambda i, places: (0, 0)),
                pl.BlockSpec((1, model_width), lambda i, places: (0, 0)),
            ],
            out_specs=[out_spec(q) for q in range(len(counts))],
            scratch_shapes=[pltpu.VMEM((rows, 128), F32)],
        ),
        out_shape=[pltpu.HBM((count, rows, width), BF16) for count in counts],
        compiler_params=pltpu.CompilerParams(vmem_limit_bytes=20 << 20),
        cost_estimate=pl.CostEstimate(
            flops=6 * rows * model_width, bytes_accessed=4 * rows * model_width, transcendentals=0
        ),
        name="norm_blocks",
    )(places, tokens, gain.reshape(1, model_width))


def fetch(refs, buffers, sem):
    copies = [pltpu.make_async_copy(r, v, sem.at[i]) for i, (r, v) in enumerate(zip(refs, buffers))]
    for copy in copies:
        copy.start()
    return copies


def partial_kernel(count, types, where_ref, *refs):
    rows, weights, sem = refs[-count - 2 : -2], refs[-2], refs[-1]
    outs = refs[-count - 2 - len(types) : -count - 2]
    given = refs[: -count - 2 - len(types)]
    half = (len(given) - count) // 2
    hid = weights.shape[2]
    order = [count + i + side * half for i in range(half) for side in range(2)]
    copies = fetch(
        [ref.at[:half] for ref in given[:count]] + [given[i] for i in order],
        list(rows) + [weights.at[i - count] for i in order],
        sem,
    )
    sums = [[jnp.zeros((ref.shape[1], hid), F32) for _ in range(2)] for ref in rows]
    for copy in copies[:count]:
        copy.wait()
    for n, i in enumerate(order):
        copies[count + n].wait()
        side, j = divmod(i - count, half)
        for ref, pair in zip(rows, sums):
            pair[side] += jnp.dot(
                ref[where_ref[j]], weights[i - count], preferred_element_type=F32
            )
    first = where_ref[half] == 0
    for (mine, other), out, kind in zip(sums, outs, types):
        out[:, :hid] = jnp.where(first, mine, other).astype(kind)
        out[:, hid:] = jnp.where(first, other, mine).astype(kind)


def partial_sums(where, inputs, weights, types):
    rows, hid = inputs[0].shape[1], weights[0].shape[1]
    depth = weights[0].shape[0] * len(weights) // 2
    return pl.pallas_call(
        functools.partial(partial_kernel, len(inputs), types),
        in_specs=[SMEM] + [HBM] * (len(inputs) + len(weights)),
        out_specs=[VMEM] * len(inputs),
        out_shape=[jax.ShapeDtypeStruct((rows, 2 * hid), kind) for kind in types],
        scratch_shapes=[pltpu.VMEM((len(weights) // 2,) + v.shape[1:], v.dtype) for v in inputs]
        + [
            pltpu.VMEM((len(weights),) + weights[0].shape, BF16),
            pltpu.SemaphoreType.DMA((len(inputs) + len(weights),)),
        ],
        compiler_params=pltpu.CompilerParams(vmem_limit_bytes=FULL),
        cost_estimate=pl.CostEstimate(
            flops=4 * len(inputs) * rows * depth * hid,
            bytes_accessed=2 * depth * (len(inputs) * rows + 2 * hid),
            transcendentals=0,
        ),
        name="partial_sums",
    )(where, *inputs, *weights)


def down_kernel(pieces, holder_ref, info_ref, live_ref, own, *refs):
    count = len(pieces)
    partials, weights, out = refs[:3], refs[3 : 3 + count], refs[3 + count]
    held, sem, results, out_sem = refs[4 + count : 4 + 2 * count], *refs[4 + 2 * count :]
    copies = fetch(weights, held, sem)
    group, here = info_ref[0], info_ref[1]
    block = out.shape[1] // holder_ref.shape[0]
    hid = own.shape[1] // 2
    total = own[...]
    for part in partials:
        total += part[...].astype(F32)
    gate, up = total[:, :hid], total[:, hid:]
    hidden = (gate / (1.0 + jnp.exp(-gate)) * up).astype(BF16)
    rows = lax.broadcasted_iota(jnp.int32, (out.shape[0], 1), 0)
    live = (rows < MEM + live_ref[0]).astype(F32)
    start, sent = 0, []
    for copy, ref, parts in zip(copies, held, pieces):
        copy.wait()
        for k, (turn, plane) in enumerate(parts):
            width = ref.shape[2]
            product = jnp.dot(hidden, ref[k], preferred_element_type=F32).astype(BF16)
            results[:, start : start + width] = (product.astype(F32) * live).astype(BF16)
            side = group ^ plane if width < block else 0
            place = holder_ref[here ^ turn] * block + side * width
            sent.append(
                pltpu.make_async_copy(
                    results.at[:, start : start + width],
                    out.at[:, pl.ds(pl.multiple_of(place, 128), width)],
                    out_sem.at[len(sent)],
                )
            )
            sent[-1].start()
            start += width
    for copy in sent:
        copy.wait()


def down_product(holder, info, seg_counts, own, partials, downs, model_width):
    rows = own.shape[0]
    weights, pieces = zip(*downs)
    hid = own.shape[1] // 2
    return pl.pallas_call(
        functools.partial(down_kernel, pieces),
        in_specs=[SMEM, SMEM, SMEM] + [VMEM] * (1 + len(partials)) + [HBM] * len(weights),
        out_specs=HBM,
        out_shape=jax.ShapeDtypeStruct((rows, model_width), BF16),
        scratch_shapes=[pltpu.VMEM(w.shape, w.dtype) for w in weights]
        + [
            pltpu.SemaphoreType.DMA((len(weights),)),
            pltpu.VMEM((rows, model_width), BF16),
            pltpu.SemaphoreType.DMA((sum(len(p) for p in pieces),)),
        ],
        compiler_params=pltpu.CompilerParams(vmem_limit_bytes=FULL),
        cost_estimate=pl.CostEstimate(
            flops=2 * rows * hid * model_width,
            bytes_accessed=2 * model_width * (rows + hid),
            transcendentals=rows * hid,
        ),
        name="down_product",
    )(holder, info, seg_counts, own, *partials, *weights)


def stack_kernel(a_ref, b_ref, out_ref):
    out_ref[0] = a_ref[0]
    out_ref[1] = b_ref[0]


def stacked(a, b, flops):
    return pl.pallas_call(
        stack_kernel,
        out_shape=jax.ShapeDtypeStruct((2,) + a.shape[1:], a.dtype),
        compiler_params=pltpu.CompilerParams(vmem_limit_bytes=8 << 20),
        cost_estimate=pl.CostEstimate(flops=flops, bytes_accessed=4 * a.size, transcendentals=0),
        name="stack_halves",
    )(a, b)


def after(value, *others):
    return lax.optimization_barrier((value, *others))[0]


def split(groups, owners, tokens, norm_gain, gate_weight, up_weight, down_weight, owner_rows, seg_counts):
    model_width = tokens.shape[1]
    half = model_width // owners // 2
    group, here = lax.axis_index("groups"), lax.axis_index("wide")
    core, across, near, far, other = (0, 1), (0, 2), (0, 4), (0, 8), (1, 0)
    both = (0, 3)

    def swap(value, way):
        pairs = [
            (g * owners + w, (g ^ way[0]) * owners + (w ^ way[1]))
            for g in range(groups)
            for w in range(owners)
        ]
        return lax.ppermute(value, ALL, pairs)

    first = group == 0
    indices = jnp.arange(owners, dtype=jnp.int32)
    holder = jnp.sum(
        indices[:, None] * (owner_rows[:, None] == indices[None, :]).astype(jnp.int32), axis=0
    )
    info = jnp.stack([group, here]).astype(jnp.int32)

    a0 = jnp.where(first, gate_weight, up_weight)
    b0 = jnp.where(first, up_weight, gate_weight)
    halves = (down_weight[:, :half], down_weight[:, half:])
    mine = jnp.where(first, halves[0], halves[1])[None]
    rest = jnp.where(first, halves[1], halves[0])[None]

    a1 = swap(a0, near)
    a2 = swap(a0, far)
    mine_x = swap(mine, across)

    quarter = owners // 4
    slots = jnp.concatenate(
        [jnp.arange(quarter, dtype=jnp.int32) * 4 + ((here & 3) ^ turn) for turn in (2, 3, 1, 0)]
    )
    t23, t1, t0 = normed_blocks(tokens, norm_gain, holder[slots], (2 * quarter, quarter, quarter))
    r23 = swap(after(t23, mine_x), across)
    r1 = swap(t1, core)
    rest_x = swap(mine_x, other)
    d0 = stacked(after(mine, a1, a2), mine_x, 10**11)

    b1 = swap(after(a1, a2, rest_x), other)
    a3 = swap(after(a2, a1), near)
    d2 = swap(d0, far)
    b2 = swap(after(a2, b1), other)

    b3 = swap(after(a3, b2), other)
    d3 = swap(after(d2, a3), near)
    d1 = swap(after(down_weight[None], a3, d2), near)
    r3 = swap(after(r23, d2, b2)[quarter:], core)
    e2 = swap(after(d2, b3), other)

    z = here >> 2
    where = jnp.stack([z, z ^ 1, z ^ 2, z ^ 3, group]).astype(jnp.int32)
    weights = (a0, a1, a2, a3, b0, b1, b2, b3)
    p2, p3 = partial_sums(where, (r23, r3), weights, (BF16, BF16))
    q2 = swap(p2, across)
    q3 = swap(p3, both)
    p0, p1 = partial_sums(where, (t0, after(r1, p2)), weights, (F32, F32))
    q1 = swap(p1, core)

    e3 = swap(after(d3, e2, p1), other)
    x1 = swap(after(d1, q2, q3), across)

    def pieces(turn, plane):
        return ((turn, plane), (turn ^ 2, plane))

    downs = [
        (down_weight[None], ((0, 0),)),
        (mine_x, ((2, 0),)),
        (rest_x, ((2, 1),)),
        (d2, pieces(8, 0)),
        (d3, pieces(12, 0)),
        (d1, ((4, 0),)),
        (e2, pieces(8, 1)),
        (x1, ((6, 0),)),
        (e3, pieces(12, 1)),
    ]
    crossed = [(swap(w, core), tuple((turn ^ 1, plane) for turn, plane in p)) for w, p in downs]
    downs = downs + crossed
    return down_product(holder, info, seg_counts, p0, (q1, q2, q3), downs, model_width)


def solution(mesh):
    placed = (
        P(("groups", "wide"), None),
        P(),
        P("wide", None),
        P("wide", None),
        P(None, "wide"),
        P(),
        P(("groups", "wide")),
    )
    groups, owners = mesh.shape["groups"], mesh.shape["wide"]
    plan = functools.partial(split, groups, owners) if (groups, owners) == (2, 16) else gathered
    return jax.shard_map(
        plan, mesh=mesh, in_specs=placed, out_specs=P(("groups", "wide"), None), check_vma=False
    )
```

time: 157 us -> 132 us (0.84)
  the two profiles are of different devices: /device:TPU:17 before, /device:TPU:0 now
where the time goes in v2:
time: 132 us
  waiting for transfers between devices  62.7 us (48%)
  starting transfers between devices  27.8 us (21%)
  Pallas kernels  26.5 us (20%)
  local copies, waits for them, and re-layouts  9.25 us (7%)
  other arithmetic  4.61 us (3%)
    ppermute x29, waiting for transfers between devices, swap(): return lax.ppermute(value, ALL, pairs)  62.7 us
    ppermute x29, starting transfers between devices, swap(): return lax.ppermute(value, ALL, pairs)  27.8 us
    pallas_call x2, Pallas kernels, partial_sums(): pl.pallas_call(functools.partial(partial_kernel, len(inputs), types), in_...  10.4 us
    pallas_call x1, Pallas kernels, normed_blocks(): pl.pallas_call(functools.partial(norm_kernel, firsts), grid_spec=pltpu.Pr...  8.76 us
    unnamed x48, local copies, waits for them, and re-layouts  7.85 us
    pallas_call x1, Pallas kernels, down_product(): pl.pallas_call(functools.partial(down_kernel, pieces), in_specs=[SMEM, SM...  7.38 us
  transfers between devices with their start and end apart: 29, of which 11 were waited for; matrix products, arithmetic and copies ran while one was open for 4% of the time, Pallas kernels for 15%

profile of v2, /device:TPU:0, one launch (start us, length us, event | category | flops | bytes accessed | tf_op | source)
XLA Modules:
  0.0 131.8 jit_solution(8440992628262246994)
XLA Ops:
  1.1 3.0 %collective-permute-start.1 = (bf16[1,256,512]{2,1,0:T(8,128)(2,1)S(1)}, bf16[1,256,512]{2,1,0:T(8,128)(2,1)S(1)}, u32[]{:S(2)}, u32[]{:S(2)}) collective-permute-start(bf16[1,256,512]{2,1,0:T(8,128)(2,1)S(1)} %select_bitcast_fusion.a_ref), channel_id=1, source_target_pairs={{0,2},{1,3},{2,0},{3,1},{4,6},{5,7},{6,4},{7,5},{8,10},{9,11},{10,... | collective-permute-start | bytes 786440 | tf_op jit(solution)/shard_map/ppermute | solution.py:260
  4.1 2.1 %broadcast_select_fusion = (bf16[1024,256]{1,0:T(8,128)(2,1)}, bf16[1024,256]{1,0:T(8,128)(2,1)S(1)}) fusion(bf16[1024,256]{1,0:T(8,128)(2,1)} %param.10, bf16[1024,256]{1,0:T(8,128)(2,1)} %param.9, pred[]{:T(512)S(6)} %eq.19), kind=kLoop, calls=%fused_computation.1 | loop fusion | flops 524288 | bytes 2097153 | tf_op jit(solution)/shard_map/jit(_where)/select_n | solution.py:270
  6.1 2.6 %collective-permute-start.4 = (bf16[1024,256]{1,0:T(8,128)(2,1)S(1)}, bf16[1024,256]{1,0:T(8,128)(2,1)}, u32[]{:S(2)}, u32[]{:S(2)}) collective-permute-start(bf16[1024,256]{1,0:T(8,128)(2,1)S(1)} %get-tuple-element.46.refs_2_), channel_id=1, source_target_pairs={{0,8},{1,9},{2,10},{3,11},{4,12},{5,13},{6,14},{7,15},{8,0},{9,1},... | collective-permute-start | bytes 1572872 | tf_op jit(solution)/shard_map/ppermute | solution.py:260
  8.7 1.6 %collective-permute-start.3 = (bf16[1024,256]{1,0:T(8,128)(2,1)S(1)}, bf16[1024,256]{1,0:T(8,128)(2,1)}, u32[]{:S(2)}, u32[]{:S(2)}) collective-permute-start(bf16[1024,256]{1,0:T(8,128)(2,1)S(1)} %get-tuple-element.46.refs_2_), channel_id=1, source_target_pairs={{0,4},{1,5},{2,6},{3,7},{4,0},{5,1},{6,2},{7,3},{8,12},{9,13},{10,... | collective-permute-start | bytes 1572872 | tf_op jit(solution)/shard_map/ppermute | solution.py:260
  10.4 1.8 %collective-permute-start.6 = (bf16[1,256,512]{2,1,0:T(8,128)(2,1)S(1)}, bf16[1,256,512]{2,1,0:T(8,128)(2,1)S(1)}, u32[]{:S(2)}, u32[]{:S(2)}) collective-permute-start(bf16[1,256,512]{2,1,0:T(8,128)(2,1)S(1)} %collective-permute-done.1.b_ref.refs_4_), channel_id=1, source_target_pairs={{0,16},{1,17},{2,18},{3,19},{4,20},{5,21},{6,22},{7,23},{8,24},{9,... | collective-permute-start | bytes 786440 | tf_op jit(solution)/shard_map/ppermute | solution.py:260
  13.6 2.2 %copy-done = bf16[128,16384]{1,0:T(8,128)(2,1)S(1)} copy-done((bf16[128,16384]{1,0:T(8,128)(2,1)S(1)}, bf16[128,16384]{1,0:T(8,128)(2,1)}, u32[]{:S(2)}) %copy-start) | copy-done | bytes 4194328
  16.7 8.8 %norm_blocks.1 = (bf16[8,128,1024]{2,1,0:T(8,128)(2,1)}, bf16[4,128,1024]{2,1,0:T(8,128)(2,1)}, bf16[4,128,1024]{2,1,0:T(8,128)(2,1)}) custom-call(s32[16]{0:T(128)S(1)} %gather_fusion, bf16[128,16384]{1,0:T(8,128)(2,1)S(1)} %copy-done, f32[1,16384]{1,0:T(1,128)S(1)} %bitcast.20), custom_call_target="tpu_custom_call" | custom-call | flops 12582912 | bytes 8388608 | tf_op jit(solution)/shard_map/norm_blocks/pallas_call | solution.py:87
  25.4 1.5 %collective-permute-start.2 = (bf16[8,128,1024]{2,1,0:T(8,128)(2,1)}, bf16[8,128,1024]{2,1,0:T(8,128)(2,1)S(1)}, u32[]{:S(2)}, u32[]{:S(2)}) collective-permute-start(bf16[8,128,1024]{2,1,0:T(8,128)(2,1)} %get-tuple-element.28), channel_id=1, source_target_pairs={{0,2},{1,3},{2,0},{3,1},{4,6},{5,7},{6,4},{7,5},{8,10},{9,11},{10,... | collective-permute-start | bytes 6291464 | tf_op jit(solution)/shard_map/ppermute | solution.py:260
  26.9 4.9 %collective-permute-done.4.refs_4_ = bf16[1024,256]{1,0:T(8,128)(2,1)} collective-permute-done((bf16[1024,256]{1,0:T(8,128)(2,1)S(1)}, bf16[1024,256]{1,0:T(8,128)(2,1)}, u32[]{:S(2)}, u32[]{:S(2)}) %collective-permute-start.4) | collective-permute-done | bytes 524320 | tf_op jit(solution)/shard_map/ppermute | solution.py:260
  32.1 1.5 %collective-permute-start.7 = (bf16[1024,256]{1,0:T(8,128)(2,1)}, bf16[1024,256]{1,0:T(8,128)(2,1)S(1)}, u32[]{:S(2)}, u32[]{:S(2)}) collective-permute-start(bf16[1024,256]{1,0:T(8,128)(2,1)} %collective-permute-done.3.refs_3_), channel_id=1, source_target_pairs={{0,16},{1,17},{2,18},{3,19},{4,20},{5,21},{6,22},{7,23},{8,24},{9,... | collective-permute-start | bytes 1572872 | tf_op jit(solution)/shard_map/ppermute | solution.py:260
  35.0 9.8 %collective-permute-done.7.refs_7_ = bf16[1024,256]{1,0:T(8,128)(2,1)S(1)} collective-permute-done((bf16[1024,256]{1,0:T(8,128)(2,1)}, bf16[1024,256]{1,0:T(8,128)(2,1)S(1)}, u32[]{:S(2)}, u32[]{:S(2)}) %collective-permute-start.7) | collective-permute-done | bytes 524320 | tf_op jit(solution)/shard_map/ppermute | solution.py:260
  44.9 1.5 %collective-permute-start.8 = (bf16[1024,256]{1,0:T(8,128)(2,1)}, bf16[1024,256]{1,0:T(8,128)(2,1)S(1)}, u32[]{:S(2)}, u32[]{:S(2)}) collective-permute-start(bf16[1024,256]{1,0:T(8,128)(2,1)} %collective-permute-done.4.refs_4_), channel_id=1, source_target_pairs={{0,16},{1,17},{2,18},{3,19},{4,20},{5,21},{6,22},{7,23},{8,24},{9,... | collective-permute-start | bytes 1572872 | tf_op jit(solution)/shard_map/ppermute | solution.py:260
  46.4 1.6 %collective-permute-start.10 = (bf16[1024,256]{1,0:T(8,128)(2,1)}, bf16[1024,256]{1,0:T(8,128)(2,1)S(1)}, u32[]{:S(2)}, u32[]{:S(2)}) collective-permute-start(bf16[1024,256]{1,0:T(8,128)(2,1)} %collective-permute-done.4.refs_4_), channel_id=1, source_target_pairs={{0,4},{1,5},{2,6},{3,7},{4,0},{5,1},{6,2},{7,3},{8,12},{9,13},{10,... | collective-permute-start | bytes 1572872 | tf_op jit(solution)/shard_map/ppermute | solution.py:260
  48.0 10.4 %collective-permute-done.5.refs_6_ = bf16[2,256,512]{2,1,0:T(8,128)(2,1)} collective-permute-done((bf16[2,256,512]{2,1,0:T(8,128)(2,1)S(1)}, bf16[2,256,512]{2,1,0:T(8,128)(2,1)}, u32[]{:S(2)}, u32[]{:S(2)}) %collective-permute-start.5) | collective-permute-done | bytes 524320 | tf_op jit(solution)/shard_map/ppermute | solution.py:260
  58.4 13.5 %collective-permute-done.2.refs_0_ = bf16[8,128,1024]{2,1,0:T(8,128)(2,1)S(1)} collective-permute-done((bf16[8,128,1024]{2,1,0:T(8,128)(2,1)}, bf16[8,128,1024]{2,1,0:T(8,128)(2,1)S(1)}, u32[]{:S(2)}, u32[]{:S(2)}) %collective-permute-start.2) | collective-permute-done | bytes 2097184 | tf_op jit(solution)/shard_map/ppermute | solution.py:260
  73.9 1.5 %collective-permute-start.15 = (bf16[2,256,512]{2,1,0:T(8,128)(2,1)}, bf16[2,256,512]{2,1,0:T(8,128)(2,1)}, u32[]{:S(2)}, u32[]{:S(2)}) collective-permute-start(bf16[2,256,512]{2,1,0:T(8,128)(2,1)} %collective-permute-done.5.refs_6_), channel_id=1, source_target_pairs={{0,4},{1,5},{2,6},{3,7},{4,0},{5,1},{6,2},{7,3},{8,12},{9,13},{10,... | collective-permute-start | bytes 1572872 | tf_op jit(solution)/shard_map/ppermute | solution.py:260
  75.4 11.8 %collective-permute-done.11.refs_9_ = bf16[1024,256]{1,0:T(8,128)(2,1)S(1)} collective-permute-done((bf16[1024,256]{1,0:T(8,128)(2,1)S(1)}, bf16[1024,256]{1,0:T(8,128)(2,1)S(1)}, u32[]{:S(2)}, u32[]{:S(2)}) %collective-permute-start.11) | collective-permute-done | bytes 524320 | tf_op jit(solution)/shard_map/ppermute | solution.py:260
  88.6 1.5 %collective-permute-start.16 = (bf16[1,256,1024]{2,1,0:T(8,128)(2,1)}, bf16[1,256,1024]{2,1,0:T(8,128)(2,1)}, u32[]{:S(2)}, u32[]{:S(2)}) collective-permute-start(bf16[1,256,1024]{2,1,0:T(8,128)(2,1)} %bitcast.13.refs_3_), channel_id=1, source_target_pairs={{0,4},{1,5},{2,6},{3,7},{4,0},{5,1},{6,2},{7,3},{8,12},{9,13},{10,... | collective-permute-start | bytes 1572872 | tf_op jit(solution)/shard_map/ppermute | solution.py:260
  91.8 5.2 %partial_sums.2 = (bf16[128,512]{1,0:T(8,128)(2,1)}, bf16[128,512]{1,0:T(8,128)(2,1)}) custom-call(s32[5]{0:T(128)} %stack.32.where_ref, bf16[8,128,1024]{2,1,0:T(8,128)(2,1)} %copy-done.5, bf16[4,128,1024]{2,1,0:T(8,128)(2,1)} %copy-done.10, bf16[1024,256]{1,0:T(8,128)(2,1)} %copy-done.4, bf16[1024,256]{1,0:T(8,128)(2,1)} %collective-permute-done.3.refs_3_, ...), custom_call_target="tpu_custom_call" | custom-call | flops 1073741824 | bytes 6291456 | tf_op jit(solution)/shard_map/partial_sums/pallas_call | solution.py:146
  97.0 1.6 %collective-permute-start.13 = (bf16[128,512]{1,0:T(8,128)(2,1)}, bf16[128,512]{1,0:T(8,128)(2,1)S(1)}, u32[]{:S(2)}, u32[]{:S(2)}) collective-permute-start(bf16[128,512]{1,0:T(8,128)(2,1)} %get-tuple-element.35), channel_id=1, source_target_pairs={{0,2},{1,3},{2,0},{3,1},{4,6},{5,7},{6,4},{7,5},{8,10},{9,11},{10,... | collective-permute-start | bytes 393224 | tf_op jit(solution)/shard_map/ppermute | solution.py:260
  98.9 5.2 %partial_sums.3 = (f32[128,512]{1,0:T(8,128)}, f32[128,512]{1,0:T(8,128)}) custom-call(s32[5]{0:T(128)} %stack.32.where_ref, bf16[4,128,1024]{2,1,0:T(8,128)(2,1)} %get-tuple-element.25.refs_0_, bf16[4,128,1024]{2,1,0:T(8,128)(2,1)} %collective-permute-done.refs_1_, bf16[1024,256]{1,0:T(8,128)(2,1)} %copy-done.4, ...), custom_call_target="tpu_custom_call" | custom-call | flops 1073741824 | bytes 6291456 | tf_op jit(solution)/shard_map/partial_sums/pallas_call | solution.py:146
  104.7 1.5 %collective-permute-start.19 = (bf16[2,256,512]{2,1,0:T(8,128)(2,1)}, bf16[2,256,512]{2,1,0:T(8,128)(2,1)S(1)}, u32[]{:S(2)}, u32[]{:S(2)}) collective-permute-start(bf16[2,256,512]{2,1,0:T(8,128)(2,1)} %collective-permute-done.15.refs_7_), channel_id=1, source_target_pairs={{0,16},{1,17},{2,18},{3,19},{4,20},{5,21},{6,22},{7,23},{8,24},{9,... | collective-permute-start | bytes 1572872 | tf_op jit(solution)/shard_map/ppermute | solution.py:260
  109.9 9.2 %collective-permute-done.19.refs_11_ = bf16[2,256,512]{2,1,0:T(8,128)(2,1)S(1)} collective-permute-done((bf16[2,256,512]{2,1,0:T(8,128)(2,1)}, bf16[2,256,512]{2,1,0:T(8,128)(2,1)S(1)}, u32[]{:S(2)}, u32[]{:S(2)}) %collective-permute-start.19) | collective-permute-done | bytes 524320 | tf_op jit(solution)/shard_map/ppermute | solution.py:260
  124.4 7.4 %down_product.1 = bf16[128,16384]{1,0:T(8,128)(2,1)} custom-call(s32[16]{0:T(128)} %copy-done.3, s32[2]{0:T(128)} %pad_add_fusion.info_ref, s32[1]{0:T(128)S(6)} %copy.8.live_ref, f32[128,512]{1,0:T(8,128)} %get-tuple-element.37.own, f32[128,512]{1,0:T(8,128)} %copy-done.22, bf16[128,512]{1,0:T(8,128)(2,1)} %copy-done.23, ...), custom_call_target="tpu_custom_call" | custom-call | flops 1073741824 | bytes 12582912 | tf_op jit(solution)/shard_map/down_product/pallas_call | solution.py:207
  (98 shorter events, 19.4 us)
Async XLA Ops:
  1.1 9.3 %collective-permute-start.1 = (bf16[1,256,512]{2,1,0:T(8,128)(2,1)S(1)}, bf16[1,256,512]{2,1,0:T(8,128)(2,1)S(1)}, u32[]{:S(2)}, u32[]{:S(2)}) collective-permute-start(bf16[1,256,512]{2,1,0:T(8,128)(2,1)S(1)} %select_bitcast_fusion.a_ref), channel_id=1, source_target_pairs={{0,2},{1,3},{2,0},{3,1},{4,6},{5,7},{6,4},{7,5},{8,10},{9,11},{10,... | collective-permute-start | bytes 786440 | tf_op jit(solution)/shard_map/ppermute | solution.py:260
  6.1 25.7 %collective-permute-start.4 = (bf16[1024,256]{1,0:T(8,128)(2,1)S(1)}, bf16[1024,256]{1,0:T(8,128)(2,1)}, u32[]{:S(2)}, u32[]{:S(2)}) collective-permute-start(bf16[1024,256]{1,0:T(8,128)(2,1)S(1)} %get-tuple-element.46.refs_2_), channel_id=1, source_target_pairs={{0,8},{1,9},{2,10},{3,11},{4,12},{5,13},{6,14},{7,15},{8,0},{9,1},... | collective-permute-start | bytes 1572872 | tf_op jit(solution)/shard_map/ppermute | solution.py:260
  8.7 23.3 %collective-permute-start.3 = (bf16[1024,256]{1,0:T(8,128)(2,1)S(1)}, bf16[1024,256]{1,0:T(8,128)(2,1)}, u32[]{:S(2)}, u32[]{:S(2)}) collective-permute-start(bf16[1024,256]{1,0:T(8,128)(2,1)S(1)} %get-tuple-element.46.refs_2_), channel_id=1, source_target_pairs={{0,4},{1,5},{2,6},{3,7},{4,0},{5,1},{6,2},{7,3},{8,12},{9,13},{10,... | collective-permute-start | bytes 1572872 | tf_op jit(solution)/shard_map/ppermute | solution.py:260
  10.4 21.7 %collective-permute-start.6 = (bf16[1,256,512]{2,1,0:T(8,128)(2,1)S(1)}, bf16[1,256,512]{2,1,0:T(8,128)(2,1)S(1)}, u32[]{:S(2)}, u32[]{:S(2)}) collective-permute-start(bf16[1,256,512]{2,1,0:T(8,128)(2,1)S(1)} %collective-permute-done.1.b_ref.refs_4_), channel_id=1, source_target_pairs={{0,16},{1,17},{2,18},{3,19},{4,20},{5,21},{6,22},{7,23},{8,24},{9,... | collective-permute-start | bytes 786440 | tf_op jit(solution)/shard_map/ppermute | solution.py:260
  25.4 46.4 %collective-permute-start.2 = (bf16[8,128,1024]{2,1,0:T(8,128)(2,1)}, bf16[8,128,1024]{2,1,0:T(8,128)(2,1)S(1)}, u32[]{:S(2)}, u32[]{:S(2)}) collective-permute-start(bf16[8,128,1024]{2,1,0:T(8,128)(2,1)} %get-tuple-element.28), channel_id=1, source_target_pairs={{0,2},{1,3},{2,0},{3,1},{4,6},{5,7},{6,4},{7,5},{8,10},{9,11},{10,... | collective-permute-start | bytes 6291464 | tf_op jit(solution)/shard_map/ppermute | solution.py:260
  32.1 12.8 %collective-permute-start.7 = (bf16[1024,256]{1,0:T(8,128)(2,1)}, bf16[1024,256]{1,0:T(8,128)(2,1)S(1)}, u32[]{:S(2)}, u32[]{:S(2)}) collective-permute-start(bf16[1024,256]{1,0:T(8,128)(2,1)} %collective-permute-done.3.refs_3_), channel_id=1, source_target_pairs={{0,16},{1,17},{2,18},{3,19},{4,20},{5,21},{6,22},{7,23},{8,24},{9,... | collective-permute-start | bytes 1572872 | tf_op jit(solution)/shard_map/ppermute | solution.py:260
  33.6 24.7 %collective-permute-start.5 = (bf16[2,256,512]{2,1,0:T(8,128)(2,1)S(1)}, bf16[2,256,512]{2,1,0:T(8,128)(2,1)}, u32[]{:S(2)}, u32[]{:S(2)}) collective-permute-start(bf16[2,256,512]{2,1,0:T(8,128)(2,1)S(1)} %stack_halves.1), channel_id=1, source_target_pairs={{0,8},{1,9},{2,10},{3,11},{4,12},{5,13},{6,14},{7,15},{8,0},{9,1},... | collective-permute-start | bytes 1572872 | tf_op jit(solution)/shard_map/ppermute | solution.py:260
  44.9 13.5 %collective-permute-start.8 = (bf16[1024,256]{1,0:T(8,128)(2,1)}, bf16[1024,256]{1,0:T(8,128)(2,1)S(1)}, u32[]{:S(2)}, u32[]{:S(2)}) collective-permute-start(bf16[1024,256]{1,0:T(8,128)(2,1)} %collective-permute-done.4.refs_4_), channel_id=1, source_target_pairs={{0,16},{1,17},{2,18},{3,19},{4,20},{5,21},{6,22},{7,23},{8,24},{9,... | collective-permute-start | bytes 1572872 | tf_op jit(solution)/shard_map/ppermute | solution.py:260
  46.4 26.1 %collective-permute-start.10 = (bf16[1024,256]{1,0:T(8,128)(2,1)}, bf16[1024,256]{1,0:T(8,128)(2,1)S(1)}, u32[]{:S(2)}, u32[]{:S(2)}) collective-permute-start(bf16[1024,256]{1,0:T(8,128)(2,1)} %collective-permute-done.4.refs_4_), channel_id=1, source_target_pairs={{0,4},{1,5},{2,6},{3,7},{4,0},{5,1},{6,2},{7,3},{8,12},{9,13},{10,... | collective-permute-start | bytes 1572872 | tf_op jit(solution)/shard_map/ppermute | solution.py:260
  71.9 18.2 %collective-permute-start.9 = (bf16[4,128,1024]{2,1,0:T(8,128)(2,1)S(1)}, bf16[4,128,1024]{2,1,0:T(8,128)(2,1)S(1)}, u32[]{:S(2)}, u32[]{:S(2)}) collective-permute-start(bf16[4,128,1024]{2,1,0:T(8,128)(2,1)S(1)} %slice.11), channel_id=1, source_target_pairs={{0,1},{1,0},{2,3},{3,2},{4,5},{5,4},{6,7},{7,6},{8,9},{9,8},{10,11... | collective-permute-start | bytes 3145736 | tf_op jit(solution)/shard_map/ppermute | solution.py:260
  72.0 24.9 %collective-permute-start = (bf16[4,128,1024]{2,1,0:T(8,128)(2,1)}, bf16[4,128,1024]{2,1,0:T(8,128)(2,1)}, u32[]{:S(2)}, u32[]{:S(2)}) collective-permute-start(bf16[4,128,1024]{2,1,0:T(8,128)(2,1)} %get-tuple-element.26), channel_id=1, source_target_pairs={{0,1},{1,0},{2,3},{3,2},{4,5},{5,4},{6,7},{7,6},{8,9},{9,8},{10,11... | collective-permute-start | bytes 3145736 | tf_op jit(solution)/shard_map/ppermute | solution.py:260
  73.3 13.9 %collective-permute-start.11 = (bf16[1024,256]{1,0:T(8,128)(2,1)S(1)}, bf16[1024,256]{1,0:T(8,128)(2,1)S(1)}, u32[]{:S(2)}, u32[]{:S(2)}) collective-permute-start(bf16[1024,256]{1,0:T(8,128)(2,1)S(1)} %collective-permute-done.10.refs_5_), channel_id=1, source_target_pairs={{0,16},{1,17},{2,18},{3,19},{4,20},{5,21},{6,22},{7,23},{8,24},{9,... | collective-permute-start | bytes 1572872 | tf_op jit(solution)/shard_map/ppermute | solution.py:260
  73.9 24.6 %collective-permute-start.15 = (bf16[2,256,512]{2,1,0:T(8,128)(2,1)}, bf16[2,256,512]{2,1,0:T(8,128)(2,1)}, u32[]{:S(2)}, u32[]{:S(2)}) collective-permute-start(bf16[2,256,512]{2,1,0:T(8,128)(2,1)} %collective-permute-done.5.refs_6_), channel_id=1, source_target_pairs={{0,4},{1,5},{2,6},{3,7},{4,0},{5,1},{6,2},{7,3},{8,12},{9,13},{10,... | collective-permute-start | bytes 1572872 | tf_op jit(solution)/shard_map/ppermute | solution.py:260
  88.0 16.1 %collective-permute-start.17 = (bf16[2,256,512]{2,1,0:T(8,128)(2,1)}, bf16[2,256,512]{2,1,0:T(8,128)(2,1)}, u32[]{:S(2)}, u32[]{:S(2)}) collective-permute-start(bf16[2,256,512]{2,1,0:T(8,128)(2,1)} %collective-permute-done.5.refs_6_), channel_id=1, source_target_pairs={{0,16},{1,17},{2,18},{3,19},{4,20},{5,21},{6,22},{7,23},{8,24},{9,... | collective-permute-start | bytes 1572872 | tf_op jit(solution)/shard_map/ppermute | solution.py:260
  88.6 15.9 %collective-permute-start.16 = (bf16[1,256,1024]{2,1,0:T(8,128)(2,1)}, bf16[1,256,1024]{2,1,0:T(8,128)(2,1)}, u32[]{:S(2)}, u32[]{:S(2)}) collective-permute-start(bf16[1,256,1024]{2,1,0:T(8,128)(2,1)} %bitcast.13.refs_3_), channel_id=1, source_target_pairs={{0,4},{1,5},{2,6},{3,7},{4,0},{5,1},{6,2},{7,3},{8,12},{9,13},{10,... | collective-permute-start | bytes 1572872 | tf_op jit(solution)/shard_map/ppermute | solution.py:260
  91.1 17.4 %collective-permute-start.20 = (bf16[1,256,1024]{2,1,0:T(8,128)(2,1)}, bf16[1,256,1024]{2,1,0:T(8,128)(2,1)}, u32[]{:S(2)}, u32[]{:S(2)}) collective-permute-start(bf16[1,256,1024]{2,1,0:T(8,128)(2,1)} %bitcast.13.refs_3_), channel_id=1, source_target_pairs={{0,1},{1,0},{2,3},{3,2},{4,5},{5,4},{6,7},{7,6},{8,9},{9,8},{10,11... | collective-permute-start | bytes 1572872 | tf_op jit(solution)/shard_map/ppermute | solution.py:260
  97.0 7.8 %collective-permute-start.13 = (bf16[128,512]{1,0:T(8,128)(2,1)}, bf16[128,512]{1,0:T(8,128)(2,1)S(1)}, u32[]{:S(2)}, u32[]{:S(2)}) collective-permute-start(bf16[128,512]{1,0:T(8,128)(2,1)} %get-tuple-element.35), channel_id=1, source_target_pairs={{0,2},{1,3},{2,0},{3,1},{4,6},{5,7},{6,4},{7,5},{8,10},{9,11},{10,... | collective-permute-start | bytes 393224 | tf_op jit(solution)/shard_map/ppermute | solution.py:260
  98.5 7.7 %collective-permute-start.14 = (bf16[128,512]{1,0:T(8,128)(2,1)}, bf16[128,512]{1,0:T(8,128)(2,1)}, u32[]{:S(2)}, u32[]{:S(2)}) collective-permute-start(bf16[128,512]{1,0:T(8,128)(2,1)} %get-tuple-element.39), channel_id=1, source_target_pairs={{0,3},{1,2},{2,1},{3,0},{4,7},{5,6},{6,5},{7,4},{8,11},{9,10},{10,... | collective-permute-start | bytes 393224 | tf_op jit(solution)/shard_map/ppermute | solution.py:260
  104.5 5.0 %collective-permute-start.23 = (bf16[2,256,512]{2,1,0:T(8,128)(2,1)}, bf16[2,256,512]{2,1,0:T(8,128)(2,1)S(1)}, u32[]{:S(2)}, u32[]{:S(2)}) collective-permute-start(bf16[2,256,512]{2,1,0:T(8,128)(2,1)} %collective-permute-done.5.refs_6_), channel_id=1, source_target_pairs={{0,1},{1,0},{2,3},{3,2},{4,5},{5,4},{6,7},{7,6},{8,9},{9,8},{10,11... | collective-permute-start | bytes 1572872 | tf_op jit(solution)/shard_map/ppermute | solution.py:260
  104.7 14.3 %collective-permute-start.19 = (bf16[2,256,512]{2,1,0:T(8,128)(2,1)}, bf16[2,256,512]{2,1,0:T(8,128)(2,1)S(1)}, u32[]{:S(2)}, u32[]{:S(2)}) collective-permute-start(bf16[2,256,512]{2,1,0:T(8,128)(2,1)} %collective-permute-done.15.refs_7_), channel_id=1, source_target_pairs={{0,16},{1,17},{2,18},{3,19},{4,20},{5,21},{6,22},{7,23},{8,24},{9,... | collective-permute-start | bytes 1572872 | tf_op jit(solution)/shard_map/ppermute | solution.py:260
  106.2 14.0 %collective-permute-start.18 = (bf16[1,256,1024]{2,1,0:T(8,128)(2,1)}, bf16[1,256,1024]{2,1,0:T(8,128)(2,1)S(1)}, u32[]{:S(2)}, u32[]{:S(2)}) collective-permute-start(bf16[1,256,1024]{2,1,0:T(8,128)(2,1)} %collective-permute-done.16.refs_8_), channel_id=1, source_target_pairs={{0,2},{1,3},{2,0},{3,1},{4,6},{5,7},{6,4},{7,5},{8,10},{9,11},{10,... | collective-permute-start | bytes 1572872 | tf_op jit(solution)/shard_map/ppermute | solution.py:260
  108.4 11.8 %collective-permute-start.25 = (bf16[1,256,1024]{2,1,0:T(8,128)(2,1)}, bf16[1,256,1024]{2,1,0:T(8,128)(2,1)S(1)}, u32[]{:S(2)}, u32[]{:S(2)}) collective-permute-start(bf16[1,256,1024]{2,1,0:T(8,128)(2,1)} %collective-permute-done.16.refs_8_), channel_id=1, source_target_pairs={{0,1},{1,0},{2,3},{3,2},{4,5},{5,4},{6,7},{7,6},{8,9},{9,8},{10,11... | collective-permute-start | bytes 1572872 | tf_op jit(solution)/shard_map/ppermute | solution.py:260
  109.3 12.8 %collective-permute-start.24 = (bf16[2,256,512]{2,1,0:T(8,128)(2,1)}, bf16[2,256,512]{2,1,0:T(8,128)(2,1)S(1)}, u32[]{:S(2)}, u32[]{:S(2)}) collective-permute-start(bf16[2,256,512]{2,1,0:T(8,128)(2,1)} %collective-permute-done.15.refs_7_), channel_id=1, source_target_pairs={{0,1},{1,0},{2,3},{3,2},{4,5},{5,4},{6,7},{7,6},{8,9},{9,8},{10,11... | collective-permute-start | bytes 1572872 | tf_op jit(solution)/shard_map/ppermute | solution.py:260
  109.5 12.6 %collective-permute-start.26 = (bf16[2,256,512]{2,1,0:T(8,128)(2,1)}, bf16[2,256,512]{2,1,0:T(8,128)(2,1)S(1)}, u32[]{:S(2)}, u32[]{:S(2)}) collective-permute-start(bf16[2,256,512]{2,1,0:T(8,128)(2,1)} %collective-permute-done.17.refs_9_), channel_id=1, source_target_pairs={{0,1},{1,0},{2,3},{3,2},{4,5},{5,4},{6,7},{7,6},{8,9},{9,8},{10,11... | collective-permute-start | bytes 1572872 | tf_op jit(solution)/shard_map/ppermute | solution.py:260
  (29 other events, 375.2 us)

commit v3 on v0

v3 whole, which is shorter than its diff:
```python
import functools

import jax
import jax.numpy as jnp
from jax import lax
from jax.experimental import pallas as pl
from jax.experimental.pallas import tpu as pltpu
from jax.sharding import PartitionSpec as P

MEM = 16
FULL = 60 << 20
ALL = ("groups", "wide")
F32, BF16 = jnp.float32, jnp.bfloat16
VMEM = pl.BlockSpec(memory_space=pltpu.VMEM)
SMEM = pl.BlockSpec(memory_space=pltpu.SMEM)
HBM = pl.BlockSpec(memory_space=pltpu.HBM)


def gathered(tokens, norm_gain, gate_weight, up_weight, down_weight, owner_rows, seg_counts):
    row_count, model_width = tokens.shape
    owners = lax.axis_size("wide")
    block_rows = model_width // owners
    indices = jnp.arange(owners, dtype=jnp.int32)
    holder = jnp.sum(
        indices[:, None] * (owner_rows[:, None] == indices[None, :]).astype(jnp.int32), axis=0
    )
    features = tokens.astype(F32)
    mean_square = jnp.mean(features * features, axis=1, keepdims=True)
    normed = (features * lax.rsqrt(mean_square + 1e-05) * norm_gain[None, :]).astype(BF16)
    stored = normed.reshape(row_count, owners, block_rows)[:, holder, :].reshape(
        row_count, model_width
    )

    def partial_product(portion):
        return jnp.dot(stored, portion, preferred_element_type=F32)

    gate_sum = partial_product(lax.all_gather(gate_weight, "wide", axis=0, tiled=True))
    up_sum = partial_product(lax.all_gather(up_weight, "wide", axis=0, tiled=True))
    hidden = (jax.nn.silu(gate_sum) * up_sum).astype(BF16)
    stored_out = jnp.dot(
        hidden,
        lax.all_gather(down_weight, "wide", axis=1, tiled=True),
        preferred_element_type=F32,
    ).astype(BF16)
    product = stored_out.reshape(row_count, owners, block_rows)[:, owner_rows, :].reshape(
        row_count, model_width
    )
    live_mask = (jnp.arange(row_count, dtype=jnp.int32) < MEM + seg_counts[0]).astype(BF16)
    return product * live_mask[:, None]


def norm_kernel(owner_ref, tokens_ref, gain_ref, *rest):
    (own, near, far), (held, made, scale_ref, in_sem, out_sem) = rest[:3], rest[3:]
    here = lax.axis_index("wide")
    rows, model_width = held.shape
    blocks = owner_ref.shape[0]
    width = model_width // blocks
    step = rows // in_sem.shape[0]
    outs = (own, near, far, far.at[blocks // 4 :])
    copies = [
        pltpu.make_async_copy(
            tokens_ref.at[r : r + step], held.at[r : r + step], in_sem.at[r // step]
        )
        for r in range(0, rows, step)
    ]
    for copy in copies:
        copy.start()
    for r, copy in zip(range(0, rows, step), copies):
        copy.wait()
        total = jnp.zeros((step, 128), F32)
        for start in range(0, model_width, 128):
            part = held[r : r + step, start : start + 128].astype(F32)
            total += part * part
        mean = jnp.sum(total, axis=1, keepdims=True) / model_width
        scale_ref[r : r + step] = jnp.broadcast_to(lax.rsqrt(mean + 1e-05), (step, 128))
    scale = scale_ref[:, :1]
    for p in range(blocks):
        columns = slice(p * width, (p + 1) * width)
        made[p] = (held[:, columns].astype(F32) * scale * gain_ref[:, columns]).astype(BF16)
        stored = owner_ref[p]
        for turn, out in enumerate(outs):

            @pl.when(((stored ^ here) & 3) == turn)
            def _(out=out, p=p, stored=stored):
                pltpu.make_async_copy(made.at[p], out.at[stored >> 2], out_sem.at[p]).start()

    for p in range(blocks):
        pltpu.make_async_copy(made.at[p], outs[0].at[0], out_sem.at[p]).wait()


def normed_quarters(tokens, gain, owner_rows):
    rows, model_width = tokens.shape
    blocks = owner_rows.shape[0]
    width = model_width // blocks
    return pl.pallas_call(
        norm_kernel,
        in_specs=[SMEM, HBM, VMEM],
        out_specs=[HBM] * 3,
        out_shape=[pltpu.HBM((n * blocks // 4, rows, width), BF16) for n in (1, 1, 2)],
        scratch_shapes=[
            pltpu.VMEM((rows, model_width), BF16),
            pltpu.VMEM((blocks, rows, width), BF16),
            pltpu.VMEM((rows, 128), F32),
            pltpu.SemaphoreType.DMA((rows // 16,)),
            pltpu.SemaphoreType.DMA((blocks,)),
        ],
        compiler_params=pltpu.CompilerParams(vmem_limit_bytes=FULL),
        cost_estimate=pl.CostEstimate(
            flops=6 * rows * model_width, bytes_accessed=4 * rows * model_width, transcendentals=0
        ),
        name="norm_quarters",
    )(owner_rows, tokens, gain.reshape(1, model_width))


def fetch(pairs, sem):
    copies = [pltpu.make_async_copy(r, v, sem.at[i]) for i, (r, v) in enumerate(pairs)]
    for copy in copies:
        copy.start()
    return copies


def partial_kernel(given, kinds, *refs):
    outs, (rows, held, mine, other, row_sem, sem) = refs[-6 - len(kinds) : -6], refs[-6:]
    inputs, weights = refs[:given], refs[given : -6 - len(kinds)]
    z, plane = lax.axis_index("wide") >> 2, lax.axis_index("groups")
    size = inputs[0].shape[1]
    hid = held.shape[2]
    hops = len(weights) // 2
    parts = [ref.at[: rows.shape[0]] for ref in inputs]
    row_copies = fetch(
        [(part, rows.at[:, k * size : (k + 1) * size]) for k, part in enumerate(parts)], row_sem
    )
    copies = fetch([(ref, held.at[i]) for i, ref in enumerate(weights)], sem)
    for copy in row_copies:
        copy.wait()
    first = plane == 0
    for hop in range(hops):
        part = rows[z ^ hop]
        for side, total in enumerate((mine, other)):
            i = 2 * hop + side
            copies[i].wait()
            product = jnp.dot(part, held[i], preferred_element_type=F32)
            total[...] = product if hop == 0 else total[...] + product
        if hop == 0:
            gate, up = mine[...], other[...]
            mine[...] = jnp.where(first, gate, up)
            other[...] = jnp.where(first, up, gate)
    for k, (out, kind) in enumerate(zip(outs, kinds)):
        a, b = mine[k * size : (k + 1) * size], other[k * size : (k + 1) * size]
        out[:, :hid] = jnp.where(first, a, b).astype(kind)
        out[:, hid:] = jnp.where(first, b, a).astype(kind)


def partial_sums(inputs, weights, kinds):
    count = len(kinds)
    hops, rows, depth = inputs[0].shape
    hid = weights[0].shape[1]
    return pl.pallas_call(
        functools.partial(partial_kernel, len(inputs), kinds),
        in_specs=[HBM] * (len(inputs) + len(weights)),
        out_specs=[VMEM] * count,
        out_shape=[jax.ShapeDtypeStruct((rows, 2 * hid), kind) for kind in kinds],
        scratch_shapes=[
            pltpu.VMEM((hops, count * rows, depth), BF16),
            pltpu.VMEM((len(weights), depth, hid), BF16),
            pltpu.VMEM((count * rows, hid), F32),
            pltpu.VMEM((count * rows, hid), F32),
            pltpu.SemaphoreType.DMA((count,)),
            pltpu.SemaphoreType.DMA((len(weights),)),
        ],
        compiler_params=pltpu.CompilerParams(vmem_limit_bytes=FULL),
        cost_estimate=pl.CostEstimate(
            flops=4 * hops * count * rows * depth * hid,
            bytes_accessed=2 * hops * depth * (count * rows + 2 * hid),
            transcendentals=0,
        ),
        name="partial_sums",
    )(*inputs, *weights)


def multiply_out(hidden, pieces, owner_ref, live_ref, weights, out, held, sem, results, out_sem, places):
    copies = fetch(list(zip(weights, held)), sem)
    group, here = lax.axis_index("groups"), lax.axis_index("wide")
    blocks = owner_ref.shape[0]
    block = out.shape[1] // blocks
    for p in range(blocks):
        places[owner_ref[p]] = p * block
    rows = lax.broadcasted_iota(jnp.int32, (out.shape[0], 1), 0)
    live = (rows < MEM + live_ref[0]).astype(F32)
    hidden = hidden()
    start, sent = 0, []
    for copy, ref, parts in zip(copies, held, pieces):
        copy.wait()
        for k, (turn, plane) in enumerate(parts):
            width = ref.shape[2]
            product = jnp.dot(hidden, ref[k], preferred_element_type=F32).astype(BF16)
            results[:, start : start + width] = (product.astype(F32) * live).astype(BF16)
            side = group ^ plane if width < block else 0
            place = places[here ^ turn] + side * width
            sent.append(
                pltpu.make_async_copy(
                    results.at[:, start : start + width],
                    out.at[:, pl.ds(pl.multiple_of(place, 128), width)],
                    out_sem.at[len(sent)],
                )
            )
            sent[-1].start()
            start += width
    for copy in sent:
        copy.wait()


def first_kernel(pieces, owner_ref, live_ref, own, *refs):
    count = len(pieces)
    partials, weights, (out, hidden_ref) = refs[:3], refs[3 : 3 + count], refs[3 + count : 5 + count]
    held, rest = refs[5 + count : 5 + 2 * count], refs[5 + 2 * count :]
    hid = own.shape[1] // 2

    def hidden():
        total = own[...]
        for part in partials:
            total += part[...].astype(F32)
        gate, up = total[:, :hid], total[:, hid:]
        hidden_ref[...] = (gate / (1.0 + jnp.exp(-gate)) * up).astype(BF16)
        return hidden_ref[...]

    multiply_out(hidden, pieces, owner_ref, live_ref, weights, out, held, *rest)


def second_kernel(pieces, owner_ref, live_ref, hidden_ref, _, *refs):
    count = len(pieces)
    weights, out, held, rest = refs[:count], refs[count], refs[count + 1 : 2 * count + 1], refs[2 * count + 1 :]
    multiply_out(lambda: hidden_ref[...], pieces, owner_ref, live_ref, weights, out, held, *rest)


def down_call(kernel, name, owner_rows, seg_counts, operands, specs, downs, outs, out_specs, aliases):
    weights, pieces = zip(*downs)
    rows = outs[0].shape[0]
    columns = sum(w.size for w in weights) // weights[0].shape[1]
    return pl.pallas_call(
        functools.partial(kernel, pieces),
        in_specs=[SMEM, SMEM] + specs + [HBM] * len(weights),
        out_specs=out_specs,
        out_shape=outs,
        scratch_shapes=[pltpu.VMEM(w.shape, w.dtype) for w in weights]
        + [
            pltpu.SemaphoreType.DMA((len(weights),)),
            pltpu.VMEM((rows, columns), BF16),
            pltpu.SemaphoreType.DMA((sum(len(p) for p in pieces),)),
            pltpu.SMEM(owner_rows.shape, jnp.int32),
        ],
        input_output_aliases=aliases,
        compiler_params=pltpu.CompilerParams(vmem_limit_bytes=FULL),
        cost_estimate=pl.CostEstimate(
            flops=2 * rows * weights[0].shape[1] * columns,
            bytes_accessed=2 * columns * (rows + weights[0].shape[1]),
            transcendentals=0,
        ),
        name=name,
    )(owner_rows, seg_counts, *operands, *weights)


def stack_kernel(a_ref, b_ref, out_ref):
    out_ref[0] = a_ref[0]
    out_ref[1] = b_ref[0]


def stacked(a, b, flops):
    return pl.pallas_call(
        stack_kernel,
        out_shape=jax.ShapeDtypeStruct((2,) + a.shape[1:], a.dtype),
        compiler_params=pltpu.CompilerParams(vmem_limit_bytes=8 << 20),
        cost_estimate=pl.CostEstimate(flops=flops, bytes_accessed=4 * a.size, transcendentals=0),
        name="stack_halves",
    )(a, b)


def after(value, *others):
    return lax.optimization_barrier((value, *others))[0]


def split(groups, owners, tokens, norm_gain, gate_weight, up_weight, down_weight, owner_rows, seg_counts):
    model_width = tokens.shape[1]
    half = model_width // owners // 2
    group, here = lax.axis_index("groups"), lax.axis_index("wide")
    core, across, near, far, other = (0, 1), (0, 2), (0, 4), (0, 8), (1, 0)
    both = (0, 3)

    def swap(value, way):
        pairs = [
            (g * owners + w, (g ^ way[0]) * owners + (w ^ way[1]))
            for g in range(groups)
            for w in range(owners)
        ]
        return lax.ppermute(value, ALL, pairs)

    first = group == 0
    a0 = jnp.where(first, gate_weight, up_weight)
    mine = jnp.where(first, down_weight[:, :half], down_weight[:, half:])[None]

    a1 = swap(a0, near)
    a2 = swap(a0, far)
    mine_x = swap(mine, across)

    t0, t1, t2 = normed_quarters(tokens, norm_gain, owner_rows)
    r2 = swap(t2, across)
    r1 = swap(t1, core)
    rest_x = swap(after(mine_x, t2), other)
    d0 = stacked(after(mine, a1, a2, t2), mine_x, 10**11)

    b1 = swap(after(a1, d0, rest_x), other)
    a3 = swap(after(a2, d0), near)
    d2 = swap(d0, far)
    b2 = swap(after(a2, d0, rest_x), other)

    b3 = swap(after(a3, b1, b2, d2), other)
    d3 = swap(after(d2, a3), near)
    d1 = swap(after(down_weight[None], d3), near)
    e2 = swap(after(d2, b3), other)

    r3 = swap(after(r2, b3, d3)[owners // 4 :], core)
    def crossed(downs):
        return downs + [
            (swap(w, core), tuple((turn ^ 1, plane) for turn, plane in p)) for w, p in downs
        ]

    crossed_first = crossed(
        [
            (down_weight[None], ((0, 0),)),
            (mine_x, ((2, 0),)),
            (rest_x, ((2, 1),)),
            (d2, ((8, 0), (10, 0))),
        ]
    )
    weights = (gate_weight, up_weight, a1, b1, a2, b2, a3, b3)
    p0, p1, p2, p3 = partial_sums(
        (t0, after(r1, *(w for w, _ in crossed_first)), r2, r3), weights, (F32, F32, BF16, BF16)
    )
    q1 = swap(p1, core)
    q2 = swap(p2, across)
    q3 = swap(p3, both)

    e3 = swap(after(d3, e2, p1), other)
    x1 = swap(after(d1, q2, q3), across)

    early = crossed_first + crossed(
        [
            (after(e2, q2), ((8, 1), (10, 1))),
            (after(d3, q2), ((12, 0), (14, 0))),
            (after(d1, q2), ((4, 0),)),
        ]
    )
    out = pltpu.HBM(tokens.shape, BF16)
    rows, hid = tokens.shape[0], gate_weight.shape[1]
    product, hidden = down_call(
        first_kernel, "down_first", owner_rows, seg_counts, (p0, q1, q2, q3), [VMEM] * 4, early,
        [out, jax.ShapeDtypeStruct((rows, hid), BF16)], [HBM, VMEM], {},
    )
    late = crossed([(after(x1, hidden), ((6, 0),)), (after(e3, hidden), ((12, 1), (14, 1)))])
    return down_call(
        second_kernel, "down_second", owner_rows, seg_counts, (hidden, product), [VMEM, HBM], late,
        [out], [HBM], {3: 0},
    )[0]


def solution(mesh):
    placed = (
        P(("groups", "wide"), None),
        P(),
        P("wide", None),
        P("wide", None),
        P(None, "wide"),
        P(),
        P(("groups", "wide")),
    )
    groups, owners = mesh.shape["groups"], mesh.shape["wide"]
    plan = functools.partial(split, groups, owners) if (groups, owners) == (2, 16) else gathered
    return jax.shard_map(
        plan, mesh=mesh, in_specs=placed, out_specs=P(("groups", "wide"), None), check_vma=False
    )
```

time: 285 us -> 116 us (0.41)
  waiting for transfers between devices: 187 us -> 56.3 us
  local copies, waits for them, and re-layouts: 46.8 us -> 2.76 us
  starting transfers between devices: 0.08 us -> 26.5 us
  Pallas kernels: 0 us -> 26.4 us
  matrix products: 19.8 us -> 0 us
  other arithmetic: 16.6 us -> 2.94 us
  between operations: 13.8 us -> 0.91 us
    all_gather x3 -> x0, waiting for transfers between devices: 185 us -> none  [the longest x1 75.4 us: shards(): lax.all_gather(down_weight, 'wide', axis=1, tiled=True)]
    ppermute x0 -> x29, waiting for transfers between devices: none -> 56.3 us  [swap(): return lax.ppermute(value, ALL, pairs)]
    ppermute x0 -> x29, starting transfers between devices: none -> 26.5 us  [swap(): return lax.ppermute(value, ALL, pairs)]
    pallas_call x0 -> x5, Pallas kernels: none -> 26.4 us  [the longest x2 10.6 us: down_call(): pl.pallas_call(functools.partial(kernel, pieces), in_specs=[SMEM, SMEM] +...]
    gather x4 -> x0, local copies, waits for them, and re-layouts: 22.9 us -> none  [the longest x2 11.5 us: shards(): stored_out.reshape(row_count, owners, block_rows)[:, owner_rows, :]]
    dot_general x2 -> x0, matrix products: 19.8 us -> none  [the longest x1 13.6 us: shards(): jnp.dot(hidden, lax.all_gather(down_weight, 'wide', axis=1, tiled=True),...]
    reshape x2 -> x0, local copies, waits for them, and re-layouts: 11.1 us -> none  [the longest x1 6.37 us: shards(): normed.reshape(row_count, owners, block_rows)[:, holder, :]]
    convert_element_type x2 -> x0, other arithmetic: 8.3 us -> none  [the longest x1 7.78 us: shards(): (features * lax.rsqrt(mean_square + 1e-05) * norm_gain[None, :]).astype(j...]
  transfers between devices with their start and end apart: 3 -> 29, of which waited for: 3 -> 15; matrix products, arithmetic and copies ran while one was open for 15% -> 1% of each run, Pallas kernels for 0% -> 20%
where the time goes in v3:
time: 116 us
  waiting for transfers between devices  56.3 us (49%)
  starting transfers between devices  26.5 us (23%)
  Pallas kernels  26.4 us (23%)
  other arithmetic  2.94 us (3%)
  local copies, waits for them, and re-layouts  2.76 us (2%)
    ppermute x29, waiting for transfers between devices, swap(): return lax.ppermute(value, ALL, pairs)  56.3 us
    ppermute x29, starting transfers between devices, swap(): return lax.ppermute(value, ALL, pairs)  26.5 us
    pallas_call x2, Pallas kernels, down_call(): pl.pallas_call(functools.partial(kernel, pieces), in_specs=[SMEM, SMEM] +...  10.6 us
    pallas_call x1, Pallas kernels, partial_sums(): pl.pallas_call(functools.partial(partial_kernel, len(inputs), kinds), in_...  9.55 us
    pallas_call x1, Pallas kernels, normed_quarters(): pl.pallas_call(norm_kernel, in_specs=[SMEM, HBM, VMEM], out_specs=[HBM] *...  6.25 us
    unnamed x48, local copies, waits for them, and re-layouts  2.69 us
  transfers between devices with their start and end apart: 29, of which 15 were waited for; matrix products, arithmetic and copies ran while one was open for 1% of the time, Pallas kernels for 20%

profile of v3, /device:TPU:0, one launch (start us, length us, event | category | flops | bytes accessed | tf_op | source)
XLA Modules:
  0.0 115.9 jit_solution(16403720703474244346)
XLA Ops:
  0.0 1.9 %broadcast_select_fusion = bf16[1024,256]{1,0:T(8,128)(2,1)} fusion(bf16[1024,256]{1,0:T(8,128)(2,1)} %refs_4_.1, bf16[1024,256]{1,0:T(8,128)(2,1)} %refs_5_.1, pred[]{:T(512)S(6)} %eq.3), kind=kLoop, calls=%fused_computation | loop fusion | flops 262144 | bytes 1572865 | tf_op jit(solution)/shard_map/jit(_where)/select_n | solution.py:298
  1.9 3.0 %collective-permute-start.3 = (bf16[1024,256]{1,0:T(8,128)(2,1)}, bf16[1024,256]{1,0:T(8,128)(2,1)S(1)}, u32[]{:S(2)}, u32[]{:S(2)}) collective-permute-start(bf16[1024,256]{1,0:T(8,128)(2,1)} %broadcast_select_fusion), channel_id=1, source_target_pairs={{0,4},{1,5},{2,6},{3,7},{4,0},{5,1},{6,2},{7,3},{8,12},{9,13},{10,... | collective-permute-start | bytes 1572872 | tf_op jit(solution)/shard_map/ppermute | solution.py:295
  4.9 2.6 %collective-permute-start.4 = (bf16[1024,256]{1,0:T(8,128)(2,1)}, bf16[1024,256]{1,0:T(8,128)(2,1)}, u32[]{:S(2)}, u32[]{:S(2)}) collective-permute-start(bf16[1024,256]{1,0:T(8,128)(2,1)} %broadcast_select_fusion), channel_id=1, source_target_pairs={{0,8},{1,9},{2,10},{3,11},{4,12},{5,13},{6,14},{7,15},{8,0},{9,1},... | collective-permute-start | bytes 1572872 | tf_op jit(solution)/shard_map/ppermute | solution.py:295
  8.6 1.6 %collective-permute-start.1 = (bf16[1,256,512]{2,1,0:T(8,128)(2,1)S(1)}, bf16[1,256,512]{2,1,0:T(8,128)(2,1)S(1)}, u32[]{:S(2)}, u32[]{:S(2)}) collective-permute-start(bf16[1,256,512]{2,1,0:T(8,128)(2,1)S(1)} %select_bitcast_fusion.a_ref), channel_id=1, source_target_pairs={{0,2},{1,3},{2,0},{3,1},{4,6},{5,7},{6,4},{7,5},{8,10},{9,11},{10,... | collective-permute-start | bytes 786440 | tf_op jit(solution)/shard_map/ppermute | solution.py:295
  10.1 6.3 %norm_quarters.1 = (bf16[4,128,1024]{2,1,0:T(8,128)(2,1)}, bf16[4,128,1024]{2,1,0:T(8,128)(2,1)}, bf16[8,128,1024]{2,1,0:T(8,128)(2,1)}) custom-call(s32[16]{0:T(128)} %owner_ref.5, bf16[128,16384]{1,0:T(8,128)(2,1)} %tokens_ref.1, f32[1,16384]{1,0:T(1,128)} %bitcast.7), custom_call_target="tpu_custom_call" | custom-call | flops 12582912 | bytes 8388608 | tf_op jit(solution)/shard_map/norm_quarters/pallas_call | solution.py:95
  17.0 1.5 %collective-permute-start.2 = (bf16[1,256,512]{2,1,0:T(8,128)(2,1)S(1)}, bf16[1,256,512]{2,1,0:T(8,128)(2,1)S(1)}, u32[]{:S(2)}, u32[]{:S(2)}) collective-permute-start(bf16[1,256,512]{2,1,0:T(8,128)(2,1)S(1)} %collective-permute-done.1.b_ref.refs_4_), channel_id=1, source_target_pairs={{0,16},{1,17},{2,18},{3,19},{4,20},{5,21},{6,22},{7,23},{8,24},{9,... | collective-permute-start | bytes 786440 | tf_op jit(solution)/shard_map/ppermute | solution.py:295
  18.5 9.6 %collective-permute-done.3.refs_6_ = bf16[1024,256]{1,0:T(8,128)(2,1)S(1)} collective-permute-done((bf16[1024,256]{1,0:T(8,128)(2,1)}, bf16[1024,256]{1,0:T(8,128)(2,1)S(1)}, u32[]{:S(2)}, u32[]{:S(2)}) %collective-permute-start.3) | collective-permute-done | bytes 524320 | tf_op jit(solution)/shard_map/ppermute | solution.py:295
  28.1 2.7 %collective-permute-done.4.refs_8_ = bf16[1024,256]{1,0:T(8,128)(2,1)} collective-permute-done((bf16[1024,256]{1,0:T(8,128)(2,1)}, bf16[1024,256]{1,0:T(8,128)(2,1)}, u32[]{:S(2)}, u32[]{:S(2)}) %collective-permute-start.4) | collective-permute-done | bytes 524320 | tf_op jit(solution)/shard_map/ppermute | solution.py:295
  31.2 2.7 %collective-permute-start.11 = (bf16[1024,256]{1,0:T(8,128)(2,1)}, bf16[1024,256]{1,0:T(8,128)(2,1)S(1)}, u32[]{:S(2)}, u32[]{:S(2)}) collective-permute-start(bf16[1024,256]{1,0:T(8,128)(2,1)} %collective-permute-done.4.refs_8_), channel_id=1, source_target_pairs={{0,4},{1,5},{2,6},{3,7},{4,0},{5,1},{6,2},{7,3},{8,12},{9,13},{10,... | collective-permute-start | bytes 1572872 | tf_op jit(solution)/shard_map/ppermute | solution.py:295
  33.9 1.6 %collective-permute-start.12 = (bf16[1024,256]{1,0:T(8,128)(2,1)S(1)}, bf16[1024,256]{1,0:T(8,128)(2,1)S(1)}, u32[]{:S(2)}, u32[]{:S(2)}) collective-permute-start(bf16[1024,256]{1,0:T(8,128)(2,1)S(1)} %collective-permute-done.3.refs_6_), channel_id=1, source_target_pairs={{0,16},{1,17},{2,18},{3,19},{4,20},{5,21},{6,22},{7,23},{8,24},{9,... | collective-permute-start | bytes 1572872 | tf_op jit(solution)/shard_map/ppermute | solution.py:295
  36.0 17.7 %collective-permute-done.5.refs_6_ = bf16[2,256,512]{2,1,0:T(8,128)(2,1)} collective-permute-done((bf16[2,256,512]{2,1,0:T(8,128)(2,1)S(1)}, bf16[2,256,512]{2,1,0:T(8,128)(2,1)}, u32[]{:S(2)}, u32[]{:S(2)}) %collective-permute-start.5) | collective-permute-done | bytes 524320 | tf_op jit(solution)/shard_map/ppermute | solution.py:295
  53.7 2.3 %collective-permute-done.13.refs_9_ = bf16[1024,256]{1,0:T(8,128)(2,1)S(1)} collective-permute-done((bf16[1024,256]{1,0:T(8,128)(2,1)}, bf16[1024,256]{1,0:T(8,128)(2,1)S(1)}, u32[]{:S(2)}, u32[]{:S(2)}) %collective-permute-start.13) | collective-permute-done | bytes 524320 | tf_op jit(solution)/shard_map/ppermute | solution.py:295
  56.0 1.8 %collective-permute-start.14 = (bf16[1024,256]{1,0:T(8,128)(2,1)S(1)}, bf16[1024,256]{1,0:T(8,128)(2,1)S(1)}, u32[]{:S(2)}, u32[]{:S(2)}) collective-permute-start(bf16[1024,256]{1,0:T(8,128)(2,1)S(1)} %collective-permute-done.11.refs_10_), channel_id=1, source_target_pairs={{0,16},{1,17},{2,18},{3,19},{4,20},{5,21},{6,22},{7,23},{8,24},{9,... | collective-permute-start | bytes 1572872 | tf_op jit(solution)/shard_map/ppermute | solution.py:295
  58.9 7.6 %collective-permute-done.14.refs_11_ = bf16[1024,256]{1,0:T(8,128)(2,1)S(1)} collective-permute-done((bf16[1024,256]{1,0:T(8,128)(2,1)S(1)}, bf16[1024,256]{1,0:T(8,128)(2,1)S(1)}, u32[]{:S(2)}, u32[]{:S(2)}) %collective-permute-start.14) | collective-permute-done | bytes 524320 | tf_op jit(solution)/shard_map/ppermute | solution.py:295
  68.5 2.8 %collective-permute-done.6.refs_7_ = bf16[1,256,1024]{2,1,0:T(8,128)(2,1)S(1)} collective-permute-done((bf16[1,256,1024]{2,1,0:T(8,128)(2,1)S(1)}, bf16[1,256,1024]{2,1,0:T(8,128)(2,1)S(1)}, u32[]{:S(2)}, u32[]{:S(2)}) %collective-permute-start.6) | collective-permute-done | bytes 524320 | tf_op jit(solution)/shard_map/ppermute | solution.py:295
  72.8 1.6 %collective-permute-start.21 = (bf16[1,256,1024]{2,1,0:T(8,128)(2,1)S(1)}, bf16[1,256,1024]{2,1,0:T(8,128)(2,1)}, u32[]{:S(2)}, u32[]{:S(2)}) collective-permute-start(bf16[1,256,1024]{2,1,0:T(8,128)(2,1)S(1)} %bitcast.6), channel_id=1, source_target_pairs={{0,4},{1,5},{2,6},{3,7},{4,0},{5,1},{6,2},{7,3},{8,12},{9,13},{10,... | collective-permute-start | bytes 1572872 | tf_op jit(solution)/shard_map/ppermute | solution.py:295
  75.2 9.6 %partial_sums.1 = (f32[128,512]{1,0:T(8,128)}, f32[128,512]{1,0:T(8,128)}, bf16[128,512]{1,0:T(8,128)(2,1)}, bf16[128,512]{1,0:T(8,128)(2,1)}) custom-call(bf16[4,128,1024]{2,1,0:T(8,128)(2,1)} %get-tuple-element.32.refs_0_, bf16[4,128,1024]{2,1,0:T(8,128)(2,1)} %collective-permute-done.refs_1_, bf16[8,128,1024]{2,1,0:T(8,128)(2,1)} %copy-done.1, ...), custom_call_target="tpu_custom_call" | custom-call | flops 2147483648 | bytes 8388608 | tf_op jit(solution)/shard_map/partial_sums/pallas_call | solution.py:158
  84.9 1.5 %collective-permute-start.18 = (bf16[128,512]{1,0:T(8,128)(2,1)}, bf16[128,512]{1,0:T(8,128)(2,1)S(1)}, u32[]{:S(2)}, u32[]{:S(2)}) collective-permute-start(bf16[128,512]{1,0:T(8,128)(2,1)} %get-tuple-element.46), channel_id=1, source_target_pairs={{0,2},{1,3},{2,0},{3,1},{4,6},{5,7},{6,4},{7,5},{8,10},{9,11},{10,... | collective-permute-start | bytes 393224 | tf_op jit(solution)/shard_map/ppermute | solution.py:295
  86.7 4.7 %collective-permute-done.18.refs_1_ = bf16[128,512]{1,0:T(8,128)(2,1)S(1)} collective-permute-done((bf16[128,512]{1,0:T(8,128)(2,1)}, bf16[128,512]{1,0:T(8,128)(2,1)S(1)}, u32[]{:S(2)}, u32[]{:S(2)}) %collective-permute-start.18) | collective-permute-done | bytes 131104 | tf_op jit(solution)/shard_map/ppermute | solution.py:295
  93.3 1.5 %collective-permute-start.25 = (bf16[1,256,1024]{2,1,0:T(8,128)(2,1)}, bf16[1,256,1024]{2,1,0:T(8,128)(2,1)S(1)}, u32[]{:S(2)}, u32[]{:S(2)}) collective-permute-start(bf16[1,256,1024]{2,1,0:T(8,128)(2,1)} %collective-permute-done.21.refs_13_), channel_id=1, source_target_pairs={{0,2},{1,3},{2,0},{3,1},{4,6},{5,7},{6,4},{7,5},{8,10},{9,11},{10,... | collective-permute-start | bytes 1572872 | tf_op jit(solution)/shard_map/ppermute | solution.py:295
  97.6 7.0 %down_first.1 = (bf16[128,16384]{1,0:T(8,128)(2,1)}, bf16[128,256]{1,0:T(8,128)(2,1)}) custom-call(s32[16]{0:T(128)} %owner_ref.5, s32[1]{0:T(128)S(6)} %copy.10.live_ref, f32[128,512]{1,0:T(8,128)} %get-tuple-element.44.own, f32[128,512]{1,0:T(8,128)} %copy-done.20, bf16[128,512]{1,0:T(8,128)(2,1)} %copy-done.21, bf16[128,512]{1,0:T(8,128)(2,1)} %copy-done.22, ...), custom_call_target="tpu_custom_call" | custom-call | flops 805306368 | bytes 9437184 | tf_op jit(solution)/shard_map/down_first/pallas_call | solution.py:240
  104.6 3.0 %collective-permute-done.25.refs_0_ = bf16[1,256,1024]{2,1,0:T(8,128)(2,1)S(1)} collective-permute-done((bf16[1,256,1024]{2,1,0:T(8,128)(2,1)}, bf16[1,256,1024]{2,1,0:T(8,128)(2,1)S(1)}, u32[]{:S(2)}, u32[]{:S(2)}) %collective-permute-start.25) | collective-permute-done | bytes 524320 | tf_op jit(solution)/shard_map/ppermute | solution.py:295
  109.4 1.4 %collective-permute-done.27.refs_2_ = bf16[1,256,1024]{2,1,0:T(8,128)(2,1)S(1)} collective-permute-done((bf16[1,256,1024]{2,1,0:T(8,128)(2,1)S(1)}, bf16[1,256,1024]{2,1,0:T(8,128)(2,1)S(1)}, u32[]{:S(2)}, u32[]{:S(2)}) %collective-permute-start.27) | collective-permute-done | bytes 524320 | tf_op jit(solution)/shard_map/ppermute | solution.py:295
  112.3 3.6 %down_second.1 = bf16[128,16384]{1,0:T(8,128)(2,1)} custom-call(s32[16]{0:T(128)} %owner_ref.5, s32[1]{0:T(128)S(6)} %copy.10.live_ref, bf16[128,256]{1,0:T(8,128)(2,1)} %get-tuple-element.53.hidden_ref, bf16[128,16384]{1,0:T(8,128)(2,1)} %get-tuple-element.54._, bf16[1,256,1024]{2,1,0:T(8,128)(2,1)} %copy-done.8, ...), custom_call_target="tpu_custom_call", output_to_operand_aliasing={{}: (3, {})} | custom-call | flops 268435456 | bytes 3145728 | tf_op jit(solution)/shard_map/down_second/pallas_call | solution.py:240
  (90 shorter events, 15.7 us)
Async XLA Ops:
  1.9 26.3 %collective-permute-start.3 = (bf16[1024,256]{1,0:T(8,128)(2,1)}, bf16[1024,256]{1,0:T(8,128)(2,1)S(1)}, u32[]{:S(2)}, u32[]{:S(2)}) collective-permute-start(bf16[1024,256]{1,0:T(8,128)(2,1)} %broadcast_select_fusion), channel_id=1, source_target_pairs={{0,4},{1,5},{2,6},{3,7},{4,0},{5,1},{6,2},{7,3},{8,12},{9,13},{10,... | collective-permute-start | bytes 1572872 | tf_op jit(solution)/shard_map/ppermute | solution.py:295
  4.9 25.9 %collective-permute-start.4 = (bf16[1024,256]{1,0:T(8,128)(2,1)}, bf16[1024,256]{1,0:T(8,128)(2,1)}, u32[]{:S(2)}, u32[]{:S(2)}) collective-permute-start(bf16[1024,256]{1,0:T(8,128)(2,1)} %broadcast_select_fusion), channel_id=1, source_target_pairs={{0,8},{1,9},{2,10},{3,11},{4,12},{5,13},{6,14},{7,15},{8,0},{9,1},... | collective-permute-start | bytes 1572872 | tf_op jit(solution)/shard_map/ppermute | solution.py:295
  8.6 8.4 %collective-permute-start.1 = (bf16[1,256,512]{2,1,0:T(8,128)(2,1)S(1)}, bf16[1,256,512]{2,1,0:T(8,128)(2,1)S(1)}, u32[]{:S(2)}, u32[]{:S(2)}) collective-permute-start(bf16[1,256,512]{2,1,0:T(8,128)(2,1)S(1)} %select_bitcast_fusion.a_ref), channel_id=1, source_target_pairs={{0,2},{1,3},{2,0},{3,1},{4,6},{5,7},{6,4},{7,5},{8,10},{9,11},{10,... | collective-permute-start | bytes 786440 | tf_op jit(solution)/shard_map/ppermute | solution.py:295
  16.4 50.9 %collective-permute-start.10 = (bf16[8,128,1024]{2,1,0:T(8,128)(2,1)}, bf16[8,128,1024]{2,1,0:T(8,128)(2,1)S(1)}, u32[]{:S(2)}, u32[]{:S(2)}) collective-permute-start(bf16[8,128,1024]{2,1,0:T(8,128)(2,1)} %get-tuple-element.34), channel_id=1, source_target_pairs={{0,2},{1,3},{2,0},{3,1},{4,6},{5,7},{6,4},{7,5},{8,10},{9,11},{10,... | collective-permute-start | bytes 6291464 | tf_op jit(solution)/shard_map/ppermute | solution.py:295
  17.0 16.9 %collective-permute-start.2 = (bf16[1,256,512]{2,1,0:T(8,128)(2,1)S(1)}, bf16[1,256,512]{2,1,0:T(8,128)(2,1)S(1)}, u32[]{:S(2)}, u32[]{:S(2)}) collective-permute-start(bf16[1,256,512]{2,1,0:T(8,128)(2,1)S(1)} %collective-permute-done.1.b_ref.refs_4_), channel_id=1, source_target_pairs={{0,16},{1,17},{2,18},{3,19},{4,20},{5,21},{6,22},{7,23},{8,24},{9,... | collective-permute-start | bytes 786440 | tf_op jit(solution)/shard_map/ppermute | solution.py:295
  30.8 22.9 %collective-permute-start.5 = (bf16[2,256,512]{2,1,0:T(8,128)(2,1)S(1)}, bf16[2,256,512]{2,1,0:T(8,128)(2,1)}, u32[]{:S(2)}, u32[]{:S(2)}) collective-permute-start(bf16[2,256,512]{2,1,0:T(8,128)(2,1)S(1)} %stack_halves.1), channel_id=1, source_target_pairs={{0,8},{1,9},{2,10},{3,11},{4,12},{5,13},{6,14},{7,15},{8,0},{9,1},... | collective-permute-start | bytes 1572872 | tf_op jit(solution)/shard_map/ppermute | solution.py:295
  31.2 22.5 %collective-permute-start.11 = (bf16[1024,256]{1,0:T(8,128)(2,1)}, bf16[1024,256]{1,0:T(8,128)(2,1)S(1)}, u32[]{:S(2)}, u32[]{:S(2)}) collective-permute-start(bf16[1024,256]{1,0:T(8,128)(2,1)} %collective-permute-done.4.refs_8_), channel_id=1, source_target_pairs={{0,4},{1,5},{2,6},{3,7},{4,0},{5,1},{6,2},{7,3},{8,12},{9,13},{10,... | collective-permute-start | bytes 1572872 | tf_op jit(solution)/shard_map/ppermute | solution.py:295
  33.9 19.8 %collective-permute-start.12 = (bf16[1024,256]{1,0:T(8,128)(2,1)S(1)}, bf16[1024,256]{1,0:T(8,128)(2,1)S(1)}, u32[]{:S(2)}, u32[]{:S(2)}) collective-permute-start(bf16[1024,256]{1,0:T(8,128)(2,1)S(1)} %collective-permute-done.3.refs_6_), channel_id=1, source_target_pairs={{0,16},{1,17},{2,18},{3,19},{4,20},{5,21},{6,22},{7,23},{8,24},{9,... | collective-permute-start | bytes 1572872 | tf_op jit(solution)/shard_map/ppermute | solution.py:295
  35.5 20.5 %collective-permute-start.13 = (bf16[1024,256]{1,0:T(8,128)(2,1)}, bf16[1024,256]{1,0:T(8,128)(2,1)S(1)}, u32[]{:S(2)}, u32[]{:S(2)}) collective-permute-start(bf16[1024,256]{1,0:T(8,128)(2,1)} %collective-permute-done.4.refs_8_), channel_id=1, source_target_pairs={{0,16},{1,17},{2,18},{3,19},{4,20},{5,21},{6,22},{7,23},{8,24},{9,... | collective-permute-start | bytes 1572872 | tf_op jit(solution)/shard_map/ppermute | solution.py:295
  56.0 10.4 %collective-permute-start.14 = (bf16[1024,256]{1,0:T(8,128)(2,1)S(1)}, bf16[1024,256]{1,0:T(8,128)(2,1)S(1)}, u32[]{:S(2)}, u32[]{:S(2)}) collective-permute-start(bf16[1024,256]{1,0:T(8,128)(2,1)S(1)} %collective-permute-done.11.refs_10_), channel_id=1, source_target_pairs={{0,16},{1,17},{2,18},{3,19},{4,20},{5,21},{6,22},{7,23},{8,24},{9,... | collective-permute-start | bytes 1572872 | tf_op jit(solution)/shard_map/ppermute | solution.py:295
  57.8 9.5 %collective-permute-start.15 = (bf16[2,256,512]{2,1,0:T(8,128)(2,1)}, bf16[2,256,512]{2,1,0:T(8,128)(2,1)}, u32[]{:S(2)}, u32[]{:S(2)}) collective-permute-start(bf16[2,256,512]{2,1,0:T(8,128)(2,1)} %collective-permute-done.5.refs_6_), channel_id=1, source_target_pairs={{0,4},{1,5},{2,6},{3,7},{4,0},{5,1},{6,2},{7,3},{8,12},{9,13},{10,... | collective-permute-start | bytes 1572872 | tf_op jit(solution)/shard_map/ppermute | solution.py:295
  58.9 15.5 %collective-permute-start = (bf16[4,128,1024]{2,1,0:T(8,128)(2,1)S(1)}, bf16[4,128,1024]{2,1,0:T(8,128)(2,1)}, u32[]{:S(2)}, u32[]{:S(2)}) collective-permute-start(bf16[4,128,1024]{2,1,0:T(8,128)(2,1)S(1)} %copy-done.23), channel_id=1, source_target_pairs={{0,1},{1,0},{2,3},{3,2},{4,5},{5,4},{6,7},{7,6},{8,9},{9,8},{10,11... | collective-permute-start | bytes 3145736 | tf_op jit(solution)/shard_map/ppermute | solution.py:295
  67.4 7.0 %collective-permute-start.16 = (bf16[4,128,1024]{2,1,0:T(8,128)(2,1)S(1)}, bf16[4,128,1024]{2,1,0:T(8,128)(2,1)}, u32[]{:S(2)}, u32[]{:S(2)}) collective-permute-start(bf16[4,128,1024]{2,1,0:T(8,128)(2,1)S(1)} %slice.11), channel_id=1, source_target_pairs={{0,1},{1,0},{2,3},{3,2},{4,5},{5,4},{6,7},{7,6},{8,9},{9,8},{10,11... | collective-permute-start | bytes 3145736 | tf_op jit(solution)/shard_map/ppermute | solution.py:295
  68.0 6.4 %collective-permute-start.9 = (bf16[2,256,512]{2,1,0:T(8,128)(2,1)}, bf16[2,256,512]{2,1,0:T(8,128)(2,1)S(1)}, u32[]{:S(2)}, u32[]{:S(2)}) collective-permute-start(bf16[2,256,512]{2,1,0:T(8,128)(2,1)} %collective-permute-done.5.refs_6_), channel_id=1, source_target_pairs={{0,1},{1,0},{2,3},{3,2},{4,5},{5,4},{6,7},{7,6},{8,9},{9,8},{10,11... | collective-permute-start | bytes 1572872 | tf_op jit(solution)/shard_map/ppermute | solution.py:295
  71.8 14.9 %collective-permute-start.20 = (bf16[2,256,512]{2,1,0:T(8,128)(2,1)}, bf16[2,256,512]{2,1,0:T(8,128)(2,1)}, u32[]{:S(2)}, u32[]{:S(2)}) collective-permute-start(bf16[2,256,512]{2,1,0:T(8,128)(2,1)} %collective-permute-done.5.refs_6_), channel_id=1, source_target_pairs={{0,16},{1,17},{2,18},{3,19},{4,20},{5,21},{6,22},{7,23},{8,24},{9,... | collective-permute-start | bytes 1572872 | tf_op jit(solution)/shard_map/ppermute | solution.py:295
  72.8 18.6 %collective-permute-start.21 = (bf16[1,256,1024]{2,1,0:T(8,128)(2,1)S(1)}, bf16[1,256,1024]{2,1,0:T(8,128)(2,1)}, u32[]{:S(2)}, u32[]{:S(2)}) collective-permute-start(bf16[1,256,1024]{2,1,0:T(8,128)(2,1)S(1)} %bitcast.6), channel_id=1, source_target_pairs={{0,4},{1,5},{2,6},{3,7},{4,0},{5,1},{6,2},{7,3},{8,12},{9,13},{10,... | collective-permute-start | bytes 1572872 | tf_op jit(solution)/shard_map/ppermute | solution.py:295
  84.7 10.1 %collective-permute-start.17 = (f32[128,512]{1,0:T(8,128)}, f32[128,512]{1,0:T(8,128)S(1)}, u32[]{:S(2)}, u32[]{:S(2)}) collective-permute-start(f32[128,512]{1,0:T(8,128)} %get-tuple-element.45), channel_id=1, source_target_pairs={{0,1},{1,0},{2,3},{3,2},{4,5},{5,4},{6,7},{7,6},{8,9},{9,8},{10,11... | collective-permute-start | bytes 786440 | tf_op jit(solution)/shard_map/ppermute | solution.py:295
  84.9 6.5 %collective-permute-start.18 = (bf16[128,512]{1,0:T(8,128)(2,1)}, bf16[128,512]{1,0:T(8,128)(2,1)S(1)}, u32[]{:S(2)}, u32[]{:S(2)}) collective-permute-start(bf16[128,512]{1,0:T(8,128)(2,1)} %get-tuple-element.46), channel_id=1, source_target_pairs={{0,2},{1,3},{2,0},{3,1},{4,6},{5,7},{6,4},{7,5},{8,10},{9,11},{10,... | collective-permute-start | bytes 393224 | tf_op jit(solution)/shard_map/ppermute | solution.py:295
  86.4 6.9 %collective-permute-start.19 = (bf16[128,512]{1,0:T(8,128)(2,1)}, bf16[128,512]{1,0:T(8,128)(2,1)S(1)}, u32[]{:S(2)}, u32[]{:S(2)}) collective-permute-start(bf16[128,512]{1,0:T(8,128)(2,1)} %get-tuple-element.47), channel_id=1, source_target_pairs={{0,3},{1,2},{2,1},{3,0},{4,7},{5,6},{6,5},{7,4},{8,11},{9,10},{10,... | collective-permute-start | bytes 393224 | tf_op jit(solution)/shard_map/ppermute | solution.py:295
  91.4 5.0 %collective-permute-start.22 = (bf16[2,256,512]{2,1,0:T(8,128)(2,1)}, bf16[2,256,512]{2,1,0:T(8,128)(2,1)S(1)}, u32[]{:S(2)}, u32[]{:S(2)}) collective-permute-start(bf16[2,256,512]{2,1,0:T(8,128)(2,1)} %collective-permute-done.20.refs_11_), channel_id=1, source_target_pairs={{0,1},{1,0},{2,3},{3,2},{4,5},{5,4},{6,7},{7,6},{8,9},{9,8},{10,11... | collective-permute-start | bytes 1572872 | tf_op jit(solution)/shard_map/ppermute | solution.py:295
  91.4 5.1 %collective-permute-start.23 = (bf16[2,256,512]{2,1,0:T(8,128)(2,1)}, bf16[2,256,512]{2,1,0:T(8,128)(2,1)S(1)}, u32[]{:S(2)}, u32[]{:S(2)}) collective-permute-start(bf16[2,256,512]{2,1,0:T(8,128)(2,1)} %collective-permute-done.15.refs_12_), channel_id=1, source_target_pairs={{0,1},{1,0},{2,3},{3,2},{4,5},{5,4},{6,7},{7,6},{8,9},{9,8},{10,11... | collective-permute-start | bytes 1572872 | tf_op jit(solution)/shard_map/ppermute | solution.py:295
  91.9 4.6 %collective-permute-start.24 = (bf16[1,256,1024]{2,1,0:T(8,128)(2,1)}, bf16[1,256,1024]{2,1,0:T(8,128)(2,1)S(1)}, u32[]{:S(2)}, u32[]{:S(2)}) collective-permute-start(bf16[1,256,1024]{2,1,0:T(8,128)(2,1)} %collective-permute-done.21.refs_13_), channel_id=1, source_target_pairs={{0,1},{1,0},{2,3},{3,2},{4,5},{5,4},{6,7},{7,6},{8,9},{9,8},{10,11... | collective-permute-start | bytes 1572872 | tf_op jit(solution)/shard_map/ppermute | solution.py:295
  93.3 14.3 %collective-permute-start.25 = (bf16[1,256,1024]{2,1,0:T(8,128)(2,1)}, bf16[1,256,1024]{2,1,0:T(8,128)(2,1)S(1)}, u32[]{:S(2)}, u32[]{:S(2)}) collective-permute-start(bf16[1,256,1024]{2,1,0:T(8,128)(2,1)} %collective-permute-done.21.refs_13_), channel_id=1, source_target_pairs={{0,2},{1,3},{2,0},{3,1},{4,6},{5,7},{6,4},{7,5},{8,10},{9,11},{10,... | collective-permute-start | bytes 1572872 | tf_op jit(solution)/shard_map/ppermute | solution.py:295
  94.8 14.0 %collective-permute-start.26 = (bf16[2,256,512]{2,1,0:T(8,128)(2,1)}, bf16[2,256,512]{2,1,0:T(8,128)(2,1)S(1)}, u32[]{:S(2)}, u32[]{:S(2)}) collective-permute-start(bf16[2,256,512]{2,1,0:T(8,128)(2,1)} %collective-permute-done.15.refs_12_), channel_id=1, source_target_pairs={{0,16},{1,17},{2,18},{3,19},{4,20},{5,21},{6,22},{7,23},{8,24},{9,... | collective-permute-start | bytes 1572872 | tf_op jit(solution)/shard_map/ppermute | solution.py:295
  (29 other events, 311.1 us)

commit v4 on v3

--- a/solution.py
+++ b/solution.py
@@ -67,16 +67,18 @@
         copy.start()
     for r, copy in zip(range(0, rows, step), copies):
         copy.wait()
-        total = jnp.zeros((step, 128), F32)
+        parts = [jnp.zeros((step, 128), F32) for _ in range(8)]
         for start in range(0, model_width, 128):
             part = held[r : r + step, start : start + 128].astype(F32)
-            total += part * part
-        mean = jnp.sum(total, axis=1, keepdims=True) / model_width
+            parts[start // 128 % 8] += part * part
+        mean = jnp.sum(sum(parts), axis=1, keepdims=True) / model_width
         scale_ref[r : r + step] = jnp.broadcast_to(lax.rsqrt(mean + 1e-05), (step, 128))
-    scale = scale_ref[:, :1]
+    scale = scale_ref[...]
     for p in range(blocks):
-        columns = slice(p * width, (p + 1) * width)
-        made[p] = (held[:, columns].astype(F32) * scale * gain_ref[:, columns]).astype(BF16)
+        for start in range(0, width, 128):
+            columns = slice(p * width + start, p * width + start + 128)
+            normed = held[:, columns].astype(F32) * scale * gain_ref[:, columns]
+            made[p, :, start : start + 128] = normed.astype(BF16)
         stored = owner_ref[p]
         for turn, out in enumerate(outs):
 
@@ -134,21 +136,30 @@
     for copy in row_copies:
         copy.wait()
     first = plane == 0
-    for hop in range(hops):
-        part = rows[z ^ hop]
-        for side, total in enumerate((mine, other)):
-            i = 2 * hop + side
+    step = hops // 2
+    for start in range(0, hops, step):
+        for i in range(2 * start, 2 * (start + step)):
             copies[i].wait()
-            product = jnp.dot(part, held[i], preferred_element_type=F32)
-            total[...] = product if hop == 0 else total[...] + product
-        if hop == 0:
-            gate, up = mine[...], other[...]
-            mine[...] = jnp.where(first, gate, up)
-            other[...] = jnp.where(first, up, gate)
-    for k, (out, kind) in enumerate(zip(outs, kinds)):
-        a, b = mine[k * size : (k + 1) * size], other[k * size : (k + 1) * size]
-        out[:, :hid] = jnp.where(first, a, b).astype(kind)
-        out[:, hid:] = jnp.where(first, b, a).astype(kind)
+        for k, (out, kind) in enumerate(zip(outs, kinds)):
+            here = slice(k * size, (k + 1) * size)
+            sums = []
+            for side in range(2):
+                total = jnp.zeros((size, hid), F32) if start == 0 else (mine, other)[side][here]
+                for hop in range(max(start, 1), start + step):
+                    total += jnp.dot(
+                        rows[z ^ hop, here], held[2 * hop + side], preferred_element_type=F32
+                    )
+                sums.append(total)
+            if start == 0:
+                (mine[here], other[here]) = sums
+            else:
+                a, b = sums
+                gate, up = (
+                    jnp.dot(rows[z, here], held[side], preferred_element_type=F32)
+                    for side in range(2)
+                )
+                out[:, :hid] = (gate + jnp.where(first, a, b)).astype(kind)
+                out[:, hid:] = (up + jnp.where(first, b, a)).astype(kind)
 
 
 def partial_sums(inputs, weights, kinds):
@@ -178,23 +189,22 @@
     )(*inputs, *weights)
 
 
-def multiply_out(hidden, pieces, owner_ref, live_ref, weights, out, held, sem, results, out_sem, places):
+def multiply_out(hidden, pieces, owner_ref, weights, out, held, sem, results, out_sem, places):
     copies = fetch(list(zip(weights, held)), sem)
     group, here = lax.axis_index("groups"), lax.axis_index("wide")
     blocks = owner_ref.shape[0]
     block = out.shape[1] // blocks
     for p in range(blocks):
         places[owner_ref[p]] = p * block
-    rows = lax.broadcasted_iota(jnp.int32, (out.shape[0], 1), 0)
-    live = (rows < MEM + live_ref[0]).astype(F32)
     hidden = hidden()
     start, sent = 0, []
     for copy, ref, parts in zip(copies, held, pieces):
         copy.wait()
         for k, (turn, plane) in enumerate(parts):
             width = ref.shape[2]
-            product = jnp.dot(hidden, ref[k], preferred_element_type=F32).astype(BF16)
-            results[:, start : start + width] = (product.astype(F32) * live).astype(BF16)
+            for n in range(0, width, 256):
+                product = jnp.dot(hidden, ref[k, :, n : n + 256], preferred_element_type=F32)
+                results[:, start + n : start + n + 256] = product.astype(BF16)
             side = group ^ plane if width < block else 0
             place = places[here ^ turn] + side * width
             sent.append(
@@ -221,16 +231,18 @@
         for part in partials:
             total += part[...].astype(F32)
         gate, up = total[:, :hid], total[:, hid:]
-        hidden_ref[...] = (gate / (1.0 + jnp.exp(-gate)) * up).astype(BF16)
+        hidden = gate / (1.0 + jnp.exp(-gate)) * up
+        rows = lax.broadcasted_iota(jnp.int32, hidden.shape, 0)
+        hidden_ref[...] = jnp.where(rows < MEM + live_ref[0], hidden, 0.0).astype(BF16)
         return hidden_ref[...]
 
-    multiply_out(hidden, pieces, owner_ref, live_ref, weights, out, held, *rest)
+    multiply_out(hidden, pieces, owner_ref, weights, out, held, *rest)
 
 
 def second_kernel(pieces, owner_ref, live_ref, hidden_ref, _, *refs):
     count = len(pieces)
     weights, out, held, rest = refs[:count], refs[count], refs[count + 1 : 2 * count + 1], refs[2 * count + 1 :]
-    multiply_out(lambda: hidden_ref[...], pieces, owner_ref, live_ref, weights, out, held, *rest)
+    multiply_out(lambda: hidden_ref[...], pieces, owner_ref, weights, out, held, *rest)
 
 
 def down_call(kernel, name, owner_rows, seg_counts, operands, specs, downs, outs, out_specs, aliases):
@@ -306,7 +318,15 @@
     r2 = swap(t2, across)
     r1 = swap(t1, core)
     rest_x = swap(after(mine_x, t2), other)
-    d0 = stacked(after(mine, a1, a2, t2), mine_x, 10**11)
+
+    def cross(weights, parts):
+        return swap(weights, core), tuple((turn ^ 1, plane) for turn, plane in parts)
+
+    own = [(down_weight[None], ((0, 0),))]
+    own = own + [cross(*w) for w in own]
+    d0 = stacked(
+        after(mine, a1, a2, t2, own[1][0]), mine_x, 10**11
+    )
 
     b1 = swap(after(a1, d0, rest_x), other)
     a3 = swap(after(a2, d0), near)
@@ -318,45 +338,31 @@
     d1 = swap(after(down_weight[None], d3), near)
     e2 = swap(after(d2, b3), other)
 
-    r3 = swap(after(r2, b3, d3)[owners // 4 :], core)
-    def crossed(downs):
-        return downs + [
-            (swap(w, core), tuple((turn ^ 1, plane) for turn, plane in p)) for w, p in downs
-        ]
-
-    crossed_first = crossed(
-        [
-            (down_weight[None], ((0, 0),)),
-            (mine_x, ((2, 0),)),
-            (rest_x, ((2, 1),)),
-            (d2, ((8, 0), (10, 0))),
-        ]
-    )
+    second = [(mine_x, ((2, 0),)), (rest_x, ((2, 1),)), (d2, ((8, 0), (10, 0))), (d3, ((12, 0), (14, 0)))]
+    second = second + [cross(*w) for w in second]
+    r3 = swap(after(r2, b3, d3, second[4][0], second[5][0], second[6][0])[owners // 4 :], core)
     weights = (gate_weight, up_weight, a1, b1, a2, b2, a3, b3)
     p0, p1, p2, p3 = partial_sums(
-        (t0, after(r1, *(w for w, _ in crossed_first)), r2, r3), weights, (F32, F32, BF16, BF16)
+        (t0, after(r1, second[7][0]), r2, r3), weights, (F32, F32, BF16, BF16)
     )
     q1 = swap(p1, core)
     q2 = swap(p2, across)
     q3 = swap(p3, both)
 
-    e3 = swap(after(d3, e2, p1), other)
-    x1 = swap(after(d1, q2, q3), across)
-
-    early = crossed_first + crossed(
-        [
-            (after(e2, q2), ((8, 1), (10, 1))),
-            (after(d3, q2), ((12, 0), (14, 0))),
-            (after(d1, q2), ((4, 0),)),
-        ]
-    )
+    e3 = swap(after(d3, e2, q1), other)
+    e0 = stacked(mine_x, rest_x, 0)
+    x1 = swap(after(e0, d1, q1), near)
+
+    third = [(e2, ((8, 1), (10, 1))), (d1, ((4, 0),))]
+    early = own + second + third
     out = pltpu.HBM(tokens.shape, BF16)
     rows, hid = tokens.shape[0], gate_weight.shape[1]
     product, hidden = down_call(
         first_kernel, "down_first", owner_rows, seg_counts, (p0, q1, q2, q3), [VMEM] * 4, early,
         [out, jax.ShapeDtypeStruct((rows, hid), BF16)], [HBM, VMEM], {},
     )
-    late = crossed([(after(x1, hidden), ((6, 0),)), (after(e3, hidden), ((12, 1), (14, 1)))])
+    late = [(after(x1, hidden), ((6, 0), (6, 1))), (after(e3, hidden), ((12, 1), (14, 1)))]
+    late = [cross(after(w, q3), parts) for w, parts in third] + late + [cross(*w) for w in late]
     return down_call(
         second_kernel, "down_second", owner_rows, seg_counts, (hidden, product), [VMEM, HBM], late,
         [out], [HBM], {3: 0},

time: 116 us -> 113 us (0.974)
  Pallas kernels: 26.4 us -> 22.7 us
  waiting for transfers between devices: 56.3 us -> 53.2 us
  local copies, waits for them, and re-layouts: 2.76 us -> 5.5 us
    ppermute x29, waiting for transfers between devices: 56.3 us -> 53.2 us  [swap(): return lax.ppermute(value, ALL, pairs)]
    pallas_call x1, Pallas kernels: 9.55 us -> 6.44 us  [partial_sums(): pl.pallas_call(functools.partial(partial_kernel, len(inputs), kinds), in_...]
    unnamed x48, local copies, waits for them, and re-layouts: 2.69 us -> 5.44 us
  transfers between devices with their start and end apart: 29 -> 29, of which waited for: 15 -> 12; matrix products, arithmetic and copies ran while one was open for 1% -> 1% of each run, Pallas kernels for 20% -> 16%
where the time goes in v4:
time: 113 us
  waiting for transfers between devices  53.2 us (47%)
  starting transfers between devices  27.4 us (24%)
  Pallas kernels  22.7 us (20%)
  local copies, waits for them, and re-layouts  5.5 us (5%)
  other arithmetic  2.95 us (3%)
    ppermute x29, waiting for transfers between devices, swap(): return lax.ppermute(value, ALL, pairs)  53.2 us
    ppermute x29, starting transfers between devices, swap(): return lax.ppermute(value, ALL, pairs)  27.4 us
    pallas_call x2, Pallas kernels, down_call(): pl.pallas_call(functools.partial(kernel, pieces), in_specs=[SMEM, SMEM] +...  10.5 us
    pallas_call x1, Pallas kernels, partial_sums(): pl.pallas_call(functools.partial(partial_kernel, len(inputs), kinds), in_...  6.44 us
    pallas_call x1, Pallas kernels, normed_quarters(): pl.pallas_call(norm_kernel, in_specs=[SMEM, HBM, VMEM], out_specs=[HBM] *...  5.66 us
    unnamed x48, local copies, waits for them, and re-layouts  5.44 us
  transfers between devices with their start and end apart: 29, of which 12 were waited for; matrix products, arithmetic and copies ran while one was open for 1% of the time, Pallas kernels for 16%

profile of v4, /device:TPU:0, one launch (start us, length us, event | category | flops | bytes accessed | tf_op | source)
XLA Modules:
  0.0 112.6 jit_solution(807331891741122609)
XLA Ops:
  0.0 1.9 %broadcast_select_fusion = bf16[1024,256]{1,0:T(8,128)(2,1)} fusion(bf16[1024,256]{1,0:T(8,128)(2,1)} %refs_4_.1, bf16[1024,256]{1,0:T(8,128)(2,1)} %refs_5_.1, pred[]{:T(512)S(6)} %eq.3), kind=kLoop, calls=%fused_computation | loop fusion | flops 262144 | bytes 1572865 | tf_op jit(solution)/shard_map/jit(_where)/select_n | solution.py:310
  1.9 3.0 %collective-permute-start.1 = (bf16[1024,256]{1,0:T(8,128)(2,1)}, bf16[1024,256]{1,0:T(8,128)(2,1)}, u32[]{:S(2)}, u32[]{:S(2)}) collective-permute-start(bf16[1024,256]{1,0:T(8,128)(2,1)} %broadcast_select_fusion), channel_id=1, source_target_pairs={{0,4},{1,5},{2,6},{3,7},{4,0},{5,1},{6,2},{7,3},{8,12},{9,13},{10,... | collective-permute-start | bytes 1572872 | tf_op jit(solution)/shard_map/ppermute | solution.py:307
  4.9 2.6 %collective-permute-start.2 = (bf16[1024,256]{1,0:T(8,128)(2,1)}, bf16[1024,256]{1,0:T(8,128)(2,1)}, u32[]{:S(2)}, u32[]{:S(2)}) collective-permute-start(bf16[1024,256]{1,0:T(8,128)(2,1)} %broadcast_select_fusion), channel_id=1, source_target_pairs={{0,8},{1,9},{2,10},{3,11},{4,12},{5,13},{6,14},{7,15},{8,0},{9,1},... | collective-permute-start | bytes 1572872 | tf_op jit(solution)/shard_map/ppermute | solution.py:307
  8.6 1.6 %collective-permute-start.4 = (bf16[1,256,512]{2,1,0:T(8,128)(2,1)S(1)}, bf16[1,256,512]{2,1,0:T(8,128)(2,1)S(1)}, u32[]{:S(2)}, u32[]{:S(2)}) collective-permute-start(bf16[1,256,512]{2,1,0:T(8,128)(2,1)S(1)} %select_bitcast_fusion.a_ref), channel_id=1, source_target_pairs={{0,2},{1,3},{2,0},{3,1},{4,6},{5,7},{6,4},{7,5},{8,10},{9,11},{10,... | collective-permute-start | bytes 786440 | tf_op jit(solution)/shard_map/ppermute | solution.py:307
  10.1 5.7 %norm_quarters.1 = (bf16[4,128,1024]{2,1,0:T(8,128)(2,1)}, bf16[4,128,1024]{2,1,0:T(8,128)(2,1)}, bf16[8,128,1024]{2,1,0:T(8,128)(2,1)}) custom-call(s32[16]{0:T(128)} %owner_ref.5, bf16[128,16384]{1,0:T(8,128)(2,1)} %tokens_ref.1, f32[1,16384]{1,0:T(1,128)} %bitcast.7), custom_call_target="tpu_custom_call" | custom-call | flops 12582912 | bytes 8388608 | tf_op jit(solution)/shard_map/norm_quarters/pallas_call | solution.py:97
  17.4 1.5 %collective-permute-start.10 = (bf16[1,256,512]{2,1,0:T(8,128)(2,1)S(1)}, bf16[1,256,512]{2,1,0:T(8,128)(2,1)S(1)}, u32[]{:S(2)}, u32[]{:S(2)}) collective-permute-start(bf16[1,256,512]{2,1,0:T(8,128)(2,1)S(1)} %collective-permute-done.4.b_ref.refs_5_.a_ref), channel_id=1, source_target_pairs={{0,16},{1,17},{2,18},{3,19},{4,20},{5,21},{6,22},{7,23},{8,24},{9,... | collective-permute-start | bytes 786440 | tf_op jit(solution)/shard_map/ppermute | solution.py:307
  18.9 9.4 %collective-permute-done.1.refs_6_ = bf16[1024,256]{1,0:T(8,128)(2,1)} collective-permute-done((bf16[1024,256]{1,0:T(8,128)(2,1)}, bf16[1024,256]{1,0:T(8,128)(2,1)}, u32[]{:S(2)}, u32[]{:S(2)}) %collective-permute-start.1) | collective-permute-done | bytes 524320 | tf_op jit(solution)/shard_map/ppermute | solution.py:307
  28.3 2.6 %collective-permute-done.2.refs_8_ = bf16[1024,256]{1,0:T(8,128)(2,1)} collective-permute-done((bf16[1024,256]{1,0:T(8,128)(2,1)}, bf16[1024,256]{1,0:T(8,128)(2,1)}, u32[]{:S(2)}, u32[]{:S(2)}) %collective-permute-start.2) | collective-permute-done | bytes 524320 | tf_op jit(solution)/shard_map/ppermute | solution.py:307
  31.9 2.7 %collective-permute-start.6 = (bf16[1024,256]{1,0:T(8,128)(2,1)}, bf16[1024,256]{1,0:T(8,128)(2,1)S(1)}, u32[]{:S(2)}, u32[]{:S(2)}) collective-permute-start(bf16[1024,256]{1,0:T(8,128)(2,1)} %collective-permute-done.2.refs_8_), channel_id=1, source_target_pairs={{0,4},{1,5},{2,6},{3,7},{4,0},{5,1},{6,2},{7,3},{8,12},{9,13},{10,... | collective-permute-start | bytes 1572872 | tf_op jit(solution)/shard_map/ppermute | solution.py:307
  34.6 1.5 %collective-permute-start.11 = (bf16[1024,256]{1,0:T(8,128)(2,1)}, bf16[1024,256]{1,0:T(8,128)(2,1)S(1)}, u32[]{:S(2)}, u32[]{:S(2)}) collective-permute-start(bf16[1024,256]{1,0:T(8,128)(2,1)} %collective-permute-done.1.refs_6_), channel_id=1, source_target_pairs={{0,16},{1,17},{2,18},{3,19},{4,20},{5,21},{6,22},{7,23},{8,24},{9,... | collective-permute-start | bytes 1572872 | tf_op jit(solution)/shard_map/ppermute | solution.py:307
  36.7 17.7 %collective-permute-done.5.refs_7_ = bf16[2,256,512]{2,1,0:T(8,128)(2,1)} collective-permute-done((bf16[2,256,512]{2,1,0:T(8,128)(2,1)S(1)}, bf16[2,256,512]{2,1,0:T(8,128)(2,1)}, u32[]{:S(2)}, u32[]{:S(2)}) %collective-permute-start.5) | collective-permute-done | bytes 524320 | tf_op jit(solution)/shard_map/ppermute | solution.py:307
  54.4 1.5 %collective-permute-start.7 = (bf16[2,256,512]{2,1,0:T(8,128)(2,1)}, bf16[2,256,512]{2,1,0:T(8,128)(2,1)S(1)}, u32[]{:S(2)}, u32[]{:S(2)}) collective-permute-start(bf16[2,256,512]{2,1,0:T(8,128)(2,1)} %collective-permute-done.5.refs_7_), channel_id=1, source_target_pairs={{0,4},{1,5},{2,6},{3,7},{4,0},{5,1},{6,2},{7,3},{8,12},{9,13},{10,... | collective-permute-start | bytes 1572872 | tf_op jit(solution)/shard_map/ppermute | solution.py:307
  56.8 1.5 %collective-permute-start.13 = (bf16[1024,256]{1,0:T(8,128)(2,1)S(1)}, bf16[1024,256]{1,0:T(8,128)(2,1)S(1)}, u32[]{:S(2)}, u32[]{:S(2)}) collective-permute-start(bf16[1024,256]{1,0:T(8,128)(2,1)S(1)} %collective-permute-done.6.refs_10_), channel_id=1, source_target_pairs={{0,16},{1,17},{2,18},{3,19},{4,20},{5,21},{6,22},{7,23},{8,24},{9,... | collective-permute-start | bytes 1572872 | tf_op jit(solution)/shard_map/ppermute | solution.py:307
  58.8 1.8 %collective-permute-done.15.refs_10_ = bf16[1,256,512]{2,1,0:T(8,128)(2,1)S(1)} collective-permute-done((bf16[1,256,512]{2,1,0:T(8,128)(2,1)S(1)}, bf16[1,256,512]{2,1,0:T(8,128)(2,1)S(1)}, u32[]{:S(2)}, u32[]{:S(2)}) %collective-permute-start.15) | collective-permute-done | bytes 262176 | tf_op jit(solution)/shard_map/ppermute | solution.py:307
  60.8 8.2 %collective-permute-done.7.refs_8_ = bf16[2,256,512]{2,1,0:T(8,128)(2,1)S(1)} collective-permute-done((bf16[2,256,512]{2,1,0:T(8,128)(2,1)}, bf16[2,256,512]{2,1,0:T(8,128)(2,1)S(1)}, u32[]{:S(2)}, u32[]{:S(2)}) %collective-permute-start.7) | collective-permute-done | bytes 524320 | tf_op jit(solution)/shard_map/ppermute | solution.py:307
  72.0 1.7 %collective-permute-start.22 = (bf16[1,256,1024]{2,1,0:T(8,128)(2,1)S(1)}, bf16[1,256,1024]{2,1,0:T(8,128)(2,1)}, u32[]{:S(2)}, u32[]{:S(2)}) collective-permute-start(bf16[1,256,1024]{2,1,0:T(8,128)(2,1)S(1)} %bitcast.6), channel_id=1, source_target_pairs={{0,4},{1,5},{2,6},{3,7},{4,0},{5,1},{6,2},{7,3},{8,12},{9,13},{10,... | collective-permute-start | bytes 1572872 | tf_op jit(solution)/shard_map/ppermute | solution.py:307
  75.8 6.4 %partial_sums.1 = (f32[128,512]{1,0:T(8,128)}, f32[128,512]{1,0:T(8,128)}, bf16[128,512]{1,0:T(8,128)(2,1)}, bf16[128,512]{1,0:T(8,128)(2,1)}) custom-call(bf16[4,128,1024]{2,1,0:T(8,128)(2,1)} %get-tuple-element.31.refs_0_, bf16[4,128,1024]{2,1,0:T(8,128)(2,1)} %collective-permute-done.refs_1_, bf16[8,128,1024]{2,1,0:T(8,128)(2,1)} %copy-done.2, ...), custom_call_target="tpu_custom_call" | custom-call | flops 2147483648 | bytes 8388608 | tf_op jit(solution)/shard_map/partial_sums/pallas_call | solution.py:169
  82.4 3.5 %collective-permute-done.22.refs_14_ = bf16[1,256,1024]{2,1,0:T(8,128)(2,1)} collective-permute-done((bf16[1,256,1024]{2,1,0:T(8,128)(2,1)S(1)}, bf16[1,256,1024]{2,1,0:T(8,128)(2,1)}, u32[]{:S(2)}, u32[]{:S(2)}) %collective-permute-start.22) | collective-permute-done | bytes 524320 | tf_op jit(solution)/shard_map/ppermute | solution.py:307
  86.0 1.7 %collective-permute-start.25 = (bf16[2,256,512]{2,1,0:T(8,128)(2,1)S(1)}, bf16[2,256,512]{2,1,0:T(8,128)(2,1)S(1)}, u32[]{:S(2)}, u32[]{:S(2)}) collective-permute-start(bf16[2,256,512]{2,1,0:T(8,128)(2,1)S(1)} %stack_halves.3), channel_id=1, source_target_pairs={{0,4},{1,5},{2,6},{3,7},{4,0},{5,1},{6,2},{7,3},{8,12},{9,13},{10,... | collective-permute-start | bytes 1572872 | tf_op jit(solution)/shard_map/ppermute | solution.py:307
  89.0 1.5 %collective-permute-start.19 = (bf16[128,512]{1,0:T(8,128)(2,1)}, bf16[128,512]{1,0:T(8,128)(2,1)S(1)}, u32[]{:S(2)}, u32[]{:S(2)}) collective-permute-start(bf16[128,512]{1,0:T(8,128)(2,1)} %get-tuple-element.45), channel_id=1, source_target_pairs={{0,2},{1,3},{2,0},{3,1},{4,6},{5,7},{6,4},{7,5},{8,10},{9,11},{10,... | collective-permute-start | bytes 393224 | tf_op jit(solution)/shard_map/ppermute | solution.py:307
  91.2 3.8 %collective-permute-done.20.refs_2_ = bf16[128,512]{1,0:T(8,128)(2,1)S(1)} collective-permute-done((bf16[128,512]{1,0:T(8,128)(2,1)}, bf16[128,512]{1,0:T(8,128)(2,1)S(1)}, u32[]{:S(2)}, u32[]{:S(2)}) %collective-permute-start.20) | collective-permute-done | bytes 131104 | tf_op jit(solution)/shard_map/ppermute | solution.py:307
  95.5 2.3 %collective-permute-done.19.refs_1_ = bf16[128,512]{1,0:T(8,128)(2,1)S(1)} collective-permute-done((bf16[128,512]{1,0:T(8,128)(2,1)}, bf16[128,512]{1,0:T(8,128)(2,1)S(1)}, u32[]{:S(2)}, u32[]{:S(2)}) %collective-permute-start.19) | collective-permute-done | bytes 131104 | tf_op jit(solution)/shard_map/ppermute | solution.py:307
  98.5 6.4 %down_first.1 = (bf16[128,16384]{1,0:T(8,128)(2,1)}, bf16[128,256]{1,0:T(8,128)(2,1)}) custom-call(s32[16]{0:T(128)} %owner_ref.5, s32[1]{0:T(128)S(6)} %copy.10.live_ref, f32[128,512]{1,0:T(8,128)} %get-tuple-element.43.own, f32[128,512]{1,0:T(8,128)} %copy-done.20, bf16[128,512]{1,0:T(8,128)(2,1)} %copy-done.22, bf16[128,512]{1,0:T(8,128)(2,1)} %copy-done.21, ...), custom_call_target="tpu_custom_call" | custom-call | flops 671088640 | bytes 7864320 | tf_op jit(solution)/shard_map/down_first/pallas_call | solution.py:252
  108.5 4.1 %down_second.1 = bf16[128,16384]{1,0:T(8,128)(2,1)} custom-call(s32[16]{0:T(128)} %owner_ref.5, s32[1]{0:T(128)S(6)} %copy.10.live_ref, bf16[128,256]{1,0:T(8,128)(2,1)} %get-tuple-element.49.hidden_ref, bf16[128,16384]{1,0:T(8,128)(2,1)} %get-tuple-element.50._, bf16[2,256,512]{2,1,0:T(8,128)(2,1)} %copy-done.14, ...), custom_call_target="tpu_custom_call", output_to_operand_aliasing={{}: (3, {})} | custom-call | flops 402653184 | bytes 4718592 | tf_op jit(solution)/shard_map/down_second/pallas_call | solution.py:252
  (91 shorter events, 17.0 us)
Async XLA Ops:
  1.9 26.4 %collective-permute-start.1 = (bf16[1024,256]{1,0:T(8,128)(2,1)}, bf16[1024,256]{1,0:T(8,128)(2,1)}, u32[]{:S(2)}, u32[]{:S(2)}) collective-permute-start(bf16[1024,256]{1,0:T(8,128)(2,1)} %broadcast_select_fusion), channel_id=1, source_target_pairs={{0,4},{1,5},{2,6},{3,7},{4,0},{5,1},{6,2},{7,3},{8,12},{9,13},{10,... | collective-permute-start | bytes 1572872 | tf_op jit(solution)/shard_map/ppermute | solution.py:307
  4.9 25.9 %collective-permute-start.2 = (bf16[1024,256]{1,0:T(8,128)(2,1)}, bf16[1024,256]{1,0:T(8,128)(2,1)}, u32[]{:S(2)}, u32[]{:S(2)}) collective-permute-start(bf16[1024,256]{1,0:T(8,128)(2,1)} %broadcast_select_fusion), channel_id=1, source_target_pairs={{0,8},{1,9},{2,10},{3,11},{4,12},{5,13},{6,14},{7,15},{8,0},{9,1},... | collective-permute-start | bytes 1572872 | tf_op jit(solution)/shard_map/ppermute | solution.py:307
  7.5 23.3 %collective-permute-start.3 = (bf16[1,256,1024]{2,1,0:T(8,128)(2,1)}, bf16[1,256,1024]{2,1,0:T(8,128)(2,1)S(1)}, u32[]{:S(2)}, u32[]{:S(2)}) collective-permute-start(bf16[1,256,1024]{2,1,0:T(8,128)(2,1)} %bitcast.4), channel_id=1, source_target_pairs={{0,1},{1,0},{2,3},{3,2},{4,5},{5,4},{6,7},{7,6},{8,9},{9,8},{10,11... | collective-permute-start | bytes 1572872 | tf_op jit(solution)/shard_map/ppermute | solution.py:307
  8.6 8.8 %collective-permute-start.4 = (bf16[1,256,512]{2,1,0:T(8,128)(2,1)S(1)}, bf16[1,256,512]{2,1,0:T(8,128)(2,1)S(1)}, u32[]{:S(2)}, u32[]{:S(2)}) collective-permute-start(bf16[1,256,512]{2,1,0:T(8,128)(2,1)S(1)} %select_bitcast_fusion.a_ref), channel_id=1, source_target_pairs={{0,2},{1,3},{2,0},{3,1},{4,6},{5,7},{6,4},{7,5},{8,10},{9,11},{10,... | collective-permute-start | bytes 786440 | tf_op jit(solution)/shard_map/ppermute | solution.py:307
  15.8 55.5 %collective-permute-start.9 = (bf16[8,128,1024]{2,1,0:T(8,128)(2,1)}, bf16[8,128,1024]{2,1,0:T(8,128)(2,1)S(1)}, u32[]{:S(2)}, u32[]{:S(2)}) collective-permute-start(bf16[8,128,1024]{2,1,0:T(8,128)(2,1)} %get-tuple-element.33), channel_id=1, source_target_pairs={{0,2},{1,3},{2,0},{3,1},{4,6},{5,7},{6,4},{7,5},{8,10},{9,11},{10,... | collective-permute-start | bytes 6291464 | tf_op jit(solution)/shard_map/ppermute | solution.py:307
  17.4 17.3 %collective-permute-start.10 = (bf16[1,256,512]{2,1,0:T(8,128)(2,1)S(1)}, bf16[1,256,512]{2,1,0:T(8,128)(2,1)S(1)}, u32[]{:S(2)}, u32[]{:S(2)}) collective-permute-start(bf16[1,256,512]{2,1,0:T(8,128)(2,1)S(1)} %collective-permute-done.4.b_ref.refs_5_.a_ref), channel_id=1, source_target_pairs={{0,16},{1,17},{2,18},{3,19},{4,20},{5,21},{6,22},{7,23},{8,24},{9,... | collective-permute-start | bytes 786440 | tf_op jit(solution)/shard_map/ppermute | solution.py:307
  31.6 22.8 %collective-permute-start.5 = (bf16[2,256,512]{2,1,0:T(8,128)(2,1)S(1)}, bf16[2,256,512]{2,1,0:T(8,128)(2,1)}, u32[]{:S(2)}, u32[]{:S(2)}) collective-permute-start(bf16[2,256,512]{2,1,0:T(8,128)(2,1)S(1)} %stack_halves.2), channel_id=1, source_target_pairs={{0,8},{1,9},{2,10},{3,11},{4,12},{5,13},{6,14},{7,15},{8,0},{9,1},... | collective-permute-start | bytes 1572872 | tf_op jit(solution)/shard_map/ppermute | solution.py:307
  31.9 22.5 %collective-permute-start.6 = (bf16[1024,256]{1,0:T(8,128)(2,1)}, bf16[1024,256]{1,0:T(8,128)(2,1)S(1)}, u32[]{:S(2)}, u32[]{:S(2)}) collective-permute-start(bf16[1024,256]{1,0:T(8,128)(2,1)} %collective-permute-done.2.refs_8_), channel_id=1, source_target_pairs={{0,4},{1,5},{2,6},{3,7},{4,0},{5,1},{6,2},{7,3},{8,12},{9,13},{10,... | collective-permute-start | bytes 1572872 | tf_op jit(solution)/shard_map/ppermute | solution.py:307
  34.6 21.3 %collective-permute-start.11 = (bf16[1024,256]{1,0:T(8,128)(2,1)}, bf16[1024,256]{1,0:T(8,128)(2,1)S(1)}, u32[]{:S(2)}, u32[]{:S(2)}) collective-permute-start(bf16[1024,256]{1,0:T(8,128)(2,1)} %collective-permute-done.1.refs_6_), channel_id=1, source_target_pairs={{0,16},{1,17},{2,18},{3,19},{4,20},{5,21},{6,22},{7,23},{8,24},{9,... | collective-permute-start | bytes 1572872 | tf_op jit(solution)/shard_map/ppermute | solution.py:307
  36.2 19.8 %collective-permute-start.12 = (bf16[1024,256]{1,0:T(8,128)(2,1)}, bf16[1024,256]{1,0:T(8,128)(2,1)S(1)}, u32[]{:S(2)}, u32[]{:S(2)}) collective-permute-start(bf16[1024,256]{1,0:T(8,128)(2,1)} %collective-permute-done.2.refs_8_), channel_id=1, source_target_pairs={{0,16},{1,17},{2,18},{3,19},{4,20},{5,21},{6,22},{7,23},{8,24},{9,... | collective-permute-start | bytes 1572872 | tf_op jit(solution)/shard_map/ppermute | solution.py:307
  54.4 3.9 %collective-permute-start.14 = (bf16[1,256,512]{2,1,0:T(8,128)(2,1)S(1)}, bf16[1,256,512]{2,1,0:T(8,128)(2,1)S(1)}, u32[]{:S(2)}, u32[]{:S(2)}) collective-permute-start(bf16[1,256,512]{2,1,0:T(8,128)(2,1)S(1)} %collective-permute-done.4.b_ref.refs_5_.a_ref), channel_id=1, source_target_pairs={{0,1},{1,0},{2,3},{3,2},{4,5},{5,4},{6,7},{7,6},{8,9},{9,8},{10,11... | collective-permute-start | bytes 786440 | tf_op jit(solution)/shard_map/ppermute | solution.py:307
  54.4 14.5 %collective-permute-start.7 = (bf16[2,256,512]{2,1,0:T(8,128)(2,1)}, bf16[2,256,512]{2,1,0:T(8,128)(2,1)S(1)}, u32[]{:S(2)}, u32[]{:S(2)}) collective-permute-start(bf16[2,256,512]{2,1,0:T(8,128)(2,1)} %collective-permute-done.5.refs_7_), channel_id=1, source_target_pairs={{0,4},{1,5},{2,6},{3,7},{4,0},{5,1},{6,2},{7,3},{8,12},{9,13},{10,... | collective-permute-start | bytes 1572872 | tf_op jit(solution)/shard_map/ppermute | solution.py:307
  56.8 12.9 %collective-permute-start.13 = (bf16[1024,256]{1,0:T(8,128)(2,1)S(1)}, bf16[1024,256]{1,0:T(8,128)(2,1)S(1)}, u32[]{:S(2)}, u32[]{:S(2)}) collective-permute-start(bf16[1024,256]{1,0:T(8,128)(2,1)S(1)} %collective-permute-done.6.refs_10_), channel_id=1, source_target_pairs={{0,16},{1,17},{2,18},{3,19},{4,20},{5,21},{6,22},{7,23},{8,24},{9,... | collective-permute-start | bytes 1572872 | tf_op jit(solution)/shard_map/ppermute | solution.py:307
  58.3 11.3 %collective-permute-start.16 = (bf16[2,256,512]{2,1,0:T(8,128)(2,1)}, bf16[2,256,512]{2,1,0:T(8,128)(2,1)S(1)}, u32[]{:S(2)}, u32[]{:S(2)}) collective-permute-start(bf16[2,256,512]{2,1,0:T(8,128)(2,1)} %collective-permute-done.5.refs_7_), channel_id=1, source_target_pairs={{0,1},{1,0},{2,3},{3,2},{4,5},{5,4},{6,7},{7,6},{8,9},{9,8},{10,11... | collective-permute-start | bytes 1572872 | tf_op jit(solution)/shard_map/ppermute | solution.py:307
  60.6 14.4 %collective-permute-start = (bf16[4,128,1024]{2,1,0:T(8,128)(2,1)S(1)}, bf16[4,128,1024]{2,1,0:T(8,128)(2,1)}, u32[]{:S(2)}, u32[]{:S(2)}) collective-permute-start(bf16[4,128,1024]{2,1,0:T(8,128)(2,1)S(1)} %copy-done.23), channel_id=1, source_target_pairs={{0,1},{1,0},{2,3},{3,2},{4,5},{5,4},{6,7},{7,6},{8,9},{9,8},{10,11... | collective-permute-start | bytes 3145736 | tf_op jit(solution)/shard_map/ppermute | solution.py:307
  72.0 14.0 %collective-permute-start.22 = (bf16[1,256,1024]{2,1,0:T(8,128)(2,1)S(1)}, bf16[1,256,1024]{2,1,0:T(8,128)(2,1)}, u32[]{:S(2)}, u32[]{:S(2)}) collective-permute-start(bf16[1,256,1024]{2,1,0:T(8,128)(2,1)S(1)} %bitcast.6), channel_id=1, source_target_pairs={{0,4},{1,5},{2,6},{3,7},{4,0},{5,1},{6,2},{7,3},{8,12},{9,13},{10,... | collective-permute-start | bytes 1572872 | tf_op jit(solution)/shard_map/ppermute | solution.py:307
  73.6 14.0 %collective-permute-start.21 = (bf16[2,256,512]{2,1,0:T(8,128)(2,1)}, bf16[2,256,512]{2,1,0:T(8,128)(2,1)}, u32[]{:S(2)}, u32[]{:S(2)}) collective-permute-start(bf16[2,256,512]{2,1,0:T(8,128)(2,1)} %collective-permute-done.5.refs_7_), channel_id=1, source_target_pairs={{0,16},{1,17},{2,18},{3,19},{4,20},{5,21},{6,22},{7,23},{8,24},{9,... | collective-permute-start | bytes 1572872 | tf_op jit(solution)/shard_map/ppermute | solution.py:307
  82.3 3.7 %collective-permute-start.18 = (f32[128,512]{1,0:T(8,128)}, f32[128,512]{1,0:T(8,128)S(1)}, u32[]{:S(2)}, u32[]{:S(2)}) collective-permute-start(f32[128,512]{1,0:T(8,128)} %get-tuple-element.44), channel_id=1, source_target_pairs={{0,1},{1,0},{2,3},{3,2},{4,5},{5,4},{6,7},{7,6},{8,9},{9,8},{10,11... | collective-permute-start | bytes 786440 | tf_op jit(solution)/shard_map/ppermute | solution.py:307
  86.0 19.0 %collective-permute-start.25 = (bf16[2,256,512]{2,1,0:T(8,128)(2,1)S(1)}, bf16[2,256,512]{2,1,0:T(8,128)(2,1)S(1)}, u32[]{:S(2)}, u32[]{:S(2)}) collective-permute-start(bf16[2,256,512]{2,1,0:T(8,128)(2,1)S(1)} %stack_halves.3), channel_id=1, source_target_pairs={{0,4},{1,5},{2,6},{3,7},{4,0},{5,1},{6,2},{7,3},{8,12},{9,13},{10,... | collective-permute-start | bytes 1572872 | tf_op jit(solution)/shard_map/ppermute | solution.py:307
  87.7 17.3 %collective-permute-start.26 = (bf16[2,256,512]{2,1,0:T(8,128)(2,1)S(1)}, bf16[2,256,512]{2,1,0:T(8,128)(2,1)S(1)}, u32[]{:S(2)}, u32[]{:S(2)}) collective-permute-start(bf16[2,256,512]{2,1,0:T(8,128)(2,1)S(1)} %collective-permute-done.7.refs_8_), channel_id=1, source_target_pairs={{0,16},{1,17},{2,18},{3,19},{4,20},{5,21},{6,22},{7,23},{8,24},{9,... | collective-permute-start | bytes 1572872 | tf_op jit(solution)/shard_map/ppermute | solution.py:307
  89.0 6.0 %collective-permute-start.20 = (bf16[128,512]{1,0:T(8,128)(2,1)}, bf16[128,512]{1,0:T(8,128)(2,1)S(1)}, u32[]{:S(2)}, u32[]{:S(2)}) collective-permute-start(bf16[128,512]{1,0:T(8,128)(2,1)} %get-tuple-element.46), channel_id=1, source_target_pairs={{0,3},{1,2},{2,1},{3,0},{4,7},{5,6},{6,5},{7,4},{8,11},{9,10},{10,... | collective-permute-start | bytes 393224 | tf_op jit(solution)/shard_map/ppermute | solution.py:307
  89.0 8.8 %collective-permute-start.19 = (bf16[128,512]{1,0:T(8,128)(2,1)}, bf16[128,512]{1,0:T(8,128)(2,1)S(1)}, u32[]{:S(2)}, u32[]{:S(2)}) collective-permute-start(bf16[128,512]{1,0:T(8,128)(2,1)} %get-tuple-element.45), channel_id=1, source_target_pairs={{0,2},{1,3},{2,0},{3,1},{4,6},{5,7},{6,4},{7,5},{8,10},{9,11},{10,... | collective-permute-start | bytes 393224 | tf_op jit(solution)/shard_map/ppermute | solution.py:307
  95.0 10.5 %collective-permute-start.23 = (bf16[2,256,512]{2,1,0:T(8,128)(2,1)}, bf16[2,256,512]{2,1,0:T(8,128)(2,1)S(1)}, u32[]{:S(2)}, u32[]{:S(2)}) collective-permute-start(bf16[2,256,512]{2,1,0:T(8,128)(2,1)} %collective-permute-done.21.refs_13_), channel_id=1, source_target_pairs={{0,1},{1,0},{2,3},{3,2},{4,5},{5,4},{6,7},{7,6},{8,9},{9,8},{10,11... | collective-permute-start | bytes 1572872 | tf_op jit(solution)/shard_map/ppermute | solution.py:307
  95.2 10.3 %collective-permute-start.24 = (bf16[1,256,1024]{2,1,0:T(8,128)(2,1)}, bf16[1,256,1024]{2,1,0:T(8,128)(2,1)S(1)}, u32[]{:S(2)}, u32[]{:S(2)}) collective-permute-start(bf16[1,256,1024]{2,1,0:T(8,128)(2,1)} %collective-permute-done.22.refs_14_), channel_id=1, source_target_pairs={{0,1},{1,0},{2,3},{3,2},{4,5},{5,4},{6,7},{7,6},{8,9},{9,8},{10,11... | collective-permute-start | bytes 1572872 | tf_op jit(solution)/shard_map/ppermute | solution.py:307
  (29 other events, 343.0 us)

commit v5 on v4

--- a/solution.py
+++ b/solution.py
@@ -122,8 +122,10 @@
 
 
 def partial_kernel(given, kinds, *refs):
-    outs, (rows, held, mine, other, row_sem, sem) = refs[-6 - len(kinds) : -6], refs[-6:]
-    inputs, weights = refs[:given], refs[given : -6 - len(kinds)]
+    count = len(kinds)
+    made, (rows, held, mine, other, row_sem, sem, out_sem) = refs[-7 - count : -7], refs[-7:]
+    outs = refs[-7 - 2 * count : -7 - count]
+    inputs, weights = refs[:given], refs[given : -7 - 2 * count]
     z, plane = lax.axis_index("wide") >> 2, lax.axis_index("groups")
     size = inputs[0].shape[1]
     hid = held.shape[2]
@@ -140,7 +142,8 @@
     for start in range(0, hops, step):
         for i in range(2 * start, 2 * (start + step)):
             copies[i].wait()
-        for k, (out, kind) in enumerate(zip(outs, kinds)):
+        sent = []
+        for k, (out, kind) in enumerate(zip(made, kinds)):
             here = slice(k * size, (k + 1) * size)
             sums = []
             for side in range(2):
@@ -160,6 +163,10 @@
                 )
                 out[:, :hid] = (gate + jnp.where(first, a, b)).astype(kind)
                 out[:, hid:] = (up + jnp.where(first, b, a)).astype(kind)
+                sent.append(pltpu.make_async_copy(out, outs[k], out_sem.at[k]))
+                sent[-1].start()
+    for copy in sent:
+        copy.wait()
 
 
 def partial_sums(inputs, weights, kinds):
@@ -169,15 +176,17 @@
     return pl.pallas_call(
         functools.partial(partial_kernel, len(inputs), kinds),
         in_specs=[HBM] * (len(inputs) + len(weights)),
-        out_specs=[VMEM] * count,
-        out_shape=[jax.ShapeDtypeStruct((rows, 2 * hid), kind) for kind in kinds],
-        scratch_shapes=[
+        out_specs=[HBM] * count,
+        out_shape=[pltpu.HBM((rows, 2 * hid), kind) for kind in kinds],
+        scratch_shapes=[pltpu.VMEM((rows, 2 * hid), kind) for kind in kinds]
+        + [
             pltpu.VMEM((hops, count * rows, depth), BF16),
             pltpu.VMEM((len(weights), depth, hid), BF16),
             pltpu.VMEM((count * rows, hid), F32),
             pltpu.VMEM((count * rows, hid), F32),
             pltpu.SemaphoreType.DMA((count,)),
             pltpu.SemaphoreType.DMA((len(weights),)),
+            pltpu.SemaphoreType.DMA((count,)),
         ],
         compiler_params=pltpu.CompilerParams(vmem_limit_bytes=FULL),
         cost_estimate=pl.CostEstimate(
@@ -189,14 +198,12 @@
     )(*inputs, *weights)
 
 
-def multiply_out(hidden, pieces, owner_ref, weights, out, held, sem, results, out_sem, places):
-    copies = fetch(list(zip(weights, held)), sem)
+def multiply_out(hidden, copies, pieces, owner, out, held, results, out_sem, places):
     group, here = lax.axis_index("groups"), lax.axis_index("wide")
-    blocks = owner_ref.shape[0]
+    blocks = owner.shape[0]
     block = out.shape[1] // blocks
     for p in range(blocks):
-        places[owner_ref[p]] = p * block
-    hidden = hidden()
+        places[owner[p]] = p * block
     start, sent = 0, []
     for copy, ref, parts in zip(copies, held, pieces):
         copy.wait()
@@ -220,56 +227,75 @@
         copy.wait()
 
 
-def first_kernel(pieces, owner_ref, live_ref, own, *refs):
+def first_kernel(pieces, live_ref, owner_ref, *refs):
     count = len(pieces)
-    partials, weights, (out, hidden_ref) = refs[:3], refs[3 : 3 + count], refs[3 + count : 5 + count]
-    held, rest = refs[5 + count : 5 + 2 * count], refs[5 + 2 * count :]
-    hid = own.shape[1] // 2
-
-    def hidden():
-        total = own[...]
-        for part in partials:
-            total += part[...].astype(F32)
-        gate, up = total[:, :hid], total[:, hid:]
-        hidden = gate / (1.0 + jnp.exp(-gate)) * up
-        rows = lax.broadcasted_iota(jnp.int32, hidden.shape, 0)
-        hidden_ref[...] = jnp.where(rows < MEM + live_ref[0], hidden, 0.0).astype(BF16)
-        return hidden_ref[...]
-
-    multiply_out(hidden, pieces, owner_ref, weights, out, held, *rest)
-
-
-def second_kernel(pieces, owner_ref, live_ref, hidden_ref, _, *refs):
+    sums, weights, (out, hidden_ref) = refs[:4], refs[4 : 4 + count], refs[4 + count : 6 + count]
+    owner, *rest = refs[6 + count :]
+    sums_held, held = rest[:4], rest[4 : 4 + count]
+    sem, results, out_sem, places, hidden, hidden_sem = rest[4 + count :]
+    first, *copies = fetch(
+        list(zip((owner_ref, *sums, *weights), (owner, *sums_held, *held))), sem
+    )
+    for copy in (first, *copies[:4]):
+        copy.wait()
+    hid = hidden.shape[1]
+    total = sums_held[0][...]
+    for part in sums_held[1:]:
+        total += part[...].astype(F32)
+    gate, up = total[:, :hid], total[:, hid:]
+    units = gate / (1.0 + jnp.exp(-gate)) * up
+    rows = lax.broadcasted_iota(jnp.int32, units.shape, 0)
+    hidden[...] = jnp.where(rows < MEM + live_ref[0], units, 0.0).astype(BF16)
+    handed = pltpu.make_async_copy(hidden, hidden_ref, hidden_sem)
+    handed.start()
+    multiply_out(hidden[...], copies[4:], pieces, owner, out, held, results, out_sem, places)
+    handed.wait()
+
+
+def second_kernel(pieces, owner_ref, hidden_ref, _, *refs):
     count = len(pieces)
-    weights, out, held, rest = refs[:count], refs[count], refs[count + 1 : 2 * count + 1], refs[2 * count + 1 :]
-    multiply_out(lambda: hidden_ref[...], pieces, owner_ref, weights, out, held, *rest)
-
-
-def down_call(kernel, name, owner_rows, seg_counts, operands, specs, downs, outs, out_specs, aliases):
+    weights, out, owner, held = refs[:count], refs[count], refs[count + 1], refs[count + 2 : 2 * count + 2]
+    sem, results, out_sem, places, hidden = refs[2 * count + 2 :]
+    first, second, *copies = fetch(
+        list(zip((owner_ref, hidden_ref, *weights), (owner, hidden, *held))), sem
+    )
+    first.wait()
+    second.wait()
+    multiply_out(hidden[...], copies, pieces, owner, out, held, results, out_sem, places)
+
+
+def down_call(kernel, name, live, fetched, passed, downs, outs, scratch, aliases):
     weights, pieces = zip(*downs)
     rows = outs[0].shape[0]
-    columns = sum(w.size for w in weights) // weights[0].shape[1]
+    hid = weights[0].shape[1]
+    columns = sum(w.size for w in weights) // hid
+    places = [pltpu.SMEM(v.shape, v.dtype) for v in fetched[:1]]
+    kept = [pltpu.VMEM(v.shape, v.dtype) for v in fetched[1:] if v.shape != (rows, hid)]
     return pl.pallas_call(
         functools.partial(kernel, pieces),
-        in_specs=[SMEM, SMEM] + specs + [HBM] * len(weights),
-        out_specs=out_specs,
+        in_specs=[SMEM] * len(live) + [HBM] * (len(fetched) + len(passed) + len(weights)),
+        out_specs=[HBM] * len(outs),
         out_shape=outs,
-        scratch_shapes=[pltpu.VMEM(w.shape, w.dtype) for w in weights]
+        scratch_shapes=places
+        + kept
+        + [pltpu.VMEM(w.shape, w.dtype) for w in weights]
         + [
-            pltpu.SemaphoreType.DMA((len(weights),)),
+            pltpu.SemaphoreType.DMA((len(fetched) + len(weights),)),
             pltpu.VMEM((rows, columns), BF16),
             pltpu.SemaphoreType.DMA((sum(len(p) for p in pieces),)),
-            pltpu.SMEM(owner_rows.shape, jnp.int32),
+            *places,
+            pltpu.VMEM((rows, hid), BF16),
+            *scratch,
         ],
         input_output_aliases=aliases,
         compiler_params=pltpu.CompilerParams(vmem_limit_bytes=FULL),
         cost_estimate=pl.CostEstimate(
-            flops=2 * rows * weights[0].shape[1] * columns,
-            bytes_accessed=2 * columns * (rows + weights[0].shape[1]),
+            flops=20 * rows * hid * columns,
+            bytes_accessed=2 * columns * (rows + hid),
             transcendentals=0,
         ),
         name=name,
-    )(owner_rows, seg_counts, *operands, *weights)
+    )(*live, *fetched, *passed, *weights)
 
 
 def stack_kernel(a_ref, b_ref, out_ref):
@@ -338,12 +364,12 @@
     d1 = swap(after(down_weight[None], d3), near)
     e2 = swap(after(d2, b3), other)
 
-    second = [(mine_x, ((2, 0),)), (rest_x, ((2, 1),)), (d2, ((8, 0), (10, 0))), (d3, ((12, 0), (14, 0)))]
+    second = [(mine_x, ((2, 0),)), (rest_x, ((2, 1),)), (d2, ((8, 0), (10, 0)))]
     second = second + [cross(*w) for w in second]
-    r3 = swap(after(r2, b3, d3, second[4][0], second[5][0], second[6][0])[owners // 4 :], core)
+    r3 = swap(after(r2, b3, d3, *(w for w, _ in second))[owners // 4 :], core)
     weights = (gate_weight, up_weight, a1, b1, a2, b2, a3, b3)
     p0, p1, p2, p3 = partial_sums(
-        (t0, after(r1, second[7][0]), r2, r3), weights, (F32, F32, BF16, BF16)
+        (t0, r1, r2, r3), weights, (F32, F32, BF16, BF16)
     )
     q1 = swap(p1, core)
     q2 = swap(p2, across)
@@ -353,19 +379,18 @@
     e0 = stacked(mine_x, rest_x, 0)
     x1 = swap(after(e0, d1, q1), near)
 
-    third = [(e2, ((8, 1), (10, 1))), (d1, ((4, 0),))]
+    third = [(d3, ((12, 0), (14, 0))), (e2, ((8, 1), (10, 1))), (d1, ((4, 0),))]
     early = own + second + third
     out = pltpu.HBM(tokens.shape, BF16)
     rows, hid = tokens.shape[0], gate_weight.shape[1]
     product, hidden = down_call(
-        first_kernel, "down_first", owner_rows, seg_counts, (p0, q1, q2, q3), [VMEM] * 4, early,
-        [out, jax.ShapeDtypeStruct((rows, hid), BF16)], [HBM, VMEM], {},
+        first_kernel, "down_first", [seg_counts], [owner_rows, p0, q1, q2, q3], [], early,
+        [out, pltpu.HBM((rows, hid), BF16)], [pltpu.SemaphoreType.DMA], {},
     )
     late = [(after(x1, hidden), ((6, 0), (6, 1))), (after(e3, hidden), ((12, 1), (14, 1)))]
-    late = [cross(after(w, q3), parts) for w, parts in third] + late + [cross(*w) for w in late]
+    late = [cross(after(w, hidden), parts) for w, parts in third] + late + [cross(*w) for w in late]
     return down_call(
-        second_kernel, "down_second", owner_rows, seg_counts, (hidden, product), [VMEM, HBM], late,
-        [out], [HBM], {3: 0},
+        second_kernel, "down_second", [], [owner_rows, hidden], [product], late, [out], [], {2: 0}
     )[0]
 
 

time: 113 us -> 109 us (0.965)
  local copies, waits for them, and re-layouts: 5.5 us -> 3.14 us
  Pallas kernels: 22.7 us -> 20.6 us
  waiting for transfers between devices: 53.2 us -> 54.7 us
    unnamed x48, local copies, waits for them, and re-layouts: 5.44 us -> 3.07 us
    pallas_call x2, Pallas kernels: 10.5 us -> 8.34 us  [down_call(): pl.pallas_call(functools.partial(kernel, pieces), in_specs=[SMEM] * len(l...]
    ppermute x29, waiting for transfers between devices: 53.2 us -> 54.7 us  [swap(): return lax.ppermute(value, ALL, pairs)]
  transfers between devices with their start and end apart: 29 -> 29, of which waited for: 12 -> 15; matrix products, arithmetic and copies ran while one was open for 1% -> 1% of each run, Pallas kernels for 16% -> 16%
where the time goes in v5:
time: 109 us
  waiting for transfers between devices  54.7 us (50%)
  starting transfers between devices  26.4 us (24%)
  Pallas kernels  20.6 us (19%)
  local copies, waits for them, and re-layouts  3.14 us (3%)
  other arithmetic  2.95 us (3%)
    ppermute x29, waiting for transfers between devices, swap(): return lax.ppermute(value, ALL, pairs)  54.7 us
    ppermute x29, starting transfers between devices, swap(): return lax.ppermute(value, ALL, pairs)  26.4 us
    pallas_call x2, Pallas kernels, down_call(): pl.pallas_call(functools.partial(kernel, pieces), in_specs=[SMEM] * len(l...  8.34 us
    pallas_call x1, Pallas kernels, partial_sums(): pl.pallas_call(functools.partial(partial_kernel, len(inputs), kinds), in_...  6.47 us
    pallas_call x1, Pallas kernels, normed_quarters(): pl.pallas_call(norm_kernel, in_specs=[SMEM, HBM, VMEM], out_specs=[HBM] *...  5.66 us
    unnamed x48, local copies, waits for them, and re-layouts  3.07 us
  transfers between devices with their start and end apart: 29, of which 15 were waited for; matrix products, arithmetic and copies ran while one was open for 1% of the time, Pallas kernels for 16%

profile of v5, /device:TPU:0, one launch (start us, length us, event | category | flops | bytes accessed | tf_op | source)
XLA Modules:
  0.0 108.7 jit_solution(12519186005153897072)
XLA Ops:
  0.0 1.9 %broadcast_select_fusion = bf16[1024,256]{1,0:T(8,128)(2,1)} fusion(bf16[1024,256]{1,0:T(8,128)(2,1)} %refs_4_.1, bf16[1024,256]{1,0:T(8,128)(2,1)} %refs_5_.1, pred[]{:T(512)S(6)} %eq.3), kind=kLoop, calls=%fused_computation | loop fusion | flops 262144 | bytes 1572865 | tf_op jit(solution)/shard_map/jit(_where)/select_n | solution.py:336
  1.9 4.0 %collective-permute-start.2 = (bf16[1024,256]{1,0:T(8,128)(2,1)}, bf16[1024,256]{1,0:T(8,128)(2,1)S(1)}, u32[]{:S(2)}, u32[]{:S(2)}) collective-permute-start(bf16[1024,256]{1,0:T(8,128)(2,1)} %broadcast_select_fusion), channel_id=1, source_target_pairs={{0,8},{1,9},{2,10},{3,11},{4,12},{5,13},{6,14},{7,15},{8,0},{9,1},... | collective-permute-start | bytes 1572872 | tf_op jit(solution)/shard_map/ppermute | solution.py:333
  5.9 1.6 %collective-permute-start.3 = (bf16[1024,256]{1,0:T(8,128)(2,1)}, bf16[1024,256]{1,0:T(8,128)(2,1)}, u32[]{:S(2)}, u32[]{:S(2)}) collective-permute-start(bf16[1024,256]{1,0:T(8,128)(2,1)} %broadcast_select_fusion), channel_id=1, source_target_pairs={{0,4},{1,5},{2,6},{3,7},{4,0},{5,1},{6,2},{7,3},{8,12},{9,13},{10,... | collective-permute-start | bytes 1572872 | tf_op jit(solution)/shard_map/ppermute | solution.py:333
  8.6 1.6 %collective-permute-start.5 = (bf16[1,256,512]{2,1,0:T(8,128)(2,1)S(1)}, bf16[1,256,512]{2,1,0:T(8,128)(2,1)S(1)}, u32[]{:S(2)}, u32[]{:S(2)}) collective-permute-start(bf16[1,256,512]{2,1,0:T(8,128)(2,1)S(1)} %select_bitcast_fusion.a_ref), channel_id=1, source_target_pairs={{0,2},{1,3},{2,0},{3,1},{4,6},{5,7},{6,4},{7,5},{8,10},{9,11},{10,... | collective-permute-start | bytes 786440 | tf_op jit(solution)/shard_map/ppermute | solution.py:333
  10.1 5.7 %norm_quarters.1 = (bf16[4,128,1024]{2,1,0:T(8,128)(2,1)}, bf16[4,128,1024]{2,1,0:T(8,128)(2,1)}, bf16[8,128,1024]{2,1,0:T(8,128)(2,1)}) custom-call(s32[16]{0:T(128)} %owner_ref.5, bf16[128,16384]{1,0:T(8,128)(2,1)} %tokens_ref.1, f32[1,16384]{1,0:T(1,128)} %bitcast.4), custom_call_target="tpu_custom_call" | custom-call | flops 12582912 | bytes 8388608 | tf_op jit(solution)/shard_map/norm_quarters/pallas_call | solution.py:97
  18.9 10.5 %collective-permute-done.2.refs_8_ = bf16[1024,256]{1,0:T(8,128)(2,1)S(1)} collective-permute-done((bf16[1024,256]{1,0:T(8,128)(2,1)}, bf16[1024,256]{1,0:T(8,128)(2,1)S(1)}, u32[]{:S(2)}, u32[]{:S(2)}) %collective-permute-start.2) | collective-permute-done | bytes 524320 | tf_op jit(solution)/shard_map/ppermute | solution.py:333
  29.7 1.6 %collective-permute-start.6 = (bf16[1024,256]{1,0:T(8,128)(2,1)S(1)}, bf16[1024,256]{1,0:T(8,128)(2,1)S(1)}, u32[]{:S(2)}, u32[]{:S(2)}) collective-permute-start(bf16[1024,256]{1,0:T(8,128)(2,1)S(1)} %collective-permute-done.2.refs_8_), channel_id=1, source_target_pairs={{0,4},{1,5},{2,6},{3,7},{4,0},{5,1},{6,2},{7,3},{8,12},{9,13},{10,... | collective-permute-start | bytes 1572872 | tf_op jit(solution)/shard_map/ppermute | solution.py:333
  31.3 1.5 %collective-permute-start.8 = (bf16[1024,256]{1,0:T(8,128)(2,1)}, bf16[1024,256]{1,0:T(8,128)(2,1)S(1)}, u32[]{:S(2)}, u32[]{:S(2)}) collective-permute-start(bf16[1024,256]{1,0:T(8,128)(2,1)} %collective-permute-done.3.refs_6_), channel_id=1, source_target_pairs={{0,16},{1,17},{2,18},{3,19},{4,20},{5,21},{6,22},{7,23},{8,24},{9,... | collective-permute-start | bytes 1572872 | tf_op jit(solution)/shard_map/ppermute | solution.py:333
  33.3 2.2 %collective-permute-start.10 = (bf16[2,256,512]{2,1,0:T(8,128)(2,1)S(1)}, bf16[2,256,512]{2,1,0:T(8,128)(2,1)}, u32[]{:S(2)}, u32[]{:S(2)}) collective-permute-start(bf16[2,256,512]{2,1,0:T(8,128)(2,1)S(1)} %stack_halves.2), channel_id=1, source_target_pairs={{0,8},{1,9},{2,10},{3,11},{4,12},{5,13},{6,14},{7,15},{8,0},{9,1},... | collective-permute-start | bytes 1572872 | tf_op jit(solution)/shard_map/ppermute | solution.py:333
  35.6 16.6 %collective-permute-done.6.refs_10_ = bf16[1024,256]{1,0:T(8,128)(2,1)S(1)} collective-permute-done((bf16[1024,256]{1,0:T(8,128)(2,1)S(1)}, bf16[1024,256]{1,0:T(8,128)(2,1)S(1)}, u32[]{:S(2)}, u32[]{:S(2)}) %collective-permute-start.6) | collective-permute-done | bytes 524320 | tf_op jit(solution)/shard_map/ppermute | solution.py:333
  52.1 3.1 %collective-permute-done.9.refs_9_ = bf16[1024,256]{1,0:T(8,128)(2,1)S(1)} collective-permute-done((bf16[1024,256]{1,0:T(8,128)(2,1)S(1)}, bf16[1024,256]{1,0:T(8,128)(2,1)S(1)}, u32[]{:S(2)}, u32[]{:S(2)}) %collective-permute-start.9) | collective-permute-done | bytes 524320 | tf_op jit(solution)/shard_map/ppermute | solution.py:333
  55.3 2.9 %collective-permute-done.10.refs_8_ = bf16[2,256,512]{2,1,0:T(8,128)(2,1)} collective-permute-done((bf16[2,256,512]{2,1,0:T(8,128)(2,1)S(1)}, bf16[2,256,512]{2,1,0:T(8,128)(2,1)}, u32[]{:S(2)}, u32[]{:S(2)}) %collective-permute-start.10) | collective-permute-done | bytes 524320 | tf_op jit(solution)/shard_map/ppermute | solution.py:333
  58.2 1.5 %collective-permute-start.11 = (bf16[1024,256]{1,0:T(8,128)(2,1)S(1)}, bf16[1024,256]{1,0:T(8,128)(2,1)S(1)}, u32[]{:S(2)}, u32[]{:S(2)}) collective-permute-start(bf16[1024,256]{1,0:T(8,128)(2,1)S(1)} %collective-permute-done.6.refs_10_), channel_id=1, source_target_pairs={{0,16},{1,17},{2,18},{3,19},{4,20},{5,21},{6,22},{7,23},{8,24},{9,... | collective-permute-start | bytes 1572872 | tf_op jit(solution)/shard_map/ppermute | solution.py:333
  60.2 1.8 %collective-permute-done.14.refs_10_ = bf16[1,256,512]{2,1,0:T(8,128)(2,1)S(1)} collective-permute-done((bf16[1,256,512]{2,1,0:T(8,128)(2,1)S(1)}, bf16[1,256,512]{2,1,0:T(8,128)(2,1)S(1)}, u32[]{:S(2)}, u32[]{:S(2)}) %collective-permute-start.14) | collective-permute-done | bytes 262176 | tf_op jit(solution)/shard_map/ppermute | solution.py:333
  62.2 5.2 %collective-permute-done.11.refs_11_ = bf16[1024,256]{1,0:T(8,128)(2,1)S(1)} collective-permute-done((bf16[1024,256]{1,0:T(8,128)(2,1)S(1)}, bf16[1024,256]{1,0:T(8,128)(2,1)S(1)}, u32[]{:S(2)}, u32[]{:S(2)}) %collective-permute-start.11) | collective-permute-done | bytes 524320 | tf_op jit(solution)/shard_map/ppermute | solution.py:333
  67.4 2.7 %collective-permute-done.12.refs_12_ = bf16[2,256,512]{2,1,0:T(8,128)(2,1)S(1)} collective-permute-done((bf16[2,256,512]{2,1,0:T(8,128)(2,1)}, bf16[2,256,512]{2,1,0:T(8,128)(2,1)S(1)}, u32[]{:S(2)}, u32[]{:S(2)}) %collective-permute-start.12) | collective-permute-done | bytes 524320 | tf_op jit(solution)/shard_map/ppermute | solution.py:333
  71.8 1.8 %collective-permute-start.21 = (bf16[1,256,1024]{2,1,0:T(8,128)(2,1)}, bf16[1,256,1024]{2,1,0:T(8,128)(2,1)}, u32[]{:S(2)}, u32[]{:S(2)}) collective-permute-start(bf16[1,256,1024]{2,1,0:T(8,128)(2,1)} %bitcast.2.refs_4_), channel_id=1, source_target_pairs={{0,4},{1,5},{2,6},{3,7},{4,0},{5,1},{6,2},{7,3},{8,12},{9,13},{10,... | collective-permute-start | bytes 1572872 | tf_op jit(solution)/shard_map/ppermute | solution.py:333
  74.6 6.5 %partial_sums.1 = (f32[128,512]{1,0:T(8,128)}, f32[128,512]{1,0:T(8,128)}, bf16[128,512]{1,0:T(8,128)(2,1)}, bf16[128,512]{1,0:T(8,128)(2,1)}) custom-call(bf16[4,128,1024]{2,1,0:T(8,128)(2,1)} %get-tuple-element.31.refs_0_, bf16[4,128,1024]{2,1,0:T(8,128)(2,1)} %collective-permute-done.refs_1_, bf16[8,128,1024]{2,1,0:T(8,128)(2,1)} %copy-done.2, ...), custom_call_target="tpu_custom_call" | custom-call | flops 2147483648 | bytes 8388608 | tf_op jit(solution)/shard_map/partial_sums/pallas_call | solution.py:176
  83.7 2.7 %collective-permute-done.21.refs_14_ = bf16[1,256,1024]{2,1,0:T(8,128)(2,1)} collective-permute-done((bf16[1,256,1024]{2,1,0:T(8,128)(2,1)}, bf16[1,256,1024]{2,1,0:T(8,128)(2,1)}, u32[]{:S(2)}, u32[]{:S(2)}) %collective-permute-start.21) | collective-permute-done | bytes 524320 | tf_op jit(solution)/shard_map/ppermute | solution.py:333
  86.4 1.7 %collective-permute-start.25 = (bf16[2,256,512]{2,1,0:T(8,128)(2,1)S(1)}, bf16[2,256,512]{2,1,0:T(8,128)(2,1)S(1)}, u32[]{:S(2)}, u32[]{:S(2)}) collective-permute-start(bf16[2,256,512]{2,1,0:T(8,128)(2,1)S(1)} %stack_halves.3), channel_id=1, source_target_pairs={{0,4},{1,5},{2,6},{3,7},{4,0},{5,1},{6,2},{7,3},{8,12},{9,13},{10,... | collective-permute-start | bytes 1572872 | tf_op jit(solution)/shard_map/ppermute | solution.py:333
  90.3 4.8 %down_first.1 = (bf16[128,16384]{1,0:T(8,128)(2,1)}, bf16[128,256]{1,0:T(8,128)(2,1)}) custom-call(s32[1]{0:T(128)S(6)} %copy.10.live_ref, s32[16]{0:T(128)} %owner_ref.5, f32[128,512]{1,0:T(8,128)} %get-tuple-element.42.refs_0_, f32[128,512]{1,0:T(8,128)} %copy-done.21, bf16[128,512]{1,0:T(8,128)(2,1)} %copy-done.22, bf16[128,512]{1,0:T(8,128)(2,1)} %copy-done.23, ...), custom_call_target="tpu_custom_call" | custom-call | flops 6039797760 | bytes 7077888 | tf_op jit(solution)/shard_map/down_first/pallas_call | solution.py:274
  96.2 3.7 %collective-permute-done.25.refs_3_ = bf16[2,256,512]{2,1,0:T(8,128)(2,1)S(1)} collective-permute-done((bf16[2,256,512]{2,1,0:T(8,128)(2,1)S(1)}, bf16[2,256,512]{2,1,0:T(8,128)(2,1)S(1)}, u32[]{:S(2)}, u32[]{:S(2)}) %collective-permute-start.25) | collective-permute-done | bytes 524320 | tf_op jit(solution)/shard_map/ppermute | solution.py:333
  99.9 1.7 %collective-permute-done.26.refs_4_ = bf16[2,256,512]{2,1,0:T(8,128)(2,1)S(1)} collective-permute-done((bf16[2,256,512]{2,1,0:T(8,128)(2,1)}, bf16[2,256,512]{2,1,0:T(8,128)(2,1)S(1)}, u32[]{:S(2)}, u32[]{:S(2)}) %collective-permute-start.26) | collective-permute-done | bytes 524320 | tf_op jit(solution)/shard_map/ppermute | solution.py:333
  105.1 3.6 %down_second.1 = bf16[128,16384]{1,0:T(8,128)(2,1)} custom-call(s32[16]{0:T(128)} %owner_ref.5, bf16[128,256]{1,0:T(8,128)(2,1)} %get-tuple-element.48.hidden_ref, bf16[128,16384]{1,0:T(8,128)(2,1)} %get-tuple-element.49._, bf16[2,256,512]{2,1,0:T(8,128)(2,1)} %copy-done.14, bf16[2,256,512]{2,1,0:T(8,128)(2,1)} %copy-done.15, ...), custom_call_target="tpu_custom_call", output_to_operand_aliasing={{}: (2, {})} | custom-call | flops 4697620480 | bytes 5505024 | tf_op jit(solution)/shard_map/down_second/pallas_call | solution.py:274
  (91 shorter events, 17.0 us)
Async XLA Ops:
  1.9 27.5 %collective-permute-start.2 = (bf16[1024,256]{1,0:T(8,128)(2,1)}, bf16[1024,256]{1,0:T(8,128)(2,1)S(1)}, u32[]{:S(2)}, u32[]{:S(2)}) collective-permute-start(bf16[1024,256]{1,0:T(8,128)(2,1)} %broadcast_select_fusion), channel_id=1, source_target_pairs={{0,8},{1,9},{2,10},{3,11},{4,12},{5,13},{6,14},{7,15},{8,0},{9,1},... | collective-permute-start | bytes 1572872 | tf_op jit(solution)/shard_map/ppermute | solution.py:333
  5.9 23.8 %collective-permute-start.3 = (bf16[1024,256]{1,0:T(8,128)(2,1)}, bf16[1024,256]{1,0:T(8,128)(2,1)}, u32[]{:S(2)}, u32[]{:S(2)}) collective-permute-start(bf16[1024,256]{1,0:T(8,128)(2,1)} %broadcast_select_fusion), channel_id=1, source_target_pairs={{0,4},{1,5},{2,6},{3,7},{4,0},{5,1},{6,2},{7,3},{8,12},{9,13},{10,... | collective-permute-start | bytes 1572872 | tf_op jit(solution)/shard_map/ppermute | solution.py:333
  7.5 22.2 %collective-permute-start.4 = (bf16[1,256,1024]{2,1,0:T(8,128)(2,1)}, bf16[1,256,1024]{2,1,0:T(8,128)(2,1)}, u32[]{:S(2)}, u32[]{:S(2)}) collective-permute-start(bf16[1,256,1024]{2,1,0:T(8,128)(2,1)} %bitcast.2.refs_4_), channel_id=1, source_target_pairs={{0,1},{1,0},{2,3},{3,2},{4,5},{5,4},{6,7},{7,6},{8,9},{9,8},{10,11... | collective-permute-start | bytes 1572872 | tf_op jit(solution)/shard_map/ppermute | solution.py:333
  8.6 8.8 %collective-permute-start.5 = (bf16[1,256,512]{2,1,0:T(8,128)(2,1)S(1)}, bf16[1,256,512]{2,1,0:T(8,128)(2,1)S(1)}, u32[]{:S(2)}, u32[]{:S(2)}) collective-permute-start(bf16[1,256,512]{2,1,0:T(8,128)(2,1)S(1)} %select_bitcast_fusion.a_ref), channel_id=1, source_target_pairs={{0,2},{1,3},{2,0},{3,1},{4,6},{5,7},{6,4},{7,5},{8,10},{9,11},{10,... | collective-permute-start | bytes 786440 | tf_op jit(solution)/shard_map/ppermute | solution.py:333
  15.8 55.8 %collective-permute-start.1 = (bf16[8,128,1024]{2,1,0:T(8,128)(2,1)}, bf16[8,128,1024]{2,1,0:T(8,128)(2,1)S(1)}, u32[]{:S(2)}, u32[]{:S(2)}) collective-permute-start(bf16[8,128,1024]{2,1,0:T(8,128)(2,1)} %get-tuple-element.33), channel_id=1, source_target_pairs={{0,2},{1,3},{2,0},{3,1},{4,6},{5,7},{6,4},{7,5},{8,10},{9,11},{10,... | collective-permute-start | bytes 6291464 | tf_op jit(solution)/shard_map/ppermute | solution.py:333
  17.4 13.9 %collective-permute-start.7 = (bf16[1,256,512]{2,1,0:T(8,128)(2,1)S(1)}, bf16[1,256,512]{2,1,0:T(8,128)(2,1)S(1)}, u32[]{:S(2)}, u32[]{:S(2)}) collective-permute-start(bf16[1,256,512]{2,1,0:T(8,128)(2,1)S(1)} %collective-permute-done.5.b_ref.refs_6_.a_ref), channel_id=1, source_target_pairs={{0,16},{1,17},{2,18},{3,19},{4,20},{5,21},{6,22},{7,23},{8,24},{9,... | collective-permute-start | bytes 786440 | tf_op jit(solution)/shard_map/ppermute | solution.py:333
  29.7 22.4 %collective-permute-start.6 = (bf16[1024,256]{1,0:T(8,128)(2,1)S(1)}, bf16[1024,256]{1,0:T(8,128)(2,1)S(1)}, u32[]{:S(2)}, u32[]{:S(2)}) collective-permute-start(bf16[1024,256]{1,0:T(8,128)(2,1)S(1)} %collective-permute-done.2.refs_8_), channel_id=1, source_target_pairs={{0,4},{1,5},{2,6},{3,7},{4,0},{5,1},{6,2},{7,3},{8,12},{9,13},{10,... | collective-permute-start | bytes 1572872 | tf_op jit(solution)/shard_map/ppermute | solution.py:333
  31.3 20.8 %collective-permute-start.8 = (bf16[1024,256]{1,0:T(8,128)(2,1)}, bf16[1024,256]{1,0:T(8,128)(2,1)S(1)}, u32[]{:S(2)}, u32[]{:S(2)}) collective-permute-start(bf16[1024,256]{1,0:T(8,128)(2,1)} %collective-permute-done.3.refs_6_), channel_id=1, source_target_pairs={{0,16},{1,17},{2,18},{3,19},{4,20},{5,21},{6,22},{7,23},{8,24},{9,... | collective-permute-start | bytes 1572872 | tf_op jit(solution)/shard_map/ppermute | solution.py:333
  32.8 22.4 %collective-permute-start.9 = (bf16[1024,256]{1,0:T(8,128)(2,1)S(1)}, bf16[1024,256]{1,0:T(8,128)(2,1)S(1)}, u32[]{:S(2)}, u32[]{:S(2)}) collective-permute-start(bf16[1024,256]{1,0:T(8,128)(2,1)S(1)} %collective-permute-done.2.refs_8_), channel_id=1, source_target_pairs={{0,16},{1,17},{2,18},{3,19},{4,20},{5,21},{6,22},{7,23},{8,24},{9,... | collective-permute-start | bytes 1572872 | tf_op jit(solution)/shard_map/ppermute | solution.py:333
  33.3 24.9 %collective-permute-start.10 = (bf16[2,256,512]{2,1,0:T(8,128)(2,1)S(1)}, bf16[2,256,512]{2,1,0:T(8,128)(2,1)}, u32[]{:S(2)}, u32[]{:S(2)}) collective-permute-start(bf16[2,256,512]{2,1,0:T(8,128)(2,1)S(1)} %stack_halves.2), channel_id=1, source_target_pairs={{0,8},{1,9},{2,10},{3,11},{4,12},{5,13},{6,14},{7,15},{8,0},{9,1},... | collective-permute-start | bytes 1572872 | tf_op jit(solution)/shard_map/ppermute | solution.py:333
  52.1 7.6 %collective-permute-start.13 = (bf16[1,256,512]{2,1,0:T(8,128)(2,1)S(1)}, bf16[1,256,512]{2,1,0:T(8,128)(2,1)S(1)}, u32[]{:S(2)}, u32[]{:S(2)}) collective-permute-start(bf16[1,256,512]{2,1,0:T(8,128)(2,1)S(1)} %collective-permute-done.5.b_ref.refs_6_.a_ref), channel_id=1, source_target_pairs={{0,1},{1,0},{2,3},{3,2},{4,5},{5,4},{6,7},{7,6},{8,9},{9,8},{10,11... | collective-permute-start | bytes 786440 | tf_op jit(solution)/shard_map/ppermute | solution.py:333
  58.2 9.2 %collective-permute-start.11 = (bf16[1024,256]{1,0:T(8,128)(2,1)S(1)}, bf16[1024,256]{1,0:T(8,128)(2,1)S(1)}, u32[]{:S(2)}, u32[]{:S(2)}) collective-permute-start(bf16[1024,256]{1,0:T(8,128)(2,1)S(1)} %collective-permute-done.6.refs_10_), channel_id=1, source_target_pairs={{0,16},{1,17},{2,18},{3,19},{4,20},{5,21},{6,22},{7,23},{8,24},{9,... | collective-permute-start | bytes 1572872 | tf_op jit(solution)/shard_map/ppermute | solution.py:333
  59.7 10.3 %collective-permute-start.12 = (bf16[2,256,512]{2,1,0:T(8,128)(2,1)}, bf16[2,256,512]{2,1,0:T(8,128)(2,1)S(1)}, u32[]{:S(2)}, u32[]{:S(2)}) collective-permute-start(bf16[2,256,512]{2,1,0:T(8,128)(2,1)} %collective-permute-done.10.refs_8_), channel_id=1, source_target_pairs={{0,4},{1,5},{2,6},{3,7},{4,0},{5,1},{6,2},{7,3},{8,12},{9,13},{10,... | collective-permute-start | bytes 1572872 | tf_op jit(solution)/shard_map/ppermute | solution.py:333
  59.7 10.3 %collective-permute-start.15 = (bf16[2,256,512]{2,1,0:T(8,128)(2,1)}, bf16[2,256,512]{2,1,0:T(8,128)(2,1)S(1)}, u32[]{:S(2)}, u32[]{:S(2)}) collective-permute-start(bf16[2,256,512]{2,1,0:T(8,128)(2,1)} %collective-permute-done.10.refs_8_), channel_id=1, source_target_pairs={{0,1},{1,0},{2,3},{3,2},{4,5},{5,4},{6,7},{7,6},{8,9},{9,8},{10,11... | collective-permute-start | bytes 1572872 | tf_op jit(solution)/shard_map/ppermute | solution.py:333
  62.0 12.6 %collective-permute-start = (bf16[4,128,1024]{2,1,0:T(8,128)(2,1)S(1)}, bf16[4,128,1024]{2,1,0:T(8,128)(2,1)}, u32[]{:S(2)}, u32[]{:S(2)}) collective-permute-start(bf16[4,128,1024]{2,1,0:T(8,128)(2,1)S(1)} %copy-done.8), channel_id=1, source_target_pairs={{0,1},{1,0},{2,3},{3,2},{4,5},{5,4},{6,7},{7,6},{8,9},{9,8},{10,11... | collective-permute-start | bytes 3145736 | tf_op jit(solution)/shard_map/ppermute | solution.py:333
  71.8 14.7 %collective-permute-start.21 = (bf16[1,256,1024]{2,1,0:T(8,128)(2,1)}, bf16[1,256,1024]{2,1,0:T(8,128)(2,1)}, u32[]{:S(2)}, u32[]{:S(2)}) collective-permute-start(bf16[1,256,1024]{2,1,0:T(8,128)(2,1)} %bitcast.2.refs_4_), channel_id=1, source_target_pairs={{0,4},{1,5},{2,6},{3,7},{4,0},{5,1},{6,2},{7,3},{8,12},{9,13},{10,... | collective-permute-start | bytes 1572872 | tf_op jit(solution)/shard_map/ppermute | solution.py:333
  73.6 14.6 %collective-permute-start.20 = (bf16[2,256,512]{2,1,0:T(8,128)(2,1)}, bf16[2,256,512]{2,1,0:T(8,128)(2,1)}, u32[]{:S(2)}, u32[]{:S(2)}) collective-permute-start(bf16[2,256,512]{2,1,0:T(8,128)(2,1)} %collective-permute-done.10.refs_8_), channel_id=1, source_target_pairs={{0,16},{1,17},{2,18},{3,19},{4,20},{5,21},{6,22},{7,23},{8,24},{9,... | collective-permute-start | bytes 1572872 | tf_op jit(solution)/shard_map/ppermute | solution.py:333
  81.2 7.9 %collective-permute-start.18 = (bf16[128,512]{1,0:T(8,128)(2,1)}, bf16[128,512]{1,0:T(8,128)(2,1)S(1)}, u32[]{:S(2)}, u32[]{:S(2)}) collective-permute-start(bf16[128,512]{1,0:T(8,128)(2,1)} %get-tuple-element.44), channel_id=1, source_target_pairs={{0,2},{1,3},{2,0},{3,1},{4,6},{5,7},{6,4},{7,5},{8,10},{9,11},{10,... | collective-permute-start | bytes 393224 | tf_op jit(solution)/shard_map/ppermute | solution.py:333
  82.7 6.9 %collective-permute-start.19 = (bf16[128,512]{1,0:T(8,128)(2,1)}, bf16[128,512]{1,0:T(8,128)(2,1)S(1)}, u32[]{:S(2)}, u32[]{:S(2)}) collective-permute-start(bf16[128,512]{1,0:T(8,128)(2,1)} %get-tuple-element.45), channel_id=1, source_target_pairs={{0,3},{1,2},{2,1},{3,0},{4,7},{5,6},{6,5},{7,4},{8,11},{9,10},{10,... | collective-permute-start | bytes 393224 | tf_op jit(solution)/shard_map/ppermute | solution.py:333
  86.4 13.5 %collective-permute-start.25 = (bf16[2,256,512]{2,1,0:T(8,128)(2,1)S(1)}, bf16[2,256,512]{2,1,0:T(8,128)(2,1)S(1)}, u32[]{:S(2)}, u32[]{:S(2)}) collective-permute-start(bf16[2,256,512]{2,1,0:T(8,128)(2,1)S(1)} %stack_halves.3), channel_id=1, source_target_pairs={{0,4},{1,5},{2,6},{3,7},{4,0},{5,1},{6,2},{7,3},{8,12},{9,13},{10,... | collective-permute-start | bytes 1572872 | tf_op jit(solution)/shard_map/ppermute | solution.py:333
  88.2 13.4 %collective-permute-start.26 = (bf16[2,256,512]{2,1,0:T(8,128)(2,1)}, bf16[2,256,512]{2,1,0:T(8,128)(2,1)S(1)}, u32[]{:S(2)}, u32[]{:S(2)}) collective-permute-start(bf16[2,256,512]{2,1,0:T(8,128)(2,1)} %copy-done.9), channel_id=1, source_target_pairs={{0,16},{1,17},{2,18},{3,19},{4,20},{5,21},{6,22},{7,23},{8,24},{9,... | collective-permute-start | bytes 1572872 | tf_op jit(solution)/shard_map/ppermute | solution.py:333
  95.0 7.1 %collective-permute-start.22 = (bf16[2,256,512]{2,1,0:T(8,128)(2,1)S(1)}, bf16[2,256,512]{2,1,0:T(8,128)(2,1)S(1)}, u32[]{:S(2)}, u32[]{:S(2)}) collective-permute-start(bf16[2,256,512]{2,1,0:T(8,128)(2,1)S(1)} %copy-done.10), channel_id=1, source_target_pairs={{0,1},{1,0},{2,3},{3,2},{4,5},{5,4},{6,7},{7,6},{8,9},{9,8},{10,11... | collective-permute-start | bytes 1572872 | tf_op jit(solution)/shard_map/ppermute | solution.py:333
  95.7 6.4 %collective-permute-start.23 = (bf16[2,256,512]{2,1,0:T(8,128)(2,1)}, bf16[2,256,512]{2,1,0:T(8,128)(2,1)S(1)}, u32[]{:S(2)}, u32[]{:S(2)}) collective-permute-start(bf16[2,256,512]{2,1,0:T(8,128)(2,1)} %collective-permute-done.20.refs_13_), channel_id=1, source_target_pairs={{0,1},{1,0},{2,3},{3,2},{4,5},{5,4},{6,7},{7,6},{8,9},{9,8},{10,11... | collective-permute-start | bytes 1572872 | tf_op jit(solution)/shard_map/ppermute | solution.py:333
  95.8 6.4 %collective-permute-start.24 = (bf16[1,256,1024]{2,1,0:T(8,128)(2,1)}, bf16[1,256,1024]{2,1,0:T(8,128)(2,1)S(1)}, u32[]{:S(2)}, u32[]{:S(2)}) collective-permute-start(bf16[1,256,1024]{2,1,0:T(8,128)(2,1)} %collective-permute-done.21.refs_14_), channel_id=1, source_target_pairs={{0,1},{1,0},{2,3},{3,2},{4,5},{5,4},{6,7},{7,6},{8,9},{9,8},{10,11... | collective-permute-start | bytes 1572872 | tf_op jit(solution)/shard_map/ppermute | solution.py:333
  (29 other events, 316.5 us)

commit v6 on v5

--- a/solution.py
+++ b/solution.py
@@ -356,17 +356,19 @@
 
     b1 = swap(after(a1, d0, rest_x), other)
     a3 = swap(after(a2, d0), near)
-    d2 = swap(d0, far)
+    d2 = swap(after(down_weight[None], d0), far)
     b2 = swap(after(a2, d0, rest_x), other)
 
-    b3 = swap(after(a3, b1, b2, d2), other)
-    d3 = swap(after(d2, a3), near)
-    d1 = swap(after(down_weight[None], d3), near)
-    e2 = swap(after(d2, b3), other)
-
-    second = [(mine_x, ((2, 0),)), (rest_x, ((2, 1),)), (d2, ((8, 0), (10, 0)))]
+    b3 = swap(after(a3, b1, b2), other)
+    d1 = swap(after(d0, a3, d2), near)
+
+    e1 = swap(after(d1, b3), other)
+    d3 = swap(after(d2, d1), near)
+    f2 = swap(after(d2, r2), across)
+
+    second = [(mine_x, ((2, 0),)), (rest_x, ((2, 1),)), (d2, ((8, 0),))]
     second = second + [cross(*w) for w in second]
-    r3 = swap(after(r2, b3, d3, *(w for w, _ in second))[owners // 4 :], core)
+    r3 = swap(after(r2, b3, d1, *(w for w, _ in second))[owners // 4 :], core)
     weights = (gate_weight, up_weight, a1, b1, a2, b2, a3, b3)
     p0, p1, p2, p3 = partial_sums(
         (t0, r1, r2, r3), weights, (F32, F32, BF16, BF16)
@@ -375,11 +377,14 @@
     q2 = swap(p2, across)
     q3 = swap(p3, both)
 
-    e3 = swap(after(d3, e2, q1), other)
-    e0 = stacked(mine_x, rest_x, 0)
-    x1 = swap(after(e0, d1, q1), near)
-
-    third = [(d3, ((12, 0), (14, 0))), (e2, ((8, 1), (10, 1))), (d1, ((4, 0),))]
+    f3 = swap(after(f2, d3, q1), near)
+
+    third = [
+        (d1, ((4, 0), (6, 0))),
+        (e1, ((4, 1), (6, 1))),
+        (f2, ((10, 0),)),
+        (d3, ((12, 0),)),
+    ]
     early = own + second + third
     out = pltpu.HBM(tokens.shape, BF16)
     rows, hid = tokens.shape[0], gate_weight.shape[1]
@@ -387,7 +392,7 @@
         first_kernel, "down_first", [seg_counts], [owner_rows, p0, q1, q2, q3], [], early,
         [out, pltpu.HBM((rows, hid), BF16)], [pltpu.SemaphoreType.DMA], {},
     )
-    late = [(after(x1, hidden), ((6, 0), (6, 1))), (after(e3, hidden), ((12, 1), (14, 1)))]
+    late = [(after(f3, hidden), ((14, 0),))]
     late = [cross(after(w, hidden), parts) for w, parts in third] + late + [cross(*w) for w in late]
     return down_call(
         second_kernel, "down_second", [], [owner_rows, hidden], [product], late, [out], [], {2: 0}

time: 109 us -> 109 us (level)
    unnamed x48 -> x50, local copies, waits for them, and re-layouts: 3.07 us -> 4 us
  transfers between devices with their start and end apart: 29 -> 29, of which waited for: 15 -> 17; matrix products, arithmetic and copies ran while one was open for 1% -> 1% of each run, Pallas kernels for 16% -> 16%
where the time goes in v6:
time: 109 us; the launch traced here: 108 us
  waiting for transfers between devices  54.6 us (50%)
  starting transfers between devices  25.5 us (23%)
  Pallas kernels  20.4 us (19%)
  local copies, waits for them, and re-layouts  4.07 us (4%)
  other arithmetic  2.96 us (3%)
    ppermute x29, waiting for transfers between devices, swap(): return lax.ppermute(value, ALL, pairs)  54.6 us
    ppermute x29, starting transfers between devices, swap(): return lax.ppermute(value, ALL, pairs)  25.5 us
    pallas_call x2, Pallas kernels, down_call(): pl.pallas_call(functools.partial(kernel, pieces), in_specs=[SMEM] * len(l...  8.28 us
    pallas_call x1, Pallas kernels, partial_sums(): pl.pallas_call(functools.partial(partial_kernel, len(inputs), kinds), in_...  6.47 us
    pallas_call x1, Pallas kernels, normed_quarters(): pl.pallas_call(norm_kernel, in_specs=[SMEM, HBM, VMEM], out_specs=[HBM] *...  5.66 us
    unnamed x50, local copies, waits for them, and re-layouts  4 us
  transfers between devices with their start and end apart: 29, of which 17 were waited for; matrix products, arithmetic and copies ran while one was open for 1% of the time, Pallas kernels for 16%

profile of v6, /device:TPU:0, one launch (start us, length us, event | category | flops | bytes accessed | tf_op | source)
XLA Modules:
  0.0 108.4 jit_solution(10398430537033154487)
XLA Ops:
  0.0 1.9 %broadcast_select_fusion = bf16[1024,256]{1,0:T(8,128)(2,1)} fusion(bf16[1024,256]{1,0:T(8,128)(2,1)} %refs_4_.1, bf16[1024,256]{1,0:T(8,128)(2,1)} %refs_5_.1, pred[]{:T(512)S(6)} %eq.3), kind=kLoop, calls=%fused_computation | loop fusion | flops 262144 | bytes 1572865 | tf_op jit(solution)/shard_map/jit(_where)/select_n | solution.py:336
  1.9 4.0 %collective-permute-start.2 = (bf16[1024,256]{1,0:T(8,128)(2,1)}, bf16[1024,256]{1,0:T(8,128)(2,1)S(1)}, u32[]{:S(2)}, u32[]{:S(2)}) collective-permute-start(bf16[1024,256]{1,0:T(8,128)(2,1)} %broadcast_select_fusion), channel_id=1, source_target_pairs={{0,8},{1,9},{2,10},{3,11},{4,12},{5,13},{6,14},{7,15},{8,0},{9,1},... | collective-permute-start | bytes 1572872 | tf_op jit(solution)/shard_map/ppermute | solution.py:333
  5.9 1.6 %collective-permute-start.3 = (bf16[1024,256]{1,0:T(8,128)(2,1)}, bf16[1024,256]{1,0:T(8,128)(2,1)S(1)}, u32[]{:S(2)}, u32[]{:S(2)}) collective-permute-start(bf16[1024,256]{1,0:T(8,128)(2,1)} %broadcast_select_fusion), channel_id=1, source_target_pairs={{0,4},{1,5},{2,6},{3,7},{4,0},{5,1},{6,2},{7,3},{8,12},{9,13},{10,... | collective-permute-start | bytes 1572872 | tf_op jit(solution)/shard_map/ppermute | solution.py:333
  8.6 1.6 %collective-permute-start.5 = (bf16[1,256,512]{2,1,0:T(8,128)(2,1)S(1)}, bf16[1,256,512]{2,1,0:T(8,128)(2,1)S(1)}, u32[]{:S(2)}, u32[]{:S(2)}) collective-permute-start(bf16[1,256,512]{2,1,0:T(8,128)(2,1)S(1)} %select_bitcast_fusion.a_ref), channel_id=1, source_target_pairs={{0,2},{1,3},{2,0},{3,1},{4,6},{5,7},{6,4},{7,5},{8,10},{9,11},{10,... | collective-permute-start | bytes 786440 | tf_op jit(solution)/shard_map/ppermute | solution.py:333
  10.1 5.7 %norm_quarters.1 = (bf16[4,128,1024]{2,1,0:T(8,128)(2,1)}, bf16[4,128,1024]{2,1,0:T(8,128)(2,1)}, bf16[8,128,1024]{2,1,0:T(8,128)(2,1)}) custom-call(s32[16]{0:T(128)} %owner_ref.5, bf16[128,16384]{1,0:T(8,128)(2,1)} %tokens_ref.1, f32[1,16384]{1,0:T(1,128)} %bitcast.7), custom_call_target="tpu_custom_call" | custom-call | flops 12582912 | bytes 8388608 | tf_op jit(solution)/shard_map/norm_quarters/pallas_call | solution.py:97
  17.4 1.5 %collective-permute-start.7 = (bf16[1,256,512]{2,1,0:T(8,128)(2,1)S(1)}, bf16[1,256,512]{2,1,0:T(8,128)(2,1)S(1)}, u32[]{:S(2)}, u32[]{:S(2)}) collective-permute-start(bf16[1,256,512]{2,1,0:T(8,128)(2,1)S(1)} %collective-permute-done.5.b_ref.refs_6_), channel_id=1, source_target_pairs={{0,16},{1,17},{2,18},{3,19},{4,20},{5,21},{6,22},{7,23},{8,24},{9,... | collective-permute-start | bytes 786440 | tf_op jit(solution)/shard_map/ppermute | solution.py:333
  18.9 10.5 %collective-permute-done.2.refs_8_ = bf16[1024,256]{1,0:T(8,128)(2,1)S(1)} collective-permute-done((bf16[1024,256]{1,0:T(8,128)(2,1)}, bf16[1024,256]{1,0:T(8,128)(2,1)S(1)}, u32[]{:S(2)}, u32[]{:S(2)}) %collective-permute-start.2) | collective-permute-done | bytes 524320 | tf_op jit(solution)/shard_map/ppermute | solution.py:333
  29.7 1.6 %collective-permute-start.9 = (bf16[1024,256]{1,0:T(8,128)(2,1)S(1)}, bf16[1024,256]{1,0:T(8,128)(2,1)S(1)}, u32[]{:S(2)}, u32[]{:S(2)}) collective-permute-start(bf16[1024,256]{1,0:T(8,128)(2,1)S(1)} %collective-permute-done.2.refs_8_), channel_id=1, source_target_pairs={{0,16},{1,17},{2,18},{3,19},{4,20},{5,21},{6,22},{7,23},{8,24},{9,... | collective-permute-start | bytes 1572872 | tf_op jit(solution)/shard_map/ppermute | solution.py:333
  33.5 2.4 %collective-permute-start.11 = (bf16[1,256,1024]{2,1,0:T(8,128)(2,1)S(1)}, bf16[1,256,1024]{2,1,0:T(8,128)(2,1)}, u32[]{:S(2)}, u32[]{:S(2)}) collective-permute-start(bf16[1,256,1024]{2,1,0:T(8,128)(2,1)S(1)} %bitcast.6), channel_id=1, source_target_pairs={{0,8},{1,9},{2,10},{3,11},{4,12},{5,13},{6,14},{7,15},{8,0},{9,1},... | collective-permute-start | bytes 1572872 | tf_op jit(solution)/shard_map/ppermute | solution.py:333
  35.8 8.8 %collective-permute-done.9.refs_9_ = bf16[1024,256]{1,0:T(8,128)(2,1)S(1)} collective-permute-done((bf16[1024,256]{1,0:T(8,128)(2,1)S(1)}, bf16[1024,256]{1,0:T(8,128)(2,1)S(1)}, u32[]{:S(2)}, u32[]{:S(2)}) %collective-permute-start.9) | collective-permute-done | bytes 524320 | tf_op jit(solution)/shard_map/ppermute | solution.py:333
  44.6 9.2 %collective-permute-done.8.refs_7_ = bf16[1024,256]{1,0:T(8,128)(2,1)S(1)} collective-permute-done((bf16[1024,256]{1,0:T(8,128)(2,1)S(1)}, bf16[1024,256]{1,0:T(8,128)(2,1)S(1)}, u32[]{:S(2)}, u32[]{:S(2)}) %collective-permute-start.8) | collective-permute-done | bytes 524320 | tf_op jit(solution)/shard_map/ppermute | solution.py:333
  53.8 1.5 %collective-permute-done.6.refs_10_ = bf16[1024,256]{1,0:T(8,128)(2,1)S(1)} collective-permute-done((bf16[1024,256]{1,0:T(8,128)(2,1)S(1)}, bf16[1024,256]{1,0:T(8,128)(2,1)S(1)}, u32[]{:S(2)}, u32[]{:S(2)}) %collective-permute-start.6) | collective-permute-done | bytes 524320 | tf_op jit(solution)/shard_map/ppermute | solution.py:333
  56.4 2.4 %collective-permute-done.11.refs_8_ = bf16[1,256,1024]{2,1,0:T(8,128)(2,1)} collective-permute-done((bf16[1,256,1024]{2,1,0:T(8,128)(2,1)S(1)}, bf16[1,256,1024]{2,1,0:T(8,128)(2,1)}, u32[]{:S(2)}, u32[]{:S(2)}) %collective-permute-start.11) | collective-permute-done | bytes 524320 | tf_op jit(solution)/shard_map/ppermute | solution.py:333
  59.6 1.8 %collective-permute-done.14.refs_10_ = bf16[1,256,512]{2,1,0:T(8,128)(2,1)S(1)} collective-permute-done((bf16[1,256,512]{2,1,0:T(8,128)(2,1)S(1)}, bf16[1,256,512]{2,1,0:T(8,128)(2,1)S(1)}, u32[]{:S(2)}, u32[]{:S(2)}) %collective-permute-start.14) | collective-permute-done | bytes 262176 | tf_op jit(solution)/shard_map/ppermute | solution.py:333
  62.2 4.7 %collective-permute-done.10.refs_11_ = bf16[1024,256]{1,0:T(8,128)(2,1)S(1)} collective-permute-done((bf16[1024,256]{1,0:T(8,128)(2,1)S(1)}, bf16[1024,256]{1,0:T(8,128)(2,1)S(1)}, u32[]{:S(2)}, u32[]{:S(2)}) %collective-permute-start.10) | collective-permute-done | bytes 524320 | tf_op jit(solution)/shard_map/ppermute | solution.py:333
  66.9 3.4 %collective-permute-done.12.refs_12_ = bf16[2,256,512]{2,1,0:T(8,128)(2,1)S(1)} collective-permute-done((bf16[2,256,512]{2,1,0:T(8,128)(2,1)S(1)}, bf16[2,256,512]{2,1,0:T(8,128)(2,1)S(1)}, u32[]{:S(2)}, u32[]{:S(2)}) %collective-permute-start.12) | collective-permute-done | bytes 524320 | tf_op jit(solution)/shard_map/ppermute | solution.py:333
  71.3 1.8 %collective-permute-start.22 = (bf16[1,256,1024]{2,1,0:T(8,128)(2,1)}, bf16[1,256,1024]{2,1,0:T(8,128)(2,1)}, u32[]{:S(2)}, u32[]{:S(2)}) collective-permute-start(bf16[1,256,1024]{2,1,0:T(8,128)(2,1)} %collective-permute-done.11.refs_8_), channel_id=1, source_target_pairs={{0,4},{1,5},{2,6},{3,7},{4,0},{5,1},{6,2},{7,3},{8,12},{9,13},{10,... | collective-permute-start | bytes 1572872 | tf_op jit(solution)/shard_map/ppermute | solution.py:333
  76.3 6.5 %partial_sums.1 = (f32[128,512]{1,0:T(8,128)}, f32[128,512]{1,0:T(8,128)}, bf16[128,512]{1,0:T(8,128)(2,1)}, bf16[128,512]{1,0:T(8,128)(2,1)}) custom-call(bf16[4,128,1024]{2,1,0:T(8,128)(2,1)} %get-tuple-element.32.refs_0_, bf16[4,128,1024]{2,1,0:T(8,128)(2,1)} %copy-done.2, bf16[8,128,1024]{2,1,0:T(8,128)(2,1)} %copy-done.1, ...), custom_call_target="tpu_custom_call" | custom-call | flops 2147483648 | bytes 8388608 | tf_op jit(solution)/shard_map/partial_sums/pallas_call | solution.py:176
  83.5 2.5 %collective-permute-done.22.refs_15_ = bf16[1,256,1024]{2,1,0:T(8,128)(2,1)} collective-permute-done((bf16[1,256,1024]{2,1,0:T(8,128)(2,1)}, bf16[1,256,1024]{2,1,0:T(8,128)(2,1)}, u32[]{:S(2)}, u32[]{:S(2)}) %collective-permute-start.22) | collective-permute-done | bytes 524320 | tf_op jit(solution)/shard_map/ppermute | solution.py:333
  89.2 1.7 %collective-permute-done.18.refs_2_ = bf16[128,512]{1,0:T(8,128)(2,1)S(1)} collective-permute-done((bf16[128,512]{1,0:T(8,128)(2,1)}, bf16[128,512]{1,0:T(8,128)(2,1)S(1)}, u32[]{:S(2)}, u32[]{:S(2)}) %collective-permute-start.18) | collective-permute-done | bytes 131104 | tf_op jit(solution)/shard_map/ppermute | solution.py:333
  92.9 4.9 %down_first.1 = (bf16[128,16384]{1,0:T(8,128)(2,1)}, bf16[128,256]{1,0:T(8,128)(2,1)}) custom-call(s32[1]{0:T(128)S(6)} %copy.10.live_ref, s32[16]{0:T(128)} %owner_ref.5, f32[128,512]{1,0:T(8,128)} %get-tuple-element.44.refs_0_, f32[128,512]{1,0:T(8,128)} %copy-done.22, bf16[128,512]{1,0:T(8,128)(2,1)} %copy-done.23, bf16[128,512]{1,0:T(8,128)(2,1)} %copy-done.24, ...), custom_call_target="tpu_custom_call" | custom-call | flops 6710886400 | bytes 7864320 | tf_op jit(solution)/shard_map/down_first/pallas_call | solution.py:274
  99.3 3.0 %collective-permute-done.27.refs_4_ = bf16[1,256,1024]{2,1,0:T(8,128)(2,1)S(1)} collective-permute-done((bf16[1,256,1024]{2,1,0:T(8,128)(2,1)}, bf16[1,256,1024]{2,1,0:T(8,128)(2,1)S(1)}, u32[]{:S(2)}, u32[]{:S(2)}) %collective-permute-start.27) | collective-permute-done | bytes 524320 | tf_op jit(solution)/shard_map/ppermute | solution.py:333
  102.8 1.5 %collective-permute-done.28.refs_5_ = bf16[1,256,1024]{2,1,0:T(8,128)(2,1)S(1)} collective-permute-done((bf16[1,256,1024]{2,1,0:T(8,128)(2,1)S(1)}, bf16[1,256,1024]{2,1,0:T(8,128)(2,1)S(1)}, u32[]{:S(2)}, u32[]{:S(2)}) %collective-permute-start.28) | collective-permute-done | bytes 524320 | tf_op jit(solution)/shard_map/ppermute | solution.py:333
  105.1 3.3 %down_second.1 = bf16[128,16384]{1,0:T(8,128)(2,1)} custom-call(s32[16]{0:T(128)} %owner_ref.5, bf16[128,256]{1,0:T(8,128)(2,1)} %get-tuple-element.51.hidden_ref, bf16[128,16384]{1,0:T(8,128)(2,1)} %get-tuple-element.52._, bf16[2,256,512]{2,1,0:T(8,128)(2,1)} %copy-done.17, bf16[2,256,512]{2,1,0:T(8,128)(2,1)} %copy-done.16, ...), custom_call_target="tpu_custom_call", output_to_operand_aliasing={{}: (2, {})} | custom-call | flops 4026531840 | bytes 4718592 | tf_op jit(solution)/shard_map/down_second/pallas_call | solution.py:274
  (92 shorter events, 19.6 us)
Async XLA Ops:
  1.9 27.5 %collective-permute-start.2 = (bf16[1024,256]{1,0:T(8,128)(2,1)}, bf16[1024,256]{1,0:T(8,128)(2,1)S(1)}, u32[]{:S(2)}, u32[]{:S(2)}) collective-permute-start(bf16[1024,256]{1,0:T(8,128)(2,1)} %broadcast_select_fusion), channel_id=1, source_target_pairs={{0,8},{1,9},{2,10},{3,11},{4,12},{5,13},{6,14},{7,15},{8,0},{9,1},... | collective-permute-start | bytes 1572872 | tf_op jit(solution)/shard_map/ppermute | solution.py:333
  5.9 23.7 %collective-permute-start.3 = (bf16[1024,256]{1,0:T(8,128)(2,1)}, bf16[1024,256]{1,0:T(8,128)(2,1)S(1)}, u32[]{:S(2)}, u32[]{:S(2)}) collective-permute-start(bf16[1024,256]{1,0:T(8,128)(2,1)} %broadcast_select_fusion), channel_id=1, source_target_pairs={{0,4},{1,5},{2,6},{3,7},{4,0},{5,1},{6,2},{7,3},{8,12},{9,13},{10,... | collective-permute-start | bytes 1572872 | tf_op jit(solution)/shard_map/ppermute | solution.py:333
  7.5 22.1 %collective-permute-start.4 = (bf16[1,256,1024]{2,1,0:T(8,128)(2,1)}, bf16[1,256,1024]{2,1,0:T(8,128)(2,1)}, u32[]{:S(2)}, u32[]{:S(2)}) collective-permute-start(bf16[1,256,1024]{2,1,0:T(8,128)(2,1)} %bitcast.4), channel_id=1, source_target_pairs={{0,1},{1,0},{2,3},{3,2},{4,5},{5,4},{6,7},{7,6},{8,9},{9,8},{10,11... | collective-permute-start | bytes 1572872 | tf_op jit(solution)/shard_map/ppermute | solution.py:333
  8.6 8.8 %collective-permute-start.5 = (bf16[1,256,512]{2,1,0:T(8,128)(2,1)S(1)}, bf16[1,256,512]{2,1,0:T(8,128)(2,1)S(1)}, u32[]{:S(2)}, u32[]{:S(2)}) collective-permute-start(bf16[1,256,512]{2,1,0:T(8,128)(2,1)S(1)} %select_bitcast_fusion.a_ref), channel_id=1, source_target_pairs={{0,2},{1,3},{2,0},{3,1},{4,6},{5,7},{6,4},{7,5},{8,10},{9,11},{10,... | collective-permute-start | bytes 786440 | tf_op jit(solution)/shard_map/ppermute | solution.py:333
  15.8 55.4 %collective-permute-start.1 = (bf16[8,128,1024]{2,1,0:T(8,128)(2,1)}, bf16[8,128,1024]{2,1,0:T(8,128)(2,1)S(1)}, u32[]{:S(2)}, u32[]{:S(2)}) collective-permute-start(bf16[8,128,1024]{2,1,0:T(8,128)(2,1)} %get-tuple-element.34), channel_id=1, source_target_pairs={{0,2},{1,3},{2,0},{3,1},{4,6},{5,7},{6,4},{7,5},{8,10},{9,11},{10,... | collective-permute-start | bytes 6291464 | tf_op jit(solution)/shard_map/ppermute | solution.py:333
  17.4 12.3 %collective-permute-start.7 = (bf16[1,256,512]{2,1,0:T(8,128)(2,1)S(1)}, bf16[1,256,512]{2,1,0:T(8,128)(2,1)S(1)}, u32[]{:S(2)}, u32[]{:S(2)}) collective-permute-start(bf16[1,256,512]{2,1,0:T(8,128)(2,1)S(1)} %collective-permute-done.5.b_ref.refs_6_), channel_id=1, source_target_pairs={{0,16},{1,17},{2,18},{3,19},{4,20},{5,21},{6,22},{7,23},{8,24},{9,... | collective-permute-start | bytes 786440 | tf_op jit(solution)/shard_map/ppermute | solution.py:333
  29.7 14.9 %collective-permute-start.9 = (bf16[1024,256]{1,0:T(8,128)(2,1)S(1)}, bf16[1024,256]{1,0:T(8,128)(2,1)S(1)}, u32[]{:S(2)}, u32[]{:S(2)}) collective-permute-start(bf16[1024,256]{1,0:T(8,128)(2,1)S(1)} %collective-permute-done.2.refs_8_), channel_id=1, source_target_pairs={{0,16},{1,17},{2,18},{3,19},{4,20},{5,21},{6,22},{7,23},{8,24},{9,... | collective-permute-start | bytes 1572872 | tf_op jit(solution)/shard_map/ppermute | solution.py:333
  31.3 22.5 %collective-permute-start.8 = (bf16[1024,256]{1,0:T(8,128)(2,1)S(1)}, bf16[1024,256]{1,0:T(8,128)(2,1)S(1)}, u32[]{:S(2)}, u32[]{:S(2)}) collective-permute-start(bf16[1024,256]{1,0:T(8,128)(2,1)S(1)} %collective-permute-done.3.refs_6_), channel_id=1, source_target_pairs={{0,16},{1,17},{2,18},{3,19},{4,20},{5,21},{6,22},{7,23},{8,24},{9,... | collective-permute-start | bytes 1572872 | tf_op jit(solution)/shard_map/ppermute | solution.py:333
  32.0 23.3 %collective-permute-start.6 = (bf16[1024,256]{1,0:T(8,128)(2,1)S(1)}, bf16[1024,256]{1,0:T(8,128)(2,1)S(1)}, u32[]{:S(2)}, u32[]{:S(2)}) collective-permute-start(bf16[1024,256]{1,0:T(8,128)(2,1)S(1)} %collective-permute-done.2.refs_8_), channel_id=1, source_target_pairs={{0,4},{1,5},{2,6},{3,7},{4,0},{5,1},{6,2},{7,3},{8,12},{9,13},{10,... | collective-permute-start | bytes 1572872 | tf_op jit(solution)/shard_map/ppermute | solution.py:333
  33.5 25.3 %collective-permute-start.11 = (bf16[1,256,1024]{2,1,0:T(8,128)(2,1)S(1)}, bf16[1,256,1024]{2,1,0:T(8,128)(2,1)}, u32[]{:S(2)}, u32[]{:S(2)}) collective-permute-start(bf16[1,256,1024]{2,1,0:T(8,128)(2,1)S(1)} %bitcast.6), channel_id=1, source_target_pairs={{0,8},{1,9},{2,10},{3,11},{4,12},{5,13},{6,14},{7,15},{8,0},{9,1},... | collective-permute-start | bytes 1572872 | tf_op jit(solution)/shard_map/ppermute | solution.py:333
  44.6 14.5 %collective-permute-start.13 = (bf16[1,256,512]{2,1,0:T(8,128)(2,1)S(1)}, bf16[1,256,512]{2,1,0:T(8,128)(2,1)S(1)}, u32[]{:S(2)}, u32[]{:S(2)}) collective-permute-start(bf16[1,256,512]{2,1,0:T(8,128)(2,1)S(1)} %collective-permute-done.5.b_ref.refs_6_), channel_id=1, source_target_pairs={{0,1},{1,0},{2,3},{3,2},{4,5},{5,4},{6,7},{7,6},{8,9},{9,8},{10,11... | collective-permute-start | bytes 786440 | tf_op jit(solution)/shard_map/ppermute | solution.py:333
  55.4 11.5 %collective-permute-start.10 = (bf16[1024,256]{1,0:T(8,128)(2,1)S(1)}, bf16[1024,256]{1,0:T(8,128)(2,1)S(1)}, u32[]{:S(2)}, u32[]{:S(2)}) collective-permute-start(bf16[1024,256]{1,0:T(8,128)(2,1)S(1)} %collective-permute-done.6.refs_10_), channel_id=1, source_target_pairs={{0,16},{1,17},{2,18},{3,19},{4,20},{5,21},{6,22},{7,23},{8,24},{9,... | collective-permute-start | bytes 1572872 | tf_op jit(solution)/shard_map/ppermute | solution.py:333
  58.8 11.5 %collective-permute-start.12 = (bf16[2,256,512]{2,1,0:T(8,128)(2,1)S(1)}, bf16[2,256,512]{2,1,0:T(8,128)(2,1)S(1)}, u32[]{:S(2)}, u32[]{:S(2)}) collective-permute-start(bf16[2,256,512]{2,1,0:T(8,128)(2,1)S(1)} %stack_halves.1), channel_id=1, source_target_pairs={{0,4},{1,5},{2,6},{3,7},{4,0},{5,1},{6,2},{7,3},{8,12},{9,13},{10,... | collective-permute-start | bytes 1572872 | tf_op jit(solution)/shard_map/ppermute | solution.py:333
  59.1 11.2 %collective-permute-start.15 = (bf16[1,256,1024]{2,1,0:T(8,128)(2,1)}, bf16[1,256,1024]{2,1,0:T(8,128)(2,1)S(1)}, u32[]{:S(2)}, u32[]{:S(2)}) collective-permute-start(bf16[1,256,1024]{2,1,0:T(8,128)(2,1)} %collective-permute-done.11.refs_8_), channel_id=1, source_target_pairs={{0,1},{1,0},{2,3},{3,2},{4,5},{5,4},{6,7},{7,6},{8,9},{9,8},{10,11... | collective-permute-start | bytes 1572872 | tf_op jit(solution)/shard_map/ppermute | solution.py:333
  62.1 13.2 %collective-permute-start = (bf16[4,128,1024]{2,1,0:T(8,128)(2,1)S(1)}, bf16[4,128,1024]{2,1,0:T(8,128)(2,1)S(1)}, u32[]{:S(2)}, u32[]{:S(2)}) collective-permute-start(bf16[4,128,1024]{2,1,0:T(8,128)(2,1)S(1)} %copy-done.10), channel_id=1, source_target_pairs={{0,1},{1,0},{2,3},{3,2},{4,5},{5,4},{6,7},{7,6},{8,9},{9,8},{10,11... | collective-permute-start | bytes 3145736 | tf_op jit(solution)/shard_map/ppermute | solution.py:333
  71.3 4.1 %collective-permute-start.16 = (bf16[4,128,1024]{2,1,0:T(8,128)(2,1)S(1)}, bf16[4,128,1024]{2,1,0:T(8,128)(2,1)}, u32[]{:S(2)}, u32[]{:S(2)}) collective-permute-start(bf16[4,128,1024]{2,1,0:T(8,128)(2,1)S(1)} %slice.11), channel_id=1, source_target_pairs={{0,1},{1,0},{2,3},{3,2},{4,5},{5,4},{6,7},{7,6},{8,9},{9,8},{10,11... | collective-permute-start | bytes 3145736 | tf_op jit(solution)/shard_map/ppermute | solution.py:333
  71.3 14.7 %collective-permute-start.22 = (bf16[1,256,1024]{2,1,0:T(8,128)(2,1)}, bf16[1,256,1024]{2,1,0:T(8,128)(2,1)}, u32[]{:S(2)}, u32[]{:S(2)}) collective-permute-start(bf16[1,256,1024]{2,1,0:T(8,128)(2,1)} %collective-permute-done.11.refs_8_), channel_id=1, source_target_pairs={{0,4},{1,5},{2,6},{3,7},{4,0},{5,1},{6,2},{7,3},{8,12},{9,13},{10,... | collective-permute-start | bytes 1572872 | tf_op jit(solution)/shard_map/ppermute | solution.py:333
  73.1 15.1 %collective-permute-start.21 = (bf16[1,256,1024]{2,1,0:T(8,128)(2,1)}, bf16[1,256,1024]{2,1,0:T(8,128)(2,1)}, u32[]{:S(2)}, u32[]{:S(2)}) collective-permute-start(bf16[1,256,1024]{2,1,0:T(8,128)(2,1)} %collective-permute-done.11.refs_8_), channel_id=1, source_target_pairs={{0,2},{1,3},{2,0},{3,1},{4,6},{5,7},{6,4},{7,5},{8,10},{9,11},{10,... | collective-permute-start | bytes 1572872 | tf_op jit(solution)/shard_map/ppermute | solution.py:333
  74.6 14.6 %collective-permute-start.20 = (bf16[2,256,512]{2,1,0:T(8,128)(2,1)S(1)}, bf16[2,256,512]{2,1,0:T(8,128)(2,1)}, u32[]{:S(2)}, u32[]{:S(2)}) collective-permute-start(bf16[2,256,512]{2,1,0:T(8,128)(2,1)S(1)} %collective-permute-done.12.refs_12_), channel_id=1, source_target_pairs={{0,16},{1,17},{2,18},{3,19},{4,20},{5,21},{6,22},{7,23},{8,24},{9,... | collective-permute-start | bytes 1572872 | tf_op jit(solution)/shard_map/ppermute | solution.py:333
  82.8 5.4 %collective-permute-start.17 = (f32[128,512]{1,0:T(8,128)}, f32[128,512]{1,0:T(8,128)S(1)}, u32[]{:S(2)}, u32[]{:S(2)}) collective-permute-start(f32[128,512]{1,0:T(8,128)} %get-tuple-element.45), channel_id=1, source_target_pairs={{0,1},{1,0},{2,3},{3,2},{4,5},{5,4},{6,7},{7,6},{8,9},{9,8},{10,11... | collective-permute-start | bytes 786440 | tf_op jit(solution)/shard_map/ppermute | solution.py:333
  82.9 8.1 %collective-permute-start.18 = (bf16[128,512]{1,0:T(8,128)(2,1)}, bf16[128,512]{1,0:T(8,128)(2,1)S(1)}, u32[]{:S(2)}, u32[]{:S(2)}) collective-permute-start(bf16[128,512]{1,0:T(8,128)(2,1)} %get-tuple-element.46), channel_id=1, source_target_pairs={{0,2},{1,3},{2,0},{3,1},{4,6},{5,7},{6,4},{7,5},{8,10},{9,11},{10,... | collective-permute-start | bytes 393224 | tf_op jit(solution)/shard_map/ppermute | solution.py:333
  86.0 6.2 %collective-permute-start.19 = (bf16[128,512]{1,0:T(8,128)(2,1)}, bf16[128,512]{1,0:T(8,128)(2,1)S(1)}, u32[]{:S(2)}, u32[]{:S(2)}) collective-permute-start(bf16[128,512]{1,0:T(8,128)(2,1)} %get-tuple-element.47), channel_id=1, source_target_pairs={{0,3},{1,2},{2,1},{3,0},{4,7},{5,6},{6,5},{7,4},{8,11},{9,10},{10,... | collective-permute-start | bytes 393224 | tf_op jit(solution)/shard_map/ppermute | solution.py:333
  88.2 14.2 %collective-permute-start.27 = (bf16[1,256,1024]{2,1,0:T(8,128)(2,1)}, bf16[1,256,1024]{2,1,0:T(8,128)(2,1)S(1)}, u32[]{:S(2)}, u32[]{:S(2)}) collective-permute-start(bf16[1,256,1024]{2,1,0:T(8,128)(2,1)} %collective-permute-done.21.refs_14_), channel_id=1, source_target_pairs={{0,4},{1,5},{2,6},{3,7},{4,0},{5,1},{6,2},{7,3},{8,12},{9,13},{10,... | collective-permute-start | bytes 1572872 | tf_op jit(solution)/shard_map/ppermute | solution.py:333
  97.8 4.6 %collective-permute-start.26 = (bf16[1,256,1024]{2,1,0:T(8,128)(2,1)}, bf16[1,256,1024]{2,1,0:T(8,128)(2,1)S(1)}, u32[]{:S(2)}, u32[]{:S(2)}) collective-permute-start(bf16[1,256,1024]{2,1,0:T(8,128)(2,1)} %collective-permute-done.22.refs_15_), channel_id=1, source_target_pairs={{0,1},{1,0},{2,3},{3,2},{4,5},{5,4},{6,7},{7,6},{8,9},{9,8},{10,11... | collective-permute-start | bytes 1572872 | tf_op jit(solution)/shard_map/ppermute | solution.py:333
  (30 other events, 289.2 us)

commit v7 on v6

--- a/solution.py
+++ b/solution.py
@@ -212,7 +212,7 @@
             for n in range(0, width, 256):
                 product = jnp.dot(hidden, ref[k, :, n : n + 256], preferred_element_type=F32)
                 results[:, start + n : start + n + 256] = product.astype(BF16)
-            side = group ^ plane if width < block else 0
+            side = (plane - 2 if plane >= 2 else group ^ plane) if width < block else 0
             place = places[here ^ turn] + side * width
             sent.append(
                 pltpu.make_async_copy(
@@ -375,9 +375,10 @@
     )
     q1 = swap(p1, core)
     q2 = swap(p2, across)
-    q3 = swap(p3, both)
-
-    f3 = swap(after(f2, d3, q1), near)
+    q3 = swap(after(p3, q1), both)
+
+    f3 = swap(after(f2, d3, q1)[:, :, :half], near)
+    g3 = swap(after(d3, f2, q1)[:, :, half:], across)
 
     third = [
         (d1, ((4, 0), (6, 0))),
@@ -392,8 +393,8 @@
         first_kernel, "down_first", [seg_counts], [owner_rows, p0, q1, q2, q3], [], early,
         [out, pltpu.HBM((rows, hid), BF16)], [pltpu.SemaphoreType.DMA], {},
     )
-    late = [(after(f3, hidden), ((14, 0),))]
-    late = [cross(after(w, hidden), parts) for w, parts in third] + late + [cross(*w) for w in late]
+    late = [(after(f3, hidden), ((14, 2),)), (after(g3, hidden), ((14, 3),))]
+    late = [cross(after(w, q2), parts) for w, parts in third[:2]] + [cross(after(w, hidden), parts) for w, parts in third[2:]] + late + [cross(*w) for w in late]
     return down_call(
         second_kernel, "down_second", [], [owner_rows, hidden], [product], late, [out], [], {2: 0}
     )[0]

time: 109 us -> 110 us (level)
  local copies, waits for them, and re-layouts: 4.07 us -> 5.25 us
    ppermute x29 -> x31, waiting for transfers between devices: 54.6 us -> 53.7 us  [swap(): return lax.ppermute(value, ALL, pairs)]
    ppermute x29 -> x31, starting transfers between devices: 25.5 us -> 25.9 us  [swap(): return lax.ppermute(value, ALL, pairs)]
    unnamed x50 -> x54, local copies, waits for them, and re-layouts: 4 us -> 4.19 us
  transfers between devices with their start and end apart: 29 -> 31, of which waited for: 17 -> 16; matrix products, arithmetic and copies ran while one was open for 1% -> 2% of each run, Pallas kernels for 16% -> 16%
where the time goes in v7:
time: 110 us; the launch traced here: 109 us
  waiting for transfers between devices  53.7 us (49%)
  starting transfers between devices  25.9 us (24%)
  Pallas kernels  20.7 us (19%)
  local copies, waits for them, and re-layouts  5.25 us (5%)
  other arithmetic  2.98 us (3%)
    ppermute x31, waiting for transfers between devices, swap(): return lax.ppermute(value, ALL, pairs)  53.7 us
    ppermute x31, starting transfers between devices, swap(): return lax.ppermute(value, ALL, pairs)  25.9 us
    pallas_call x2, Pallas kernels, down_call(): pl.pallas_call(functools.partial(kernel, pieces), in_specs=[SMEM] * len(l...  8.55 us
    pallas_call x1, Pallas kernels, partial_sums(): pl.pallas_call(functools.partial(partial_kernel, len(inputs), kinds), in_...  6.47 us
    pallas_call x1, Pallas kernels, normed_quarters(): pl.pallas_call(norm_kernel, in_specs=[SMEM, HBM, VMEM], out_specs=[HBM] *...  5.66 us
    unnamed x54, local copies, waits for them, and re-layouts  4.19 us
  transfers between devices with their start and end apart: 31, of which 16 were waited for; matrix products, arithmetic and copies ran while one was open for 2% of the time, Pallas kernels for 16%

profile of v7, /device:TPU:0, one launch (start us, length us, event | category | flops | bytes accessed | tf_op | source)
XLA Modules:
  0.0 109.4 jit_solution(14790039839570605113)
XLA Ops:
  0.0 1.9 %broadcast_select_fusion = bf16[1024,256]{1,0:T(8,128)(2,1)} fusion(bf16[1024,256]{1,0:T(8,128)(2,1)} %refs_4_.1, bf16[1024,256]{1,0:T(8,128)(2,1)} %refs_5_.1, pred[]{:T(512)S(6)} %eq.3), kind=kLoop, calls=%fused_computation | loop fusion | flops 262144 | bytes 1572865 | tf_op jit(solution)/shard_map/jit(_where)/select_n | solution.py:336
  1.9 4.0 %collective-permute-start.2 = (bf16[1024,256]{1,0:T(8,128)(2,1)}, bf16[1024,256]{1,0:T(8,128)(2,1)S(1)}, u32[]{:S(2)}, u32[]{:S(2)}) collective-permute-start(bf16[1024,256]{1,0:T(8,128)(2,1)} %broadcast_select_fusion), channel_id=1, source_target_pairs={{0,8},{1,9},{2,10},{3,11},{4,12},{5,13},{6,14},{7,15},{8,0},{9,1},... | collective-permute-start | bytes 1572872 | tf_op jit(solution)/shard_map/ppermute | solution.py:333
  6.0 1.6 %collective-permute-start.3 = (bf16[1024,256]{1,0:T(8,128)(2,1)}, bf16[1024,256]{1,0:T(8,128)(2,1)S(1)}, u32[]{:S(2)}, u32[]{:S(2)}) collective-permute-start(bf16[1024,256]{1,0:T(8,128)(2,1)} %broadcast_select_fusion), channel_id=1, source_target_pairs={{0,4},{1,5},{2,6},{3,7},{4,0},{5,1},{6,2},{7,3},{8,12},{9,13},{10,... | collective-permute-start | bytes 1572872 | tf_op jit(solution)/shard_map/ppermute | solution.py:333
  8.6 1.6 %collective-permute-start.5 = (bf16[1,256,512]{2,1,0:T(8,128)(2,1)S(1)}, bf16[1,256,512]{2,1,0:T(8,128)(2,1)S(1)}, u32[]{:S(2)}, u32[]{:S(2)}) collective-permute-start(bf16[1,256,512]{2,1,0:T(8,128)(2,1)S(1)} %select_bitcast_fusion.a_ref), channel_id=1, source_target_pairs={{0,2},{1,3},{2,0},{3,1},{4,6},{5,7},{6,4},{7,5},{8,10},{9,11},{10,... | collective-permute-start | bytes 786440 | tf_op jit(solution)/shard_map/ppermute | solution.py:333
  10.2 5.7 %norm_quarters.1 = (bf16[4,128,1024]{2,1,0:T(8,128)(2,1)}, bf16[4,128,1024]{2,1,0:T(8,128)(2,1)}, bf16[8,128,1024]{2,1,0:T(8,128)(2,1)}) custom-call(s32[16]{0:T(128)} %owner_ref.5, bf16[128,16384]{1,0:T(8,128)(2,1)} %tokens_ref.1, f32[1,16384]{1,0:T(1,128)} %bitcast.7), custom_call_target="tpu_custom_call" | custom-call | flops 12582912 | bytes 8388608 | tf_op jit(solution)/shard_map/norm_quarters/pallas_call | solution.py:97
  17.4 1.5 %collective-permute-start.7 = (bf16[1,256,512]{2,1,0:T(8,128)(2,1)S(1)}, bf16[1,256,512]{2,1,0:T(8,128)(2,1)S(1)}, u32[]{:S(2)}, u32[]{:S(2)}) collective-permute-start(bf16[1,256,512]{2,1,0:T(8,128)(2,1)S(1)} %collective-permute-done.5.b_ref.refs_6_), channel_id=1, source_target_pairs={{0,16},{1,17},{2,18},{3,19},{4,20},{5,21},{6,22},{7,23},{8,24},{9,... | collective-permute-start | bytes 786440 | tf_op jit(solution)/shard_map/ppermute | solution.py:333
  18.9 10.5 %collective-permute-done.2.refs_8_ = bf16[1024,256]{1,0:T(8,128)(2,1)S(1)} collective-permute-done((bf16[1024,256]{1,0:T(8,128)(2,1)}, bf16[1024,256]{1,0:T(8,128)(2,1)S(1)}, u32[]{:S(2)}, u32[]{:S(2)}) %collective-permute-start.2) | collective-permute-done | bytes 524320 | tf_op jit(solution)/shard_map/ppermute | solution.py:333
  29.7 1.6 %collective-permute-start.9 = (bf16[1024,256]{1,0:T(8,128)(2,1)S(1)}, bf16[1024,256]{1,0:T(8,128)(2,1)S(1)}, u32[]{:S(2)}, u32[]{:S(2)}) collective-permute-start(bf16[1024,256]{1,0:T(8,128)(2,1)S(1)} %collective-permute-done.2.refs_8_), channel_id=1, source_target_pairs={{0,16},{1,17},{2,18},{3,19},{4,20},{5,21},{6,22},{7,23},{8,24},{9,... | collective-permute-start | bytes 1572872 | tf_op jit(solution)/shard_map/ppermute | solution.py:333
  33.5 2.4 %collective-permute-start.11 = (bf16[1,256,1024]{2,1,0:T(8,128)(2,1)S(1)}, bf16[1,256,1024]{2,1,0:T(8,128)(2,1)}, u32[]{:S(2)}, u32[]{:S(2)}) collective-permute-start(bf16[1,256,1024]{2,1,0:T(8,128)(2,1)S(1)} %bitcast.6), channel_id=1, source_target_pairs={{0,8},{1,9},{2,10},{3,11},{4,12},{5,13},{6,14},{7,15},{8,0},{9,1},... | collective-permute-start | bytes 1572872 | tf_op jit(solution)/shard_map/ppermute | solution.py:333
  35.8 8.8 %collective-permute-done.9.refs_9_ = bf16[1024,256]{1,0:T(8,128)(2,1)S(1)} collective-permute-done((bf16[1024,256]{1,0:T(8,128)(2,1)S(1)}, bf16[1024,256]{1,0:T(8,128)(2,1)S(1)}, u32[]{:S(2)}, u32[]{:S(2)}) %collective-permute-start.9) | collective-permute-done | bytes 524320 | tf_op jit(solution)/shard_map/ppermute | solution.py:333
  44.6 9.2 %collective-permute-done.8.refs_7_ = bf16[1024,256]{1,0:T(8,128)(2,1)S(1)} collective-permute-done((bf16[1024,256]{1,0:T(8,128)(2,1)S(1)}, bf16[1024,256]{1,0:T(8,128)(2,1)S(1)}, u32[]{:S(2)}, u32[]{:S(2)}) %collective-permute-start.8) | collective-permute-done | bytes 524320 | tf_op jit(solution)/shard_map/ppermute | solution.py:333
  53.9 1.5 %collective-permute-done.6.refs_10_ = bf16[1024,256]{1,0:T(8,128)(2,1)S(1)} collective-permute-done((bf16[1024,256]{1,0:T(8,128)(2,1)S(1)}, bf16[1024,256]{1,0:T(8,128)(2,1)S(1)}, u32[]{:S(2)}, u32[]{:S(2)}) %collective-permute-start.6) | collective-permute-done | bytes 524320 | tf_op jit(solution)/shard_map/ppermute | solution.py:333
  56.4 2.4 %collective-permute-done.11.refs_8_ = bf16[1,256,1024]{2,1,0:T(8,128)(2,1)} collective-permute-done((bf16[1,256,1024]{2,1,0:T(8,128)(2,1)S(1)}, bf16[1,256,1024]{2,1,0:T(8,128)(2,1)}, u32[]{:S(2)}, u32[]{:S(2)}) %collective-permute-start.11) | collective-permute-done | bytes 524320 | tf_op jit(solution)/shard_map/ppermute | solution.py:333
  59.6 1.8 %collective-permute-done.14.refs_10_ = bf16[1,256,512]{2,1,0:T(8,128)(2,1)S(1)} collective-permute-done((bf16[1,256,512]{2,1,0:T(8,128)(2,1)S(1)}, bf16[1,256,512]{2,1,0:T(8,128)(2,1)S(1)}, u32[]{:S(2)}, u32[]{:S(2)}) %collective-permute-start.14) | collective-permute-done | bytes 262176 | tf_op jit(solution)/shard_map/ppermute | solution.py:333
  62.2 4.7 %collective-permute-done.10.refs_11_ = bf16[1024,256]{1,0:T(8,128)(2,1)S(1)} collective-permute-done((bf16[1024,256]{1,0:T(8,128)(2,1)S(1)}, bf16[1024,256]{1,0:T(8,128)(2,1)S(1)}, u32[]{:S(2)}, u32[]{:S(2)}) %collective-permute-start.10) | collective-permute-done | bytes 524320 | tf_op jit(solution)/shard_map/ppermute | solution.py:333
  66.9 3.5 %collective-permute-done.12.refs_12_ = bf16[2,256,512]{2,1,0:T(8,128)(2,1)} collective-permute-done((bf16[2,256,512]{2,1,0:T(8,128)(2,1)S(1)}, bf16[2,256,512]{2,1,0:T(8,128)(2,1)}, u32[]{:S(2)}, u32[]{:S(2)}) %collective-permute-start.12) | collective-permute-done | bytes 524320 | tf_op jit(solution)/shard_map/ppermute | solution.py:333
  71.4 1.8 %collective-permute-start.22 = (bf16[1,256,1024]{2,1,0:T(8,128)(2,1)}, bf16[1,256,1024]{2,1,0:T(8,128)(2,1)S(1)}, u32[]{:S(2)}, u32[]{:S(2)}) collective-permute-start(bf16[1,256,1024]{2,1,0:T(8,128)(2,1)} %collective-permute-done.11.refs_8_), channel_id=1, source_target_pairs={{0,4},{1,5},{2,6},{3,7},{4,0},{5,1},{6,2},{7,3},{8,12},{9,13},{10,... | collective-permute-start | bytes 1572872 | tf_op jit(solution)/shard_map/ppermute | solution.py:333
  73.9 1.5 %collective-permute-start.21 = (bf16[1,256,1024]{2,1,0:T(8,128)(2,1)}, bf16[1,256,1024]{2,1,0:T(8,128)(2,1)}, u32[]{:S(2)}, u32[]{:S(2)}) collective-permute-start(bf16[1,256,1024]{2,1,0:T(8,128)(2,1)} %collective-permute-done.11.refs_8_), channel_id=1, source_target_pairs={{0,2},{1,3},{2,0},{3,1},{4,6},{5,7},{6,4},{7,5},{8,10},{9,11},{10,... | collective-permute-start | bytes 1572872 | tf_op jit(solution)/shard_map/ppermute | solution.py:333
  76.4 6.5 %partial_sums.1 = (f32[128,512]{1,0:T(8,128)}, f32[128,512]{1,0:T(8,128)}, bf16[128,512]{1,0:T(8,128)(2,1)}, bf16[128,512]{1,0:T(8,128)(2,1)}) custom-call(bf16[4,128,1024]{2,1,0:T(8,128)(2,1)} %get-tuple-element.35.refs_0_, bf16[4,128,1024]{2,1,0:T(8,128)(2,1)} %copy-done.2, bf16[8,128,1024]{2,1,0:T(8,128)(2,1)} %copy-done.1, ...), custom_call_target="tpu_custom_call" | custom-call | flops 2147483648 | bytes 8388608 | tf_op jit(solution)/shard_map/partial_sums/pallas_call | solution.py:176
  85.6 1.9 %collective-permute-done.20.refs_13_ = bf16[2,256,512]{2,1,0:T(8,128)(2,1)} collective-permute-done((bf16[2,256,512]{2,1,0:T(8,128)(2,1)}, bf16[2,256,512]{2,1,0:T(8,128)(2,1)}, u32[]{:S(2)}, u32[]{:S(2)}) %collective-permute-start.20) | collective-permute-done | bytes 524320 | tf_op jit(solution)/shard_map/ppermute | solution.py:333
  87.5 4.2 %collective-permute-done.18.refs_2_ = bf16[128,512]{1,0:T(8,128)(2,1)S(1)} collective-permute-done((bf16[128,512]{1,0:T(8,128)(2,1)}, bf16[128,512]{1,0:T(8,128)(2,1)S(1)}, u32[]{:S(2)}, u32[]{:S(2)}) %collective-permute-start.18) | collective-permute-done | bytes 131104 | tf_op jit(solution)/shard_map/ppermute | solution.py:333
  92.3 1.6 %collective-permute-start.28 = (bf16[1,256,512]{2,1,0:T(8,128)(2,1)S(1)}, bf16[1,256,512]{2,1,0:T(8,128)(2,1)S(1)}, u32[]{:S(2)}, u32[]{:S(2)}) collective-permute-start(bf16[1,256,512]{2,1,0:T(8,128)(2,1)S(1)} %slice.19), channel_id=1, source_target_pairs={{0,2},{1,3},{2,0},{3,1},{4,6},{5,7},{6,4},{7,5},{8,10},{9,11},{10,... | collective-permute-start | bytes 786440 | tf_op jit(solution)/shard_map/ppermute | solution.py:333
  95.8 4.9 %down_first.1 = (bf16[128,16384]{1,0:T(8,128)(2,1)}, bf16[128,256]{1,0:T(8,128)(2,1)}) custom-call(s32[1]{0:T(128)S(6)} %copy.10.live_ref, s32[16]{0:T(128)} %owner_ref.5, f32[128,512]{1,0:T(8,128)} %get-tuple-element.47.refs_0_, f32[128,512]{1,0:T(8,128)} %copy-done.22, bf16[128,512]{1,0:T(8,128)(2,1)} %copy-done.25, bf16[128,512]{1,0:T(8,128)(2,1)} %copy-done.26, ...), custom_call_target="tpu_custom_call" | custom-call | flops 6710886400 | bytes 7864320 | tf_op jit(solution)/shard_map/down_first/pallas_call | solution.py:274
  105.8 3.6 %down_second.1 = bf16[128,16384]{1,0:T(8,128)(2,1)} custom-call(s32[16]{0:T(128)} %owner_ref.5, bf16[128,256]{1,0:T(8,128)(2,1)} %get-tuple-element.55.hidden_ref, bf16[128,16384]{1,0:T(8,128)(2,1)} %get-tuple-element.56._, bf16[2,256,512]{2,1,0:T(8,128)(2,1)} %copy-done.14, bf16[2,256,512]{2,1,0:T(8,128)(2,1)} %copy-done.13, ...), custom_call_target="tpu_custom_call", output_to_operand_aliasing={{}: (2, {})} | custom-call | flops 4026531840 | bytes 4718592 | tf_op jit(solution)/shard_map/down_second/pallas_call | solution.py:274
  (102 shorter events, 19.9 us)
Async XLA Ops:
  1.9 27.5 %collective-permute-start.2 = (bf16[1024,256]{1,0:T(8,128)(2,1)}, bf16[1024,256]{1,0:T(8,128)(2,1)S(1)}, u32[]{:S(2)}, u32[]{:S(2)}) collective-permute-start(bf16[1024,256]{1,0:T(8,128)(2,1)} %broadcast_select_fusion), channel_id=1, source_target_pairs={{0,8},{1,9},{2,10},{3,11},{4,12},{5,13},{6,14},{7,15},{8,0},{9,1},... | collective-permute-start | bytes 1572872 | tf_op jit(solution)/shard_map/ppermute | solution.py:333
  6.0 23.7 %collective-permute-start.3 = (bf16[1024,256]{1,0:T(8,128)(2,1)}, bf16[1024,256]{1,0:T(8,128)(2,1)S(1)}, u32[]{:S(2)}, u32[]{:S(2)}) collective-permute-start(bf16[1024,256]{1,0:T(8,128)(2,1)} %broadcast_select_fusion), channel_id=1, source_target_pairs={{0,4},{1,5},{2,6},{3,7},{4,0},{5,1},{6,2},{7,3},{8,12},{9,13},{10,... | collective-permute-start | bytes 1572872 | tf_op jit(solution)/shard_map/ppermute | solution.py:333
  7.5 22.1 %collective-permute-start.4 = (bf16[1,256,1024]{2,1,0:T(8,128)(2,1)}, bf16[1,256,1024]{2,1,0:T(8,128)(2,1)}, u32[]{:S(2)}, u32[]{:S(2)}) collective-permute-start(bf16[1,256,1024]{2,1,0:T(8,128)(2,1)} %bitcast.4), channel_id=1, source_target_pairs={{0,1},{1,0},{2,3},{3,2},{4,5},{5,4},{6,7},{7,6},{8,9},{9,8},{10,11... | collective-permute-start | bytes 1572872 | tf_op jit(solution)/shard_map/ppermute | solution.py:333
  8.6 8.8 %collective-permute-start.5 = (bf16[1,256,512]{2,1,0:T(8,128)(2,1)S(1)}, bf16[1,256,512]{2,1,0:T(8,128)(2,1)S(1)}, u32[]{:S(2)}, u32[]{:S(2)}) collective-permute-start(bf16[1,256,512]{2,1,0:T(8,128)(2,1)S(1)} %select_bitcast_fusion.a_ref), channel_id=1, source_target_pairs={{0,2},{1,3},{2,0},{3,1},{4,6},{5,7},{6,4},{7,5},{8,10},{9,11},{10,... | collective-permute-start | bytes 786440 | tf_op jit(solution)/shard_map/ppermute | solution.py:333
  15.8 55.4 %collective-permute-start.1 = (bf16[8,128,1024]{2,1,0:T(8,128)(2,1)}, bf16[8,128,1024]{2,1,0:T(8,128)(2,1)S(1)}, u32[]{:S(2)}, u32[]{:S(2)}) collective-permute-start(bf16[8,128,1024]{2,1,0:T(8,128)(2,1)} %get-tuple-element.37), channel_id=1, source_target_pairs={{0,2},{1,3},{2,0},{3,1},{4,6},{5,7},{6,4},{7,5},{8,10},{9,11},{10,... | collective-permute-start | bytes 6291464 | tf_op jit(solution)/shard_map/ppermute | solution.py:333
  17.4 12.3 %collective-permute-start.7 = (bf16[1,256,512]{2,1,0:T(8,128)(2,1)S(1)}, bf16[1,256,512]{2,1,0:T(8,128)(2,1)S(1)}, u32[]{:S(2)}, u32[]{:S(2)}) collective-permute-start(bf16[1,256,512]{2,1,0:T(8,128)(2,1)S(1)} %collective-permute-done.5.b_ref.refs_6_), channel_id=1, source_target_pairs={{0,16},{1,17},{2,18},{3,19},{4,20},{5,21},{6,22},{7,23},{8,24},{9,... | collective-permute-start | bytes 786440 | tf_op jit(solution)/shard_map/ppermute | solution.py:333
  29.7 14.9 %collective-permute-start.9 = (bf16[1024,256]{1,0:T(8,128)(2,1)S(1)}, bf16[1024,256]{1,0:T(8,128)(2,1)S(1)}, u32[]{:S(2)}, u32[]{:S(2)}) collective-permute-start(bf16[1024,256]{1,0:T(8,128)(2,1)S(1)} %collective-permute-done.2.refs_8_), channel_id=1, source_target_pairs={{0,16},{1,17},{2,18},{3,19},{4,20},{5,21},{6,22},{7,23},{8,24},{9,... | collective-permute-start | bytes 1572872 | tf_op jit(solution)/shard_map/ppermute | solution.py:333
  31.3 22.5 %collective-permute-start.8 = (bf16[1024,256]{1,0:T(8,128)(2,1)S(1)}, bf16[1024,256]{1,0:T(8,128)(2,1)S(1)}, u32[]{:S(2)}, u32[]{:S(2)}) collective-permute-start(bf16[1024,256]{1,0:T(8,128)(2,1)S(1)} %collective-permute-done.3.refs_6_), channel_id=1, source_target_pairs={{0,16},{1,17},{2,18},{3,19},{4,20},{5,21},{6,22},{7,23},{8,24},{9,... | collective-permute-start | bytes 1572872 | tf_op jit(solution)/shard_map/ppermute | solution.py:333
  32.0 23.4 %collective-permute-start.6 = (bf16[1024,256]{1,0:T(8,128)(2,1)S(1)}, bf16[1024,256]{1,0:T(8,128)(2,1)S(1)}, u32[]{:S(2)}, u32[]{:S(2)}) collective-permute-start(bf16[1024,256]{1,0:T(8,128)(2,1)S(1)} %collective-permute-done.2.refs_8_), channel_id=1, source_target_pairs={{0,4},{1,5},{2,6},{3,7},{4,0},{5,1},{6,2},{7,3},{8,12},{9,13},{10,... | collective-permute-start | bytes 1572872 | tf_op jit(solution)/shard_map/ppermute | solution.py:333
  33.5 25.3 %collective-permute-start.11 = (bf16[1,256,1024]{2,1,0:T(8,128)(2,1)S(1)}, bf16[1,256,1024]{2,1,0:T(8,128)(2,1)}, u32[]{:S(2)}, u32[]{:S(2)}) collective-permute-start(bf16[1,256,1024]{2,1,0:T(8,128)(2,1)S(1)} %bitcast.6), channel_id=1, source_target_pairs={{0,8},{1,9},{2,10},{3,11},{4,12},{5,13},{6,14},{7,15},{8,0},{9,1},... | collective-permute-start | bytes 1572872 | tf_op jit(solution)/shard_map/ppermute | solution.py:333
  44.6 14.5 %collective-permute-start.13 = (bf16[1,256,512]{2,1,0:T(8,128)(2,1)S(1)}, bf16[1,256,512]{2,1,0:T(8,128)(2,1)S(1)}, u32[]{:S(2)}, u32[]{:S(2)}) collective-permute-start(bf16[1,256,512]{2,1,0:T(8,128)(2,1)S(1)} %collective-permute-done.5.b_ref.refs_6_), channel_id=1, source_target_pairs={{0,1},{1,0},{2,3},{3,2},{4,5},{5,4},{6,7},{7,6},{8,9},{9,8},{10,11... | collective-permute-start | bytes 786440 | tf_op jit(solution)/shard_map/ppermute | solution.py:333
  55.4 11.5 %collective-permute-start.10 = (bf16[1024,256]{1,0:T(8,128)(2,1)S(1)}, bf16[1024,256]{1,0:T(8,128)(2,1)S(1)}, u32[]{:S(2)}, u32[]{:S(2)}) collective-permute-start(bf16[1024,256]{1,0:T(8,128)(2,1)S(1)} %collective-permute-done.6.refs_10_), channel_id=1, source_target_pairs={{0,16},{1,17},{2,18},{3,19},{4,20},{5,21},{6,22},{7,23},{8,24},{9,... | collective-permute-start | bytes 1572872 | tf_op jit(solution)/shard_map/ppermute | solution.py:333
  58.8 11.6 %collective-permute-start.12 = (bf16[2,256,512]{2,1,0:T(8,128)(2,1)S(1)}, bf16[2,256,512]{2,1,0:T(8,128)(2,1)}, u32[]{:S(2)}, u32[]{:S(2)}) collective-permute-start(bf16[2,256,512]{2,1,0:T(8,128)(2,1)S(1)} %stack_halves.1), channel_id=1, source_target_pairs={{0,4},{1,5},{2,6},{3,7},{4,0},{5,1},{6,2},{7,3},{8,12},{9,13},{10,... | collective-permute-start | bytes 1572872 | tf_op jit(solution)/shard_map/ppermute | solution.py:333
  59.1 11.3 %collective-permute-start.15 = (bf16[1,256,1024]{2,1,0:T(8,128)(2,1)}, bf16[1,256,1024]{2,1,0:T(8,128)(2,1)S(1)}, u32[]{:S(2)}, u32[]{:S(2)}) collective-permute-start(bf16[1,256,1024]{2,1,0:T(8,128)(2,1)} %collective-permute-done.11.refs_8_), channel_id=1, source_target_pairs={{0,1},{1,0},{2,3},{3,2},{4,5},{5,4},{6,7},{7,6},{8,9},{9,8},{10,11... | collective-permute-start | bytes 1572872 | tf_op jit(solution)/shard_map/ppermute | solution.py:333
  62.1 13.3 %collective-permute-start = (bf16[4,128,1024]{2,1,0:T(8,128)(2,1)S(1)}, bf16[4,128,1024]{2,1,0:T(8,128)(2,1)S(1)}, u32[]{:S(2)}, u32[]{:S(2)}) collective-permute-start(bf16[4,128,1024]{2,1,0:T(8,128)(2,1)S(1)} %copy-done.11), channel_id=1, source_target_pairs={{0,1},{1,0},{2,3},{3,2},{4,5},{5,4},{6,7},{7,6},{8,9},{9,8},{10,11... | collective-permute-start | bytes 3145736 | tf_op jit(solution)/shard_map/ppermute | solution.py:333
  71.4 20.8 %collective-permute-start.22 = (bf16[1,256,1024]{2,1,0:T(8,128)(2,1)}, bf16[1,256,1024]{2,1,0:T(8,128)(2,1)S(1)}, u32[]{:S(2)}, u32[]{:S(2)}) collective-permute-start(bf16[1,256,1024]{2,1,0:T(8,128)(2,1)} %collective-permute-done.11.refs_8_), channel_id=1, source_target_pairs={{0,4},{1,5},{2,6},{3,7},{4,0},{5,1},{6,2},{7,3},{8,12},{9,13},{10,... | collective-permute-start | bytes 1572872 | tf_op jit(solution)/shard_map/ppermute | solution.py:333
  73.2 14.3 %collective-permute-start.20 = (bf16[2,256,512]{2,1,0:T(8,128)(2,1)}, bf16[2,256,512]{2,1,0:T(8,128)(2,1)}, u32[]{:S(2)}, u32[]{:S(2)}) collective-permute-start(bf16[2,256,512]{2,1,0:T(8,128)(2,1)} %collective-permute-done.12.refs_12_), channel_id=1, source_target_pairs={{0,16},{1,17},{2,18},{3,19},{4,20},{5,21},{6,22},{7,23},{8,24},{9,... | collective-permute-start | bytes 1572872 | tf_op jit(solution)/shard_map/ppermute | solution.py:333
  73.9 18.3 %collective-permute-start.21 = (bf16[1,256,1024]{2,1,0:T(8,128)(2,1)}, bf16[1,256,1024]{2,1,0:T(8,128)(2,1)}, u32[]{:S(2)}, u32[]{:S(2)}) collective-permute-start(bf16[1,256,1024]{2,1,0:T(8,128)(2,1)} %collective-permute-done.11.refs_8_), channel_id=1, source_target_pairs={{0,2},{1,3},{2,0},{3,1},{4,6},{5,7},{6,4},{7,5},{8,10},{9,11},{10,... | collective-permute-start | bytes 1572872 | tf_op jit(solution)/shard_map/ppermute | solution.py:333
  82.9 8.8 %collective-permute-start.18 = (bf16[128,512]{1,0:T(8,128)(2,1)}, bf16[128,512]{1,0:T(8,128)(2,1)S(1)}, u32[]{:S(2)}, u32[]{:S(2)}) collective-permute-start(bf16[128,512]{1,0:T(8,128)(2,1)} %get-tuple-element.49), channel_id=1, source_target_pairs={{0,2},{1,3},{2,0},{3,1},{4,6},{5,7},{6,4},{7,5},{8,10},{9,11},{10,... | collective-permute-start | bytes 393224 | tf_op jit(solution)/shard_map/ppermute | solution.py:333
  84.7 10.5 %collective-permute-start.19 = (bf16[128,512]{1,0:T(8,128)(2,1)}, bf16[128,512]{1,0:T(8,128)(2,1)S(1)}, u32[]{:S(2)}, u32[]{:S(2)}) collective-permute-start(bf16[128,512]{1,0:T(8,128)(2,1)} %get-tuple-element.51), channel_id=1, source_target_pairs={{0,3},{1,2},{2,1},{3,0},{4,7},{5,6},{6,5},{7,4},{8,11},{9,10},{10,... | collective-permute-start | bytes 393224 | tf_op jit(solution)/shard_map/ppermute | solution.py:333
  91.7 11.1 %collective-permute-start.24 = (bf16[2,256,512]{2,1,0:T(8,128)(2,1)}, bf16[2,256,512]{2,1,0:T(8,128)(2,1)S(1)}, u32[]{:S(2)}, u32[]{:S(2)}) collective-permute-start(bf16[2,256,512]{2,1,0:T(8,128)(2,1)} %collective-permute-done.20.refs_13_), channel_id=1, source_target_pairs={{0,1},{1,0},{2,3},{3,2},{4,5},{5,4},{6,7},{7,6},{8,9},{9,8},{10,11... | collective-permute-start | bytes 1572872 | tf_op jit(solution)/shard_map/ppermute | solution.py:333
  91.7 11.6 %collective-permute-start.23 = (bf16[2,256,512]{2,1,0:T(8,128)(2,1)}, bf16[2,256,512]{2,1,0:T(8,128)(2,1)S(1)}, u32[]{:S(2)}, u32[]{:S(2)}) collective-permute-start(bf16[2,256,512]{2,1,0:T(8,128)(2,1)} %collective-permute-done.12.refs_12_), channel_id=1, source_target_pairs={{0,1},{1,0},{2,3},{3,2},{4,5},{5,4},{6,7},{7,6},{8,9},{9,8},{10,11... | collective-permute-start | bytes 1572872 | tf_op jit(solution)/shard_map/ppermute | solution.py:333
  92.3 8.5 %collective-permute-start.28 = (bf16[1,256,512]{2,1,0:T(8,128)(2,1)S(1)}, bf16[1,256,512]{2,1,0:T(8,128)(2,1)S(1)}, u32[]{:S(2)}, u32[]{:S(2)}) collective-permute-start(bf16[1,256,512]{2,1,0:T(8,128)(2,1)S(1)} %slice.19), channel_id=1, source_target_pairs={{0,2},{1,3},{2,0},{3,1},{4,6},{5,7},{6,4},{7,5},{8,10},{9,11},{10,... | collective-permute-start | bytes 786440 | tf_op jit(solution)/shard_map/ppermute | solution.py:333
  94.8 8.0 %collective-permute-start.27 = (bf16[1,256,512]{2,1,0:T(8,128)(2,1)S(1)}, bf16[1,256,512]{2,1,0:T(8,128)(2,1)S(1)}, u32[]{:S(2)}, u32[]{:S(2)}) collective-permute-start(bf16[1,256,512]{2,1,0:T(8,128)(2,1)S(1)} %slice.18), channel_id=1, source_target_pairs={{0,4},{1,5},{2,6},{3,7},{4,0},{5,1},{6,2},{7,3},{8,12},{9,13},{10,... | collective-permute-start | bytes 786440 | tf_op jit(solution)/shard_map/ppermute | solution.py:333
  (34 other events, 280.4 us)

commit v8 on v7

--- a/solution.py
+++ b/solution.py
@@ -50,13 +50,12 @@
 
 
 def norm_kernel(owner_ref, tokens_ref, gain_ref, *rest):
-    (own, near, far), (held, made, scale_ref, in_sem, out_sem) = rest[:3], rest[3:]
+    outs, (held, made, scale_ref, in_sem, out_sem) = rest[:2], rest[2:]
     here = lax.axis_index("wide")
     rows, model_width = held.shape
     blocks = owner_ref.shape[0]
     width = model_width // blocks
     step = rows // in_sem.shape[0]
-    outs = (own, near, far, far.at[blocks // 4 :])
     copies = [
         pltpu.make_async_copy(
             tokens_ref.at[r : r + step], held.at[r : r + step], in_sem.at[r // step]
@@ -82,23 +81,24 @@
         stored = owner_ref[p]
         for turn, out in enumerate(outs):
 
-            @pl.when(((stored ^ here) & 3) == turn)
+            @pl.when(((stored ^ here) & 2) == 2 * turn)
             def _(out=out, p=p, stored=stored):
-                pltpu.make_async_copy(made.at[p], out.at[stored >> 2], out_sem.at[p]).start()
+                place = (stored >> 2) * 2 + (stored & 1)
+                pltpu.make_async_copy(made.at[p], out.at[place], out_sem.at[p]).start()
 
     for p in range(blocks):
         pltpu.make_async_copy(made.at[p], outs[0].at[0], out_sem.at[p]).wait()
 
 
-def normed_quarters(tokens, gain, owner_rows):
+def normed_halves(tokens, gain, owner_rows):
     rows, model_width = tokens.shape
     blocks = owner_rows.shape[0]
     width = model_width // blocks
     return pl.pallas_call(
         norm_kernel,
         in_specs=[SMEM, HBM, VMEM],
-        out_specs=[HBM] * 3,
-        out_shape=[pltpu.HBM((n * blocks // 4, rows, width), BF16) for n in (1, 1, 2)],
+        out_specs=[HBM] * 2,
+        out_shape=[pltpu.HBM((blocks // 2, rows, width), BF16)] * 2,
         scratch_shapes=[
             pltpu.VMEM((rows, model_width), BF16),
             pltpu.VMEM((blocks, rows, width), BF16),
@@ -110,7 +110,7 @@
         cost_estimate=pl.CostEstimate(
             flops=6 * rows * model_width, bytes_accessed=4 * rows * model_width, transcendentals=0
         ),
-        name="norm_quarters",
+        name="norm_halves",
     )(owner_rows, tokens, gain.reshape(1, model_width))
 
 
@@ -121,48 +121,50 @@
     return copies
 
 
-def partial_kernel(given, kinds, *refs):
+def partial_kernel(kinds, *refs):
     count = len(kinds)
     made, (rows, held, mine, other, row_sem, sem, out_sem) = refs[-7 - count : -7], refs[-7:]
     outs = refs[-7 - 2 * count : -7 - count]
-    inputs, weights = refs[:given], refs[given : -7 - 2 * count]
-    z, plane = lax.axis_index("wide") >> 2, lax.axis_index("groups")
+    inputs, weights = refs[:count], refs[count : -7 - 2 * count]
+    here, first = lax.axis_index("wide"), lax.axis_index("groups") == 0
+    z, core = here >> 2, here & 1
     size = inputs[0].shape[1]
     hid = held.shape[2]
-    hops = len(weights) // 2
-    parts = [ref.at[: rows.shape[0]] for ref in inputs]
+    hops = len(weights) // 4
     row_copies = fetch(
-        [(part, rows.at[:, k * size : (k + 1) * size]) for k, part in enumerate(parts)], row_sem
-    )
-    copies = fetch([(ref, held.at[i]) for i, ref in enumerate(weights)], sem)
+        [(ref, rows.at[:, k * size : (k + 1) * size]) for k, ref in enumerate(inputs)], row_sem
+    )
+    order = [(turn * hops + hop) * 2 + side for hop in range(hops) for turn in range(2) for side in range(2)]
+    copies = dict(zip(order, fetch([(weights[i], held.at[i]) for i in order], sem)))
     for copy in row_copies:
         copy.wait()
-    first = plane == 0
+
+    def summed(total, places, side, turns):
+        for hop in turns:
+            for turn in range(2):
+                total += jnp.dot(
+                    rows[(z ^ hop) * 2 + (core ^ turn), places],
+                    held[(turn * hops + hop) * 2 + side],
+                    preferred_element_type=F32,
+                )
+        return total
+
     step = hops // 2
     for start in range(0, hops, step):
-        for i in range(2 * start, 2 * (start + step)):
+        for i in order[4 * start : 4 * (start + step)]:
             copies[i].wait()
         sent = []
         for k, (out, kind) in enumerate(zip(made, kinds)):
-            here = slice(k * size, (k + 1) * size)
-            sums = []
-            for side in range(2):
-                total = jnp.zeros((size, hid), F32) if start == 0 else (mine, other)[side][here]
-                for hop in range(max(start, 1), start + step):
-                    total += jnp.dot(
-                        rows[z ^ hop, here], held[2 * hop + side], preferred_element_type=F32
-                    )
-                sums.append(total)
+            places = slice(k * size, (k + 1) * size)
+            turns = range(max(start, 1), start + step)
             if start == 0:
-                (mine[here], other[here]) = sums
+                mine[places] = summed(jnp.zeros((size, hid), F32), places, 0, turns)
+                other[places] = summed(jnp.zeros((size, hid), F32), places, 1, turns)
             else:
-                a, b = sums
-                gate, up = (
-                    jnp.dot(rows[z, here], held[side], preferred_element_type=F32)
-                    for side in range(2)
-                )
-                out[:, :hid] = (gate + jnp.where(first, a, b)).astype(kind)
-                out[:, hid:] = (up + jnp.where(first, b, a)).astype(kind)
+                a = summed(mine[places], places, 0, turns)
+                b = summed(other[places], places, 1, turns)
+                out[:, :hid] = summed(jnp.where(first, a, b), places, 0, (0,)).astype(kind)
+                out[:, hid:] = summed(jnp.where(first, b, a), places, 1, (0,)).astype(kind)
                 sent.append(pltpu.make_async_copy(out, outs[k], out_sem.at[k]))
                 sent[-1].start()
     for copy in sent:
@@ -171,16 +173,16 @@
 
 def partial_sums(inputs, weights, kinds):
     count = len(kinds)
-    hops, rows, depth = inputs[0].shape
+    blocks, rows, depth = inputs[0].shape
     hid = weights[0].shape[1]
     return pl.pallas_call(
-        functools.partial(partial_kernel, len(inputs), kinds),
-        in_specs=[HBM] * (len(inputs) + len(weights)),
+        functools.partial(partial_kernel, kinds),
+        in_specs=[HBM] * (count + len(weights)),
         out_specs=[HBM] * count,
         out_shape=[pltpu.HBM((rows, 2 * hid), kind) for kind in kinds],
         scratch_shapes=[pltpu.VMEM((rows, 2 * hid), kind) for kind in kinds]
         + [
-            pltpu.VMEM((hops, count * rows, depth), BF16),
+            pltpu.VMEM((blocks, count * rows, depth), BF16),
             pltpu.VMEM((len(weights), depth, hid), BF16),
             pltpu.VMEM((count * rows, hid), F32),
             pltpu.VMEM((count * rows, hid), F32),
@@ -190,8 +192,8 @@
         ],
         compiler_params=pltpu.CompilerParams(vmem_limit_bytes=FULL),
         cost_estimate=pl.CostEstimate(
-            flops=4 * hops * count * rows * depth * hid,
-            bytes_accessed=2 * hops * depth * (count * rows + 2 * hid),
+            flops=4 * blocks * count * rows * depth * hid,
+            bytes_accessed=2 * blocks * depth * (count * rows + 2 * hid),
             transcendentals=0,
         ),
         name="partial_sums",
@@ -229,26 +231,24 @@
 
 def first_kernel(pieces, live_ref, owner_ref, *refs):
     count = len(pieces)
-    sums, weights, (out, hidden_ref) = refs[:4], refs[4 : 4 + count], refs[4 + count : 6 + count]
-    owner, *rest = refs[6 + count :]
-    sums_held, held = rest[:4], rest[4 : 4 + count]
-    sem, results, out_sem, places, hidden, hidden_sem = rest[4 + count :]
+    sums, weights, (out, hidden_ref) = refs[:2], refs[2 : 2 + count], refs[2 + count : 4 + count]
+    owner, *rest = refs[4 + count :]
+    sums_held, held = rest[:2], rest[2 : 2 + count]
+    sem, results, out_sem, places, hidden, hidden_sem = rest[2 + count :]
     first, *copies = fetch(
         list(zip((owner_ref, *sums, *weights), (owner, *sums_held, *held))), sem
     )
-    for copy in (first, *copies[:4]):
+    for copy in (first, *copies[:2]):
         copy.wait()
     hid = hidden.shape[1]
-    total = sums_held[0][...]
-    for part in sums_held[1:]:
-        total += part[...].astype(F32)
+    total = sums_held[0][...] + sums_held[1][...].astype(F32)
     gate, up = total[:, :hid], total[:, hid:]
     units = gate / (1.0 + jnp.exp(-gate)) * up
     rows = lax.broadcasted_iota(jnp.int32, units.shape, 0)
     hidden[...] = jnp.where(rows < MEM + live_ref[0], units, 0.0).astype(BF16)
     handed = pltpu.make_async_copy(hidden, hidden_ref, hidden_sem)
     handed.start()
-    multiply_out(hidden[...], copies[4:], pieces, owner, out, held, results, out_sem, places)
+    multiply_out(hidden[...], copies[2:], pieces, owner, out, held, results, out_sem, places)
     handed.wait()
 
 
@@ -322,7 +322,6 @@
     half = model_width // owners // 2
     group, here = lax.axis_index("groups"), lax.axis_index("wide")
     core, across, near, far, other = (0, 1), (0, 2), (0, 4), (0, 8), (1, 0)
-    both = (0, 3)
 
     def swap(value, way):
         pairs = [
@@ -340,9 +339,8 @@
     a2 = swap(a0, far)
     mine_x = swap(mine, across)
 
-    t0, t1, t2 = normed_quarters(tokens, norm_gain, owner_rows)
+    t0, t2 = normed_halves(tokens, norm_gain, owner_rows)
     r2 = swap(t2, across)
-    r1 = swap(t1, core)
     rest_x = swap(after(mine_x, t2), other)
 
     def cross(weights, parts):
@@ -350,8 +348,9 @@
 
     own = [(down_weight[None], ((0, 0),))]
     own = own + [cross(*w) for w in own]
+    gate_c, up_c = swap(gate_weight, core), swap(up_weight, core)
     d0 = stacked(
-        after(mine, a1, a2, t2, own[1][0]), mine_x, 10**11
+        after(mine, a1, a2, t2, gate_c), mine_x, 10**11
     )
 
     b1 = swap(after(a1, d0, rest_x), other)
@@ -368,17 +367,13 @@
 
     second = [(mine_x, ((2, 0),)), (rest_x, ((2, 1),)), (d2, ((8, 0),))]
     second = second + [cross(*w) for w in second]
-    r3 = swap(after(r2, b3, d1, *(w for w, _ in second))[owners // 4 :], core)
     weights = (gate_weight, up_weight, a1, b1, a2, b2, a3, b3)
-    p0, p1, p2, p3 = partial_sums(
-        (t0, r1, r2, r3), weights, (F32, F32, BF16, BF16)
-    )
-    q1 = swap(p1, core)
+    weights = weights + (gate_c, up_c) + tuple(swap(w, core) for w in weights[2:])
+    p0, p2 = partial_sums((t0, r2), weights, (F32, BF16))
     q2 = swap(p2, across)
-    q3 = swap(after(p3, q1), both)
-
-    f3 = swap(after(f2, d3, q1)[:, :, :half], near)
-    g3 = swap(after(d3, f2, q1)[:, :, half:], across)
+
+    f3 = swap(after(f2, d3, p2)[:, :, :half], near)
+    g3 = swap(after(d3, f2, p2)[:, :, half:], across)
 
     third = [
         (d1, ((4, 0), (6, 0))),
@@ -390,7 +385,7 @@
     out = pltpu.HBM(tokens.shape, BF16)
     rows, hid = tokens.shape[0], gate_weight.shape[1]
     product, hidden = down_call(
-        first_kernel, "down_first", [seg_counts], [owner_rows, p0, q1, q2, q3], [], early,
+        first_kernel, "down_first", [seg_counts], [owner_rows, p0, q2], [], early,
         [out, pltpu.HBM((rows, hid), BF16)], [pltpu.SemaphoreType.DMA], {},
     )
     late = [(after(f3, hidden), ((14, 2),)), (after(g3, hidden), ((14, 3),))]

time: 110 us -> 110 us (level)
  local copies, waits for them, and re-layouts: 5.25 us -> 3.08 us
  Pallas kernels: 20.7 us -> 22 us
    unnamed x54 -> x56, local copies, waits for them, and re-layouts: 4.19 us -> 1.15 us
    pallas_call x2, Pallas kernels: 12.1 us -> 13.5 us  [the longest x1 7.8 us: partial_sums(): pl.pallas_call(functools.partial(partial_kernel, kinds), in_specs=[HBM] *...]
    ppermute x31 -> x35, starting transfers between devices: 25.9 us -> 26.4 us  [swap(): return lax.ppermute(value, ALL, pairs)]
    ppermute x31 -> x35, waiting for transfers between devices: 53.7 us -> 54 us  [swap(): return lax.ppermute(value, ALL, pairs)]
  transfers between devices with their start and end apart: 31 -> 35, of which waited for: 16 -> 15; matrix products, arithmetic and copies ran while one was open for 2% -> 3% of each run, Pallas kernels for 16% -> 17%
where the time goes in v8:
time: 110 us; the launch traced here: 109 us
  waiting for transfers between devices  54 us (49%)
  starting transfers between devices  26.4 us (24%)
  Pallas kernels  22 us (20%)
  local copies, waits for them, and re-layouts  3.08 us (3%)
  other arithmetic  2.94 us (3%)
    ppermute x35, waiting for transfers between devices, swap(): return lax.ppermute(value, ALL, pairs)  54 us
    ppermute x35, starting transfers between devices, swap(): return lax.ppermute(value, ALL, pairs)  26.4 us
    pallas_call x2, Pallas kernels, down_call(): pl.pallas_call(functools.partial(kernel, pieces), in_specs=[SMEM] * len(l...  8.45 us
    pallas_call x1, Pallas kernels, partial_sums(): pl.pallas_call(functools.partial(partial_kernel, kinds), in_specs=[HBM] *...  7.8 us
    pallas_call x1, Pallas kernels, normed_halves(): pl.pallas_call(norm_kernel, in_specs=[SMEM, HBM, VMEM], out_specs=[HBM] *...  5.67 us
  transfers between devices with their start and end apart: 35, of which 15 were waited for; matrix products, arithmetic and copies ran while one was open for 3% of the time, Pallas kernels for 17%

profile of v8, /device:TPU:0, one launch (start us, length us, event | category | flops | bytes accessed | tf_op | source)
XLA Modules:
  0.0 109.4 jit_solution(16973024392319086471)
XLA Ops:
  0.0 1.9 %broadcast_select_fusion = bf16[1024,256]{1,0:T(8,128)(2,1)} fusion(bf16[1024,256]{1,0:T(8,128)(2,1)} %refs_2_.1, bf16[1024,256]{1,0:T(8,128)(2,1)} %refs_3_.1, pred[]{:T(512)S(6)} %eq.3), kind=kLoop, calls=%fused_computation | loop fusion | flops 262144 | bytes 1572865 | tf_op jit(solution)/shard_map/jit(_where)/select_n | solution.py:335
  1.9 3.0 %collective-permute-start.1 = (bf16[1024,256]{1,0:T(8,128)(2,1)}, bf16[1024,256]{1,0:T(8,128)(2,1)S(1)}, u32[]{:S(2)}, u32[]{:S(2)}) collective-permute-start(bf16[1024,256]{1,0:T(8,128)(2,1)} %broadcast_select_fusion), channel_id=1, source_target_pairs={{0,4},{1,5},{2,6},{3,7},{4,0},{5,1},{6,2},{7,3},{8,12},{9,13},{10,... | collective-permute-start | bytes 1572872 | tf_op jit(solution)/shard_map/ppermute | solution.py:332
  4.9 2.6 %collective-permute-start.2 = (bf16[1024,256]{1,0:T(8,128)(2,1)}, bf16[1024,256]{1,0:T(8,128)(2,1)}, u32[]{:S(2)}, u32[]{:S(2)}) collective-permute-start(bf16[1024,256]{1,0:T(8,128)(2,1)} %broadcast_select_fusion), channel_id=1, source_target_pairs={{0,8},{1,9},{2,10},{3,11},{4,12},{5,13},{6,14},{7,15},{8,0},{9,1},... | collective-permute-start | bytes 1572872 | tf_op jit(solution)/shard_map/ppermute | solution.py:332
  8.6 1.6 %collective-permute-start.4 = (bf16[1,256,512]{2,1,0:T(8,128)(2,1)S(1)}, bf16[1,256,512]{2,1,0:T(8,128)(2,1)S(1)}, u32[]{:S(2)}, u32[]{:S(2)}) collective-permute-start(bf16[1,256,512]{2,1,0:T(8,128)(2,1)S(1)} %select_bitcast_fusion.a_ref), channel_id=1, source_target_pairs={{0,2},{1,3},{2,0},{3,1},{4,6},{5,7},{6,4},{7,5},{8,10},{9,11},{10,... | collective-permute-start | bytes 786440 | tf_op jit(solution)/shard_map/ppermute | solution.py:332
  10.1 5.7 %norm_halves.1 = (bf16[8,128,1024]{2,1,0:T(8,128)(2,1)}, bf16[8,128,1024]{2,1,0:T(8,128)(2,1)}) custom-call(s32[16]{0:T(128)} %owner_ref.5, bf16[128,16384]{1,0:T(8,128)(2,1)} %tokens_ref.1, f32[1,16384]{1,0:T(1,128)} %bitcast.4), custom_call_target="tpu_custom_call" | custom-call | flops 12582912 | bytes 8388608 | tf_op jit(solution)/shard_map/norm_halves/pallas_call | solution.py:97
  17.3 1.5 %collective-permute-start.5 = (bf16[1,256,512]{2,1,0:T(8,128)(2,1)S(1)}, bf16[1,256,512]{2,1,0:T(8,128)(2,1)S(1)}, u32[]{:S(2)}, u32[]{:S(2)}) collective-permute-start(bf16[1,256,512]{2,1,0:T(8,128)(2,1)S(1)} %collective-permute-done.4.b_ref.refs_4_), channel_id=1, source_target_pairs={{0,16},{1,17},{2,18},{3,19},{4,20},{5,21},{6,22},{7,23},{8,24},{9,... | collective-permute-start | bytes 786440 | tf_op jit(solution)/shard_map/ppermute | solution.py:332
  18.9 9.3 %collective-permute-done.1.refs_4_ = bf16[1024,256]{1,0:T(8,128)(2,1)S(1)} collective-permute-done((bf16[1024,256]{1,0:T(8,128)(2,1)}, bf16[1024,256]{1,0:T(8,128)(2,1)S(1)}, u32[]{:S(2)}, u32[]{:S(2)}) %collective-permute-start.1) | collective-permute-done | bytes 524320 | tf_op jit(solution)/shard_map/ppermute | solution.py:332
  28.1 2.7 %collective-permute-done.2.refs_6_ = bf16[1024,256]{1,0:T(8,128)(2,1)} collective-permute-done((bf16[1024,256]{1,0:T(8,128)(2,1)}, bf16[1024,256]{1,0:T(8,128)(2,1)}, u32[]{:S(2)}, u32[]{:S(2)}) %collective-permute-start.2) | collective-permute-done | bytes 524320 | tf_op jit(solution)/shard_map/ppermute | solution.py:332
  30.9 1.6 %collective-permute-start.6 = (bf16[1024,256]{1,0:T(8,128)(2,1)S(1)}, bf16[1024,256]{1,0:T(8,128)(2,1)S(1)}, u32[]{:S(2)}, u32[]{:S(2)}) collective-permute-start(bf16[1024,256]{1,0:T(8,128)(2,1)S(1)} %collective-permute-done.1.refs_4_), channel_id=1, source_target_pairs={{0,16},{1,17},{2,18},{3,19},{4,20},{5,21},{6,22},{7,23},{8,24},{9,... | collective-permute-start | bytes 1572872 | tf_op jit(solution)/shard_map/ppermute | solution.py:332
  33.4 2.6 %collective-permute-start.19 = (bf16[1,256,1024]{2,1,0:T(8,128)(2,1)}, bf16[1,256,1024]{2,1,0:T(8,128)(2,1)S(1)}, u32[]{:S(2)}, u32[]{:S(2)}) collective-permute-start(bf16[1,256,1024]{2,1,0:T(8,128)(2,1)} %bitcast.2.refs_2_), channel_id=1, source_target_pairs={{0,8},{1,9},{2,10},{3,11},{4,12},{5,13},{6,14},{7,15},{8,0},{9,1},... | collective-permute-start | bytes 1572872 | tf_op jit(solution)/shard_map/ppermute | solution.py:332
  36.0 9.8 %collective-permute-done.6.refs_5_ = bf16[1024,256]{1,0:T(8,128)(2,1)S(1)} collective-permute-done((bf16[1024,256]{1,0:T(8,128)(2,1)S(1)}, bf16[1024,256]{1,0:T(8,128)(2,1)S(1)}, u32[]{:S(2)}, u32[]{:S(2)}) %collective-permute-start.6) | collective-permute-done | bytes 524320 | tf_op jit(solution)/shard_map/ppermute | solution.py:332
  45.8 6.9 %collective-permute-done.7.refs_7_ = bf16[1024,256]{1,0:T(8,128)(2,1)S(1)} collective-permute-done((bf16[1024,256]{1,0:T(8,128)(2,1)}, bf16[1024,256]{1,0:T(8,128)(2,1)S(1)}, u32[]{:S(2)}, u32[]{:S(2)}) %collective-permute-start.7) | collective-permute-done | bytes 524320 | tf_op jit(solution)/shard_map/ppermute | solution.py:332
  54.1 3.6 %collective-permute-done.19.refs_6_ = bf16[1,256,1024]{2,1,0:T(8,128)(2,1)S(1)} collective-permute-done((bf16[1,256,1024]{2,1,0:T(8,128)(2,1)}, bf16[1,256,1024]{2,1,0:T(8,128)(2,1)S(1)}, u32[]{:S(2)}, u32[]{:S(2)}) %collective-permute-start.19) | collective-permute-done | bytes 524320 | tf_op jit(solution)/shard_map/ppermute | solution.py:332
  57.7 1.5 %collective-permute-start.9 = (bf16[1024,256]{1,0:T(8,128)(2,1)S(1)}, bf16[1024,256]{1,0:T(8,128)(2,1)S(1)}, u32[]{:S(2)}, u32[]{:S(2)}) collective-permute-start(bf16[1024,256]{1,0:T(8,128)(2,1)S(1)} %collective-permute-done.8.refs_8_), channel_id=1, source_target_pairs={{0,16},{1,17},{2,18},{3,19},{4,20},{5,21},{6,22},{7,23},{8,24},{9,... | collective-permute-start | bytes 1572872 | tf_op jit(solution)/shard_map/ppermute | solution.py:332
  59.8 8.6 %collective-permute-done.9.refs_9_ = bf16[1024,256]{1,0:T(8,128)(2,1)S(1)} collective-permute-done((bf16[1024,256]{1,0:T(8,128)(2,1)S(1)}, bf16[1024,256]{1,0:T(8,128)(2,1)S(1)}, u32[]{:S(2)}, u32[]{:S(2)}) %collective-permute-start.9) | collective-permute-done | bytes 524320 | tf_op jit(solution)/shard_map/ppermute | solution.py:332
  72.6 1.6 %collective-permute-start.25 = (bf16[1,256,1024]{2,1,0:T(8,128)(2,1)S(1)}, bf16[1,256,1024]{2,1,0:T(8,128)(2,1)}, u32[]{:S(2)}, u32[]{:S(2)}) collective-permute-start(bf16[1,256,1024]{2,1,0:T(8,128)(2,1)S(1)} %collective-permute-done.19.refs_6_), channel_id=1, source_target_pairs={{0,2},{1,3},{2,0},{3,1},{4,6},{5,7},{6,4},{7,5},{8,10},{9,11},{10,... | collective-permute-start | bytes 1572872 | tf_op jit(solution)/shard_map/ppermute | solution.py:332
  74.2 7.8 %partial_sums.1 = (f32[128,512]{1,0:T(8,128)}, bf16[128,512]{1,0:T(8,128)(2,1)}) custom-call(bf16[8,128,1024]{2,1,0:T(8,128)(2,1)} %get-tuple-element.30.refs_0_, bf16[8,128,1024]{2,1,0:T(8,128)(2,1)} %copy-done.2, bf16[1024,256]{1,0:T(8,128)(2,1)} %refs_2_.1, bf16[1024,256]{1,0:T(8,128)(2,1)} %refs_3_.1, bf16[1024,256]{1,0:T(8,128)(2,1)} %copy-done.3, ...), custom_call_target="tpu_custom_call" | custom-call | flops 2147483648 | bytes 12582912 | tf_op jit(solution)/shard_map/partial_sums/pallas_call | solution.py:178
  82.0 2.4 %collective-permute-done.24.refs_11_ = bf16[2,256,512]{2,1,0:T(8,128)(2,1)} collective-permute-done((bf16[2,256,512]{2,1,0:T(8,128)(2,1)}, bf16[2,256,512]{2,1,0:T(8,128)(2,1)}, u32[]{:S(2)}, u32[]{:S(2)}) %collective-permute-start.24) | collective-permute-done | bytes 524320 | tf_op jit(solution)/shard_map/ppermute | solution.py:332
  84.4 1.5 %collective-permute-start.17 = (bf16[128,512]{1,0:T(8,128)(2,1)}, bf16[128,512]{1,0:T(8,128)(2,1)S(1)}, u32[]{:S(2)}, u32[]{:S(2)}) collective-permute-start(bf16[128,512]{1,0:T(8,128)(2,1)} %get-tuple-element.39), channel_id=1, source_target_pairs={{0,2},{1,3},{2,0},{3,1},{4,6},{5,7},{6,4},{7,5},{8,10},{9,11},{10,... | collective-permute-start | bytes 393224 | tf_op jit(solution)/shard_map/ppermute | solution.py:332
  85.9 3.8 %collective-permute-done.17.refs_1_ = bf16[128,512]{1,0:T(8,128)(2,1)S(1)} collective-permute-done((bf16[128,512]{1,0:T(8,128)(2,1)}, bf16[128,512]{1,0:T(8,128)(2,1)S(1)}, u32[]{:S(2)}, u32[]{:S(2)}) %collective-permute-start.17) | collective-permute-done | bytes 131104 | tf_op jit(solution)/shard_map/ppermute | solution.py:332
  93.0 1.4 %collective-permute-start.31 = (bf16[1,256,512]{2,1,0:T(8,128)(2,1)S(1)}, bf16[1,256,512]{2,1,0:T(8,128)(2,1)S(1)}, u32[]{:S(2)}, u32[]{:S(2)}) collective-permute-start(bf16[1,256,512]{2,1,0:T(8,128)(2,1)S(1)} %slice.14), channel_id=1, source_target_pairs={{0,4},{1,5},{2,6},{3,7},{4,0},{5,1},{6,2},{7,3},{8,12},{9,13},{10,... | collective-permute-start | bytes 786440 | tf_op jit(solution)/shard_map/ppermute | solution.py:332
  94.4 1.5 %collective-permute-start.32 = (bf16[1,256,512]{2,1,0:T(8,128)(2,1)S(1)}, bf16[1,256,512]{2,1,0:T(8,128)(2,1)S(1)}, u32[]{:S(2)}, u32[]{:S(2)}) collective-permute-start(bf16[1,256,512]{2,1,0:T(8,128)(2,1)S(1)} %slice.15), channel_id=1, source_target_pairs={{0,2},{1,3},{2,0},{3,1},{4,6},{5,7},{6,4},{7,5},{8,10},{9,11},{10,... | collective-permute-start | bytes 786440 | tf_op jit(solution)/shard_map/ppermute | solution.py:332
  95.9 4.8 %down_first.1 = (bf16[128,16384]{1,0:T(8,128)(2,1)}, bf16[128,256]{1,0:T(8,128)(2,1)}) custom-call(s32[1]{0:T(128)S(6)} %copy.10.live_ref, s32[16]{0:T(128)} %owner_ref.5, f32[128,512]{1,0:T(8,128)} %get-tuple-element.38.refs_0_, bf16[128,512]{1,0:T(8,128)(2,1)} %copy-done.27, bf16[1,256,1024]{2,1,0:T(8,128)(2,1)} %bitcast.2.refs_2_, ...), custom_call_target="tpu_custom_call" | custom-call | flops 6710886400 | bytes 7864320 | tf_op jit(solution)/shard_map/down_first/pallas_call | solution.py:274
  105.8 3.6 %down_second.1 = bf16[128,16384]{1,0:T(8,128)(2,1)} custom-call(s32[16]{0:T(128)} %owner_ref.5, bf16[128,256]{1,0:T(8,128)(2,1)} %get-tuple-element.45.hidden_ref, bf16[128,16384]{1,0:T(8,128)(2,1)} %get-tuple-element.46._, bf16[2,256,512]{2,1,0:T(8,128)(2,1)} %copy-done.16, bf16[2,256,512]{2,1,0:T(8,128)(2,1)} %copy-done.17, ...), custom_call_target="tpu_custom_call", output_to_operand_aliasing={{}: (2, {})} | custom-call | flops 4026531840 | bytes 4718592 | tf_op jit(solution)/shard_map/down_second/pallas_call | solution.py:274
  (111 shorter events, 17.2 us)
Async XLA Ops:
  1.9 26.3 %collective-permute-start.1 = (bf16[1024,256]{1,0:T(8,128)(2,1)}, bf16[1024,256]{1,0:T(8,128)(2,1)S(1)}, u32[]{:S(2)}, u32[]{:S(2)}) collective-permute-start(bf16[1024,256]{1,0:T(8,128)(2,1)} %broadcast_select_fusion), channel_id=1, source_target_pairs={{0,4},{1,5},{2,6},{3,7},{4,0},{5,1},{6,2},{7,3},{8,12},{9,13},{10,... | collective-permute-start | bytes 1572872 | tf_op jit(solution)/shard_map/ppermute | solution.py:332
  4.9 25.9 %collective-permute-start.2 = (bf16[1024,256]{1,0:T(8,128)(2,1)}, bf16[1024,256]{1,0:T(8,128)(2,1)}, u32[]{:S(2)}, u32[]{:S(2)}) collective-permute-start(bf16[1024,256]{1,0:T(8,128)(2,1)} %broadcast_select_fusion), channel_id=1, source_target_pairs={{0,8},{1,9},{2,10},{3,11},{4,12},{5,13},{6,14},{7,15},{8,0},{9,1},... | collective-permute-start | bytes 1572872 | tf_op jit(solution)/shard_map/ppermute | solution.py:332
  7.5 23.3 %collective-permute-start.3 = (bf16[1024,256]{1,0:T(8,128)(2,1)}, bf16[1024,256]{1,0:T(8,128)(2,1)}, u32[]{:S(2)}, u32[]{:S(2)}) collective-permute-start(bf16[1024,256]{1,0:T(8,128)(2,1)} %refs_2_.1), channel_id=1, source_target_pairs={{0,1},{1,0},{2,3},{3,2},{4,5},{5,4},{6,7},{7,6},{8,9},{9,8},{10,11... | collective-permute-start | bytes 1572872 | tf_op jit(solution)/shard_map/ppermute | solution.py:332
  8.6 8.8 %collective-permute-start.4 = (bf16[1,256,512]{2,1,0:T(8,128)(2,1)S(1)}, bf16[1,256,512]{2,1,0:T(8,128)(2,1)S(1)}, u32[]{:S(2)}, u32[]{:S(2)}) collective-permute-start(bf16[1,256,512]{2,1,0:T(8,128)(2,1)S(1)} %select_bitcast_fusion.a_ref), channel_id=1, source_target_pairs={{0,2},{1,3},{2,0},{3,1},{4,6},{5,7},{6,4},{7,5},{8,10},{9,11},{10,... | collective-permute-start | bytes 786440 | tf_op jit(solution)/shard_map/ppermute | solution.py:332
  15.8 54.8 %collective-permute-start = (bf16[8,128,1024]{2,1,0:T(8,128)(2,1)}, bf16[8,128,1024]{2,1,0:T(8,128)(2,1)S(1)}, u32[]{:S(2)}, u32[]{:S(2)}) collective-permute-start(bf16[8,128,1024]{2,1,0:T(8,128)(2,1)} %get-tuple-element.31), channel_id=1, source_target_pairs={{0,2},{1,3},{2,0},{3,1},{4,6},{5,7},{6,4},{7,5},{8,10},{9,11},{10,... | collective-permute-start | bytes 6291464 | tf_op jit(solution)/shard_map/ppermute | solution.py:332
  17.3 13.5 %collective-permute-start.5 = (bf16[1,256,512]{2,1,0:T(8,128)(2,1)S(1)}, bf16[1,256,512]{2,1,0:T(8,128)(2,1)S(1)}, u32[]{:S(2)}, u32[]{:S(2)}) collective-permute-start(bf16[1,256,512]{2,1,0:T(8,128)(2,1)S(1)} %collective-permute-done.4.b_ref.refs_4_), channel_id=1, source_target_pairs={{0,16},{1,17},{2,18},{3,19},{4,20},{5,21},{6,22},{7,23},{8,24},{9,... | collective-permute-start | bytes 786440 | tf_op jit(solution)/shard_map/ppermute | solution.py:332
  30.9 14.9 %collective-permute-start.6 = (bf16[1024,256]{1,0:T(8,128)(2,1)S(1)}, bf16[1024,256]{1,0:T(8,128)(2,1)S(1)}, u32[]{:S(2)}, u32[]{:S(2)}) collective-permute-start(bf16[1024,256]{1,0:T(8,128)(2,1)S(1)} %collective-permute-done.1.refs_4_), channel_id=1, source_target_pairs={{0,16},{1,17},{2,18},{3,19},{4,20},{5,21},{6,22},{7,23},{8,24},{9,... | collective-permute-start | bytes 1572872 | tf_op jit(solution)/shard_map/ppermute | solution.py:332
  32.4 20.3 %collective-permute-start.7 = (bf16[1024,256]{1,0:T(8,128)(2,1)}, bf16[1024,256]{1,0:T(8,128)(2,1)S(1)}, u32[]{:S(2)}, u32[]{:S(2)}) collective-permute-start(bf16[1024,256]{1,0:T(8,128)(2,1)} %collective-permute-done.2.refs_6_), channel_id=1, source_target_pairs={{0,16},{1,17},{2,18},{3,19},{4,20},{5,21},{6,22},{7,23},{8,24},{9,... | collective-permute-start | bytes 1572872 | tf_op jit(solution)/shard_map/ppermute | solution.py:332
  33.0 21.1 %collective-permute-start.8 = (bf16[1024,256]{1,0:T(8,128)(2,1)}, bf16[1024,256]{1,0:T(8,128)(2,1)S(1)}, u32[]{:S(2)}, u32[]{:S(2)}) collective-permute-start(bf16[1024,256]{1,0:T(8,128)(2,1)} %collective-permute-done.2.refs_6_), channel_id=1, source_target_pairs={{0,4},{1,5},{2,6},{3,7},{4,0},{5,1},{6,2},{7,3},{8,12},{9,13},{10,... | collective-permute-start | bytes 1572872 | tf_op jit(solution)/shard_map/ppermute | solution.py:332
  33.4 24.3 %collective-permute-start.19 = (bf16[1,256,1024]{2,1,0:T(8,128)(2,1)}, bf16[1,256,1024]{2,1,0:T(8,128)(2,1)S(1)}, u32[]{:S(2)}, u32[]{:S(2)}) collective-permute-start(bf16[1,256,1024]{2,1,0:T(8,128)(2,1)} %bitcast.2.refs_2_), channel_id=1, source_target_pairs={{0,8},{1,9},{2,10},{3,11},{4,12},{5,13},{6,14},{7,15},{8,0},{9,1},... | collective-permute-start | bytes 1572872 | tf_op jit(solution)/shard_map/ppermute | solution.py:332
  45.8 13.4 %collective-permute-start.10 = (bf16[1024,256]{1,0:T(8,128)(2,1)S(1)}, bf16[1024,256]{1,0:T(8,128)(2,1)S(1)}, u32[]{:S(2)}, u32[]{:S(2)}) collective-permute-start(bf16[1024,256]{1,0:T(8,128)(2,1)S(1)} %copy-done.1), channel_id=1, source_target_pairs={{0,1},{1,0},{2,3},{3,2},{4,5},{5,4},{6,7},{7,6},{8,9},{9,8},{10,11... | collective-permute-start | bytes 1572872 | tf_op jit(solution)/shard_map/ppermute | solution.py:332
  57.7 10.7 %collective-permute-start.9 = (bf16[1024,256]{1,0:T(8,128)(2,1)S(1)}, bf16[1024,256]{1,0:T(8,128)(2,1)S(1)}, u32[]{:S(2)}, u32[]{:S(2)}) collective-permute-start(bf16[1024,256]{1,0:T(8,128)(2,1)S(1)} %collective-permute-done.8.refs_8_), channel_id=1, source_target_pairs={{0,16},{1,17},{2,18},{3,19},{4,20},{5,21},{6,22},{7,23},{8,24},{9,... | collective-permute-start | bytes 1572872 | tf_op jit(solution)/shard_map/ppermute | solution.py:332
  59.2 10.5 %collective-permute-start.23 = (bf16[2,256,512]{2,1,0:T(8,128)(2,1)S(1)}, bf16[2,256,512]{2,1,0:T(8,128)(2,1)}, u32[]{:S(2)}, u32[]{:S(2)}) collective-permute-start(bf16[2,256,512]{2,1,0:T(8,128)(2,1)S(1)} %stack_halves.1), channel_id=1, source_target_pairs={{0,4},{1,5},{2,6},{3,7},{4,0},{5,1},{6,2},{7,3},{8,12},{9,13},{10,... | collective-permute-start | bytes 1572872 | tf_op jit(solution)/shard_map/ppermute | solution.py:332
  59.3 10.5 %collective-permute-start.12 = (bf16[1024,256]{1,0:T(8,128)(2,1)S(1)}, bf16[1024,256]{1,0:T(8,128)(2,1)S(1)}, u32[]{:S(2)}, u32[]{:S(2)}) collective-permute-start(bf16[1024,256]{1,0:T(8,128)(2,1)S(1)} %collective-permute-done.6.refs_5_), channel_id=1, source_target_pairs={{0,1},{1,0},{2,3},{3,2},{4,5},{5,4},{6,7},{7,6},{8,9},{9,8},{10,11... | collective-permute-start | bytes 1572872 | tf_op jit(solution)/shard_map/ppermute | solution.py:332
  59.4 12.5 %collective-permute-start.14 = (bf16[1024,256]{1,0:T(8,128)(2,1)S(1)}, bf16[1024,256]{1,0:T(8,128)(2,1)S(1)}, u32[]{:S(2)}, u32[]{:S(2)}) collective-permute-start(bf16[1024,256]{1,0:T(8,128)(2,1)S(1)} %collective-permute-done.7.refs_7_), channel_id=1, source_target_pairs={{0,1},{1,0},{2,3},{3,2},{4,5},{5,4},{6,7},{7,6},{8,9},{9,8},{10,11... | collective-permute-start | bytes 1572872 | tf_op jit(solution)/shard_map/ppermute | solution.py:332
  69.8 14.7 %collective-permute-start.24 = (bf16[2,256,512]{2,1,0:T(8,128)(2,1)}, bf16[2,256,512]{2,1,0:T(8,128)(2,1)}, u32[]{:S(2)}, u32[]{:S(2)}) collective-permute-start(bf16[2,256,512]{2,1,0:T(8,128)(2,1)} %collective-permute-done.23.refs_10_), channel_id=1, source_target_pairs={{0,16},{1,17},{2,18},{3,19},{4,20},{5,21},{6,22},{7,23},{8,24},{9,... | collective-permute-start | bytes 1572872 | tf_op jit(solution)/shard_map/ppermute | solution.py:332
  70.6 15.3 %collective-permute-start.26 = (bf16[1,256,1024]{2,1,0:T(8,128)(2,1)S(1)}, bf16[1,256,1024]{2,1,0:T(8,128)(2,1)}, u32[]{:S(2)}, u32[]{:S(2)}) collective-permute-start(bf16[1,256,1024]{2,1,0:T(8,128)(2,1)S(1)} %collective-permute-done.19.refs_6_), channel_id=1, source_target_pairs={{0,4},{1,5},{2,6},{3,7},{4,0},{5,1},{6,2},{7,3},{8,12},{9,13},{10,... | collective-permute-start | bytes 1572872 | tf_op jit(solution)/shard_map/ppermute | solution.py:332
  71.9 21.0 %collective-permute-start.18 = (bf16[1,256,1024]{2,1,0:T(8,128)(2,1)}, bf16[1,256,1024]{2,1,0:T(8,128)(2,1)}, u32[]{:S(2)}, u32[]{:S(2)}) collective-permute-start(bf16[1,256,1024]{2,1,0:T(8,128)(2,1)} %bitcast.2.refs_2_), channel_id=1, source_target_pairs={{0,1},{1,0},{2,3},{3,2},{4,5},{5,4},{6,7},{7,6},{8,9},{9,8},{10,11... | collective-permute-start | bytes 1572872 | tf_op jit(solution)/shard_map/ppermute | solution.py:332
  72.0 23.9 %collective-permute-start.22 = (bf16[1,256,1024]{2,1,0:T(8,128)(2,1)S(1)}, bf16[1,256,1024]{2,1,0:T(8,128)(2,1)}, u32[]{:S(2)}, u32[]{:S(2)}) collective-permute-start(bf16[1,256,1024]{2,1,0:T(8,128)(2,1)S(1)} %collective-permute-done.19.refs_6_), channel_id=1, source_target_pairs={{0,1},{1,0},{2,3},{3,2},{4,5},{5,4},{6,7},{7,6},{8,9},{9,8},{10,11... | collective-permute-start | bytes 1572872 | tf_op jit(solution)/shard_map/ppermute | solution.py:332
  72.6 17.8 %collective-permute-start.25 = (bf16[1,256,1024]{2,1,0:T(8,128)(2,1)S(1)}, bf16[1,256,1024]{2,1,0:T(8,128)(2,1)}, u32[]{:S(2)}, u32[]{:S(2)}) collective-permute-start(bf16[1,256,1024]{2,1,0:T(8,128)(2,1)S(1)} %collective-permute-done.19.refs_6_), channel_id=1, source_target_pairs={{0,2},{1,3},{2,0},{3,1},{4,6},{5,7},{6,4},{7,5},{8,10},{9,11},{10,... | collective-permute-start | bytes 1572872 | tf_op jit(solution)/shard_map/ppermute | solution.py:332
  90.3 12.4 %collective-permute-start.27 = (bf16[2,256,512]{2,1,0:T(8,128)(2,1)}, bf16[2,256,512]{2,1,0:T(8,128)(2,1)S(1)}, u32[]{:S(2)}, u32[]{:S(2)}) collective-permute-start(bf16[2,256,512]{2,1,0:T(8,128)(2,1)} %collective-permute-done.23.refs_10_), channel_id=1, source_target_pairs={{0,1},{1,0},{2,3},{3,2},{4,5},{5,4},{6,7},{7,6},{8,9},{9,8},{10,11... | collective-permute-start | bytes 1572872 | tf_op jit(solution)/shard_map/ppermute | solution.py:332
  92.9 10.4 %collective-permute-start.28 = (bf16[2,256,512]{2,1,0:T(8,128)(2,1)}, bf16[2,256,512]{2,1,0:T(8,128)(2,1)S(1)}, u32[]{:S(2)}, u32[]{:S(2)}) collective-permute-start(bf16[2,256,512]{2,1,0:T(8,128)(2,1)} %collective-permute-done.24.refs_11_), channel_id=1, source_target_pairs={{0,1},{1,0},{2,3},{3,2},{4,5},{5,4},{6,7},{7,6},{8,9},{9,8},{10,11... | collective-permute-start | bytes 1572872 | tf_op jit(solution)/shard_map/ppermute | solution.py:332
  93.0 8.7 %collective-permute-start.31 = (bf16[1,256,512]{2,1,0:T(8,128)(2,1)S(1)}, bf16[1,256,512]{2,1,0:T(8,128)(2,1)S(1)}, u32[]{:S(2)}, u32[]{:S(2)}) collective-permute-start(bf16[1,256,512]{2,1,0:T(8,128)(2,1)S(1)} %slice.14), channel_id=1, source_target_pairs={{0,4},{1,5},{2,6},{3,7},{4,0},{5,1},{6,2},{7,3},{8,12},{9,13},{10,... | collective-permute-start | bytes 786440 | tf_op jit(solution)/shard_map/ppermute | solution.py:332
  94.4 8.4 %collective-permute-start.32 = (bf16[1,256,512]{2,1,0:T(8,128)(2,1)S(1)}, bf16[1,256,512]{2,1,0:T(8,128)(2,1)S(1)}, u32[]{:S(2)}, u32[]{:S(2)}) collective-permute-start(bf16[1,256,512]{2,1,0:T(8,128)(2,1)S(1)} %slice.15), channel_id=1, source_target_pairs={{0,2},{1,3},{2,0},{3,1},{4,6},{5,7},{6,4},{7,5},{8,10},{9,11},{10,... | collective-permute-start | bytes 786440 | tf_op jit(solution)/shard_map/ppermute | solution.py:332
  (39 other events, 352.7 us)

commit v9 on v8

--- a/solution.py
+++ b/solution.py
@@ -369,7 +369,8 @@
     second = second + [cross(*w) for w in second]
     weights = (gate_weight, up_weight, a1, b1, a2, b2, a3, b3)
     weights = weights + (gate_c, up_c) + tuple(swap(w, core) for w in weights[2:])
-    p0, p2 = partial_sums((t0, r2), weights, (F32, BF16))
+    crossings = (own[1][0], *(w for w, _ in second[3:]))
+    p0, p2 = partial_sums((after(t0, *crossings), r2), weights, (F32, BF16))
     q2 = swap(p2, across)
 
     f3 = swap(after(f2, d3, p2)[:, :, :half], near)
@@ -389,7 +390,7 @@
         [out, pltpu.HBM((rows, hid), BF16)], [pltpu.SemaphoreType.DMA], {},
     )
     late = [(after(f3, hidden), ((14, 2),)), (after(g3, hidden), ((14, 3),))]
-    late = [cross(after(w, q2), parts) for w, parts in third[:2]] + [cross(after(w, hidden), parts) for w, parts in third[2:]] + late + [cross(*w) for w in late]
+    late = [cross(after(w, hidden), parts) for w, parts in third[:2]] + [cross(after(w, hidden), parts) for w, parts in third[2:]] + late + [cross(*w) for w in late]
     return down_call(
         second_kernel, "down_second", [], [owner_rows, hidden], [product], late, [out], [], {2: 0}
     )[0]

time: 110 us -> 113 us (1.027)
  local copies, waits for them, and re-layouts: 3.08 us -> 4.82 us
  waiting for transfers between devices: 54 us -> 55.6 us
    unnamed x56, local copies, waits for them, and re-layouts: 1.15 us -> 2.89 us
    ppermute x35, waiting for transfers between devices: 54 us -> 55.6 us  [swap(): return lax.ppermute(value, ALL, pairs)]
  transfers between devices with their start and end apart: 35 -> 35, of which waited for: 15 -> 14; matrix products, arithmetic and copies ran while one was open for 3% -> 3% of each run, Pallas kernels for 17% -> 16%
where the time goes in v9:
time: 113 us; the launch traced here: 112 us
  waiting for transfers between devices  55.6 us (49%)
  starting transfers between devices  26.1 us (23%)
  Pallas kernels  21.9 us (19%)
  local copies, waits for them, and re-layouts  4.82 us (4%)
  other arithmetic  2.95 us (3%)
    ppermute x35, waiting for transfers between devices, swap(): return lax.ppermute(value, ALL, pairs)  55.6 us
    ppermute x35, starting transfers between devices, swap(): return lax.ppermute(value, ALL, pairs)  26.1 us
    pallas_call x2, Pallas kernels, down_call(): pl.pallas_call(functools.partial(kernel, pieces), in_specs=[SMEM] * len(l...  8.45 us
    pallas_call x1, Pallas kernels, partial_sums(): pl.pallas_call(functools.partial(partial_kernel, kinds), in_specs=[HBM] *...  7.8 us
    pallas_call x1, Pallas kernels, normed_halves(): pl.pallas_call(norm_kernel, in_specs=[SMEM, HBM, VMEM], out_specs=[HBM] *...  5.66 us
    unnamed x56, local copies, waits for them, and re-layouts  2.89 us
  transfers between devices with their start and end apart: 35, of which 14 were waited for; matrix products, arithmetic and copies ran while one was open for 3% of the time, Pallas kernels for 16%

profile of v9, /device:TPU:0, one launch (start us, length us, event | category | flops | bytes accessed | tf_op | source)
XLA Modules:
  0.0 112.5 jit_solution(16528633361437669549)
XLA Ops:
  0.0 1.9 %broadcast_select_fusion = bf16[1024,256]{1,0:T(8,128)(2,1)} fusion(bf16[1024,256]{1,0:T(8,128)(2,1)} %refs_2_.1, bf16[1024,256]{1,0:T(8,128)(2,1)} %refs_3_.1, pred[]{:T(512)S(6)} %eq.3), kind=kLoop, calls=%fused_computation | loop fusion | flops 262144 | bytes 1572865 | tf_op jit(solution)/shard_map/jit(_where)/select_n | solution.py:335
  1.9 3.0 %collective-permute-start.5 = (bf16[1024,256]{1,0:T(8,128)(2,1)}, bf16[1024,256]{1,0:T(8,128)(2,1)S(1)}, u32[]{:S(2)}, u32[]{:S(2)}) collective-permute-start(bf16[1024,256]{1,0:T(8,128)(2,1)} %broadcast_select_fusion), channel_id=1, source_target_pairs={{0,4},{1,5},{2,6},{3,7},{4,0},{5,1},{6,2},{7,3},{8,12},{9,13},{10,... | collective-permute-start | bytes 1572872 | tf_op jit(solution)/shard_map/ppermute | solution.py:332
  4.9 2.6 %collective-permute-start.6 = (bf16[1024,256]{1,0:T(8,128)(2,1)}, bf16[1024,256]{1,0:T(8,128)(2,1)S(1)}, u32[]{:S(2)}, u32[]{:S(2)}) collective-permute-start(bf16[1024,256]{1,0:T(8,128)(2,1)} %broadcast_select_fusion), channel_id=1, source_target_pairs={{0,8},{1,9},{2,10},{3,11},{4,12},{5,13},{6,14},{7,15},{8,0},{9,1},... | collective-permute-start | bytes 1572872 | tf_op jit(solution)/shard_map/ppermute | solution.py:332
  8.6 1.6 %collective-permute-start.1 = (bf16[1,256,512]{2,1,0:T(8,128)(2,1)S(1)}, bf16[1,256,512]{2,1,0:T(8,128)(2,1)S(1)}, u32[]{:S(2)}, u32[]{:S(2)}) collective-permute-start(bf16[1,256,512]{2,1,0:T(8,128)(2,1)S(1)} %select_bitcast_fusion.a_ref), channel_id=1, source_target_pairs={{0,2},{1,3},{2,0},{3,1},{4,6},{5,7},{6,4},{7,5},{8,10},{9,11},{10,... | collective-permute-start | bytes 786440 | tf_op jit(solution)/shard_map/ppermute | solution.py:332
  10.4 5.7 %norm_halves.1 = (bf16[8,128,1024]{2,1,0:T(8,128)(2,1)}, bf16[8,128,1024]{2,1,0:T(8,128)(2,1)}) custom-call(s32[16]{0:T(128)} %owner_ref.5, bf16[128,16384]{1,0:T(8,128)(2,1)} %tokens_ref.1, f32[1,16384]{1,0:T(1,128)} %bitcast.7), custom_call_target="tpu_custom_call" | custom-call | flops 12582912 | bytes 8388608 | tf_op jit(solution)/shard_map/norm_halves/pallas_call | solution.py:97
  18.8 9.3 %collective-permute-done.5.refs_4_ = bf16[1024,256]{1,0:T(8,128)(2,1)S(1)} collective-permute-done((bf16[1024,256]{1,0:T(8,128)(2,1)}, bf16[1024,256]{1,0:T(8,128)(2,1)S(1)}, u32[]{:S(2)}, u32[]{:S(2)}) %collective-permute-start.5) | collective-permute-done | bytes 524320 | tf_op jit(solution)/shard_map/ppermute | solution.py:332
  28.2 2.5 %collective-permute-done.6.refs_6_ = bf16[1024,256]{1,0:T(8,128)(2,1)S(1)} collective-permute-done((bf16[1024,256]{1,0:T(8,128)(2,1)}, bf16[1024,256]{1,0:T(8,128)(2,1)S(1)}, u32[]{:S(2)}, u32[]{:S(2)}) %collective-permute-start.6) | collective-permute-done | bytes 524320 | tf_op jit(solution)/shard_map/ppermute | solution.py:332
  30.7 1.5 %collective-permute-start.3 = (bf16[1,256,512]{2,1,0:T(8,128)(2,1)S(1)}, bf16[1,256,512]{2,1,0:T(8,128)(2,1)S(1)}, u32[]{:S(2)}, u32[]{:S(2)}) collective-permute-start(bf16[1,256,512]{2,1,0:T(8,128)(2,1)S(1)} %collective-permute-done.1.b_ref.refs_4_), channel_id=1, source_target_pairs={{0,16},{1,17},{2,18},{3,19},{4,20},{5,21},{6,22},{7,23},{8,24},{9,... | collective-permute-start | bytes 786440 | tf_op jit(solution)/shard_map/ppermute | solution.py:332
  32.3 5.0 %collective-permute-done.3.refs_5_ = bf16[1,256,512]{2,1,0:T(8,128)(2,1)S(1)} collective-permute-done((bf16[1,256,512]{2,1,0:T(8,128)(2,1)S(1)}, bf16[1,256,512]{2,1,0:T(8,128)(2,1)S(1)}, u32[]{:S(2)}, u32[]{:S(2)}) %collective-permute-start.3) | collective-permute-done | bytes 262176 | tf_op jit(solution)/shard_map/ppermute | solution.py:332
  40.3 1.9 %collective-permute-start.8 = (bf16[1,256,1024]{2,1,0:T(8,128)(2,1)S(1)}, bf16[1,256,1024]{2,1,0:T(8,128)(2,1)}, u32[]{:S(2)}, u32[]{:S(2)}) collective-permute-start(bf16[1,256,1024]{2,1,0:T(8,128)(2,1)S(1)} %bitcast.6), channel_id=1, source_target_pairs={{0,8},{1,9},{2,10},{3,11},{4,12},{5,13},{6,14},{7,15},{8,0},{9,1},... | collective-permute-start | bytes 1572872 | tf_op jit(solution)/shard_map/ppermute | solution.py:332
  42.2 10.0 %collective-permute-done.11.refs_5_ = bf16[1024,256]{1,0:T(8,128)(2,1)S(1)} collective-permute-done((bf16[1024,256]{1,0:T(8,128)(2,1)S(1)}, bf16[1024,256]{1,0:T(8,128)(2,1)S(1)}, u32[]{:S(2)}, u32[]{:S(2)}) %collective-permute-start.11) | collective-permute-done | bytes 524320 | tf_op jit(solution)/shard_map/ppermute | solution.py:332
  52.2 7.4 %collective-permute-done.12.refs_7_ = bf16[1024,256]{1,0:T(8,128)(2,1)S(1)} collective-permute-done((bf16[1024,256]{1,0:T(8,128)(2,1)S(1)}, bf16[1024,256]{1,0:T(8,128)(2,1)S(1)}, u32[]{:S(2)}, u32[]{:S(2)}) %collective-permute-start.12) | collective-permute-done | bytes 524320 | tf_op jit(solution)/shard_map/ppermute | solution.py:332
  60.1 3.4 %collective-permute-done.8.refs_6_ = bf16[1,256,1024]{2,1,0:T(8,128)(2,1)} collective-permute-done((bf16[1,256,1024]{2,1,0:T(8,128)(2,1)S(1)}, bf16[1,256,1024]{2,1,0:T(8,128)(2,1)}, u32[]{:S(2)}, u32[]{:S(2)}) %collective-permute-start.8) | collective-permute-done | bytes 524320 | tf_op jit(solution)/shard_map/ppermute | solution.py:332
  63.6 1.6 %collective-permute-start.14 = (bf16[1024,256]{1,0:T(8,128)(2,1)S(1)}, bf16[1024,256]{1,0:T(8,128)(2,1)S(1)}, u32[]{:S(2)}, u32[]{:S(2)}) collective-permute-start(bf16[1024,256]{1,0:T(8,128)(2,1)S(1)} %collective-permute-done.13.refs_8_), channel_id=1, source_target_pairs={{0,16},{1,17},{2,18},{3,19},{4,20},{5,21},{6,22},{7,23},{8,24},{9,... | collective-permute-start | bytes 1572872 | tf_op jit(solution)/shard_map/ppermute | solution.py:332
  65.7 8.4 %collective-permute-done.14.refs_9_ = bf16[1024,256]{1,0:T(8,128)(2,1)S(1)} collective-permute-done((bf16[1024,256]{1,0:T(8,128)(2,1)S(1)}, bf16[1024,256]{1,0:T(8,128)(2,1)S(1)}, u32[]{:S(2)}, u32[]{:S(2)}) %collective-permute-start.14) | collective-permute-done | bytes 524320 | tf_op jit(solution)/shard_map/ppermute | solution.py:332
  76.1 1.7 %collective-permute-start.26 = (bf16[1,256,1024]{2,1,0:T(8,128)(2,1)}, bf16[1,256,1024]{2,1,0:T(8,128)(2,1)}, u32[]{:S(2)}, u32[]{:S(2)}) collective-permute-start(bf16[1,256,1024]{2,1,0:T(8,128)(2,1)} %collective-permute-done.8.refs_6_), channel_id=1, source_target_pairs={{0,4},{1,5},{2,6},{3,7},{4,0},{5,1},{6,2},{7,3},{8,12},{9,13},{10,... | collective-permute-start | bytes 1572872 | tf_op jit(solution)/shard_map/ppermute | solution.py:332
  77.8 1.6 %collective-permute-start.25 = (bf16[1,256,1024]{2,1,0:T(8,128)(2,1)}, bf16[1,256,1024]{2,1,0:T(8,128)(2,1)}, u32[]{:S(2)}, u32[]{:S(2)}) collective-permute-start(bf16[1,256,1024]{2,1,0:T(8,128)(2,1)} %collective-permute-done.8.refs_6_), channel_id=1, source_target_pairs={{0,2},{1,3},{2,0},{3,1},{4,6},{5,7},{6,4},{7,5},{8,10},{9,11},{10,... | collective-permute-start | bytes 1572872 | tf_op jit(solution)/shard_map/ppermute | solution.py:332
  80.7 7.8 %partial_sums.1 = (f32[128,512]{1,0:T(8,128)}, bf16[128,512]{1,0:T(8,128)(2,1)}) custom-call(bf16[8,128,1024]{2,1,0:T(8,128)(2,1)} %get-tuple-element.36.refs_0_, bf16[8,128,1024]{2,1,0:T(8,128)(2,1)} %copy-done.1, bf16[1024,256]{1,0:T(8,128)(2,1)} %refs_2_.1, bf16[1024,256]{1,0:T(8,128)(2,1)} %refs_3_.1, bf16[1024,256]{1,0:T(8,128)(2,1)} %copy-done.2, ...), custom_call_target="tpu_custom_call" | custom-call | flops 2147483648 | bytes 12582912 | tf_op jit(solution)/shard_map/partial_sums/pallas_call | solution.py:178
  90.3 2.4 %collective-permute-done.25.refs_12_ = bf16[1,256,1024]{2,1,0:T(8,128)(2,1)} collective-permute-done((bf16[1,256,1024]{2,1,0:T(8,128)(2,1)}, bf16[1,256,1024]{2,1,0:T(8,128)(2,1)}, u32[]{:S(2)}, u32[]{:S(2)}) %collective-permute-start.25) | collective-permute-done | bytes 524320 | tf_op jit(solution)/shard_map/ppermute | solution.py:332
  94.8 2.1 %collective-permute-start.32 = (bf16[1,256,512]{2,1,0:T(8,128)(2,1)S(1)}, bf16[1,256,512]{2,1,0:T(8,128)(2,1)S(1)}, u32[]{:S(2)}, u32[]{:S(2)}) collective-permute-start(bf16[1,256,512]{2,1,0:T(8,128)(2,1)S(1)} %slice.15), channel_id=1, source_target_pairs={{0,2},{1,3},{2,0},{3,1},{4,6},{5,7},{6,4},{7,5},{8,10},{9,11},{10,... | collective-permute-start | bytes 786440 | tf_op jit(solution)/shard_map/ppermute | solution.py:332
  97.5 4.8 %down_first.1 = (bf16[128,16384]{1,0:T(8,128)(2,1)}, bf16[128,256]{1,0:T(8,128)(2,1)}) custom-call(s32[1]{0:T(128)S(6)} %copy.10.live_ref, s32[16]{0:T(128)} %owner_ref.5, f32[128,512]{1,0:T(8,128)} %get-tuple-element.41.refs_0_, bf16[128,512]{1,0:T(8,128)(2,1)} %copy-done.27, bf16[1,256,1024]{2,1,0:T(8,128)(2,1)} %bitcast.5, ...), custom_call_target="tpu_custom_call" | custom-call | flops 6710886400 | bytes 7864320 | tf_op jit(solution)/shard_map/down_first/pallas_call | solution.py:274
  103.5 1.5 %collective-permute-done.33.refs_6_ = bf16[1,256,512]{2,1,0:T(8,128)(2,1)S(1)} collective-permute-done((bf16[1,256,512]{2,1,0:T(8,128)(2,1)S(1)}, bf16[1,256,512]{2,1,0:T(8,128)(2,1)S(1)}, u32[]{:S(2)}, u32[]{:S(2)}) %collective-permute-start.33) | collective-permute-done | bytes 262176 | tf_op jit(solution)/shard_map/ppermute | solution.py:332
  105.2 2.1 %collective-permute-done.34.refs_7_ = bf16[1,256,512]{2,1,0:T(8,128)(2,1)S(1)} collective-permute-done((bf16[1,256,512]{2,1,0:T(8,128)(2,1)S(1)}, bf16[1,256,512]{2,1,0:T(8,128)(2,1)S(1)}, u32[]{:S(2)}, u32[]{:S(2)}) %collective-permute-start.34) | collective-permute-done | bytes 262176 | tf_op jit(solution)/shard_map/ppermute | solution.py:332
  108.8 3.6 %down_second.1 = bf16[128,16384]{1,0:T(8,128)(2,1)} custom-call(s32[16]{0:T(128)} %owner_ref.5, bf16[128,256]{1,0:T(8,128)(2,1)} %get-tuple-element.47.hidden_ref, bf16[128,16384]{1,0:T(8,128)(2,1)} %get-tuple-element.48._, bf16[2,256,512]{2,1,0:T(8,128)(2,1)} %copy-done.16, bf16[2,256,512]{2,1,0:T(8,128)(2,1)} %copy-done.17, ...), custom_call_target="tpu_custom_call", output_to_operand_aliasing={{}: (2, {})} | custom-call | flops 4026531840 | bytes 4718592 | tf_op jit(solution)/shard_map/down_second/pallas_call | solution.py:274
  (111 shorter events, 18.2 us)
Async XLA Ops:
  1.9 26.3 %collective-permute-start.5 = (bf16[1024,256]{1,0:T(8,128)(2,1)}, bf16[1024,256]{1,0:T(8,128)(2,1)S(1)}, u32[]{:S(2)}, u32[]{:S(2)}) collective-permute-start(bf16[1024,256]{1,0:T(8,128)(2,1)} %broadcast_select_fusion), channel_id=1, source_target_pairs={{0,4},{1,5},{2,6},{3,7},{4,0},{5,1},{6,2},{7,3},{8,12},{9,13},{10,... | collective-permute-start | bytes 1572872 | tf_op jit(solution)/shard_map/ppermute | solution.py:332
  4.9 25.8 %collective-permute-start.6 = (bf16[1024,256]{1,0:T(8,128)(2,1)}, bf16[1024,256]{1,0:T(8,128)(2,1)S(1)}, u32[]{:S(2)}, u32[]{:S(2)}) collective-permute-start(bf16[1024,256]{1,0:T(8,128)(2,1)} %broadcast_select_fusion), channel_id=1, source_target_pairs={{0,8},{1,9},{2,10},{3,11},{4,12},{5,13},{6,14},{7,15},{8,0},{9,1},... | collective-permute-start | bytes 1572872 | tf_op jit(solution)/shard_map/ppermute | solution.py:332
  7.5 24.7 %collective-permute-start.7 = (bf16[1024,256]{1,0:T(8,128)(2,1)}, bf16[1024,256]{1,0:T(8,128)(2,1)}, u32[]{:S(2)}, u32[]{:S(2)}) collective-permute-start(bf16[1024,256]{1,0:T(8,128)(2,1)} %refs_2_.1), channel_id=1, source_target_pairs={{0,1},{1,0},{2,3},{3,2},{4,5},{5,4},{6,7},{7,6},{8,9},{9,8},{10,11... | collective-permute-start | bytes 1572872 | tf_op jit(solution)/shard_map/ppermute | solution.py:332
  8.6 8.8 %collective-permute-start.1 = (bf16[1,256,512]{2,1,0:T(8,128)(2,1)S(1)}, bf16[1,256,512]{2,1,0:T(8,128)(2,1)S(1)}, u32[]{:S(2)}, u32[]{:S(2)}) collective-permute-start(bf16[1,256,512]{2,1,0:T(8,128)(2,1)S(1)} %select_bitcast_fusion.a_ref), channel_id=1, source_target_pairs={{0,2},{1,3},{2,0},{3,1},{4,6},{5,7},{6,4},{7,5},{8,10},{9,11},{10,... | collective-permute-start | bytes 786440 | tf_op jit(solution)/shard_map/ppermute | solution.py:332
  10.1 30.2 %collective-permute-start.15 = (bf16[1024,256]{1,0:T(8,128)(2,1)}, bf16[1024,256]{1,0:T(8,128)(2,1)}, u32[]{:S(2)}, u32[]{:S(2)}) collective-permute-start(bf16[1024,256]{1,0:T(8,128)(2,1)} %refs_3_.1), channel_id=1, source_target_pairs={{0,1},{1,0},{2,3},{3,2},{4,5},{5,4},{6,7},{7,6},{8,9},{9,8},{10,11... | collective-permute-start | bytes 1572872 | tf_op jit(solution)/shard_map/ppermute | solution.py:332
  17.4 58.1 %collective-permute-start.10 = (bf16[8,128,1024]{2,1,0:T(8,128)(2,1)}, bf16[8,128,1024]{2,1,0:T(8,128)(2,1)S(1)}, u32[]{:S(2)}, u32[]{:S(2)}) collective-permute-start(bf16[8,128,1024]{2,1,0:T(8,128)(2,1)} %get-tuple-element.32), channel_id=1, source_target_pairs={{0,2},{1,3},{2,0},{3,1},{4,6},{5,7},{6,4},{7,5},{8,10},{9,11},{10,... | collective-permute-start | bytes 6291464 | tf_op jit(solution)/shard_map/ppermute | solution.py:332
  28.2 10.5 %collective-permute-start = (bf16[1,256,1024]{2,1,0:T(8,128)(2,1)}, bf16[1,256,1024]{2,1,0:T(8,128)(2,1)S(1)}, u32[]{:S(2)}, u32[]{:S(2)}) collective-permute-start(bf16[1,256,1024]{2,1,0:T(8,128)(2,1)} %bitcast.4), channel_id=1, source_target_pairs={{0,1},{1,0},{2,3},{3,2},{4,5},{5,4},{6,7},{7,6},{8,9},{9,8},{10,11... | collective-permute-start | bytes 1572872 | tf_op jit(solution)/shard_map/ppermute | solution.py:332
  30.7 6.6 %collective-permute-start.3 = (bf16[1,256,512]{2,1,0:T(8,128)(2,1)S(1)}, bf16[1,256,512]{2,1,0:T(8,128)(2,1)S(1)}, u32[]{:S(2)}, u32[]{:S(2)}) collective-permute-start(bf16[1,256,512]{2,1,0:T(8,128)(2,1)S(1)} %collective-permute-done.1.b_ref.refs_4_), channel_id=1, source_target_pairs={{0,16},{1,17},{2,18},{3,19},{4,20},{5,21},{6,22},{7,23},{8,24},{9,... | collective-permute-start | bytes 786440 | tf_op jit(solution)/shard_map/ppermute | solution.py:332
  32.2 7.1 %collective-permute-start.2 = (bf16[1,256,512]{2,1,0:T(8,128)(2,1)S(1)}, bf16[1,256,512]{2,1,0:T(8,128)(2,1)S(1)}, u32[]{:S(2)}, u32[]{:S(2)}) collective-permute-start(bf16[1,256,512]{2,1,0:T(8,128)(2,1)S(1)} %collective-permute-done.1.b_ref.refs_4_), channel_id=1, source_target_pairs={{0,1},{1,0},{2,3},{3,2},{4,5},{5,4},{6,7},{7,6},{8,9},{9,8},{10,11... | collective-permute-start | bytes 786440 | tf_op jit(solution)/shard_map/ppermute | solution.py:332
  37.3 14.9 %collective-permute-start.11 = (bf16[1024,256]{1,0:T(8,128)(2,1)S(1)}, bf16[1024,256]{1,0:T(8,128)(2,1)S(1)}, u32[]{:S(2)}, u32[]{:S(2)}) collective-permute-start(bf16[1024,256]{1,0:T(8,128)(2,1)S(1)} %collective-permute-done.5.refs_4_), channel_id=1, source_target_pairs={{0,16},{1,17},{2,18},{3,19},{4,20},{5,21},{6,22},{7,23},{8,24},{9,... | collective-permute-start | bytes 1572872 | tf_op jit(solution)/shard_map/ppermute | solution.py:332
  38.7 20.9 %collective-permute-start.12 = (bf16[1024,256]{1,0:T(8,128)(2,1)S(1)}, bf16[1024,256]{1,0:T(8,128)(2,1)S(1)}, u32[]{:S(2)}, u32[]{:S(2)}) collective-permute-start(bf16[1024,256]{1,0:T(8,128)(2,1)S(1)} %collective-permute-done.6.refs_6_), channel_id=1, source_target_pairs={{0,16},{1,17},{2,18},{3,19},{4,20},{5,21},{6,22},{7,23},{8,24},{9,... | collective-permute-start | bytes 1572872 | tf_op jit(solution)/shard_map/ppermute | solution.py:332
  39.3 20.5 %collective-permute-start.13 = (bf16[1024,256]{1,0:T(8,128)(2,1)S(1)}, bf16[1024,256]{1,0:T(8,128)(2,1)S(1)}, u32[]{:S(2)}, u32[]{:S(2)}) collective-permute-start(bf16[1024,256]{1,0:T(8,128)(2,1)S(1)} %collective-permute-done.6.refs_6_), channel_id=1, source_target_pairs={{0,4},{1,5},{2,6},{3,7},{4,0},{5,1},{6,2},{7,3},{8,12},{9,13},{10,... | collective-permute-start | bytes 1572872 | tf_op jit(solution)/shard_map/ppermute | solution.py:332
  40.3 23.3 %collective-permute-start.8 = (bf16[1,256,1024]{2,1,0:T(8,128)(2,1)S(1)}, bf16[1,256,1024]{2,1,0:T(8,128)(2,1)}, u32[]{:S(2)}, u32[]{:S(2)}) collective-permute-start(bf16[1,256,1024]{2,1,0:T(8,128)(2,1)S(1)} %bitcast.6), channel_id=1, source_target_pairs={{0,8},{1,9},{2,10},{3,11},{4,12},{5,13},{6,14},{7,15},{8,0},{9,1},... | collective-permute-start | bytes 1572872 | tf_op jit(solution)/shard_map/ppermute | solution.py:332
  52.2 12.9 %collective-permute-start.4 = (bf16[1,256,512]{2,1,0:T(8,128)(2,1)S(1)}, bf16[1,256,512]{2,1,0:T(8,128)(2,1)S(1)}, u32[]{:S(2)}, u32[]{:S(2)}) collective-permute-start(bf16[1,256,512]{2,1,0:T(8,128)(2,1)S(1)} %collective-permute-done.3.refs_5_), channel_id=1, source_target_pairs={{0,1},{1,0},{2,3},{3,2},{4,5},{5,4},{6,7},{7,6},{8,9},{9,8},{10,11... | collective-permute-start | bytes 786440 | tf_op jit(solution)/shard_map/ppermute | solution.py:332
  63.6 10.6 %collective-permute-start.14 = (bf16[1024,256]{1,0:T(8,128)(2,1)S(1)}, bf16[1024,256]{1,0:T(8,128)(2,1)S(1)}, u32[]{:S(2)}, u32[]{:S(2)}) collective-permute-start(bf16[1024,256]{1,0:T(8,128)(2,1)S(1)} %collective-permute-done.13.refs_8_), channel_id=1, source_target_pairs={{0,16},{1,17},{2,18},{3,19},{4,20},{5,21},{6,22},{7,23},{8,24},{9,... | collective-permute-start | bytes 1572872 | tf_op jit(solution)/shard_map/ppermute | solution.py:332
  65.1 10.4 %collective-permute-start.23 = (bf16[2,256,512]{2,1,0:T(8,128)(2,1)S(1)}, bf16[2,256,512]{2,1,0:T(8,128)(2,1)}, u32[]{:S(2)}, u32[]{:S(2)}) collective-permute-start(bf16[2,256,512]{2,1,0:T(8,128)(2,1)S(1)} %stack_halves.1), channel_id=1, source_target_pairs={{0,4},{1,5},{2,6},{3,7},{4,0},{5,1},{6,2},{7,3},{8,12},{9,13},{10,... | collective-permute-start | bytes 1572872 | tf_op jit(solution)/shard_map/ppermute | solution.py:332
  65.2 10.9 %collective-permute-start.9 = (bf16[1,256,1024]{2,1,0:T(8,128)(2,1)}, bf16[1,256,1024]{2,1,0:T(8,128)(2,1)S(1)}, u32[]{:S(2)}, u32[]{:S(2)}) collective-permute-start(bf16[1,256,1024]{2,1,0:T(8,128)(2,1)} %collective-permute-done.8.refs_6_), channel_id=1, source_target_pairs={{0,1},{1,0},{2,3},{3,2},{4,5},{5,4},{6,7},{7,6},{8,9},{9,8},{10,11... | collective-permute-start | bytes 1572872 | tf_op jit(solution)/shard_map/ppermute | solution.py:332
  65.2 12.5 %collective-permute-start.17 = (bf16[1024,256]{1,0:T(8,128)(2,1)S(1)}, bf16[1024,256]{1,0:T(8,128)(2,1)S(1)}, u32[]{:S(2)}, u32[]{:S(2)}) collective-permute-start(bf16[1024,256]{1,0:T(8,128)(2,1)S(1)} %collective-permute-done.11.refs_5_), channel_id=1, source_target_pairs={{0,1},{1,0},{2,3},{3,2},{4,5},{5,4},{6,7},{7,6},{8,9},{9,8},{10,11... | collective-permute-start | bytes 1572872 | tf_op jit(solution)/shard_map/ppermute | solution.py:332
  76.1 14.2 %collective-permute-start.26 = (bf16[1,256,1024]{2,1,0:T(8,128)(2,1)}, bf16[1,256,1024]{2,1,0:T(8,128)(2,1)}, u32[]{:S(2)}, u32[]{:S(2)}) collective-permute-start(bf16[1,256,1024]{2,1,0:T(8,128)(2,1)} %collective-permute-done.8.refs_6_), channel_id=1, source_target_pairs={{0,4},{1,5},{2,6},{3,7},{4,0},{5,1},{6,2},{7,3},{8,12},{9,13},{10,... | collective-permute-start | bytes 1572872 | tf_op jit(solution)/shard_map/ppermute | solution.py:332
  77.8 14.9 %collective-permute-start.25 = (bf16[1,256,1024]{2,1,0:T(8,128)(2,1)}, bf16[1,256,1024]{2,1,0:T(8,128)(2,1)}, u32[]{:S(2)}, u32[]{:S(2)}) collective-permute-start(bf16[1,256,1024]{2,1,0:T(8,128)(2,1)} %collective-permute-done.8.refs_6_), channel_id=1, source_target_pairs={{0,2},{1,3},{2,0},{3,1},{4,6},{5,7},{6,4},{7,5},{8,10},{9,11},{10,... | collective-permute-start | bytes 1572872 | tf_op jit(solution)/shard_map/ppermute | solution.py:332
  79.3 17.6 %collective-permute-start.24 = (bf16[2,256,512]{2,1,0:T(8,128)(2,1)}, bf16[2,256,512]{2,1,0:T(8,128)(2,1)}, u32[]{:S(2)}, u32[]{:S(2)}) collective-permute-start(bf16[2,256,512]{2,1,0:T(8,128)(2,1)} %collective-permute-done.23.refs_10_), channel_id=1, source_target_pairs={{0,16},{1,17},{2,18},{3,19},{4,20},{5,21},{6,22},{7,23},{8,24},{9,... | collective-permute-start | bytes 1572872 | tf_op jit(solution)/shard_map/ppermute | solution.py:332
  88.5 8.4 %collective-permute-start.22 = (bf16[128,512]{1,0:T(8,128)(2,1)}, bf16[128,512]{1,0:T(8,128)(2,1)S(1)}, u32[]{:S(2)}, u32[]{:S(2)}) collective-permute-start(bf16[128,512]{1,0:T(8,128)(2,1)} %get-tuple-element.42), channel_id=1, source_target_pairs={{0,2},{1,3},{2,0},{3,1},{4,6},{5,7},{6,4},{7,5},{8,10},{9,11},{10,... | collective-permute-start | bytes 393224 | tf_op jit(solution)/shard_map/ppermute | solution.py:332
  93.6 9.3 %collective-permute-start.31 = (bf16[1,256,512]{2,1,0:T(8,128)(2,1)S(1)}, bf16[1,256,512]{2,1,0:T(8,128)(2,1)S(1)}, u32[]{:S(2)}, u32[]{:S(2)}) collective-permute-start(bf16[1,256,512]{2,1,0:T(8,128)(2,1)S(1)} %slice.14), channel_id=1, source_target_pairs={{0,4},{1,5},{2,6},{3,7},{4,0},{5,1},{6,2},{7,3},{8,12},{9,13},{10,... | collective-permute-start | bytes 786440 | tf_op jit(solution)/shard_map/ppermute | solution.py:332
  94.8 8.6 %collective-permute-start.32 = (bf16[1,256,512]{2,1,0:T(8,128)(2,1)S(1)}, bf16[1,256,512]{2,1,0:T(8,128)(2,1)S(1)}, u32[]{:S(2)}, u32[]{:S(2)}) collective-permute-start(bf16[1,256,512]{2,1,0:T(8,128)(2,1)S(1)} %slice.15), channel_id=1, source_target_pairs={{0,2},{1,3},{2,0},{3,1},{4,6},{5,7},{6,4},{7,5},{8,10},{9,11},{10,... | collective-permute-start | bytes 786440 | tf_op jit(solution)/shard_map/ppermute | solution.py:332
  (39 other events, 414.2 us)

commit v10 on v9

--- a/solution.py
+++ b/solution.py
@@ -347,10 +347,9 @@
         return swap(weights, core), tuple((turn ^ 1, plane) for turn, plane in parts)
 
     own = [(down_weight[None], ((0, 0),))]
-    own = own + [cross(*w) for w in own]
-    gate_c, up_c = swap(gate_weight, core), swap(up_weight, core)
+    gate_c = swap(gate_weight, core)
     d0 = stacked(
-        after(mine, a1, a2, t2, gate_c), mine_x, 10**11
+        after(mine, a1, a2, t2, gate_c, rest_x), mine_x, 10**11
     )
 
     b1 = swap(after(a1, d0, rest_x), other)
@@ -365,11 +364,11 @@
     d3 = swap(after(d2, d1), near)
     f2 = swap(after(d2, r2), across)
 
-    second = [(mine_x, ((2, 0),)), (rest_x, ((2, 1),)), (d2, ((8, 0),))]
-    second = second + [cross(*w) for w in second]
+    second = own + [(mine_x, ((2, 0),)), (rest_x, ((2, 1),)), (d2, ((8, 0),))]
+    second = second + [cross(after(w, a3), parts) for w, parts in second]
     weights = (gate_weight, up_weight, a1, b1, a2, b2, a3, b3)
-    weights = weights + (gate_c, up_c) + tuple(swap(w, core) for w in weights[2:])
-    crossings = (own[1][0], *(w for w, _ in second[3:]))
+    weights = weights + (gate_c, swap(after(up_weight, a3), core)) + tuple(swap(w, core) for w in weights[2:])
+    crossings = [w for w, _ in second[4:]]
     p0, p2 = partial_sums((after(t0, *crossings), r2), weights, (F32, BF16))
     q2 = swap(p2, across)
 
@@ -382,7 +381,7 @@
         (f2, ((10, 0),)),
         (d3, ((12, 0),)),
     ]
-    early = own + second + third
+    early = second + third
     out = pltpu.HBM(tokens.shape, BF16)
     rows, hid = tokens.shape[0], gate_weight.shape[1]
     product, hidden = down_call(

time: 113 us -> 112 us (level)
    unnamed x56 -> x60, local copies, waits for them, and re-layouts: 2.89 us -> 3.99 us
  transfers between devices with their start and end apart: 35 -> 35, of which waited for: 14 -> 12; matrix products, arithmetic and copies ran while one was open for 3% -> 3% of each run, Pallas kernels for 16% -> 16%
where the time goes in v10:
time: 112 us; the launch traced here: 111 us
  waiting for transfers between devices  55.1 us (49%)
  starting transfers between devices  25.3 us (23%)
  Pallas kernels  21.9 us (20%)
  local copies, waits for them, and re-layouts  4.97 us (4%)
  other arithmetic  2.95 us (3%)
    ppermute x35, waiting for transfers between devices, swap(): return lax.ppermute(value, ALL, pairs)  55.1 us
    ppermute x35, starting transfers between devices, swap(): return lax.ppermute(value, ALL, pairs)  25.3 us
    pallas_call x2, Pallas kernels, down_call(): pl.pallas_call(functools.partial(kernel, pieces), in_specs=[SMEM] * len(l...  8.44 us
    pallas_call x1, Pallas kernels, partial_sums(): pl.pallas_call(functools.partial(partial_kernel, kinds), in_specs=[HBM] *...  7.8 us
    pallas_call x1, Pallas kernels, normed_halves(): pl.pallas_call(norm_kernel, in_specs=[SMEM, HBM, VMEM], out_specs=[HBM] *...  5.66 us
    unnamed x60, local copies, waits for them, and re-layouts  3.99 us
  transfers between devices with their start and end apart: 35, of which 12 were waited for; matrix products, arithmetic and copies ran while one was open for 3% of the time, Pallas kernels for 16%

profile of v10, /device:TPU:0, one launch (start us, length us, event | category | flops | bytes accessed | tf_op | source)
XLA Modules:
  0.0 111.3 jit_solution(4146657162064619781)
XLA Ops:
  1.1 3.0 %collective-permute-start.3 = (bf16[1,256,512]{2,1,0:T(8,128)(2,1)S(1)}, bf16[1,256,512]{2,1,0:T(8,128)(2,1)S(1)}, u32[]{:S(2)}, u32[]{:S(2)}) collective-permute-start(bf16[1,256,512]{2,1,0:T(8,128)(2,1)S(1)} %select_bitcast_fusion.a_ref), channel_id=1, source_target_pairs={{0,2},{1,3},{2,0},{3,1},{4,6},{5,7},{6,4},{7,5},{8,10},{9,11},{10,... | collective-permute-start | bytes 786440 | tf_op jit(solution)/shard_map/ppermute | solution.py:332
  4.1 1.9 %broadcast_select_fusion = bf16[1024,256]{1,0:T(8,128)(2,1)} fusion(bf16[1024,256]{1,0:T(8,128)(2,1)} %refs_2_.1, bf16[1024,256]{1,0:T(8,128)(2,1)} %refs_3_.1, pred[]{:T(512)S(6)} %eq.3), kind=kLoop, calls=%fused_computation | loop fusion | flops 262144 | bytes 1572865 | tf_op jit(solution)/shard_map/jit(_where)/select_n | solution.py:335
  6.0 2.6 %collective-permute-start = (bf16[1024,256]{1,0:T(8,128)(2,1)}, bf16[1024,256]{1,0:T(8,128)(2,1)S(1)}, u32[]{:S(2)}, u32[]{:S(2)}) collective-permute-start(bf16[1024,256]{1,0:T(8,128)(2,1)} %broadcast_select_fusion), channel_id=1, source_target_pairs={{0,8},{1,9},{2,10},{3,11},{4,12},{5,13},{6,14},{7,15},{8,0},{9,1},... | collective-permute-start | bytes 1572872 | tf_op jit(solution)/shard_map/ppermute | solution.py:332
  8.5 1.6 %collective-permute-start.1 = (bf16[1024,256]{1,0:T(8,128)(2,1)}, bf16[1024,256]{1,0:T(8,128)(2,1)}, u32[]{:S(2)}, u32[]{:S(2)}) collective-permute-start(bf16[1024,256]{1,0:T(8,128)(2,1)} %broadcast_select_fusion), channel_id=1, source_target_pairs={{0,4},{1,5},{2,6},{3,7},{4,0},{5,1},{6,2},{7,3},{8,12},{9,13},{10,... | collective-permute-start | bytes 1572872 | tf_op jit(solution)/shard_map/ppermute | solution.py:332
  10.1 5.7 %norm_halves.1 = (bf16[8,128,1024]{2,1,0:T(8,128)(2,1)}, bf16[8,128,1024]{2,1,0:T(8,128)(2,1)}) custom-call(s32[16]{0:T(128)} %owner_ref.5, bf16[128,16384]{1,0:T(8,128)(2,1)} %tokens_ref.1, f32[1,16384]{1,0:T(1,128)} %bitcast.7), custom_call_target="tpu_custom_call" | custom-call | flops 12582912 | bytes 8388608 | tf_op jit(solution)/shard_map/norm_halves/pallas_call | solution.py:97
  15.8 1.6 %collective-permute-start.4 = (bf16[1,256,512]{2,1,0:T(8,128)(2,1)S(1)}, bf16[1,256,512]{2,1,0:T(8,128)(2,1)S(1)}, u32[]{:S(2)}, u32[]{:S(2)}) collective-permute-start(bf16[1,256,512]{2,1,0:T(8,128)(2,1)S(1)} %collective-permute-done.3.b_ref.refs_3_), channel_id=1, source_target_pairs={{0,16},{1,17},{2,18},{3,19},{4,20},{5,21},{6,22},{7,23},{8,24},{9,... | collective-permute-start | bytes 786440 | tf_op jit(solution)/shard_map/ppermute | solution.py:332
  18.0 13.8 %collective-permute-done.refs_6_ = bf16[1024,256]{1,0:T(8,128)(2,1)S(1)} collective-permute-done((bf16[1024,256]{1,0:T(8,128)(2,1)}, bf16[1024,256]{1,0:T(8,128)(2,1)S(1)}, u32[]{:S(2)}, u32[]{:S(2)}) %collective-permute-start) | collective-permute-done | bytes 524320 | tf_op jit(solution)/shard_map/ppermute | solution.py:332
  32.1 1.5 %collective-permute-start.5 = (bf16[1024,256]{1,0:T(8,128)(2,1)S(1)}, bf16[1024,256]{1,0:T(8,128)(2,1)S(1)}, u32[]{:S(2)}, u32[]{:S(2)}) collective-permute-start(bf16[1024,256]{1,0:T(8,128)(2,1)S(1)} %collective-permute-done.refs_6_), channel_id=1, source_target_pairs={{0,4},{1,5},{2,6},{3,7},{4,0},{5,1},{6,2},{7,3},{8,12},{9,13},{10,... | collective-permute-start | bytes 1572872 | tf_op jit(solution)/shard_map/ppermute | solution.py:332
  33.6 2.2 %collective-permute-start.9 = (bf16[1,256,1024]{2,1,0:T(8,128)(2,1)S(1)}, bf16[1,256,1024]{2,1,0:T(8,128)(2,1)}, u32[]{:S(2)}, u32[]{:S(2)}) collective-permute-start(bf16[1,256,1024]{2,1,0:T(8,128)(2,1)S(1)} %bitcast.5), channel_id=1, source_target_pairs={{0,8},{1,9},{2,10},{3,11},{4,12},{5,13},{6,14},{7,15},{8,0},{9,1},... | collective-permute-start | bytes 1572872 | tf_op jit(solution)/shard_map/ppermute | solution.py:332
  35.9 1.5 %collective-permute-start.12 = (bf16[1024,256]{1,0:T(8,128)(2,1)}, bf16[1024,256]{1,0:T(8,128)(2,1)S(1)}, u32[]{:S(2)}, u32[]{:S(2)}) collective-permute-start(bf16[1024,256]{1,0:T(8,128)(2,1)} %collective-permute-done.1.refs_4_), channel_id=1, source_target_pairs={{0,16},{1,17},{2,18},{3,19},{4,20},{5,21},{6,22},{7,23},{8,24},{9,... | collective-permute-start | bytes 1572872 | tf_op jit(solution)/shard_map/ppermute | solution.py:332
  37.9 17.8 %collective-permute-done.5.refs_8_ = bf16[1024,256]{1,0:T(8,128)(2,1)S(1)} collective-permute-done((bf16[1024,256]{1,0:T(8,128)(2,1)S(1)}, bf16[1024,256]{1,0:T(8,128)(2,1)S(1)}, u32[]{:S(2)}, u32[]{:S(2)}) %collective-permute-start.5) | collective-permute-done | bytes 524320 | tf_op jit(solution)/shard_map/ppermute | solution.py:332
  55.7 3.4 %collective-permute-done.9.refs_5_ = bf16[1,256,1024]{2,1,0:T(8,128)(2,1)} collective-permute-done((bf16[1,256,1024]{2,1,0:T(8,128)(2,1)S(1)}, bf16[1,256,1024]{2,1,0:T(8,128)(2,1)}, u32[]{:S(2)}, u32[]{:S(2)}) %collective-permute-start.9) | collective-permute-done | bytes 524320 | tf_op jit(solution)/shard_map/ppermute | solution.py:332
  61.4 1.5 %collective-permute-start.14 = (bf16[1024,256]{1,0:T(8,128)(2,1)S(1)}, bf16[1024,256]{1,0:T(8,128)(2,1)S(1)}, u32[]{:S(2)}, u32[]{:S(2)}) collective-permute-start(bf16[1024,256]{1,0:T(8,128)(2,1)S(1)} %collective-permute-done.5.refs_8_), channel_id=1, source_target_pairs={{0,16},{1,17},{2,18},{3,19},{4,20},{5,21},{6,22},{7,23},{8,24},{9,... | collective-permute-start | bytes 1572872 | tf_op jit(solution)/shard_map/ppermute | solution.py:332
  64.4 11.1 %collective-permute-done.14.refs_9_ = bf16[1024,256]{1,0:T(8,128)(2,1)S(1)} collective-permute-done((bf16[1024,256]{1,0:T(8,128)(2,1)S(1)}, bf16[1024,256]{1,0:T(8,128)(2,1)S(1)}, u32[]{:S(2)}, u32[]{:S(2)}) %collective-permute-start.14) | collective-permute-done | bytes 524320 | tf_op jit(solution)/shard_map/ppermute | solution.py:332
  75.5 1.3 %collective-permute-done.23.refs_10_ = bf16[2,256,512]{2,1,0:T(8,128)(2,1)} collective-permute-done((bf16[2,256,512]{2,1,0:T(8,128)(2,1)S(1)}, bf16[2,256,512]{2,1,0:T(8,128)(2,1)}, u32[]{:S(2)}, u32[]{:S(2)}) %collective-permute-start.23) | collective-permute-done | bytes 524320 | tf_op jit(solution)/shard_map/ppermute | solution.py:332
  80.2 7.8 %partial_sums.1 = (f32[128,512]{1,0:T(8,128)}, bf16[128,512]{1,0:T(8,128)(2,1)}) custom-call(bf16[8,128,1024]{2,1,0:T(8,128)(2,1)} %get-tuple-element.46.refs_0_, bf16[8,128,1024]{2,1,0:T(8,128)(2,1)} %copy-done.2, bf16[1024,256]{1,0:T(8,128)(2,1)} %refs_2_.1, bf16[1024,256]{1,0:T(8,128)(2,1)} %refs_3_.1, bf16[1024,256]{1,0:T(8,128)(2,1)} %collective-permute-done.1.refs_4_, ...), custom_call_target="tpu_custom_call" | custom-call | flops 2147483648 | bytes 12582912 | tf_op jit(solution)/shard_map/partial_sums/pallas_call | solution.py:178
  88.0 1.6 %collective-permute-start.22 = (bf16[128,512]{1,0:T(8,128)(2,1)}, bf16[128,512]{1,0:T(8,128)(2,1)S(1)}, u32[]{:S(2)}, u32[]{:S(2)}) collective-permute-start(bf16[128,512]{1,0:T(8,128)(2,1)} %get-tuple-element.52), channel_id=1, source_target_pairs={{0,2},{1,3},{2,0},{3,1},{4,6},{5,7},{6,4},{7,5},{8,10},{9,11},{10,... | collective-permute-start | bytes 393224 | tf_op jit(solution)/shard_map/ppermute | solution.py:332
  90.2 1.4 %collective-permute-done.26.refs_13_ = bf16[1,256,1024]{2,1,0:T(8,128)(2,1)S(1)} collective-permute-done((bf16[1,256,1024]{2,1,0:T(8,128)(2,1)}, bf16[1,256,1024]{2,1,0:T(8,128)(2,1)S(1)}, u32[]{:S(2)}, u32[]{:S(2)}) %collective-permute-start.26) | collective-permute-done | bytes 524320 | tf_op jit(solution)/shard_map/ppermute | solution.py:332
  91.5 1.2 %collective-permute-done.25.refs_12_ = bf16[1,256,1024]{2,1,0:T(8,128)(2,1)} collective-permute-done((bf16[1,256,1024]{2,1,0:T(8,128)(2,1)}, bf16[1,256,1024]{2,1,0:T(8,128)(2,1)}, u32[]{:S(2)}, u32[]{:S(2)}) %collective-permute-start.25) | collective-permute-done | bytes 524320 | tf_op jit(solution)/shard_map/ppermute | solution.py:332
  93.7 1.9 %collective-permute-start.31 = (bf16[1,256,512]{2,1,0:T(8,128)(2,1)S(1)}, bf16[1,256,512]{2,1,0:T(8,128)(2,1)S(1)}, u32[]{:S(2)}, u32[]{:S(2)}) collective-permute-start(bf16[1,256,512]{2,1,0:T(8,128)(2,1)S(1)} %slice.14), channel_id=1, source_target_pairs={{0,4},{1,5},{2,6},{3,7},{4,0},{5,1},{6,2},{7,3},{8,12},{9,13},{10,... | collective-permute-start | bytes 786440 | tf_op jit(solution)/shard_map/ppermute | solution.py:332
  96.4 4.8 %down_first.1 = (bf16[128,16384]{1,0:T(8,128)(2,1)}, bf16[128,256]{1,0:T(8,128)(2,1)}) custom-call(s32[1]{0:T(128)S(6)} %copy.10.live_ref, s32[16]{0:T(128)} %owner_ref.5, f32[128,512]{1,0:T(8,128)} %get-tuple-element.51.refs_0_, bf16[128,512]{1,0:T(8,128)(2,1)} %copy-done.29, bf16[1,256,1024]{2,1,0:T(8,128)(2,1)} %bitcast.4, bf16[1,256,512]{2,1,0:T(8,128)(2,1)} %copy-done, ...), custom_call_target="tpu_custom_call" | custom-call | flops 6710886400 | bytes 7864320 | tf_op jit(solution)/shard_map/down_first/pallas_call | solution.py:274
  102.4 1.5 %collective-permute-done.33.refs_6_ = bf16[1,256,512]{2,1,0:T(8,128)(2,1)S(1)} collective-permute-done((bf16[1,256,512]{2,1,0:T(8,128)(2,1)S(1)}, bf16[1,256,512]{2,1,0:T(8,128)(2,1)S(1)}, u32[]{:S(2)}, u32[]{:S(2)}) %collective-permute-start.33) | collective-permute-done | bytes 262176 | tf_op jit(solution)/shard_map/ppermute | solution.py:332
  104.1 2.1 %collective-permute-done.34.refs_7_ = bf16[1,256,512]{2,1,0:T(8,128)(2,1)S(1)} collective-permute-done((bf16[1,256,512]{2,1,0:T(8,128)(2,1)S(1)}, bf16[1,256,512]{2,1,0:T(8,128)(2,1)S(1)}, u32[]{:S(2)}, u32[]{:S(2)}) %collective-permute-start.34) | collective-permute-done | bytes 262176 | tf_op jit(solution)/shard_map/ppermute | solution.py:332
  107.7 3.6 %down_second.1 = bf16[128,16384]{1,0:T(8,128)(2,1)} custom-call(s32[16]{0:T(128)} %owner_ref.5, bf16[128,256]{1,0:T(8,128)(2,1)} %get-tuple-element.57.hidden_ref, bf16[128,16384]{1,0:T(8,128)(2,1)} %get-tuple-element.58._, bf16[2,256,512]{2,1,0:T(8,128)(2,1)} %copy-done.18, bf16[2,256,512]{2,1,0:T(8,128)(2,1)} %copy-done.19, ...), custom_call_target="tpu_custom_call", output_to_operand_aliasing={{}: (2, {})} | custom-call | flops 4026531840 | bytes 4718592 | tf_op jit(solution)/shard_map/down_second/pallas_call | solution.py:274
  (115 shorter events, 13.9 us)
Async XLA Ops:
  1.1 14.7 %collective-permute-start.3 = (bf16[1,256,512]{2,1,0:T(8,128)(2,1)S(1)}, bf16[1,256,512]{2,1,0:T(8,128)(2,1)S(1)}, u32[]{:S(2)}, u32[]{:S(2)}) collective-permute-start(bf16[1,256,512]{2,1,0:T(8,128)(2,1)S(1)} %select_bitcast_fusion.a_ref), channel_id=1, source_target_pairs={{0,2},{1,3},{2,0},{3,1},{4,6},{5,7},{6,4},{7,5},{8,10},{9,11},{10,... | collective-permute-start | bytes 786440 | tf_op jit(solution)/shard_map/ppermute | solution.py:332
  6.0 25.8 %collective-permute-start = (bf16[1024,256]{1,0:T(8,128)(2,1)}, bf16[1024,256]{1,0:T(8,128)(2,1)S(1)}, u32[]{:S(2)}, u32[]{:S(2)}) collective-permute-start(bf16[1024,256]{1,0:T(8,128)(2,1)} %broadcast_select_fusion), channel_id=1, source_target_pairs={{0,8},{1,9},{2,10},{3,11},{4,12},{5,13},{6,14},{7,15},{8,0},{9,1},... | collective-permute-start | bytes 1572872 | tf_op jit(solution)/shard_map/ppermute | solution.py:332
  8.5 23.5 %collective-permute-start.1 = (bf16[1024,256]{1,0:T(8,128)(2,1)}, bf16[1024,256]{1,0:T(8,128)(2,1)}, u32[]{:S(2)}, u32[]{:S(2)}) collective-permute-start(bf16[1024,256]{1,0:T(8,128)(2,1)} %broadcast_select_fusion), channel_id=1, source_target_pairs={{0,4},{1,5},{2,6},{3,7},{4,0},{5,1},{6,2},{7,3},{8,12},{9,13},{10,... | collective-permute-start | bytes 1572872 | tf_op jit(solution)/shard_map/ppermute | solution.py:332
  10.1 22.0 %collective-permute-start.2 = (bf16[1024,256]{1,0:T(8,128)(2,1)}, bf16[1024,256]{1,0:T(8,128)(2,1)}, u32[]{:S(2)}, u32[]{:S(2)}) collective-permute-start(bf16[1024,256]{1,0:T(8,128)(2,1)} %refs_2_.1), channel_id=1, source_target_pairs={{0,1},{1,0},{2,3},{3,2},{4,5},{5,4},{6,7},{7,6},{8,9},{9,8},{10,11... | collective-permute-start | bytes 1572872 | tf_op jit(solution)/shard_map/ppermute | solution.py:332
  15.8 16.3 %collective-permute-start.4 = (bf16[1,256,512]{2,1,0:T(8,128)(2,1)S(1)}, bf16[1,256,512]{2,1,0:T(8,128)(2,1)S(1)}, u32[]{:S(2)}, u32[]{:S(2)}) collective-permute-start(bf16[1,256,512]{2,1,0:T(8,128)(2,1)S(1)} %collective-permute-done.3.b_ref.refs_3_), channel_id=1, source_target_pairs={{0,16},{1,17},{2,18},{3,19},{4,20},{5,21},{6,22},{7,23},{8,24},{9,... | collective-permute-start | bytes 786440 | tf_op jit(solution)/shard_map/ppermute | solution.py:332
  17.4 59.4 %collective-permute-start.11 = (bf16[8,128,1024]{2,1,0:T(8,128)(2,1)}, bf16[8,128,1024]{2,1,0:T(8,128)(2,1)S(1)}, u32[]{:S(2)}, u32[]{:S(2)}) collective-permute-start(bf16[8,128,1024]{2,1,0:T(8,128)(2,1)} %get-tuple-element.37), channel_id=1, source_target_pairs={{0,2},{1,3},{2,0},{3,1},{4,6},{5,7},{6,4},{7,5},{8,10},{9,11},{10,... | collective-permute-start | bytes 6291464 | tf_op jit(solution)/shard_map/ppermute | solution.py:332
  32.1 23.6 %collective-permute-start.5 = (bf16[1024,256]{1,0:T(8,128)(2,1)S(1)}, bf16[1024,256]{1,0:T(8,128)(2,1)S(1)}, u32[]{:S(2)}, u32[]{:S(2)}) collective-permute-start(bf16[1024,256]{1,0:T(8,128)(2,1)S(1)} %collective-permute-done.refs_6_), channel_id=1, source_target_pairs={{0,4},{1,5},{2,6},{3,7},{4,0},{5,1},{6,2},{7,3},{8,12},{9,13},{10,... | collective-permute-start | bytes 1572872 | tf_op jit(solution)/shard_map/ppermute | solution.py:332
  33.6 25.4 %collective-permute-start.9 = (bf16[1,256,1024]{2,1,0:T(8,128)(2,1)S(1)}, bf16[1,256,1024]{2,1,0:T(8,128)(2,1)}, u32[]{:S(2)}, u32[]{:S(2)}) collective-permute-start(bf16[1,256,1024]{2,1,0:T(8,128)(2,1)S(1)} %bitcast.5), channel_id=1, source_target_pairs={{0,8},{1,9},{2,10},{3,11},{4,12},{5,13},{6,14},{7,15},{8,0},{9,1},... | collective-permute-start | bytes 1572872 | tf_op jit(solution)/shard_map/ppermute | solution.py:332
  35.9 23.2 %collective-permute-start.12 = (bf16[1024,256]{1,0:T(8,128)(2,1)}, bf16[1024,256]{1,0:T(8,128)(2,1)S(1)}, u32[]{:S(2)}, u32[]{:S(2)}) collective-permute-start(bf16[1024,256]{1,0:T(8,128)(2,1)} %collective-permute-done.1.refs_4_), channel_id=1, source_target_pairs={{0,16},{1,17},{2,18},{3,19},{4,20},{5,21},{6,22},{7,23},{8,24},{9,... | collective-permute-start | bytes 1572872 | tf_op jit(solution)/shard_map/ppermute | solution.py:332
  37.4 23.2 %collective-permute-start.13 = (bf16[1024,256]{1,0:T(8,128)(2,1)S(1)}, bf16[1024,256]{1,0:T(8,128)(2,1)S(1)}, u32[]{:S(2)}, u32[]{:S(2)}) collective-permute-start(bf16[1024,256]{1,0:T(8,128)(2,1)S(1)} %collective-permute-done.refs_6_), channel_id=1, source_target_pairs={{0,16},{1,17},{2,18},{3,19},{4,20},{5,21},{6,22},{7,23},{8,24},{9,... | collective-permute-start | bytes 1572872 | tf_op jit(solution)/shard_map/ppermute | solution.py:332
  55.7 4.9 %collective-permute-start.16 = (bf16[1024,256]{1,0:T(8,128)(2,1)}, bf16[1024,256]{1,0:T(8,128)(2,1)S(1)}, u32[]{:S(2)}, u32[]{:S(2)}) collective-permute-start(bf16[1024,256]{1,0:T(8,128)(2,1)} %collective-permute-done.1.refs_4_), channel_id=1, source_target_pairs={{0,1},{1,0},{2,3},{3,2},{4,5},{5,4},{6,7},{7,6},{8,9},{9,8},{10,11... | collective-permute-start | bytes 1572872 | tf_op jit(solution)/shard_map/ppermute | solution.py:332
  61.4 14.1 %collective-permute-start.14 = (bf16[1024,256]{1,0:T(8,128)(2,1)S(1)}, bf16[1024,256]{1,0:T(8,128)(2,1)S(1)}, u32[]{:S(2)}, u32[]{:S(2)}) collective-permute-start(bf16[1024,256]{1,0:T(8,128)(2,1)S(1)} %collective-permute-done.5.refs_8_), channel_id=1, source_target_pairs={{0,16},{1,17},{2,18},{3,19},{4,20},{5,21},{6,22},{7,23},{8,24},{9,... | collective-permute-start | bytes 1572872 | tf_op jit(solution)/shard_map/ppermute | solution.py:332
  62.9 13.9 %collective-permute-start.23 = (bf16[2,256,512]{2,1,0:T(8,128)(2,1)S(1)}, bf16[2,256,512]{2,1,0:T(8,128)(2,1)}, u32[]{:S(2)}, u32[]{:S(2)}) collective-permute-start(bf16[2,256,512]{2,1,0:T(8,128)(2,1)S(1)} %stack_halves.1), channel_id=1, source_target_pairs={{0,4},{1,5},{2,6},{3,7},{4,0},{5,1},{6,2},{7,3},{8,12},{9,13},{10,... | collective-permute-start | bytes 1572872 | tf_op jit(solution)/shard_map/ppermute | solution.py:332
  63.6 13.8 %collective-permute-start.15 = (bf16[1024,256]{1,0:T(8,128)(2,1)S(1)}, bf16[1024,256]{1,0:T(8,128)(2,1)S(1)}, u32[]{:S(2)}, u32[]{:S(2)}) collective-permute-start(bf16[1024,256]{1,0:T(8,128)(2,1)S(1)} %copy-done.1), channel_id=1, source_target_pairs={{0,1},{1,0},{2,3},{3,2},{4,5},{5,4},{6,7},{7,6},{8,9},{9,8},{10,11... | collective-permute-start | bytes 1572872 | tf_op jit(solution)/shard_map/ppermute | solution.py:332
  64.4 13.4 %collective-permute-start.17 = (bf16[1024,256]{1,0:T(8,128)(2,1)S(1)}, bf16[1024,256]{1,0:T(8,128)(2,1)S(1)}, u32[]{:S(2)}, u32[]{:S(2)}) collective-permute-start(bf16[1024,256]{1,0:T(8,128)(2,1)S(1)} %collective-permute-done.12.refs_5_), channel_id=1, source_target_pairs={{0,1},{1,0},{2,3},{3,2},{4,5},{5,4},{6,7},{7,6},{8,9},{9,8},{10,11... | collective-permute-start | bytes 1572872 | tf_op jit(solution)/shard_map/ppermute | solution.py:332
  77.4 14.2 %collective-permute-start.26 = (bf16[1,256,1024]{2,1,0:T(8,128)(2,1)}, bf16[1,256,1024]{2,1,0:T(8,128)(2,1)S(1)}, u32[]{:S(2)}, u32[]{:S(2)}) collective-permute-start(bf16[1,256,1024]{2,1,0:T(8,128)(2,1)} %collective-permute-done.9.refs_5_), channel_id=1, source_target_pairs={{0,4},{1,5},{2,6},{3,7},{4,0},{5,1},{6,2},{7,3},{8,12},{9,13},{10,... | collective-permute-start | bytes 1572872 | tf_op jit(solution)/shard_map/ppermute | solution.py:332
  77.8 14.9 %collective-permute-start.25 = (bf16[1,256,1024]{2,1,0:T(8,128)(2,1)}, bf16[1,256,1024]{2,1,0:T(8,128)(2,1)}, u32[]{:S(2)}, u32[]{:S(2)}) collective-permute-start(bf16[1,256,1024]{2,1,0:T(8,128)(2,1)} %collective-permute-done.9.refs_5_), channel_id=1, source_target_pairs={{0,2},{1,3},{2,0},{3,1},{4,6},{5,7},{6,4},{7,5},{8,10},{9,11},{10,... | collective-permute-start | bytes 1572872 | tf_op jit(solution)/shard_map/ppermute | solution.py:332
  78.3 17.4 %collective-permute-start.24 = (bf16[2,256,512]{2,1,0:T(8,128)(2,1)}, bf16[2,256,512]{2,1,0:T(8,128)(2,1)}, u32[]{:S(2)}, u32[]{:S(2)}) collective-permute-start(bf16[2,256,512]{2,1,0:T(8,128)(2,1)} %collective-permute-done.23.refs_10_), channel_id=1, source_target_pairs={{0,16},{1,17},{2,18},{3,19},{4,20},{5,21},{6,22},{7,23},{8,24},{9,... | collective-permute-start | bytes 1572872 | tf_op jit(solution)/shard_map/ppermute | solution.py:332
  88.0 7.8 %collective-permute-start.22 = (bf16[128,512]{1,0:T(8,128)(2,1)}, bf16[128,512]{1,0:T(8,128)(2,1)S(1)}, u32[]{:S(2)}, u32[]{:S(2)}) collective-permute-start(bf16[128,512]{1,0:T(8,128)(2,1)} %get-tuple-element.52), channel_id=1, source_target_pairs={{0,2},{1,3},{2,0},{3,1},{4,6},{5,7},{6,4},{7,5},{8,10},{9,11},{10,... | collective-permute-start | bytes 393224 | tf_op jit(solution)/shard_map/ppermute | solution.py:332
  93.7 8.1 %collective-permute-start.31 = (bf16[1,256,512]{2,1,0:T(8,128)(2,1)S(1)}, bf16[1,256,512]{2,1,0:T(8,128)(2,1)S(1)}, u32[]{:S(2)}, u32[]{:S(2)}) collective-permute-start(bf16[1,256,512]{2,1,0:T(8,128)(2,1)S(1)} %slice.14), channel_id=1, source_target_pairs={{0,4},{1,5},{2,6},{3,7},{4,0},{5,1},{6,2},{7,3},{8,12},{9,13},{10,... | collective-permute-start | bytes 786440 | tf_op jit(solution)/shard_map/ppermute | solution.py:332
  95.7 6.7 %collective-permute-start.32 = (bf16[1,256,512]{2,1,0:T(8,128)(2,1)S(1)}, bf16[1,256,512]{2,1,0:T(8,128)(2,1)S(1)}, u32[]{:S(2)}, u32[]{:S(2)}) collective-permute-start(bf16[1,256,512]{2,1,0:T(8,128)(2,1)S(1)} %slice.15), channel_id=1, source_target_pairs={{0,2},{1,3},{2,0},{3,1},{4,6},{5,7},{6,4},{7,5},{8,10},{9,11},{10,... | collective-permute-start | bytes 786440 | tf_op jit(solution)/shard_map/ppermute | solution.py:332
  101.2 5.0 %collective-permute-start.27 = (bf16[2,256,512]{2,1,0:T(8,128)(2,1)}, bf16[2,256,512]{2,1,0:T(8,128)(2,1)S(1)}, u32[]{:S(2)}, u32[]{:S(2)}) collective-permute-start(bf16[2,256,512]{2,1,0:T(8,128)(2,1)} %collective-permute-done.23.refs_10_), channel_id=1, source_target_pairs={{0,1},{1,0},{2,3},{3,2},{4,5},{5,4},{6,7},{7,6},{8,9},{9,8},{10,11... | collective-permute-start | bytes 1572872 | tf_op jit(solution)/shard_map/ppermute | solution.py:332
  101.3 4.9 %collective-permute-start.28 = (bf16[2,256,512]{2,1,0:T(8,128)(2,1)}, bf16[2,256,512]{2,1,0:T(8,128)(2,1)S(1)}, u32[]{:S(2)}, u32[]{:S(2)}) collective-permute-start(bf16[2,256,512]{2,1,0:T(8,128)(2,1)} %collective-permute-done.24.refs_11_), channel_id=1, source_target_pairs={{0,1},{1,0},{2,3},{3,2},{4,5},{5,4},{6,7},{7,6},{8,9},{9,8},{10,11... | collective-permute-start | bytes 1572872 | tf_op jit(solution)/shard_map/ppermute | solution.py:332
  101.9 4.3 %collective-permute-start.29 = (bf16[1,256,1024]{2,1,0:T(8,128)(2,1)}, bf16[1,256,1024]{2,1,0:T(8,128)(2,1)S(1)}, u32[]{:S(2)}, u32[]{:S(2)}) collective-permute-start(bf16[1,256,1024]{2,1,0:T(8,128)(2,1)} %collective-permute-done.25.refs_12_), channel_id=1, source_target_pairs={{0,1},{1,0},{2,3},{3,2},{4,5},{5,4},{6,7},{7,6},{8,9},{9,8},{10,11... | collective-permute-start | bytes 1572872 | tf_op jit(solution)/shard_map/ppermute | solution.py:332
  (41 other events, 343.1 us)

commit v11 on v9

--- a/solution.py
+++ b/solution.py
@@ -347,7 +347,6 @@
         return swap(weights, core), tuple((turn ^ 1, plane) for turn, plane in parts)
 
     own = [(down_weight[None], ((0, 0),))]
-    own = own + [cross(*w) for w in own]
     gate_c, up_c = swap(gate_weight, core), swap(up_weight, core)
     d0 = stacked(
         after(mine, a1, a2, t2, gate_c), mine_x, 10**11
@@ -365,12 +364,11 @@
     d3 = swap(after(d2, d1), near)
     f2 = swap(after(d2, r2), across)
 
-    second = [(mine_x, ((2, 0),)), (rest_x, ((2, 1),)), (d2, ((8, 0),))]
-    second = second + [cross(*w) for w in second]
+    second = own + [(mine_x, ((2, 0),)), (rest_x, ((2, 1),)), (d2, ((8, 0),))]
     weights = (gate_weight, up_weight, a1, b1, a2, b2, a3, b3)
     weights = weights + (gate_c, up_c) + tuple(swap(w, core) for w in weights[2:])
-    crossings = (own[1][0], *(w for w, _ in second[3:]))
-    p0, p2 = partial_sums((after(t0, *crossings), r2), weights, (F32, BF16))
+    held = [cross(after(w, b1, b2, a3), parts) for w, parts in (second[0], second[3])]
+    p0, p2 = partial_sums((after(t0, held[0][0], held[1][0]), r2), weights, (F32, BF16))
     q2 = swap(p2, across)
 
     f3 = swap(after(f2, d3, p2)[:, :, :half], near)
@@ -382,7 +380,7 @@
         (f2, ((10, 0),)),
         (d3, ((12, 0),)),
     ]
-    early = own + second + third
+    early = second + held + [cross(after(w, q2), parts) for w, parts in second[1:3]] + third
     out = pltpu.HBM(tokens.shape, BF16)
     rows, hid = tokens.shape[0], gate_weight.shape[1]
     product, hidden = down_call(

time: 113 us -> 114 us (level)
  local copies, waits for them, and re-layouts: 4.82 us -> 6.19 us
    unnamed x56 -> x60, local copies, waits for them, and re-layouts: 2.89 us -> 4.26 us
  transfers between devices with their start and end apart: 35 -> 35, of which waited for: 14 -> 12; matrix products, arithmetic and copies ran while one was open for 3% -> 3% of each run, Pallas kernels for 16% -> 16%
where the time goes in v11:
time: 114 us; the launch traced here: 113 us
  waiting for transfers between devices  56.2 us (49%)
  starting transfers between devices  25.3 us (22%)
  Pallas kernels  21.9 us (19%)
  local copies, waits for them, and re-layouts  6.19 us (5%)
  other arithmetic  2.95 us (3%)
    ppermute x35, waiting for transfers between devices, swap(): return lax.ppermute(value, ALL, pairs)  56.2 us
    ppermute x35, starting transfers between devices, swap(): return lax.ppermute(value, ALL, pairs)  25.3 us
    pallas_call x2, Pallas kernels, down_call(): pl.pallas_call(functools.partial(kernel, pieces), in_specs=[SMEM] * len(l...  8.44 us
    pallas_call x1, Pallas kernels, partial_sums(): pl.pallas_call(functools.partial(partial_kernel, kinds), in_specs=[HBM] *...  7.81 us
    pallas_call x1, Pallas kernels, normed_halves(): pl.pallas_call(norm_kernel, in_specs=[SMEM, HBM, VMEM], out_specs=[HBM] *...  5.65 us
    unnamed x60, local copies, waits for them, and re-layouts  4.26 us
  transfers between devices with their start and end apart: 35, of which 12 were waited for; matrix products, arithmetic and copies ran while one was open for 3% of the time, Pallas kernels for 16%

profile of v11, /device:TPU:0, one launch (start us, length us, event | category | flops | bytes accessed | tf_op | source)
XLA Modules:
  0.0 113.5 jit_solution(17132062381555900625)
XLA Ops:
  0.0 1.9 %broadcast_select_fusion = bf16[1024,256]{1,0:T(8,128)(2,1)} fusion(bf16[1024,256]{1,0:T(8,128)(2,1)} %refs_2_.1, bf16[1024,256]{1,0:T(8,128)(2,1)} %refs_3_.1, pred[]{:T(512)S(6)} %eq.3), kind=kLoop, calls=%fused_computation | loop fusion | flops 262144 | bytes 1572865 | tf_op jit(solution)/shard_map/jit(_where)/select_n | solution.py:335
  1.9 3.0 %collective-permute-start = (bf16[1024,256]{1,0:T(8,128)(2,1)}, bf16[1024,256]{1,0:T(8,128)(2,1)S(1)}, u32[]{:S(2)}, u32[]{:S(2)}) collective-permute-start(bf16[1024,256]{1,0:T(8,128)(2,1)} %broadcast_select_fusion), channel_id=1, source_target_pairs={{0,4},{1,5},{2,6},{3,7},{4,0},{5,1},{6,2},{7,3},{8,12},{9,13},{10,... | collective-permute-start | bytes 1572872 | tf_op jit(solution)/shard_map/ppermute | solution.py:332
  4.9 2.6 %collective-permute-start.1 = (bf16[1024,256]{1,0:T(8,128)(2,1)}, bf16[1024,256]{1,0:T(8,128)(2,1)}, u32[]{:S(2)}, u32[]{:S(2)}) collective-permute-start(bf16[1024,256]{1,0:T(8,128)(2,1)} %broadcast_select_fusion), channel_id=1, source_target_pairs={{0,8},{1,9},{2,10},{3,11},{4,12},{5,13},{6,14},{7,15},{8,0},{9,1},... | collective-permute-start | bytes 1572872 | tf_op jit(solution)/shard_map/ppermute | solution.py:332
  8.6 1.6 %collective-permute-start.3 = (bf16[1,256,512]{2,1,0:T(8,128)(2,1)S(1)}, bf16[1,256,512]{2,1,0:T(8,128)(2,1)S(1)}, u32[]{:S(2)}, u32[]{:S(2)}) collective-permute-start(bf16[1,256,512]{2,1,0:T(8,128)(2,1)S(1)} %select_bitcast_fusion.a_ref), channel_id=1, source_target_pairs={{0,2},{1,3},{2,0},{3,1},{4,6},{5,7},{6,4},{7,5},{8,10},{9,11},{10,... | collective-permute-start | bytes 786440 | tf_op jit(solution)/shard_map/ppermute | solution.py:332
  10.1 5.7 %norm_halves.1 = (bf16[8,128,1024]{2,1,0:T(8,128)(2,1)}, bf16[8,128,1024]{2,1,0:T(8,128)(2,1)}) custom-call(s32[16]{0:T(128)} %owner_ref.5, bf16[128,16384]{1,0:T(8,128)(2,1)} %tokens_ref.1, f32[1,16384]{1,0:T(1,128)} %bitcast.7), custom_call_target="tpu_custom_call" | custom-call | flops 12582912 | bytes 8388608 | tf_op jit(solution)/shard_map/norm_halves/pallas_call | solution.py:97
  18.9 9.3 %collective-permute-done.refs_4_ = bf16[1024,256]{1,0:T(8,128)(2,1)S(1)} collective-permute-done((bf16[1024,256]{1,0:T(8,128)(2,1)}, bf16[1024,256]{1,0:T(8,128)(2,1)S(1)}, u32[]{:S(2)}, u32[]{:S(2)}) %collective-permute-start) | collective-permute-done | bytes 524320 | tf_op jit(solution)/shard_map/ppermute | solution.py:332
  28.1 2.7 %collective-permute-done.1.refs_6_ = bf16[1024,256]{1,0:T(8,128)(2,1)} collective-permute-done((bf16[1024,256]{1,0:T(8,128)(2,1)}, bf16[1024,256]{1,0:T(8,128)(2,1)}, u32[]{:S(2)}, u32[]{:S(2)}) %collective-permute-start.1) | collective-permute-done | bytes 524320 | tf_op jit(solution)/shard_map/ppermute | solution.py:332
  30.9 1.6 %collective-permute-start.5 = (bf16[1024,256]{1,0:T(8,128)(2,1)S(1)}, bf16[1024,256]{1,0:T(8,128)(2,1)S(1)}, u32[]{:S(2)}, u32[]{:S(2)}) collective-permute-start(bf16[1024,256]{1,0:T(8,128)(2,1)S(1)} %collective-permute-done.refs_4_), channel_id=1, source_target_pairs={{0,16},{1,17},{2,18},{3,19},{4,20},{5,21},{6,22},{7,23},{8,24},{9,... | collective-permute-start | bytes 1572872 | tf_op jit(solution)/shard_map/ppermute | solution.py:332
  33.4 2.6 %collective-permute-start.9 = (bf16[1,256,1024]{2,1,0:T(8,128)(2,1)S(1)}, bf16[1,256,1024]{2,1,0:T(8,128)(2,1)}, u32[]{:S(2)}, u32[]{:S(2)}) collective-permute-start(bf16[1,256,1024]{2,1,0:T(8,128)(2,1)S(1)} %bitcast.5), channel_id=1, source_target_pairs={{0,8},{1,9},{2,10},{3,11},{4,12},{5,13},{6,14},{7,15},{8,0},{9,1},... | collective-permute-start | bytes 1572872 | tf_op jit(solution)/shard_map/ppermute | solution.py:332
  36.0 9.8 %collective-permute-done.5.refs_5_ = bf16[1024,256]{1,0:T(8,128)(2,1)S(1)} collective-permute-done((bf16[1024,256]{1,0:T(8,128)(2,1)S(1)}, bf16[1024,256]{1,0:T(8,128)(2,1)S(1)}, u32[]{:S(2)}, u32[]{:S(2)}) %collective-permute-start.5) | collective-permute-done | bytes 524320 | tf_op jit(solution)/shard_map/ppermute | solution.py:332
  45.8 6.9 %collective-permute-done.6.refs_7_ = bf16[1024,256]{1,0:T(8,128)(2,1)S(1)} collective-permute-done((bf16[1024,256]{1,0:T(8,128)(2,1)}, bf16[1024,256]{1,0:T(8,128)(2,1)S(1)}, u32[]{:S(2)}, u32[]{:S(2)}) %collective-permute-start.6) | collective-permute-done | bytes 524320 | tf_op jit(solution)/shard_map/ppermute | solution.py:332
  52.7 1.5 %collective-permute-done.7.refs_8_ = bf16[1024,256]{1,0:T(8,128)(2,1)S(1)} collective-permute-done((bf16[1024,256]{1,0:T(8,128)(2,1)}, bf16[1024,256]{1,0:T(8,128)(2,1)S(1)}, u32[]{:S(2)}, u32[]{:S(2)}) %collective-permute-start.7) | collective-permute-done | bytes 524320 | tf_op jit(solution)/shard_map/ppermute | solution.py:332
  54.3 3.3 %collective-permute-done.9.refs_5_ = bf16[1,256,1024]{2,1,0:T(8,128)(2,1)} collective-permute-done((bf16[1,256,1024]{2,1,0:T(8,128)(2,1)S(1)}, bf16[1,256,1024]{2,1,0:T(8,128)(2,1)}, u32[]{:S(2)}, u32[]{:S(2)}) %collective-permute-start.9) | collective-permute-done | bytes 524320 | tf_op jit(solution)/shard_map/ppermute | solution.py:332
  57.6 1.6 %collective-permute-start.12 = (bf16[1024,256]{1,0:T(8,128)(2,1)S(1)}, bf16[1024,256]{1,0:T(8,128)(2,1)S(1)}, u32[]{:S(2)}, u32[]{:S(2)}) collective-permute-start(bf16[1024,256]{1,0:T(8,128)(2,1)S(1)} %collective-permute-done.7.refs_8_), channel_id=1, source_target_pairs={{0,16},{1,17},{2,18},{3,19},{4,20},{5,21},{6,22},{7,23},{8,24},{9,... | collective-permute-start | bytes 1572872 | tf_op jit(solution)/shard_map/ppermute | solution.py:332
  60.8 11.1 %collective-permute-done.12.refs_9_ = bf16[1024,256]{1,0:T(8,128)(2,1)S(1)} collective-permute-done((bf16[1024,256]{1,0:T(8,128)(2,1)S(1)}, bf16[1024,256]{1,0:T(8,128)(2,1)S(1)}, u32[]{:S(2)}, u32[]{:S(2)}) %collective-permute-start.12) | collective-permute-done | bytes 524320 | tf_op jit(solution)/shard_map/ppermute | solution.py:332
  74.6 1.6 %collective-permute-start.25 = (bf16[1,256,1024]{2,1,0:T(8,128)(2,1)}, bf16[1,256,1024]{2,1,0:T(8,128)(2,1)}, u32[]{:S(2)}, u32[]{:S(2)}) collective-permute-start(bf16[1,256,1024]{2,1,0:T(8,128)(2,1)} %collective-permute-done.9.refs_5_), channel_id=1, source_target_pairs={{0,2},{1,3},{2,0},{3,1},{4,6},{5,7},{6,4},{7,5},{8,10},{9,11},{10,... | collective-permute-start | bytes 1572872 | tf_op jit(solution)/shard_map/ppermute | solution.py:332
  77.0 7.8 %partial_sums.1 = (f32[128,512]{1,0:T(8,128)}, bf16[128,512]{1,0:T(8,128)(2,1)}) custom-call(bf16[8,128,1024]{2,1,0:T(8,128)(2,1)} %get-tuple-element.45.refs_0_, bf16[8,128,1024]{2,1,0:T(8,128)(2,1)} %copy-done.2, bf16[1024,256]{1,0:T(8,128)(2,1)} %refs_2_.1, bf16[1024,256]{1,0:T(8,128)(2,1)} %refs_3_.1, bf16[1024,256]{1,0:T(8,128)(2,1)} %copy-done.3, ...), custom_call_target="tpu_custom_call" | custom-call | flops 2147483648 | bytes 12582912 | tf_op jit(solution)/shard_map/partial_sums/pallas_call | solution.py:178
  85.6 5.7 %collective-permute-done.20.refs_1_ = bf16[128,512]{1,0:T(8,128)(2,1)S(1)} collective-permute-done((bf16[128,512]{1,0:T(8,128)(2,1)}, bf16[128,512]{1,0:T(8,128)(2,1)S(1)}, u32[]{:S(2)}, u32[]{:S(2)}) %collective-permute-start.20) | collective-permute-done | bytes 131104 | tf_op jit(solution)/shard_map/ppermute | solution.py:332
  93.5 1.8 %collective-permute-start.31 = (bf16[1,256,512]{2,1,0:T(8,128)(2,1)S(1)}, bf16[1,256,512]{2,1,0:T(8,128)(2,1)S(1)}, u32[]{:S(2)}, u32[]{:S(2)}) collective-permute-start(bf16[1,256,512]{2,1,0:T(8,128)(2,1)S(1)} %slice.14), channel_id=1, source_target_pairs={{0,4},{1,5},{2,6},{3,7},{4,0},{5,1},{6,2},{7,3},{8,12},{9,13},{10,... | collective-permute-start | bytes 786440 | tf_op jit(solution)/shard_map/ppermute | solution.py:332
  96.2 1.6 %collective-permute-start.32 = (bf16[1,256,512]{2,1,0:T(8,128)(2,1)S(1)}, bf16[1,256,512]{2,1,0:T(8,128)(2,1)S(1)}, u32[]{:S(2)}, u32[]{:S(2)}) collective-permute-start(bf16[1,256,512]{2,1,0:T(8,128)(2,1)S(1)} %slice.15), channel_id=1, source_target_pairs={{0,2},{1,3},{2,0},{3,1},{4,6},{5,7},{6,4},{7,5},{8,10},{9,11},{10,... | collective-permute-start | bytes 786440 | tf_op jit(solution)/shard_map/ppermute | solution.py:332
  98.6 4.8 %down_first.1 = (bf16[128,16384]{1,0:T(8,128)(2,1)}, bf16[128,256]{1,0:T(8,128)(2,1)}) custom-call(s32[1]{0:T(128)S(6)} %copy.10.live_ref, s32[16]{0:T(128)} %owner_ref.5, f32[128,512]{1,0:T(8,128)} %get-tuple-element.47.refs_0_, bf16[128,512]{1,0:T(8,128)(2,1)} %copy-done.29, bf16[1,256,1024]{2,1,0:T(8,128)(2,1)} %bitcast.4, bf16[1,256,512]{2,1,0:T(8,128)(2,1)} %copy-done, ...), custom_call_target="tpu_custom_call" | custom-call | flops 6710886400 | bytes 7864320 | tf_op jit(solution)/shard_map/down_first/pallas_call | solution.py:274
  104.6 1.5 %collective-permute-done.33.refs_6_ = bf16[1,256,512]{2,1,0:T(8,128)(2,1)S(1)} collective-permute-done((bf16[1,256,512]{2,1,0:T(8,128)(2,1)S(1)}, bf16[1,256,512]{2,1,0:T(8,128)(2,1)S(1)}, u32[]{:S(2)}, u32[]{:S(2)}) %collective-permute-start.33) | collective-permute-done | bytes 262176 | tf_op jit(solution)/shard_map/ppermute | solution.py:332
  106.3 2.1 %collective-permute-done.34.refs_7_ = bf16[1,256,512]{2,1,0:T(8,128)(2,1)S(1)} collective-permute-done((bf16[1,256,512]{2,1,0:T(8,128)(2,1)S(1)}, bf16[1,256,512]{2,1,0:T(8,128)(2,1)S(1)}, u32[]{:S(2)}, u32[]{:S(2)}) %collective-permute-start.34) | collective-permute-done | bytes 262176 | tf_op jit(solution)/shard_map/ppermute | solution.py:332
  109.9 3.6 %down_second.1 = bf16[128,16384]{1,0:T(8,128)(2,1)} custom-call(s32[16]{0:T(128)} %owner_ref.5, bf16[128,256]{1,0:T(8,128)(2,1)} %get-tuple-element.55.hidden_ref, bf16[128,16384]{1,0:T(8,128)(2,1)} %get-tuple-element.56._, bf16[2,256,512]{2,1,0:T(8,128)(2,1)} %copy-done.18, bf16[2,256,512]{2,1,0:T(8,128)(2,1)} %copy-done.19, ...), custom_call_target="tpu_custom_call", output_to_operand_aliasing={{}: (2, {})} | custom-call | flops 4026531840 | bytes 4718592 | tf_op jit(solution)/shard_map/down_second/pallas_call | solution.py:274
  (115 shorter events, 17.0 us)
Async XLA Ops:
  1.9 26.3 %collective-permute-start = (bf16[1024,256]{1,0:T(8,128)(2,1)}, bf16[1024,256]{1,0:T(8,128)(2,1)S(1)}, u32[]{:S(2)}, u32[]{:S(2)}) collective-permute-start(bf16[1024,256]{1,0:T(8,128)(2,1)} %broadcast_select_fusion), channel_id=1, source_target_pairs={{0,4},{1,5},{2,6},{3,7},{4,0},{5,1},{6,2},{7,3},{8,12},{9,13},{10,... | collective-permute-start | bytes 1572872 | tf_op jit(solution)/shard_map/ppermute | solution.py:332
  4.9 25.9 %collective-permute-start.1 = (bf16[1024,256]{1,0:T(8,128)(2,1)}, bf16[1024,256]{1,0:T(8,128)(2,1)}, u32[]{:S(2)}, u32[]{:S(2)}) collective-permute-start(bf16[1024,256]{1,0:T(8,128)(2,1)} %broadcast_select_fusion), channel_id=1, source_target_pairs={{0,8},{1,9},{2,10},{3,11},{4,12},{5,13},{6,14},{7,15},{8,0},{9,1},... | collective-permute-start | bytes 1572872 | tf_op jit(solution)/shard_map/ppermute | solution.py:332
  7.5 23.3 %collective-permute-start.2 = (bf16[1024,256]{1,0:T(8,128)(2,1)}, bf16[1024,256]{1,0:T(8,128)(2,1)}, u32[]{:S(2)}, u32[]{:S(2)}) collective-permute-start(bf16[1024,256]{1,0:T(8,128)(2,1)} %refs_2_.1), channel_id=1, source_target_pairs={{0,1},{1,0},{2,3},{3,2},{4,5},{5,4},{6,7},{7,6},{8,9},{9,8},{10,11... | collective-permute-start | bytes 1572872 | tf_op jit(solution)/shard_map/ppermute | solution.py:332
  8.6 8.8 %collective-permute-start.3 = (bf16[1,256,512]{2,1,0:T(8,128)(2,1)S(1)}, bf16[1,256,512]{2,1,0:T(8,128)(2,1)S(1)}, u32[]{:S(2)}, u32[]{:S(2)}) collective-permute-start(bf16[1,256,512]{2,1,0:T(8,128)(2,1)S(1)} %select_bitcast_fusion.a_ref), channel_id=1, source_target_pairs={{0,2},{1,3},{2,0},{3,1},{4,6},{5,7},{6,4},{7,5},{8,10},{9,11},{10,... | collective-permute-start | bytes 786440 | tf_op jit(solution)/shard_map/ppermute | solution.py:332
  15.8 57.4 %collective-permute-start.11 = (bf16[8,128,1024]{2,1,0:T(8,128)(2,1)}, bf16[8,128,1024]{2,1,0:T(8,128)(2,1)S(1)}, u32[]{:S(2)}, u32[]{:S(2)}) collective-permute-start(bf16[8,128,1024]{2,1,0:T(8,128)(2,1)} %get-tuple-element.36), channel_id=1, source_target_pairs={{0,2},{1,3},{2,0},{3,1},{4,6},{5,7},{6,4},{7,5},{8,10},{9,11},{10,... | collective-permute-start | bytes 6291464 | tf_op jit(solution)/shard_map/ppermute | solution.py:332
  17.4 13.5 %collective-permute-start.4 = (bf16[1,256,512]{2,1,0:T(8,128)(2,1)S(1)}, bf16[1,256,512]{2,1,0:T(8,128)(2,1)S(1)}, u32[]{:S(2)}, u32[]{:S(2)}) collective-permute-start(bf16[1,256,512]{2,1,0:T(8,128)(2,1)S(1)} %collective-permute-done.3.b_ref.refs_3_), channel_id=1, source_target_pairs={{0,16},{1,17},{2,18},{3,19},{4,20},{5,21},{6,22},{7,23},{8,24},{9,... | collective-permute-start | bytes 786440 | tf_op jit(solution)/shard_map/ppermute | solution.py:332
  30.9 14.9 %collective-permute-start.5 = (bf16[1024,256]{1,0:T(8,128)(2,1)S(1)}, bf16[1024,256]{1,0:T(8,128)(2,1)S(1)}, u32[]{:S(2)}, u32[]{:S(2)}) collective-permute-start(bf16[1024,256]{1,0:T(8,128)(2,1)S(1)} %collective-permute-done.refs_4_), channel_id=1, source_target_pairs={{0,16},{1,17},{2,18},{3,19},{4,20},{5,21},{6,22},{7,23},{8,24},{9,... | collective-permute-start | bytes 1572872 | tf_op jit(solution)/shard_map/ppermute | solution.py:332
  32.5 20.3 %collective-permute-start.6 = (bf16[1024,256]{1,0:T(8,128)(2,1)}, bf16[1024,256]{1,0:T(8,128)(2,1)S(1)}, u32[]{:S(2)}, u32[]{:S(2)}) collective-permute-start(bf16[1024,256]{1,0:T(8,128)(2,1)} %collective-permute-done.1.refs_6_), channel_id=1, source_target_pairs={{0,16},{1,17},{2,18},{3,19},{4,20},{5,21},{6,22},{7,23},{8,24},{9,... | collective-permute-start | bytes 1572872 | tf_op jit(solution)/shard_map/ppermute | solution.py:332
  33.0 21.3 %collective-permute-start.7 = (bf16[1024,256]{1,0:T(8,128)(2,1)}, bf16[1024,256]{1,0:T(8,128)(2,1)S(1)}, u32[]{:S(2)}, u32[]{:S(2)}) collective-permute-start(bf16[1024,256]{1,0:T(8,128)(2,1)} %collective-permute-done.1.refs_6_), channel_id=1, source_target_pairs={{0,4},{1,5},{2,6},{3,7},{4,0},{5,1},{6,2},{7,3},{8,12},{9,13},{10,... | collective-permute-start | bytes 1572872 | tf_op jit(solution)/shard_map/ppermute | solution.py:332
  33.4 24.2 %collective-permute-start.9 = (bf16[1,256,1024]{2,1,0:T(8,128)(2,1)S(1)}, bf16[1,256,1024]{2,1,0:T(8,128)(2,1)}, u32[]{:S(2)}, u32[]{:S(2)}) collective-permute-start(bf16[1,256,1024]{2,1,0:T(8,128)(2,1)S(1)} %bitcast.5), channel_id=1, source_target_pairs={{0,8},{1,9},{2,10},{3,11},{4,12},{5,13},{6,14},{7,15},{8,0},{9,1},... | collective-permute-start | bytes 1572872 | tf_op jit(solution)/shard_map/ppermute | solution.py:332
  45.8 11.8 %collective-permute-start.13 = (bf16[1024,256]{1,0:T(8,128)(2,1)S(1)}, bf16[1024,256]{1,0:T(8,128)(2,1)S(1)}, u32[]{:S(2)}, u32[]{:S(2)}) collective-permute-start(bf16[1024,256]{1,0:T(8,128)(2,1)S(1)} %copy-done.1), channel_id=1, source_target_pairs={{0,1},{1,0},{2,3},{3,2},{4,5},{5,4},{6,7},{7,6},{8,9},{9,8},{10,11... | collective-permute-start | bytes 1572872 | tf_op jit(solution)/shard_map/ppermute | solution.py:332
  52.7 6.4 %collective-permute-start.14 = (bf16[1024,256]{1,0:T(8,128)(2,1)S(1)}, bf16[1024,256]{1,0:T(8,128)(2,1)S(1)}, u32[]{:S(2)}, u32[]{:S(2)}) collective-permute-start(bf16[1024,256]{1,0:T(8,128)(2,1)S(1)} %collective-permute-done.refs_4_), channel_id=1, source_target_pairs={{0,1},{1,0},{2,3},{3,2},{4,5},{5,4},{6,7},{7,6},{8,9},{9,8},{10,11... | collective-permute-start | bytes 1572872 | tf_op jit(solution)/shard_map/ppermute | solution.py:332
  57.6 14.3 %collective-permute-start.12 = (bf16[1024,256]{1,0:T(8,128)(2,1)S(1)}, bf16[1024,256]{1,0:T(8,128)(2,1)S(1)}, u32[]{:S(2)}, u32[]{:S(2)}) collective-permute-start(bf16[1024,256]{1,0:T(8,128)(2,1)S(1)} %collective-permute-done.7.refs_8_), channel_id=1, source_target_pairs={{0,16},{1,17},{2,18},{3,19},{4,20},{5,21},{6,22},{7,23},{8,24},{9,... | collective-permute-start | bytes 1572872 | tf_op jit(solution)/shard_map/ppermute | solution.py:332
  59.2 14.0 %collective-permute-start.23 = (bf16[2,256,512]{2,1,0:T(8,128)(2,1)S(1)}, bf16[2,256,512]{2,1,0:T(8,128)(2,1)S(1)}, u32[]{:S(2)}, u32[]{:S(2)}) collective-permute-start(bf16[2,256,512]{2,1,0:T(8,128)(2,1)S(1)} %stack_halves.1), channel_id=1, source_target_pairs={{0,4},{1,5},{2,6},{3,7},{4,0},{5,1},{6,2},{7,3},{8,12},{9,13},{10,... | collective-permute-start | bytes 1572872 | tf_op jit(solution)/shard_map/ppermute | solution.py:332
  59.2 14.5 %collective-permute-start.16 = (bf16[1024,256]{1,0:T(8,128)(2,1)}, bf16[1024,256]{1,0:T(8,128)(2,1)S(1)}, u32[]{:S(2)}, u32[]{:S(2)}) collective-permute-start(bf16[1024,256]{1,0:T(8,128)(2,1)} %collective-permute-done.1.refs_6_), channel_id=1, source_target_pairs={{0,1},{1,0},{2,3},{3,2},{4,5},{5,4},{6,7},{7,6},{8,9},{9,8},{10,11... | collective-permute-start | bytes 1572872 | tf_op jit(solution)/shard_map/ppermute | solution.py:332
  60.0 14.2 %collective-permute-start.15 = (bf16[1024,256]{1,0:T(8,128)(2,1)S(1)}, bf16[1024,256]{1,0:T(8,128)(2,1)S(1)}, u32[]{:S(2)}, u32[]{:S(2)}) collective-permute-start(bf16[1024,256]{1,0:T(8,128)(2,1)S(1)} %collective-permute-done.5.refs_5_), channel_id=1, source_target_pairs={{0,1},{1,0},{2,3},{3,2},{4,5},{5,4},{6,7},{7,6},{8,9},{9,8},{10,11... | collective-permute-start | bytes 1572872 | tf_op jit(solution)/shard_map/ppermute | solution.py:332
  73.8 24.0 %collective-permute-start.24 = (bf16[2,256,512]{2,1,0:T(8,128)(2,1)S(1)}, bf16[2,256,512]{2,1,0:T(8,128)(2,1)}, u32[]{:S(2)}, u32[]{:S(2)}) collective-permute-start(bf16[2,256,512]{2,1,0:T(8,128)(2,1)S(1)} %collective-permute-done.23.refs_10_), channel_id=1, source_target_pairs={{0,16},{1,17},{2,18},{3,19},{4,20},{5,21},{6,22},{7,23},{8,24},{9,... | collective-permute-start | bytes 1572872 | tf_op jit(solution)/shard_map/ppermute | solution.py:332
  74.3 18.2 %collective-permute-start.26 = (bf16[1,256,1024]{2,1,0:T(8,128)(2,1)}, bf16[1,256,1024]{2,1,0:T(8,128)(2,1)}, u32[]{:S(2)}, u32[]{:S(2)}) collective-permute-start(bf16[1,256,1024]{2,1,0:T(8,128)(2,1)} %collective-permute-done.9.refs_5_), channel_id=1, source_target_pairs={{0,4},{1,5},{2,6},{3,7},{4,0},{5,1},{6,2},{7,3},{8,12},{9,13},{10,... | collective-permute-start | bytes 1572872 | tf_op jit(solution)/shard_map/ppermute | solution.py:332
  74.6 17.9 %collective-permute-start.25 = (bf16[1,256,1024]{2,1,0:T(8,128)(2,1)}, bf16[1,256,1024]{2,1,0:T(8,128)(2,1)}, u32[]{:S(2)}, u32[]{:S(2)}) collective-permute-start(bf16[1,256,1024]{2,1,0:T(8,128)(2,1)} %collective-permute-done.9.refs_5_), channel_id=1, source_target_pairs={{0,2},{1,3},{2,0},{3,1},{4,6},{5,7},{6,4},{7,5},{8,10},{9,11},{10,... | collective-permute-start | bytes 1572872 | tf_op jit(solution)/shard_map/ppermute | solution.py:332
  84.8 6.5 %collective-permute-start.20 = (bf16[128,512]{1,0:T(8,128)(2,1)}, bf16[128,512]{1,0:T(8,128)(2,1)S(1)}, u32[]{:S(2)}, u32[]{:S(2)}) collective-permute-start(bf16[128,512]{1,0:T(8,128)(2,1)} %get-tuple-element.48), channel_id=1, source_target_pairs={{0,2},{1,3},{2,0},{3,1},{4,6},{5,7},{6,4},{7,5},{8,10},{9,11},{10,... | collective-permute-start | bytes 393224 | tf_op jit(solution)/shard_map/ppermute | solution.py:332
  91.3 6.5 %collective-permute-start.21 = (bf16[1,256,512]{2,1,0:T(8,128)(2,1)S(1)}, bf16[1,256,512]{2,1,0:T(8,128)(2,1)S(1)}, u32[]{:S(2)}, u32[]{:S(2)}) collective-permute-start(bf16[1,256,512]{2,1,0:T(8,128)(2,1)S(1)} %collective-permute-done.3.b_ref.refs_3_), channel_id=1, source_target_pairs={{0,1},{1,0},{2,3},{3,2},{4,5},{5,4},{6,7},{7,6},{8,9},{9,8},{10,11... | collective-permute-start | bytes 786440 | tf_op jit(solution)/shard_map/ppermute | solution.py:332
  91.3 6.5 %collective-permute-start.22 = (bf16[1,256,512]{2,1,0:T(8,128)(2,1)}, bf16[1,256,512]{2,1,0:T(8,128)(2,1)S(1)}, u32[]{:S(2)}, u32[]{:S(2)}) collective-permute-start(bf16[1,256,512]{2,1,0:T(8,128)(2,1)} %copy-done.22), channel_id=1, source_target_pairs={{0,1},{1,0},{2,3},{3,2},{4,5},{5,4},{6,7},{7,6},{8,9},{9,8},{10,11... | collective-permute-start | bytes 786440 | tf_op jit(solution)/shard_map/ppermute | solution.py:332
  93.5 10.5 %collective-permute-start.31 = (bf16[1,256,512]{2,1,0:T(8,128)(2,1)S(1)}, bf16[1,256,512]{2,1,0:T(8,128)(2,1)S(1)}, u32[]{:S(2)}, u32[]{:S(2)}) collective-permute-start(bf16[1,256,512]{2,1,0:T(8,128)(2,1)S(1)} %slice.14), channel_id=1, source_target_pairs={{0,4},{1,5},{2,6},{3,7},{4,0},{5,1},{6,2},{7,3},{8,12},{9,13},{10,... | collective-permute-start | bytes 786440 | tf_op jit(solution)/shard_map/ppermute | solution.py:332
  96.2 8.3 %collective-permute-start.32 = (bf16[1,256,512]{2,1,0:T(8,128)(2,1)S(1)}, bf16[1,256,512]{2,1,0:T(8,128)(2,1)S(1)}, u32[]{:S(2)}, u32[]{:S(2)}) collective-permute-start(bf16[1,256,512]{2,1,0:T(8,128)(2,1)S(1)} %slice.15), channel_id=1, source_target_pairs={{0,2},{1,3},{2,0},{3,1},{4,6},{5,7},{6,4},{7,5},{8,10},{9,11},{10,... | collective-permute-start | bytes 786440 | tf_op jit(solution)/shard_map/ppermute | solution.py:332
  (41 other events, 402.5 us)

commit v12 on v6

--- a/solution.py
+++ b/solution.py
@@ -360,7 +360,7 @@
     b2 = swap(after(a2, d0, rest_x), other)
 
     b3 = swap(after(a3, b1, b2), other)
-    d1 = swap(after(d0, a3, d2), near)
+    d1 = swap(after(d0, a3), near)
 
     e1 = swap(after(d1, b3), other)
     d3 = swap(after(d2, d1), near)
@@ -375,7 +375,7 @@
     )
     q1 = swap(p1, core)
     q2 = swap(p2, across)
-    q3 = swap(p3, both)
+    q3 = swap(after(p3, q1), both)
 
     f3 = swap(after(f2, d3, q1), near)
 

time: 109 us -> 106 us (0.972)
  waiting for transfers between devices: 54.6 us -> 51.5 us
    ppermute x29, waiting for transfers between devices: 54.6 us -> 51.5 us  [swap(): return lax.ppermute(value, ALL, pairs)]
  transfers between devices with their start and end apart: 29 -> 29, of which waited for: 17 -> 19; matrix products, arithmetic and copies ran while one was open for 1% -> 1% of each run, Pallas kernels for 16% -> 16%
where the time goes in v12:
time: 106 us; the launch traced here: 105 us
  waiting for transfers between devices  51.5 us (49%)
  starting transfers between devices  25.1 us (24%)
  Pallas kernels  20.4 us (19%)
  local copies, waits for them, and re-layouts  4.33 us (4%)
  other arithmetic  2.96 us (3%)
    ppermute x29, waiting for transfers between devices, swap(): return lax.ppermute(value, ALL, pairs)  51.5 us
    ppermute x29, starting transfers between devices, swap(): return lax.ppermute(value, ALL, pairs)  25.1 us
    pallas_call x2, Pallas kernels, down_call(): pl.pallas_call(functools.partial(kernel, pieces), in_specs=[SMEM] * len(l...  8.27 us
    pallas_call x1, Pallas kernels, partial_sums(): pl.pallas_call(functools.partial(partial_kernel, len(inputs), kinds), in_...  6.47 us
    pallas_call x1, Pallas kernels, normed_quarters(): pl.pallas_call(norm_kernel, in_specs=[SMEM, HBM, VMEM], out_specs=[HBM] *...  5.66 us
    unnamed x50, local copies, waits for them, and re-layouts  4.26 us
  transfers between devices with their start and end apart: 29, of which 19 were waited for; matrix products, arithmetic and copies ran while one was open for 1% of the time, Pallas kernels for 16%

profile of v12, /device:TPU:0, one launch (start us, length us, event | category | flops | bytes accessed | tf_op | source)
XLA Modules:
  0.0 105.2 jit_solution(4039605245498668811)
XLA Ops:
  0.0 1.9 %broadcast_select_fusion = bf16[1024,256]{1,0:T(8,128)(2,1)} fusion(bf16[1024,256]{1,0:T(8,128)(2,1)} %refs_4_.1, bf16[1024,256]{1,0:T(8,128)(2,1)} %refs_5_.1, pred[]{:T(512)S(6)} %eq.3), kind=kLoop, calls=%fused_computation | loop fusion | flops 262144 | bytes 1572865 | tf_op jit(solution)/shard_map/jit(_where)/select_n | solution.py:336
  1.9 4.0 %collective-permute-start.2 = (bf16[1024,256]{1,0:T(8,128)(2,1)}, bf16[1024,256]{1,0:T(8,128)(2,1)S(1)}, u32[]{:S(2)}, u32[]{:S(2)}) collective-permute-start(bf16[1024,256]{1,0:T(8,128)(2,1)} %broadcast_select_fusion), channel_id=1, source_target_pairs={{0,8},{1,9},{2,10},{3,11},{4,12},{5,13},{6,14},{7,15},{8,0},{9,1},... | collective-permute-start | bytes 1572872 | tf_op jit(solution)/shard_map/ppermute | solution.py:333
  5.9 1.6 %collective-permute-start.3 = (bf16[1024,256]{1,0:T(8,128)(2,1)}, bf16[1024,256]{1,0:T(8,128)(2,1)S(1)}, u32[]{:S(2)}, u32[]{:S(2)}) collective-permute-start(bf16[1024,256]{1,0:T(8,128)(2,1)} %broadcast_select_fusion), channel_id=1, source_target_pairs={{0,4},{1,5},{2,6},{3,7},{4,0},{5,1},{6,2},{7,3},{8,12},{9,13},{10,... | collective-permute-start | bytes 1572872 | tf_op jit(solution)/shard_map/ppermute | solution.py:333
  8.6 1.6 %collective-permute-start.5 = (bf16[1,256,512]{2,1,0:T(8,128)(2,1)S(1)}, bf16[1,256,512]{2,1,0:T(8,128)(2,1)S(1)}, u32[]{:S(2)}, u32[]{:S(2)}) collective-permute-start(bf16[1,256,512]{2,1,0:T(8,128)(2,1)S(1)} %select_bitcast_fusion.a_ref), channel_id=1, source_target_pairs={{0,2},{1,3},{2,0},{3,1},{4,6},{5,7},{6,4},{7,5},{8,10},{9,11},{10,... | collective-permute-start | bytes 786440 | tf_op jit(solution)/shard_map/ppermute | solution.py:333
  10.1 5.7 %norm_quarters.1 = (bf16[4,128,1024]{2,1,0:T(8,128)(2,1)}, bf16[4,128,1024]{2,1,0:T(8,128)(2,1)}, bf16[8,128,1024]{2,1,0:T(8,128)(2,1)}) custom-call(s32[16]{0:T(128)} %owner_ref.5, bf16[128,16384]{1,0:T(8,128)(2,1)} %tokens_ref.1, f32[1,16384]{1,0:T(1,128)} %bitcast.7), custom_call_target="tpu_custom_call" | custom-call | flops 12582912 | bytes 8388608 | tf_op jit(solution)/shard_map/norm_quarters/pallas_call | solution.py:97
  17.4 1.5 %collective-permute-start.7 = (bf16[1,256,512]{2,1,0:T(8,128)(2,1)S(1)}, bf16[1,256,512]{2,1,0:T(8,128)(2,1)S(1)}, u32[]{:S(2)}, u32[]{:S(2)}) collective-permute-start(bf16[1,256,512]{2,1,0:T(8,128)(2,1)S(1)} %collective-permute-done.5.b_ref.refs_6_), channel_id=1, source_target_pairs={{0,16},{1,17},{2,18},{3,19},{4,20},{5,21},{6,22},{7,23},{8,24},{9,... | collective-permute-start | bytes 786440 | tf_op jit(solution)/shard_map/ppermute | solution.py:333
  18.9 10.5 %collective-permute-done.2.refs_8_ = bf16[1024,256]{1,0:T(8,128)(2,1)S(1)} collective-permute-done((bf16[1024,256]{1,0:T(8,128)(2,1)}, bf16[1024,256]{1,0:T(8,128)(2,1)S(1)}, u32[]{:S(2)}, u32[]{:S(2)}) %collective-permute-start.2) | collective-permute-done | bytes 524320 | tf_op jit(solution)/shard_map/ppermute | solution.py:333
  29.7 1.6 %collective-permute-start.9 = (bf16[1024,256]{1,0:T(8,128)(2,1)S(1)}, bf16[1024,256]{1,0:T(8,128)(2,1)S(1)}, u32[]{:S(2)}, u32[]{:S(2)}) collective-permute-start(bf16[1024,256]{1,0:T(8,128)(2,1)S(1)} %collective-permute-done.2.refs_8_), channel_id=1, source_target_pairs={{0,16},{1,17},{2,18},{3,19},{4,20},{5,21},{6,22},{7,23},{8,24},{9,... | collective-permute-start | bytes 1572872 | tf_op jit(solution)/shard_map/ppermute | solution.py:333
  32.0 1.4 %collective-permute-start.6 = (bf16[1024,256]{1,0:T(8,128)(2,1)S(1)}, bf16[1024,256]{1,0:T(8,128)(2,1)S(1)}, u32[]{:S(2)}, u32[]{:S(2)}) collective-permute-start(bf16[1024,256]{1,0:T(8,128)(2,1)S(1)} %collective-permute-done.2.refs_8_), channel_id=1, source_target_pairs={{0,4},{1,5},{2,6},{3,7},{4,0},{5,1},{6,2},{7,3},{8,12},{9,13},{10,... | collective-permute-start | bytes 1572872 | tf_op jit(solution)/shard_map/ppermute | solution.py:333
  33.5 2.4 %collective-permute-start.12 = (bf16[1,256,1024]{2,1,0:T(8,128)(2,1)S(1)}, bf16[1,256,1024]{2,1,0:T(8,128)(2,1)}, u32[]{:S(2)}, u32[]{:S(2)}) collective-permute-start(bf16[1,256,1024]{2,1,0:T(8,128)(2,1)S(1)} %bitcast.6), channel_id=1, source_target_pairs={{0,8},{1,9},{2,10},{3,11},{4,12},{5,13},{6,14},{7,15},{8,0},{9,1},... | collective-permute-start | bytes 1572872 | tf_op jit(solution)/shard_map/ppermute | solution.py:333
  35.8 8.8 %collective-permute-done.9.refs_9_ = bf16[1024,256]{1,0:T(8,128)(2,1)S(1)} collective-permute-done((bf16[1024,256]{1,0:T(8,128)(2,1)S(1)}, bf16[1024,256]{1,0:T(8,128)(2,1)S(1)}, u32[]{:S(2)}, u32[]{:S(2)}) %collective-permute-start.9) | collective-permute-done | bytes 524320 | tf_op jit(solution)/shard_map/ppermute | solution.py:333
  44.6 9.2 %collective-permute-done.8.refs_7_ = bf16[1024,256]{1,0:T(8,128)(2,1)S(1)} collective-permute-done((bf16[1024,256]{1,0:T(8,128)(2,1)S(1)}, bf16[1024,256]{1,0:T(8,128)(2,1)S(1)}, u32[]{:S(2)}, u32[]{:S(2)}) %collective-permute-start.8) | collective-permute-done | bytes 524320 | tf_op jit(solution)/shard_map/ppermute | solution.py:333
  53.8 1.5 %collective-permute-done.6.refs_10_ = bf16[1024,256]{1,0:T(8,128)(2,1)S(1)} collective-permute-done((bf16[1024,256]{1,0:T(8,128)(2,1)S(1)}, bf16[1024,256]{1,0:T(8,128)(2,1)S(1)}, u32[]{:S(2)}, u32[]{:S(2)}) %collective-permute-start.6) | collective-permute-done | bytes 524320 | tf_op jit(solution)/shard_map/ppermute | solution.py:333
  56.9 1.9 %collective-permute-done.12.refs_8_ = bf16[1,256,1024]{2,1,0:T(8,128)(2,1)} collective-permute-done((bf16[1,256,1024]{2,1,0:T(8,128)(2,1)S(1)}, bf16[1,256,1024]{2,1,0:T(8,128)(2,1)}, u32[]{:S(2)}, u32[]{:S(2)}) %collective-permute-start.12) | collective-permute-done | bytes 524320 | tf_op jit(solution)/shard_map/ppermute | solution.py:333
  59.4 1.8 %collective-permute-done.14.refs_10_ = bf16[1,256,512]{2,1,0:T(8,128)(2,1)S(1)} collective-permute-done((bf16[1,256,512]{2,1,0:T(8,128)(2,1)S(1)}, bf16[1,256,512]{2,1,0:T(8,128)(2,1)S(1)}, u32[]{:S(2)}, u32[]{:S(2)}) %collective-permute-start.14) | collective-permute-done | bytes 262176 | tf_op jit(solution)/shard_map/ppermute | solution.py:333
  62.0 4.9 %collective-permute-done.10.refs_11_ = bf16[1024,256]{1,0:T(8,128)(2,1)S(1)} collective-permute-done((bf16[1024,256]{1,0:T(8,128)(2,1)S(1)}, bf16[1024,256]{1,0:T(8,128)(2,1)S(1)}, u32[]{:S(2)}, u32[]{:S(2)}) %collective-permute-start.10) | collective-permute-done | bytes 524320 | tf_op jit(solution)/shard_map/ppermute | solution.py:333
  70.9 1.5 %collective-permute-start.21 = (bf16[1,256,1024]{2,1,0:T(8,128)(2,1)}, bf16[1,256,1024]{2,1,0:T(8,128)(2,1)}, u32[]{:S(2)}, u32[]{:S(2)}) collective-permute-start(bf16[1,256,1024]{2,1,0:T(8,128)(2,1)} %collective-permute-done.12.refs_8_), channel_id=1, source_target_pairs={{0,2},{1,3},{2,0},{3,1},{4,6},{5,7},{6,4},{7,5},{8,10},{9,11},{10,... | collective-permute-start | bytes 1572872 | tf_op jit(solution)/shard_map/ppermute | solution.py:333
  73.3 6.5 %partial_sums.1 = (f32[128,512]{1,0:T(8,128)}, f32[128,512]{1,0:T(8,128)}, bf16[128,512]{1,0:T(8,128)(2,1)}, bf16[128,512]{1,0:T(8,128)(2,1)}) custom-call(bf16[4,128,1024]{2,1,0:T(8,128)(2,1)} %get-tuple-element.33.refs_0_, bf16[4,128,1024]{2,1,0:T(8,128)(2,1)} %copy-done.2, bf16[8,128,1024]{2,1,0:T(8,128)(2,1)} %copy-done.1, ...), custom_call_target="tpu_custom_call" | custom-call | flops 2147483648 | bytes 8388608 | tf_op jit(solution)/shard_map/partial_sums/pallas_call | solution.py:176
  83.3 2.6 %collective-permute-done.21.refs_14_ = bf16[1,256,1024]{2,1,0:T(8,128)(2,1)} collective-permute-done((bf16[1,256,1024]{2,1,0:T(8,128)(2,1)}, bf16[1,256,1024]{2,1,0:T(8,128)(2,1)}, u32[]{:S(2)}, u32[]{:S(2)}) %collective-permute-start.21) | collective-permute-done | bytes 524320 | tf_op jit(solution)/shard_map/ppermute | solution.py:333
  87.1 1.5 %collective-permute-done.18.refs_2_ = bf16[128,512]{1,0:T(8,128)(2,1)S(1)} collective-permute-done((bf16[128,512]{1,0:T(8,128)(2,1)}, bf16[128,512]{1,0:T(8,128)(2,1)S(1)}, u32[]{:S(2)}, u32[]{:S(2)}) %collective-permute-start.18) | collective-permute-done | bytes 131104 | tf_op jit(solution)/shard_map/ppermute | solution.py:333
  90.2 4.9 %down_first.1 = (bf16[128,16384]{1,0:T(8,128)(2,1)}, bf16[128,256]{1,0:T(8,128)(2,1)}) custom-call(s32[1]{0:T(128)S(6)} %copy.10.live_ref, s32[16]{0:T(128)} %owner_ref.5, f32[128,512]{1,0:T(8,128)} %get-tuple-element.45.refs_0_, f32[128,512]{1,0:T(8,128)} %copy-done.22, bf16[128,512]{1,0:T(8,128)(2,1)} %copy-done.23, bf16[128,512]{1,0:T(8,128)(2,1)} %copy-done.24, ...), custom_call_target="tpu_custom_call" | custom-call | flops 6710886400 | bytes 7864320 | tf_op jit(solution)/shard_map/down_first/pallas_call | solution.py:274
  96.8 1.2 %collective-permute-done.27.refs_4_ = bf16[1,256,1024]{2,1,0:T(8,128)(2,1)S(1)} collective-permute-done((bf16[1,256,1024]{2,1,0:T(8,128)(2,1)}, bf16[1,256,1024]{2,1,0:T(8,128)(2,1)S(1)}, u32[]{:S(2)}, u32[]{:S(2)}) %collective-permute-start.27) | collective-permute-done | bytes 524320 | tf_op jit(solution)/shard_map/ppermute | solution.py:333
  99.4 1.5 %collective-permute-done.23.refs_0_ = bf16[2,256,512]{2,1,0:T(8,128)(2,1)S(1)} collective-permute-done((bf16[2,256,512]{2,1,0:T(8,128)(2,1)}, bf16[2,256,512]{2,1,0:T(8,128)(2,1)S(1)}, u32[]{:S(2)}, u32[]{:S(2)}) %collective-permute-start.23) | collective-permute-done | bytes 524320 | tf_op jit(solution)/shard_map/ppermute | solution.py:333
  101.9 3.3 %down_second.1 = bf16[128,16384]{1,0:T(8,128)(2,1)} custom-call(s32[16]{0:T(128)} %owner_ref.5, bf16[128,256]{1,0:T(8,128)(2,1)} %get-tuple-element.53.hidden_ref, bf16[128,16384]{1,0:T(8,128)(2,1)} %get-tuple-element.54._, bf16[2,256,512]{2,1,0:T(8,128)(2,1)} %copy-done.17, bf16[2,256,512]{2,1,0:T(8,128)(2,1)} %copy-done.16, ...), custom_call_target="tpu_custom_call", output_to_operand_aliasing={{}: (2, {})} | custom-call | flops 4026531840 | bytes 4718592 | tf_op jit(solution)/shard_map/down_second/pallas_call | solution.py:274
  (92 shorter events, 21.0 us)
Async XLA Ops:
  1.9 27.5 %collective-permute-start.2 = (bf16[1024,256]{1,0:T(8,128)(2,1)}, bf16[1024,256]{1,0:T(8,128)(2,1)S(1)}, u32[]{:S(2)}, u32[]{:S(2)}) collective-permute-start(bf16[1024,256]{1,0:T(8,128)(2,1)} %broadcast_select_fusion), channel_id=1, source_target_pairs={{0,8},{1,9},{2,10},{3,11},{4,12},{5,13},{6,14},{7,15},{8,0},{9,1},... | collective-permute-start | bytes 1572872 | tf_op jit(solution)/shard_map/ppermute | solution.py:333
  5.9 23.7 %collective-permute-start.3 = (bf16[1024,256]{1,0:T(8,128)(2,1)}, bf16[1024,256]{1,0:T(8,128)(2,1)S(1)}, u32[]{:S(2)}, u32[]{:S(2)}) collective-permute-start(bf16[1024,256]{1,0:T(8,128)(2,1)} %broadcast_select_fusion), channel_id=1, source_target_pairs={{0,4},{1,5},{2,6},{3,7},{4,0},{5,1},{6,2},{7,3},{8,12},{9,13},{10,... | collective-permute-start | bytes 1572872 | tf_op jit(solution)/shard_map/ppermute | solution.py:333
  7.5 22.1 %collective-permute-start.4 = (bf16[1,256,1024]{2,1,0:T(8,128)(2,1)}, bf16[1,256,1024]{2,1,0:T(8,128)(2,1)}, u32[]{:S(2)}, u32[]{:S(2)}) collective-permute-start(bf16[1,256,1024]{2,1,0:T(8,128)(2,1)} %bitcast.4), channel_id=1, source_target_pairs={{0,1},{1,0},{2,3},{3,2},{4,5},{5,4},{6,7},{7,6},{8,9},{9,8},{10,11... | collective-permute-start | bytes 1572872 | tf_op jit(solution)/shard_map/ppermute | solution.py:333
  8.6 8.8 %collective-permute-start.5 = (bf16[1,256,512]{2,1,0:T(8,128)(2,1)S(1)}, bf16[1,256,512]{2,1,0:T(8,128)(2,1)S(1)}, u32[]{:S(2)}, u32[]{:S(2)}) collective-permute-start(bf16[1,256,512]{2,1,0:T(8,128)(2,1)S(1)} %select_bitcast_fusion.a_ref), channel_id=1, source_target_pairs={{0,2},{1,3},{2,0},{3,1},{4,6},{5,7},{6,4},{7,5},{8,10},{9,11},{10,... | collective-permute-start | bytes 786440 | tf_op jit(solution)/shard_map/ppermute | solution.py:333
  15.8 52.7 %collective-permute-start.1 = (bf16[8,128,1024]{2,1,0:T(8,128)(2,1)}, bf16[8,128,1024]{2,1,0:T(8,128)(2,1)S(1)}, u32[]{:S(2)}, u32[]{:S(2)}) collective-permute-start(bf16[8,128,1024]{2,1,0:T(8,128)(2,1)} %get-tuple-element.35), channel_id=1, source_target_pairs={{0,2},{1,3},{2,0},{3,1},{4,6},{5,7},{6,4},{7,5},{8,10},{9,11},{10,... | collective-permute-start | bytes 6291464 | tf_op jit(solution)/shard_map/ppermute | solution.py:333
  17.4 12.3 %collective-permute-start.7 = (bf16[1,256,512]{2,1,0:T(8,128)(2,1)S(1)}, bf16[1,256,512]{2,1,0:T(8,128)(2,1)S(1)}, u32[]{:S(2)}, u32[]{:S(2)}) collective-permute-start(bf16[1,256,512]{2,1,0:T(8,128)(2,1)S(1)} %collective-permute-done.5.b_ref.refs_6_), channel_id=1, source_target_pairs={{0,16},{1,17},{2,18},{3,19},{4,20},{5,21},{6,22},{7,23},{8,24},{9,... | collective-permute-start | bytes 786440 | tf_op jit(solution)/shard_map/ppermute | solution.py:333
  29.7 14.9 %collective-permute-start.9 = (bf16[1024,256]{1,0:T(8,128)(2,1)S(1)}, bf16[1024,256]{1,0:T(8,128)(2,1)S(1)}, u32[]{:S(2)}, u32[]{:S(2)}) collective-permute-start(bf16[1024,256]{1,0:T(8,128)(2,1)S(1)} %collective-permute-done.2.refs_8_), channel_id=1, source_target_pairs={{0,16},{1,17},{2,18},{3,19},{4,20},{5,21},{6,22},{7,23},{8,24},{9,... | collective-permute-start | bytes 1572872 | tf_op jit(solution)/shard_map/ppermute | solution.py:333
  31.3 22.5 %collective-permute-start.8 = (bf16[1024,256]{1,0:T(8,128)(2,1)S(1)}, bf16[1024,256]{1,0:T(8,128)(2,1)S(1)}, u32[]{:S(2)}, u32[]{:S(2)}) collective-permute-start(bf16[1024,256]{1,0:T(8,128)(2,1)S(1)} %collective-permute-done.3.refs_6_), channel_id=1, source_target_pairs={{0,16},{1,17},{2,18},{3,19},{4,20},{5,21},{6,22},{7,23},{8,24},{9,... | collective-permute-start | bytes 1572872 | tf_op jit(solution)/shard_map/ppermute | solution.py:333
  32.0 23.3 %collective-permute-start.6 = (bf16[1024,256]{1,0:T(8,128)(2,1)S(1)}, bf16[1024,256]{1,0:T(8,128)(2,1)S(1)}, u32[]{:S(2)}, u32[]{:S(2)}) collective-permute-start(bf16[1024,256]{1,0:T(8,128)(2,1)S(1)} %collective-permute-done.2.refs_8_), channel_id=1, source_target_pairs={{0,4},{1,5},{2,6},{3,7},{4,0},{5,1},{6,2},{7,3},{8,12},{9,13},{10,... | collective-permute-start | bytes 1572872 | tf_op jit(solution)/shard_map/ppermute | solution.py:333
  33.5 25.4 %collective-permute-start.12 = (bf16[1,256,1024]{2,1,0:T(8,128)(2,1)S(1)}, bf16[1,256,1024]{2,1,0:T(8,128)(2,1)}, u32[]{:S(2)}, u32[]{:S(2)}) collective-permute-start(bf16[1,256,1024]{2,1,0:T(8,128)(2,1)S(1)} %bitcast.6), channel_id=1, source_target_pairs={{0,8},{1,9},{2,10},{3,11},{4,12},{5,13},{6,14},{7,15},{8,0},{9,1},... | collective-permute-start | bytes 1572872 | tf_op jit(solution)/shard_map/ppermute | solution.py:333
  44.6 14.3 %collective-permute-start.13 = (bf16[1,256,512]{2,1,0:T(8,128)(2,1)S(1)}, bf16[1,256,512]{2,1,0:T(8,128)(2,1)S(1)}, u32[]{:S(2)}, u32[]{:S(2)}) collective-permute-start(bf16[1,256,512]{2,1,0:T(8,128)(2,1)S(1)} %collective-permute-done.5.b_ref.refs_6_), channel_id=1, source_target_pairs={{0,1},{1,0},{2,3},{3,2},{4,5},{5,4},{6,7},{7,6},{8,9},{9,8},{10,11... | collective-permute-start | bytes 786440 | tf_op jit(solution)/shard_map/ppermute | solution.py:333
  55.4 11.5 %collective-permute-start.10 = (bf16[1024,256]{1,0:T(8,128)(2,1)S(1)}, bf16[1024,256]{1,0:T(8,128)(2,1)S(1)}, u32[]{:S(2)}, u32[]{:S(2)}) collective-permute-start(bf16[1024,256]{1,0:T(8,128)(2,1)S(1)} %collective-permute-done.6.refs_10_), channel_id=1, source_target_pairs={{0,16},{1,17},{2,18},{3,19},{4,20},{5,21},{6,22},{7,23},{8,24},{9,... | collective-permute-start | bytes 1572872 | tf_op jit(solution)/shard_map/ppermute | solution.py:333
  56.4 11.2 %collective-permute-start.11 = (bf16[2,256,512]{2,1,0:T(8,128)(2,1)S(1)}, bf16[2,256,512]{2,1,0:T(8,128)(2,1)S(1)}, u32[]{:S(2)}, u32[]{:S(2)}) collective-permute-start(bf16[2,256,512]{2,1,0:T(8,128)(2,1)S(1)} %stack_halves.1), channel_id=1, source_target_pairs={{0,4},{1,5},{2,6},{3,7},{4,0},{5,1},{6,2},{7,3},{8,12},{9,13},{10,... | collective-permute-start | bytes 1572872 | tf_op jit(solution)/shard_map/ppermute | solution.py:333
  58.9 8.7 %collective-permute-start.15 = (bf16[1,256,1024]{2,1,0:T(8,128)(2,1)}, bf16[1,256,1024]{2,1,0:T(8,128)(2,1)S(1)}, u32[]{:S(2)}, u32[]{:S(2)}) collective-permute-start(bf16[1,256,1024]{2,1,0:T(8,128)(2,1)} %collective-permute-done.12.refs_8_), channel_id=1, source_target_pairs={{0,1},{1,0},{2,3},{3,2},{4,5},{5,4},{6,7},{7,6},{8,9},{9,8},{10,11... | collective-permute-start | bytes 1572872 | tf_op jit(solution)/shard_map/ppermute | solution.py:333
  61.9 10.5 %collective-permute-start = (bf16[4,128,1024]{2,1,0:T(8,128)(2,1)S(1)}, bf16[4,128,1024]{2,1,0:T(8,128)(2,1)S(1)}, u32[]{:S(2)}, u32[]{:S(2)}) collective-permute-start(bf16[4,128,1024]{2,1,0:T(8,128)(2,1)S(1)} %copy-done.10), channel_id=1, source_target_pairs={{0,1},{1,0},{2,3},{3,2},{4,5},{5,4},{6,7},{7,6},{8,9},{9,8},{10,11... | collective-permute-start | bytes 3145736 | tf_op jit(solution)/shard_map/ppermute | solution.py:333
  68.6 3.7 %collective-permute-start.16 = (bf16[4,128,1024]{2,1,0:T(8,128)(2,1)S(1)}, bf16[4,128,1024]{2,1,0:T(8,128)(2,1)}, u32[]{:S(2)}, u32[]{:S(2)}) collective-permute-start(bf16[4,128,1024]{2,1,0:T(8,128)(2,1)S(1)} %slice.11), channel_id=1, source_target_pairs={{0,1},{1,0},{2,3},{3,2},{4,5},{5,4},{6,7},{7,6},{8,9},{9,8},{10,11... | collective-permute-start | bytes 3145736 | tf_op jit(solution)/shard_map/ppermute | solution.py:333
  68.7 14.7 %collective-permute-start.22 = (bf16[1,256,1024]{2,1,0:T(8,128)(2,1)}, bf16[1,256,1024]{2,1,0:T(8,128)(2,1)}, u32[]{:S(2)}, u32[]{:S(2)}) collective-permute-start(bf16[1,256,1024]{2,1,0:T(8,128)(2,1)} %collective-permute-done.12.refs_8_), channel_id=1, source_target_pairs={{0,4},{1,5},{2,6},{3,7},{4,0},{5,1},{6,2},{7,3},{8,12},{9,13},{10,... | collective-permute-start | bytes 1572872 | tf_op jit(solution)/shard_map/ppermute | solution.py:333
  69.9 17.3 %collective-permute-start.20 = (bf16[2,256,512]{2,1,0:T(8,128)(2,1)S(1)}, bf16[2,256,512]{2,1,0:T(8,128)(2,1)}, u32[]{:S(2)}, u32[]{:S(2)}) collective-permute-start(bf16[2,256,512]{2,1,0:T(8,128)(2,1)S(1)} %collective-permute-done.11.refs_12_), channel_id=1, source_target_pairs={{0,16},{1,17},{2,18},{3,19},{4,20},{5,21},{6,22},{7,23},{8,24},{9,... | collective-permute-start | bytes 1572872 | tf_op jit(solution)/shard_map/ppermute | solution.py:333
  70.9 15.1 %collective-permute-start.21 = (bf16[1,256,1024]{2,1,0:T(8,128)(2,1)}, bf16[1,256,1024]{2,1,0:T(8,128)(2,1)}, u32[]{:S(2)}, u32[]{:S(2)}) collective-permute-start(bf16[1,256,1024]{2,1,0:T(8,128)(2,1)} %collective-permute-done.12.refs_8_), channel_id=1, source_target_pairs={{0,2},{1,3},{2,0},{3,1},{4,6},{5,7},{6,4},{7,5},{8,10},{9,11},{10,... | collective-permute-start | bytes 1572872 | tf_op jit(solution)/shard_map/ppermute | solution.py:333
  79.9 8.8 %collective-permute-start.18 = (bf16[128,512]{1,0:T(8,128)(2,1)}, bf16[128,512]{1,0:T(8,128)(2,1)S(1)}, u32[]{:S(2)}, u32[]{:S(2)}) collective-permute-start(bf16[128,512]{1,0:T(8,128)(2,1)} %get-tuple-element.47), channel_id=1, source_target_pairs={{0,2},{1,3},{2,0},{3,1},{4,6},{5,7},{6,4},{7,5},{8,10},{9,11},{10,... | collective-permute-start | bytes 393224 | tf_op jit(solution)/shard_map/ppermute | solution.py:333
  81.6 7.9 %collective-permute-start.19 = (bf16[128,512]{1,0:T(8,128)(2,1)}, bf16[128,512]{1,0:T(8,128)(2,1)S(1)}, u32[]{:S(2)}, u32[]{:S(2)}) collective-permute-start(bf16[128,512]{1,0:T(8,128)(2,1)} %get-tuple-element.49), channel_id=1, source_target_pairs={{0,3},{1,2},{2,1},{3,0},{4,7},{5,6},{6,5},{7,4},{8,11},{9,10},{10,... | collective-permute-start | bytes 393224 | tf_op jit(solution)/shard_map/ppermute | solution.py:333
  86.0 12.0 %collective-permute-start.27 = (bf16[1,256,1024]{2,1,0:T(8,128)(2,1)}, bf16[1,256,1024]{2,1,0:T(8,128)(2,1)S(1)}, u32[]{:S(2)}, u32[]{:S(2)}) collective-permute-start(bf16[1,256,1024]{2,1,0:T(8,128)(2,1)} %collective-permute-done.21.refs_14_), channel_id=1, source_target_pairs={{0,4},{1,5},{2,6},{3,7},{4,0},{5,1},{6,2},{7,3},{8,12},{9,13},{10,... | collective-permute-start | bytes 1572872 | tf_op jit(solution)/shard_map/ppermute | solution.py:333
  96.3 3.2 %collective-permute-start.24 = (bf16[2,256,512]{2,1,0:T(8,128)(2,1)}, bf16[2,256,512]{2,1,0:T(8,128)(2,1)S(1)}, u32[]{:S(2)}, u32[]{:S(2)}) collective-permute-start(bf16[2,256,512]{2,1,0:T(8,128)(2,1)} %collective-permute-done.20.refs_13_), channel_id=1, source_target_pairs={{0,1},{1,0},{2,3},{3,2},{4,5},{5,4},{6,7},{7,6},{8,9},{9,8},{10,11... | collective-permute-start | bytes 1572872 | tf_op jit(solution)/shard_map/ppermute | solution.py:333
  96.7 4.2 %collective-permute-start.23 = (bf16[2,256,512]{2,1,0:T(8,128)(2,1)}, bf16[2,256,512]{2,1,0:T(8,128)(2,1)S(1)}, u32[]{:S(2)}, u32[]{:S(2)}) collective-permute-start(bf16[2,256,512]{2,1,0:T(8,128)(2,1)} %copy-done.11), channel_id=1, source_target_pairs={{0,1},{1,0},{2,3},{3,2},{4,5},{5,4},{6,7},{7,6},{8,9},{9,8},{10,11... | collective-permute-start | bytes 1572872 | tf_op jit(solution)/shard_map/ppermute | solution.py:333
  (30 other events, 275.2 us)

commit v13 on v12

--- a/solution.py
+++ b/solution.py
@@ -393,7 +393,7 @@
         [out, pltpu.HBM((rows, hid), BF16)], [pltpu.SemaphoreType.DMA], {},
     )
     late = [(after(f3, hidden), ((14, 0),))]
-    late = [cross(after(w, hidden), parts) for w, parts in third] + late + [cross(*w) for w in late]
+    late = [cross(after(w, q1), parts) for w, parts in third[:1]] + [cross(after(w, hidden), parts) for w, parts in third[1:]] + late + [cross(*w) for w in late]
     return down_call(
         second_kernel, "down_second", [], [owner_rows, hidden], [product], late, [out], [], {2: 0}
     )[0]

time: 106 us -> 105 us (level)
  no operation moved by 1% of the time
where the time goes in v13:
time: 105 us; the launch traced here: 104 us
  waiting for transfers between devices  50.6 us (48%)
  starting transfers between devices  25.1 us (24%)
  Pallas kernels  20.4 us (19%)
  local copies, waits for them, and re-layouts  4.17 us (4%)
  other arithmetic  2.96 us (3%)
    ppermute x29, waiting for transfers between devices, swap(): return lax.ppermute(value, ALL, pairs)  50.6 us
    ppermute x29, starting transfers between devices, swap(): return lax.ppermute(value, ALL, pairs)  25.1 us
    pallas_call x2, Pallas kernels, down_call(): pl.pallas_call(functools.partial(kernel, pieces), in_specs=[SMEM] * len(l...  8.28 us
    pallas_call x1, Pallas kernels, partial_sums(): pl.pallas_call(functools.partial(partial_kernel, len(inputs), kinds), in_...  6.47 us
    pallas_call x1, Pallas kernels, normed_quarters(): pl.pallas_call(norm_kernel, in_specs=[SMEM, HBM, VMEM], out_specs=[HBM] *...  5.66 us
    unnamed x50, local copies, waits for them, and re-layouts  4.1 us
  transfers between devices with their start and end apart: 29, of which 19 were waited for; matrix products, arithmetic and copies ran while one was open for 1% of the time, Pallas kernels for 16%

profile of v13, /device:TPU:0, one launch (start us, length us, event | category | flops | bytes accessed | tf_op | source)
XLA Modules:
  0.0 104.1 jit_solution(13805029859002982855)
XLA Ops:
  0.0 1.9 %broadcast_select_fusion = bf16[1024,256]{1,0:T(8,128)(2,1)} fusion(bf16[1024,256]{1,0:T(8,128)(2,1)} %refs_4_.1, bf16[1024,256]{1,0:T(8,128)(2,1)} %refs_5_.1, pred[]{:T(512)S(6)} %eq.3), kind=kLoop, calls=%fused_computation | loop fusion | flops 262144 | bytes 1572865 | tf_op jit(solution)/shard_map/jit(_where)/select_n | solution.py:336
  1.9 4.0 %collective-permute-start.2 = (bf16[1024,256]{1,0:T(8,128)(2,1)}, bf16[1024,256]{1,0:T(8,128)(2,1)S(1)}, u32[]{:S(2)}, u32[]{:S(2)}) collective-permute-start(bf16[1024,256]{1,0:T(8,128)(2,1)} %broadcast_select_fusion), channel_id=1, source_target_pairs={{0,8},{1,9},{2,10},{3,11},{4,12},{5,13},{6,14},{7,15},{8,0},{9,1},... | collective-permute-start | bytes 1572872 | tf_op jit(solution)/shard_map/ppermute | solution.py:333
  5.9 1.6 %collective-permute-start.3 = (bf16[1024,256]{1,0:T(8,128)(2,1)}, bf16[1024,256]{1,0:T(8,128)(2,1)S(1)}, u32[]{:S(2)}, u32[]{:S(2)}) collective-permute-start(bf16[1024,256]{1,0:T(8,128)(2,1)} %broadcast_select_fusion), channel_id=1, source_target_pairs={{0,4},{1,5},{2,6},{3,7},{4,0},{5,1},{6,2},{7,3},{8,12},{9,13},{10,... | collective-permute-start | bytes 1572872 | tf_op jit(solution)/shard_map/ppermute | solution.py:333
  8.6 1.6 %collective-permute-start.5 = (bf16[1,256,512]{2,1,0:T(8,128)(2,1)S(1)}, bf16[1,256,512]{2,1,0:T(8,128)(2,1)S(1)}, u32[]{:S(2)}, u32[]{:S(2)}) collective-permute-start(bf16[1,256,512]{2,1,0:T(8,128)(2,1)S(1)} %select_bitcast_fusion.a_ref), channel_id=1, source_target_pairs={{0,2},{1,3},{2,0},{3,1},{4,6},{5,7},{6,4},{7,5},{8,10},{9,11},{10,... | collective-permute-start | bytes 786440 | tf_op jit(solution)/shard_map/ppermute | solution.py:333
  10.1 5.7 %norm_quarters.1 = (bf16[4,128,1024]{2,1,0:T(8,128)(2,1)}, bf16[4,128,1024]{2,1,0:T(8,128)(2,1)}, bf16[8,128,1024]{2,1,0:T(8,128)(2,1)}) custom-call(s32[16]{0:T(128)} %owner_ref.5, bf16[128,16384]{1,0:T(8,128)(2,1)} %tokens_ref.1, f32[1,16384]{1,0:T(1,128)} %bitcast.7), custom_call_target="tpu_custom_call" | custom-call | flops 12582912 | bytes 8388608 | tf_op jit(solution)/shard_map/norm_quarters/pallas_call | solution.py:97
  17.4 1.5 %collective-permute-start.7 = (bf16[1,256,512]{2,1,0:T(8,128)(2,1)S(1)}, bf16[1,256,512]{2,1,0:T(8,128)(2,1)S(1)}, u32[]{:S(2)}, u32[]{:S(2)}) collective-permute-start(bf16[1,256,512]{2,1,0:T(8,128)(2,1)S(1)} %collective-permute-done.5.b_ref.refs_6_), channel_id=1, source_target_pairs={{0,16},{1,17},{2,18},{3,19},{4,20},{5,21},{6,22},{7,23},{8,24},{9,... | collective-permute-start | bytes 786440 | tf_op jit(solution)/shard_map/ppermute | solution.py:333
  18.9 10.5 %collective-permute-done.2.refs_8_ = bf16[1024,256]{1,0:T(8,128)(2,1)S(1)} collective-permute-done((bf16[1024,256]{1,0:T(8,128)(2,1)}, bf16[1024,256]{1,0:T(8,128)(2,1)S(1)}, u32[]{:S(2)}, u32[]{:S(2)}) %collective-permute-start.2) | collective-permute-done | bytes 524320 | tf_op jit(solution)/shard_map/ppermute | solution.py:333
  29.7 1.6 %collective-permute-start.9 = (bf16[1024,256]{1,0:T(8,128)(2,1)S(1)}, bf16[1024,256]{1,0:T(8,128)(2,1)S(1)}, u32[]{:S(2)}, u32[]{:S(2)}) collective-permute-start(bf16[1024,256]{1,0:T(8,128)(2,1)S(1)} %collective-permute-done.2.refs_8_), channel_id=1, source_target_pairs={{0,16},{1,17},{2,18},{3,19},{4,20},{5,21},{6,22},{7,23},{8,24},{9,... | collective-permute-start | bytes 1572872 | tf_op jit(solution)/shard_map/ppermute | solution.py:333
  32.0 1.4 %collective-permute-start.6 = (bf16[1024,256]{1,0:T(8,128)(2,1)S(1)}, bf16[1024,256]{1,0:T(8,128)(2,1)S(1)}, u32[]{:S(2)}, u32[]{:S(2)}) collective-permute-start(bf16[1024,256]{1,0:T(8,128)(2,1)S(1)} %collective-permute-done.2.refs_8_), channel_id=1, source_target_pairs={{0,4},{1,5},{2,6},{3,7},{4,0},{5,1},{6,2},{7,3},{8,12},{9,13},{10,... | collective-permute-start | bytes 1572872 | tf_op jit(solution)/shard_map/ppermute | solution.py:333
  33.5 2.4 %collective-permute-start.12 = (bf16[1,256,1024]{2,1,0:T(8,128)(2,1)S(1)}, bf16[1,256,1024]{2,1,0:T(8,128)(2,1)}, u32[]{:S(2)}, u32[]{:S(2)}) collective-permute-start(bf16[1,256,1024]{2,1,0:T(8,128)(2,1)S(1)} %bitcast.6), channel_id=1, source_target_pairs={{0,8},{1,9},{2,10},{3,11},{4,12},{5,13},{6,14},{7,15},{8,0},{9,1},... | collective-permute-start | bytes 1572872 | tf_op jit(solution)/shard_map/ppermute | solution.py:333
  35.8 8.8 %collective-permute-done.9.refs_9_ = bf16[1024,256]{1,0:T(8,128)(2,1)S(1)} collective-permute-done((bf16[1024,256]{1,0:T(8,128)(2,1)S(1)}, bf16[1024,256]{1,0:T(8,128)(2,1)S(1)}, u32[]{:S(2)}, u32[]{:S(2)}) %collective-permute-start.9) | collective-permute-done | bytes 524320 | tf_op jit(solution)/shard_map/ppermute | solution.py:333
  44.6 9.2 %collective-permute-done.8.refs_7_ = bf16[1024,256]{1,0:T(8,128)(2,1)S(1)} collective-permute-done((bf16[1024,256]{1,0:T(8,128)(2,1)S(1)}, bf16[1024,256]{1,0:T(8,128)(2,1)S(1)}, u32[]{:S(2)}, u32[]{:S(2)}) %collective-permute-start.8) | collective-permute-done | bytes 524320 | tf_op jit(solution)/shard_map/ppermute | solution.py:333
  53.8 1.5 %collective-permute-done.6.refs_10_ = bf16[1024,256]{1,0:T(8,128)(2,1)S(1)} collective-permute-done((bf16[1024,256]{1,0:T(8,128)(2,1)S(1)}, bf16[1024,256]{1,0:T(8,128)(2,1)S(1)}, u32[]{:S(2)}, u32[]{:S(2)}) %collective-permute-start.6) | collective-permute-done | bytes 524320 | tf_op jit(solution)/shard_map/ppermute | solution.py:333
  56.9 1.9 %collective-permute-done.12.refs_8_ = bf16[1,256,1024]{2,1,0:T(8,128)(2,1)} collective-permute-done((bf16[1,256,1024]{2,1,0:T(8,128)(2,1)S(1)}, bf16[1,256,1024]{2,1,0:T(8,128)(2,1)}, u32[]{:S(2)}, u32[]{:S(2)}) %collective-permute-start.12) | collective-permute-done | bytes 524320 | tf_op jit(solution)/shard_map/ppermute | solution.py:333
  59.4 1.8 %collective-permute-done.14.refs_10_ = bf16[1,256,512]{2,1,0:T(8,128)(2,1)S(1)} collective-permute-done((bf16[1,256,512]{2,1,0:T(8,128)(2,1)S(1)}, bf16[1,256,512]{2,1,0:T(8,128)(2,1)S(1)}, u32[]{:S(2)}, u32[]{:S(2)}) %collective-permute-start.14) | collective-permute-done | bytes 262176 | tf_op jit(solution)/shard_map/ppermute | solution.py:333
  62.0 4.9 %collective-permute-done.10.refs_11_ = bf16[1024,256]{1,0:T(8,128)(2,1)S(1)} collective-permute-done((bf16[1024,256]{1,0:T(8,128)(2,1)S(1)}, bf16[1024,256]{1,0:T(8,128)(2,1)S(1)}, u32[]{:S(2)}, u32[]{:S(2)}) %collective-permute-start.10) | collective-permute-done | bytes 524320 | tf_op jit(solution)/shard_map/ppermute | solution.py:333
  68.7 1.2 %collective-permute-start.22 = (bf16[1,256,1024]{2,1,0:T(8,128)(2,1)}, bf16[1,256,1024]{2,1,0:T(8,128)(2,1)}, u32[]{:S(2)}, u32[]{:S(2)}) collective-permute-start(bf16[1,256,1024]{2,1,0:T(8,128)(2,1)} %collective-permute-done.12.refs_8_), channel_id=1, source_target_pairs={{0,4},{1,5},{2,6},{3,7},{4,0},{5,1},{6,2},{7,3},{8,12},{9,13},{10,... | collective-permute-start | bytes 1572872 | tf_op jit(solution)/shard_map/ppermute | solution.py:333
  70.9 1.5 %collective-permute-start.21 = (bf16[1,256,1024]{2,1,0:T(8,128)(2,1)}, bf16[1,256,1024]{2,1,0:T(8,128)(2,1)}, u32[]{:S(2)}, u32[]{:S(2)}) collective-permute-start(bf16[1,256,1024]{2,1,0:T(8,128)(2,1)} %collective-permute-done.12.refs_8_), channel_id=1, source_target_pairs={{0,2},{1,3},{2,0},{3,1},{4,6},{5,7},{6,4},{7,5},{8,10},{9,11},{10,... | collective-permute-start | bytes 1572872 | tf_op jit(solution)/shard_map/ppermute | solution.py:333
  73.4 6.5 %partial_sums.1 = (f32[128,512]{1,0:T(8,128)}, f32[128,512]{1,0:T(8,128)}, bf16[128,512]{1,0:T(8,128)(2,1)}, bf16[128,512]{1,0:T(8,128)(2,1)}) custom-call(bf16[4,128,1024]{2,1,0:T(8,128)(2,1)} %get-tuple-element.33.refs_0_, bf16[4,128,1024]{2,1,0:T(8,128)(2,1)} %copy-done.2, bf16[8,128,1024]{2,1,0:T(8,128)(2,1)} %copy-done.1, ...), custom_call_target="tpu_custom_call" | custom-call | flops 2147483648 | bytes 8388608 | tf_op jit(solution)/shard_map/partial_sums/pallas_call | solution.py:176
  83.3 2.7 %collective-permute-done.21.refs_14_ = bf16[1,256,1024]{2,1,0:T(8,128)(2,1)} collective-permute-done((bf16[1,256,1024]{2,1,0:T(8,128)(2,1)}, bf16[1,256,1024]{2,1,0:T(8,128)(2,1)}, u32[]{:S(2)}, u32[]{:S(2)}) %collective-permute-start.21) | collective-permute-done | bytes 524320 | tf_op jit(solution)/shard_map/ppermute | solution.py:333
  87.2 1.6 %collective-permute-done.18.refs_2_ = bf16[128,512]{1,0:T(8,128)(2,1)S(1)} collective-permute-done((bf16[128,512]{1,0:T(8,128)(2,1)}, bf16[128,512]{1,0:T(8,128)(2,1)S(1)}, u32[]{:S(2)}, u32[]{:S(2)}) %collective-permute-start.18) | collective-permute-done | bytes 131104 | tf_op jit(solution)/shard_map/ppermute | solution.py:333
  90.2 4.9 %down_first.1 = (bf16[128,16384]{1,0:T(8,128)(2,1)}, bf16[128,256]{1,0:T(8,128)(2,1)}) custom-call(s32[1]{0:T(128)S(6)} %copy.10.live_ref, s32[16]{0:T(128)} %owner_ref.5, f32[128,512]{1,0:T(8,128)} %get-tuple-element.45.refs_0_, f32[128,512]{1,0:T(8,128)} %copy-done.22, bf16[128,512]{1,0:T(8,128)(2,1)} %copy-done.23, bf16[128,512]{1,0:T(8,128)(2,1)} %copy-done.24, ...), custom_call_target="tpu_custom_call" | custom-call | flops 6710886400 | bytes 7864320 | tf_op jit(solution)/shard_map/down_first/pallas_call | solution.py:274
  96.7 1.3 %collective-permute-done.27.refs_4_ = bf16[1,256,1024]{2,1,0:T(8,128)(2,1)S(1)} collective-permute-done((bf16[1,256,1024]{2,1,0:T(8,128)(2,1)}, bf16[1,256,1024]{2,1,0:T(8,128)(2,1)S(1)}, u32[]{:S(2)}, u32[]{:S(2)}) %collective-permute-start.27) | collective-permute-done | bytes 524320 | tf_op jit(solution)/shard_map/ppermute | solution.py:333
  100.8 3.3 %down_second.1 = bf16[128,16384]{1,0:T(8,128)(2,1)} custom-call(s32[16]{0:T(128)} %owner_ref.5, bf16[128,256]{1,0:T(8,128)(2,1)} %get-tuple-element.53.hidden_ref, bf16[128,16384]{1,0:T(8,128)(2,1)} %get-tuple-element.54._, bf16[2,256,512]{2,1,0:T(8,128)(2,1)} %copy-done.14, bf16[2,256,512]{2,1,0:T(8,128)(2,1)} %copy-done.17, ...), custom_call_target="tpu_custom_call", output_to_operand_aliasing={{}: (2, {})} | custom-call | flops 4026531840 | bytes 4718592 | tf_op jit(solution)/shard_map/down_second/pallas_call | solution.py:274
  (92 shorter events, 20.0 us)
Async XLA Ops:
  1.9 27.5 %collective-permute-start.2 = (bf16[1024,256]{1,0:T(8,128)(2,1)}, bf16[1024,256]{1,0:T(8,128)(2,1)S(1)}, u32[]{:S(2)}, u32[]{:S(2)}) collective-permute-start(bf16[1024,256]{1,0:T(8,128)(2,1)} %broadcast_select_fusion), channel_id=1, source_target_pairs={{0,8},{1,9},{2,10},{3,11},{4,12},{5,13},{6,14},{7,15},{8,0},{9,1},... | collective-permute-start | bytes 1572872 | tf_op jit(solution)/shard_map/ppermute | solution.py:333
  5.9 23.7 %collective-permute-start.3 = (bf16[1024,256]{1,0:T(8,128)(2,1)}, bf16[1024,256]{1,0:T(8,128)(2,1)S(1)}, u32[]{:S(2)}, u32[]{:S(2)}) collective-permute-start(bf16[1024,256]{1,0:T(8,128)(2,1)} %broadcast_select_fusion), channel_id=1, source_target_pairs={{0,4},{1,5},{2,6},{3,7},{4,0},{5,1},{6,2},{7,3},{8,12},{9,13},{10,... | collective-permute-start | bytes 1572872 | tf_op jit(solution)/shard_map/ppermute | solution.py:333
  7.5 22.1 %collective-permute-start.4 = (bf16[1,256,1024]{2,1,0:T(8,128)(2,1)}, bf16[1,256,1024]{2,1,0:T(8,128)(2,1)}, u32[]{:S(2)}, u32[]{:S(2)}) collective-permute-start(bf16[1,256,1024]{2,1,0:T(8,128)(2,1)} %bitcast.4), channel_id=1, source_target_pairs={{0,1},{1,0},{2,3},{3,2},{4,5},{5,4},{6,7},{7,6},{8,9},{9,8},{10,11... | collective-permute-start | bytes 1572872 | tf_op jit(solution)/shard_map/ppermute | solution.py:333
  8.6 8.8 %collective-permute-start.5 = (bf16[1,256,512]{2,1,0:T(8,128)(2,1)S(1)}, bf16[1,256,512]{2,1,0:T(8,128)(2,1)S(1)}, u32[]{:S(2)}, u32[]{:S(2)}) collective-permute-start(bf16[1,256,512]{2,1,0:T(8,128)(2,1)S(1)} %select_bitcast_fusion.a_ref), channel_id=1, source_target_pairs={{0,2},{1,3},{2,0},{3,1},{4,6},{5,7},{6,4},{7,5},{8,10},{9,11},{10,... | collective-permute-start | bytes 786440 | tf_op jit(solution)/shard_map/ppermute | solution.py:333
  15.8 52.7 %collective-permute-start.1 = (bf16[8,128,1024]{2,1,0:T(8,128)(2,1)}, bf16[8,128,1024]{2,1,0:T(8,128)(2,1)S(1)}, u32[]{:S(2)}, u32[]{:S(2)}) collective-permute-start(bf16[8,128,1024]{2,1,0:T(8,128)(2,1)} %get-tuple-element.35), channel_id=1, source_target_pairs={{0,2},{1,3},{2,0},{3,1},{4,6},{5,7},{6,4},{7,5},{8,10},{9,11},{10,... | collective-permute-start | bytes 6291464 | tf_op jit(solution)/shard_map/ppermute | solution.py:333
  17.4 12.3 %collective-permute-start.7 = (bf16[1,256,512]{2,1,0:T(8,128)(2,1)S(1)}, bf16[1,256,512]{2,1,0:T(8,128)(2,1)S(1)}, u32[]{:S(2)}, u32[]{:S(2)}) collective-permute-start(bf16[1,256,512]{2,1,0:T(8,128)(2,1)S(1)} %collective-permute-done.5.b_ref.refs_6_), channel_id=1, source_target_pairs={{0,16},{1,17},{2,18},{3,19},{4,20},{5,21},{6,22},{7,23},{8,24},{9,... | collective-permute-start | bytes 786440 | tf_op jit(solution)/shard_map/ppermute | solution.py:333
  29.7 14.9 %collective-permute-start.9 = (bf16[1024,256]{1,0:T(8,128)(2,1)S(1)}, bf16[1024,256]{1,0:T(8,128)(2,1)S(1)}, u32[]{:S(2)}, u32[]{:S(2)}) collective-permute-start(bf16[1024,256]{1,0:T(8,128)(2,1)S(1)} %collective-permute-done.2.refs_8_), channel_id=1, source_target_pairs={{0,16},{1,17},{2,18},{3,19},{4,20},{5,21},{6,22},{7,23},{8,24},{9,... | collective-permute-start | bytes 1572872 | tf_op jit(solution)/shard_map/ppermute | solution.py:333
  31.3 22.5 %collective-permute-start.8 = (bf16[1024,256]{1,0:T(8,128)(2,1)S(1)}, bf16[1024,256]{1,0:T(8,128)(2,1)S(1)}, u32[]{:S(2)}, u32[]{:S(2)}) collective-permute-start(bf16[1024,256]{1,0:T(8,128)(2,1)S(1)} %collective-permute-done.3.refs_6_), channel_id=1, source_target_pairs={{0,16},{1,17},{2,18},{3,19},{4,20},{5,21},{6,22},{7,23},{8,24},{9,... | collective-permute-start | bytes 1572872 | tf_op jit(solution)/shard_map/ppermute | solution.py:333
  32.0 23.3 %collective-permute-start.6 = (bf16[1024,256]{1,0:T(8,128)(2,1)S(1)}, bf16[1024,256]{1,0:T(8,128)(2,1)S(1)}, u32[]{:S(2)}, u32[]{:S(2)}) collective-permute-start(bf16[1024,256]{1,0:T(8,128)(2,1)S(1)} %collective-permute-done.2.refs_8_), channel_id=1, source_target_pairs={{0,4},{1,5},{2,6},{3,7},{4,0},{5,1},{6,2},{7,3},{8,12},{9,13},{10,... | collective-permute-start | bytes 1572872 | tf_op jit(solution)/shard_map/ppermute | solution.py:333
  33.5 25.4 %collective-permute-start.12 = (bf16[1,256,1024]{2,1,0:T(8,128)(2,1)S(1)}, bf16[1,256,1024]{2,1,0:T(8,128)(2,1)}, u32[]{:S(2)}, u32[]{:S(2)}) collective-permute-start(bf16[1,256,1024]{2,1,0:T(8,128)(2,1)S(1)} %bitcast.6), channel_id=1, source_target_pairs={{0,8},{1,9},{2,10},{3,11},{4,12},{5,13},{6,14},{7,15},{8,0},{9,1},... | collective-permute-start | bytes 1572872 | tf_op jit(solution)/shard_map/ppermute | solution.py:333
  44.6 14.3 %collective-permute-start.13 = (bf16[1,256,512]{2,1,0:T(8,128)(2,1)S(1)}, bf16[1,256,512]{2,1,0:T(8,128)(2,1)S(1)}, u32[]{:S(2)}, u32[]{:S(2)}) collective-permute-start(bf16[1,256,512]{2,1,0:T(8,128)(2,1)S(1)} %collective-permute-done.5.b_ref.refs_6_), channel_id=1, source_target_pairs={{0,1},{1,0},{2,3},{3,2},{4,5},{5,4},{6,7},{7,6},{8,9},{9,8},{10,11... | collective-permute-start | bytes 786440 | tf_op jit(solution)/shard_map/ppermute | solution.py:333
  55.4 11.5 %collective-permute-start.10 = (bf16[1024,256]{1,0:T(8,128)(2,1)S(1)}, bf16[1024,256]{1,0:T(8,128)(2,1)S(1)}, u32[]{:S(2)}, u32[]{:S(2)}) collective-permute-start(bf16[1024,256]{1,0:T(8,128)(2,1)S(1)} %collective-permute-done.6.refs_10_), channel_id=1, source_target_pairs={{0,16},{1,17},{2,18},{3,19},{4,20},{5,21},{6,22},{7,23},{8,24},{9,... | collective-permute-start | bytes 1572872 | tf_op jit(solution)/shard_map/ppermute | solution.py:333
  56.4 11.2 %collective-permute-start.11 = (bf16[2,256,512]{2,1,0:T(8,128)(2,1)S(1)}, bf16[2,256,512]{2,1,0:T(8,128)(2,1)S(1)}, u32[]{:S(2)}, u32[]{:S(2)}) collective-permute-start(bf16[2,256,512]{2,1,0:T(8,128)(2,1)S(1)} %stack_halves.1), channel_id=1, source_target_pairs={{0,4},{1,5},{2,6},{3,7},{4,0},{5,1},{6,2},{7,3},{8,12},{9,13},{10,... | collective-permute-start | bytes 1572872 | tf_op jit(solution)/shard_map/ppermute | solution.py:333
  58.9 8.7 %collective-permute-start.15 = (bf16[1,256,1024]{2,1,0:T(8,128)(2,1)}, bf16[1,256,1024]{2,1,0:T(8,128)(2,1)S(1)}, u32[]{:S(2)}, u32[]{:S(2)}) collective-permute-start(bf16[1,256,1024]{2,1,0:T(8,128)(2,1)} %collective-permute-done.12.refs_8_), channel_id=1, source_target_pairs={{0,1},{1,0},{2,3},{3,2},{4,5},{5,4},{6,7},{7,6},{8,9},{9,8},{10,11... | collective-permute-start | bytes 1572872 | tf_op jit(solution)/shard_map/ppermute | solution.py:333
  61.9 10.5 %collective-permute-start = (bf16[4,128,1024]{2,1,0:T(8,128)(2,1)S(1)}, bf16[4,128,1024]{2,1,0:T(8,128)(2,1)S(1)}, u32[]{:S(2)}, u32[]{:S(2)}) collective-permute-start(bf16[4,128,1024]{2,1,0:T(8,128)(2,1)S(1)} %copy-done.10), channel_id=1, source_target_pairs={{0,1},{1,0},{2,3},{3,2},{4,5},{5,4},{6,7},{7,6},{8,9},{9,8},{10,11... | collective-permute-start | bytes 3145736 | tf_op jit(solution)/shard_map/ppermute | solution.py:333
  68.6 3.8 %collective-permute-start.16 = (bf16[4,128,1024]{2,1,0:T(8,128)(2,1)S(1)}, bf16[4,128,1024]{2,1,0:T(8,128)(2,1)}, u32[]{:S(2)}, u32[]{:S(2)}) collective-permute-start(bf16[4,128,1024]{2,1,0:T(8,128)(2,1)S(1)} %slice.11), channel_id=1, source_target_pairs={{0,1},{1,0},{2,3},{3,2},{4,5},{5,4},{6,7},{7,6},{8,9},{9,8},{10,11... | collective-permute-start | bytes 3145736 | tf_op jit(solution)/shard_map/ppermute | solution.py:333
  68.7 14.7 %collective-permute-start.22 = (bf16[1,256,1024]{2,1,0:T(8,128)(2,1)}, bf16[1,256,1024]{2,1,0:T(8,128)(2,1)}, u32[]{:S(2)}, u32[]{:S(2)}) collective-permute-start(bf16[1,256,1024]{2,1,0:T(8,128)(2,1)} %collective-permute-done.12.refs_8_), channel_id=1, source_target_pairs={{0,4},{1,5},{2,6},{3,7},{4,0},{5,1},{6,2},{7,3},{8,12},{9,13},{10,... | collective-permute-start | bytes 1572872 | tf_op jit(solution)/shard_map/ppermute | solution.py:333
  69.9 17.3 %collective-permute-start.20 = (bf16[2,256,512]{2,1,0:T(8,128)(2,1)S(1)}, bf16[2,256,512]{2,1,0:T(8,128)(2,1)}, u32[]{:S(2)}, u32[]{:S(2)}) collective-permute-start(bf16[2,256,512]{2,1,0:T(8,128)(2,1)S(1)} %collective-permute-done.11.refs_12_), channel_id=1, source_target_pairs={{0,16},{1,17},{2,18},{3,19},{4,20},{5,21},{6,22},{7,23},{8,24},{9,... | collective-permute-start | bytes 1572872 | tf_op jit(solution)/shard_map/ppermute | solution.py:333
  70.9 15.1 %collective-permute-start.21 = (bf16[1,256,1024]{2,1,0:T(8,128)(2,1)}, bf16[1,256,1024]{2,1,0:T(8,128)(2,1)}, u32[]{:S(2)}, u32[]{:S(2)}) collective-permute-start(bf16[1,256,1024]{2,1,0:T(8,128)(2,1)} %collective-permute-done.12.refs_8_), channel_id=1, source_target_pairs={{0,2},{1,3},{2,0},{3,1},{4,6},{5,7},{6,4},{7,5},{8,10},{9,11},{10,... | collective-permute-start | bytes 1572872 | tf_op jit(solution)/shard_map/ppermute | solution.py:333
  79.9 8.8 %collective-permute-start.18 = (bf16[128,512]{1,0:T(8,128)(2,1)}, bf16[128,512]{1,0:T(8,128)(2,1)S(1)}, u32[]{:S(2)}, u32[]{:S(2)}) collective-permute-start(bf16[128,512]{1,0:T(8,128)(2,1)} %get-tuple-element.47), channel_id=1, source_target_pairs={{0,2},{1,3},{2,0},{3,1},{4,6},{5,7},{6,4},{7,5},{8,10},{9,11},{10,... | collective-permute-start | bytes 393224 | tf_op jit(solution)/shard_map/ppermute | solution.py:333
  81.7 7.9 %collective-permute-start.19 = (bf16[128,512]{1,0:T(8,128)(2,1)}, bf16[128,512]{1,0:T(8,128)(2,1)S(1)}, u32[]{:S(2)}, u32[]{:S(2)}) collective-permute-start(bf16[128,512]{1,0:T(8,128)(2,1)} %get-tuple-element.49), channel_id=1, source_target_pairs={{0,3},{1,2},{2,1},{3,0},{4,7},{5,6},{6,5},{7,4},{8,11},{9,10},{10,... | collective-permute-start | bytes 393224 | tf_op jit(solution)/shard_map/ppermute | solution.py:333
  86.0 12.0 %collective-permute-start.27 = (bf16[1,256,1024]{2,1,0:T(8,128)(2,1)}, bf16[1,256,1024]{2,1,0:T(8,128)(2,1)S(1)}, u32[]{:S(2)}, u32[]{:S(2)}) collective-permute-start(bf16[1,256,1024]{2,1,0:T(8,128)(2,1)} %collective-permute-done.21.refs_14_), channel_id=1, source_target_pairs={{0,4},{1,5},{2,6},{3,7},{4,0},{5,1},{6,2},{7,3},{8,12},{9,13},{10,... | collective-permute-start | bytes 1572872 | tf_op jit(solution)/shard_map/ppermute | solution.py:333
  87.1 10.8 %collective-permute-start.23 = (bf16[2,256,512]{2,1,0:T(8,128)(2,1)S(1)}, bf16[2,256,512]{2,1,0:T(8,128)(2,1)S(1)}, u32[]{:S(2)}, u32[]{:S(2)}) collective-permute-start(bf16[2,256,512]{2,1,0:T(8,128)(2,1)S(1)} %collective-permute-done.11.refs_12_), channel_id=1, source_target_pairs={{0,1},{1,0},{2,3},{3,2},{4,5},{5,4},{6,7},{7,6},{8,9},{9,8},{10,11... | collective-permute-start | bytes 1572872 | tf_op jit(solution)/shard_map/ppermute | solution.py:333
  96.3 3.2 %collective-permute-start.24 = (bf16[2,256,512]{2,1,0:T(8,128)(2,1)}, bf16[2,256,512]{2,1,0:T(8,128)(2,1)S(1)}, u32[]{:S(2)}, u32[]{:S(2)}) collective-permute-start(bf16[2,256,512]{2,1,0:T(8,128)(2,1)} %collective-permute-done.20.refs_13_), channel_id=1, source_target_pairs={{0,1},{1,0},{2,3},{3,2},{4,5},{5,4},{6,7},{7,6},{8,9},{9,8},{10,11... | collective-permute-start | bytes 1572872 | tf_op jit(solution)/shard_map/ppermute | solution.py:333
  (30 other events, 271.7 us)
